TPU v7x, 32 devices: a whole 2x2x4 slice. The times are simulated.
32 devices in a mesh: bucket: 4 (over z), blk: 8 (over y, x, core).
Axes of the slice: x: 2, y: 2, z: 4, core: 2. Of those that a mesh axis runs over, the one named last changes fastest.
Arguments:
- residual_in: bfloat16 [5120, 767], P(('bucket', 'blk'))
- out_cotangent: bfloat16 [5120, 767], P(('bucket', 'blk')), may hold values from -6 to 6
- first_gain: float32 [768], replicated, may hold values from 0.1 to 1.9
- input_weight: bfloat16 [768, 2304], replicated, may hold values from -0.21875 to 0.21875
- query_bias: float32 [768], replicated, may hold values from -3 to 3
- value_bias: float32 [768], replicated, may hold values from -0.3 to 0.3
- output_weight: bfloat16 [768, 767], replicated, may hold values from -1.25 to 1.25
- output_bias: float32 [767], replicated, may hold values from -1.8 to 1.8
- second_gain: float32 [768], replicated, may hold values from 0.1 to 1.9
- up_weight: bfloat16 [768, 3072], replicated, may hold values from -0.21875 to 0.21875
- up_bias: float32 [3072], replicated, may hold values from -1.8 to 1.8
- down_weight: bfloat16 [3072, 767], replicated, may hold values from -0.109375 to 0.109375
- down_bias: float32 [767], replicated, may hold values from -1.8 to 1.8
- lengths: int32 [4, 2], replicated, may hold values from 128 to 1152, as said below
- offsets: int32 [4, 2], P('bucket'), may hold values from 0 to 1152, as said below
- span_order: int32 [16], replicated, may hold values from 0 to 15, as said below
Outputs:
- residual_out: bfloat16 [5120, 767], P(('bucket', 'blk'))
- residual_grad: bfloat16 [5120, 767], P(('bucket', 'blk'))
- first_gain_grad: float32 [768], replicated
- input_weight_grad: float32 [768, 2304], P(('bucket', 'blk'))
- query_bias_grad: float32 [768], replicated
- value_bias_grad: float32 [768], replicated
- output_weight_grad: float32 [768, 767], P(('bucket', 'blk'))
- output_bias_grad: float32 [767], replicated
- second_gain_grad: float32 [768], replicated
- up_weight_grad: float32 [768, 3072], P(('bucket', 'blk'))
- up_bias_grad: float32 [3072], replicated
- down_weight_grad: float32 [3072, 767], P(('bucket', 'blk'))
- down_bias_grad: float32 [767], replicated
- mean_norms: float32 [2], replicated
Inputs may be any that keep to these rules, and one draw needn't show every extreme that they name: Bucket b holds two sequences: sequence s covers positions offsets[b,s] to offsets[b,s] + lengths[b,s] - 1 of the bucket's 1280 positions; lengths[b,0] >= 1024; the two sequences don't intersect; other positions are padding. offsets[b,0] = 0 and offsets[b,1] >= lengths[b,0]. Each of the 16 blocks of 80 positions appears once; for device i of blk, span_order[2i] < 8 and span_order[2i+1] = 15 - span_order[2i].
All inputs are finite; a program needn't handle non-finite values.
Results may differ from a plain program's by a relative error of at most 0.014.
Values may be sent and summed in bfloat16 or wider, within the bound.
No kernel may reach another device: no remote copies, remote signals or barrier semaphores. Data moves between devices by JAX's collectives and lax.ppermute only.
A program may use at most 256 MiB of HBM per device.

v0:
```python
import jax
import jax.numpy as jnp
from jax import lax
from jax.sharding import PartitionSpec as P

D = 768
HEADS = 12
HEAD_DIM = 64


epsilon = 1e-05
masked_value = -1e30


def center_norm(resid, gain):
    full = jnp.concatenate([resid, -jnp.sum(resid, axis=1, keepdims=True)], axis=1)
    root = jnp.sqrt(jnp.mean(full * full, axis=1, keepdims=True) + epsilon)
    return (full / root * gain, root[:, 0])


def gelu_tanh(inputs):
    return jax.nn.gelu(inputs, approximate=True)


def heads_of(block):
    return block.reshape(block.shape[0], HEADS, HEAD_DIM)


def places_of(span_order, begin, count, half_rows):
    spans = lax.dynamic_slice_in_dim(span_order, begin // half_rows, count // half_rows)
    inner = jnp.arange(half_rows, dtype=jnp.int32)
    return (spans[:, None] * half_rows + inner[None, :]).reshape(count)


def documents_of(places, lengths, offsets):
    first_in = (places >= offsets[0, 0]) & (places < offsets[0, 0] + lengths[0, 0])
    second_in = (places >= offsets[0, 1]) & (places < offsets[0, 1] + lengths[0, 1])
    return jnp.where(first_in, 0, jnp.where(second_in, 1, -1)).astype(jnp.int32)


def allowed_of(query_places, query_docs, key_places, key_docs):
    same = (query_docs[:, None] == key_docs[None, :]) & (query_docs[:, None] >= 0)
    return (same & (key_places[None, :] <= query_places[:, None]))[None]


def block_shape(count, unit):
    shards = count // unit
    width = max(1, 1024 // unit)
    while shards % width != 0:
        width = width - 1
    return (shards // width, width * unit)


def body(
    residual_in,
    out_cotangent,
    first_gain,
    input_weight,
    query_bias,
    value_bias,
    output_weight,
    output_bias,
    second_gain,
    up_weight,
    up_bias,
    down_weight,
    down_bias,
    lengths,
    offsets,
    span_order,
):
    rows = residual_in.shape[0]
    half_rows = rows // 2
    score_scale = HEAD_DIM ** (-0.5)
    index = lax.axis_index("blk")
    bucket_index = lax.axis_index("bucket")
    own_lengths = lax.dynamic_slice_in_dim(lengths, bucket_index, 1, 0)
    valid_count = jnp.sum(lengths.astype(jnp.float32))
    query_places = places_of(span_order, index * rows, rows, half_rows)
    query_docs = documents_of(query_places, own_lengths, offsets)
    valid = (query_docs >= 0).astype(jnp.float32)
    resid = residual_in.astype(jnp.float32)
    normed, first_back, first_root = jax.vjp(center_norm, resid, first_gain, has_aux=True)
    hidden_in = normed.astype(jnp.bfloat16)
    projected = jnp.dot(hidden_in, input_weight, preferred_element_type=jnp.float32)
    query = (projected[:, :D] + query_bias).astype(jnp.bfloat16)
    keys = projected[:, D : 2 * D].astype(jnp.bfloat16)
    values = (projected[:, 2 * D :] + value_bias).astype(jnp.bfloat16)
    query_heads = heads_of(query)
    key_heads = heads_of(keys)
    value_heads = heads_of(values)
    initial = (
        jnp.full((HEADS, rows), masked_value, jnp.float32),
        jnp.zeros((HEADS, rows), jnp.float32),
        jnp.zeros((HEADS, rows, HEAD_DIM), jnp.float32),
    )
    state = initial
    key_piece = lax.all_gather(keys, "blk", axis=0, tiled=True)
    value_piece = lax.all_gather(values, "blk", axis=0, tiled=True)
    count = key_piece.shape[0]
    number, width = block_shape(count, rows)
    key_places = places_of(span_order, jnp.int32(0), count, half_rows)
    key_docs = documents_of(key_places, own_lengths, offsets)

    def forward_advance(state, parts):
        key_block, value_block, places_block, docs_block = parts
        peak, total, summed = state
        scores = (
            jnp.einsum(
                "qhd,khd->hqk", query_heads, heads_of(key_block), preferred_element_type=jnp.float32
            )
            * score_scale
        )
        allowed = allowed_of(query_places, query_docs, places_block, docs_block)
        masked = jnp.where(allowed, scores, masked_value)
        new_peak = jnp.maximum(peak, jnp.max(masked, axis=2))
        decay = jnp.exp(peak - new_peak)
        weights = jnp.where(allowed, jnp.exp(masked - new_peak[:, :, None]), 0.0)
        total = total * decay + jnp.sum(weights, axis=2)
        summed = summed * decay[:, :, None] + jnp.einsum(
            "hqk,khd->hqd",
            weights.astype(jnp.bfloat16),
            heads_of(value_block),
            preferred_element_type=jnp.float32,
        )
        return ((new_peak, total, summed), None)

    state, _ = lax.scan(
        forward_advance,
        state,
        (
            key_piece.reshape(number, width, D),
            value_piece.reshape(number, width, D),
            key_places.reshape(number, width),
            key_docs.reshape(number, width),
        ),
    )
    peak, total, summed = state
    denominator = total + 1.0 - valid[None, :]
    attended = summed / denominator[:, :, None]
    log_total = peak + jnp.log(denominator)
    mixed = attended.transpose(1, 0, 2).reshape(rows, D).astype(jnp.bfloat16)
    branch = jnp.dot(mixed, output_weight, preferred_element_type=jnp.float32) + output_bias
    middle = resid + branch
    normed_two, second_back, second_root = jax.vjp(center_norm, middle, second_gain, has_aux=True)
    hidden_two = normed_two.astype(jnp.bfloat16)
    upward = jnp.dot(hidden_two, up_weight, preferred_element_type=jnp.float32) + up_bias
    active_float, gelu_back = jax.vjp(gelu_tanh, upward)
    active = active_float.astype(jnp.bfloat16)
    closing = jnp.dot(active, down_weight, preferred_element_type=jnp.float32) + down_bias
    residual_out = (middle + closing).astype(jnp.bfloat16)
    stat_sums = jnp.stack([jnp.sum(valid * first_root), jnp.sum(valid * second_root)])
    stat_sums = lax.psum(stat_sums, ("bucket", "blk"))
    cotangent = out_cotangent.astype(jnp.float32)
    down_grad = jnp.einsum("rf,rc->fc", active, out_cotangent, preferred_element_type=jnp.float32)
    down_bias_grad = jnp.sum(cotangent, axis=0)
    active_grad = jnp.einsum(
        "rc,fc->rf", out_cotangent, down_weight, preferred_element_type=jnp.float32
    )
    (upward_float,) = gelu_back(active_grad)
    upward_grad = upward_float.astype(jnp.bfloat16)
    up_grad = jnp.einsum("rd,rf->df", hidden_two, upward_grad, preferred_element_type=jnp.float32)
    up_bias_grad = jnp.sum(upward_grad.astype(jnp.float32), axis=0)
    hidden_two_grad = jnp.einsum(
        "rf,df->rd", upward_grad, up_weight, preferred_element_type=jnp.float32
    )
    middle_part, second_gain_grad = second_back(hidden_two_grad)
    middle_grad = cotangent + middle_part
    branch_grad = middle_grad.astype(jnp.bfloat16)
    output_grad = jnp.einsum("rd,rc->dc", mixed, branch_grad, preferred_element_type=jnp.float32)
    output_bias_grad = jnp.sum(branch_grad.astype(jnp.float32), axis=0)
    attended_grad = jnp.einsum(
        "rc,dc->rd", branch_grad, output_weight, preferred_element_type=jnp.float32
    ).astype(jnp.bfloat16)
    grad_heads = heads_of(attended_grad)
    delta = jnp.einsum("rhd,hrd->hr", grad_heads.astype(jnp.float32), attended)
    query_zero = jnp.zeros((rows, HEADS, HEAD_DIM), jnp.float32)
    accum = query_zero
    key_piece = lax.all_gather(keys, "blk", axis=0, tiled=True)
    value_piece = lax.all_gather(values, "blk", axis=0, tiled=True)
    count = key_piece.shape[0]
    number, width = block_shape(count, rows)
    key_places = places_of(span_order, jnp.int32(0), count, half_rows)
    key_docs = documents_of(key_places, own_lengths, offsets)

    def query_advance(accum, parts):
        key_block, value_block, places_block, docs_block = parts
        block_keys = heads_of(key_block)
        scores = (
            jnp.einsum("qhd,khd->hqk", query_heads, block_keys, preferred_element_type=jnp.float32)
            * score_scale
        )
        allowed = allowed_of(query_places, query_docs, places_block, docs_block)
        chance = jnp.where(
            allowed, jnp.exp(jnp.where(allowed, scores, masked_value) - log_total[:, :, None]), 0.0
        )
        push = jnp.einsum(
            "qhd,khd->hqk", grad_heads, heads_of(value_block), preferred_element_type=jnp.float32
        )
        slope = (chance * (push - delta[:, :, None])).astype(jnp.bfloat16)
        accum = (
            accum
            + jnp.einsum("hqk,khd->qhd", slope, block_keys, preferred_element_type=jnp.float32)
            * score_scale
        )
        return (accum, None)

    accum, _ = lax.scan(
        query_advance,
        accum,
        (
            key_piece.reshape(number, width, D),
            value_piece.reshape(number, width, D),
            key_places.reshape(number, width),
            key_docs.reshape(number, width),
        ),
    )
    log_all, delta_all = (
        lax.all_gather(log_total.T, "blk", axis=0, tiled=True),
        lax.all_gather(delta.T, "blk", axis=0, tiled=True),
    )
    key_zero = jnp.zeros((rows, HEADS, HEAD_DIM), jnp.float32)
    state = (key_zero, key_zero)
    begin = jnp.int32(0)
    query_piece = lax.all_gather(query, "blk", axis=0, tiled=True)
    grad_piece = lax.all_gather(attended_grad, "blk", axis=0, tiled=True)
    count = query_piece.shape[0]
    number, width = block_shape(count, rows)
    piece_places = places_of(span_order, begin, count, half_rows)
    piece_docs = documents_of(piece_places, own_lengths, offsets)
    piece_log = lax.dynamic_slice_in_dim(log_all, begin, count, 0)
    piece_delta = lax.dynamic_slice_in_dim(delta_all, begin, count, 0)

    def key_advance(state, parts):
        query_block, grad_block, places_block, docs_block, log_block, delta_block = parts
        key_sum, value_sum = state
        block_query = heads_of(query_block)
        block_grad = heads_of(grad_block)
        scores = (
            jnp.einsum("qhd,khd->hqk", block_query, key_heads, preferred_element_type=jnp.float32)
            * score_scale
        )
        allowed = allowed_of(places_block, docs_block, query_places, query_docs)
        chance = jnp.where(
            allowed,
            jnp.exp(jnp.where(allowed, scores, masked_value) - log_block.T[:, :, None]),
            0.0,
        )
        value_sum = value_sum + jnp.einsum(
            "hqk,qhd->khd",
            chance.astype(jnp.bfloat16),
            block_grad,
            preferred_element_type=jnp.float32,
        )
        push = jnp.einsum(
            "qhd,khd->hqk", block_grad, value_heads, preferred_element_type=jnp.float32
        )
        slope = (chance * (push - delta_block.T[:, :, None])).astype(jnp.bfloat16)
        key_sum = (
            key_sum
            + jnp.einsum("hqk,qhd->khd", slope, block_query, preferred_element_type=jnp.float32)
            * score_scale
        )
        return ((key_sum, value_sum), None)

    state, _ = lax.scan(
        key_advance,
        state,
        (
            query_piece.reshape(number, width, D),
            grad_piece.reshape(number, width, D),
            piece_places.reshape(number, width),
            piece_docs.reshape(number, width),
            piece_log.reshape(number, width, HEADS),
            piece_delta.reshape(number, width, HEADS),
        ),
    )
    key_sum, value_sum = state
    query_low = accum.reshape(rows, D).astype(jnp.bfloat16)
    key_low = key_sum.reshape(rows, D).astype(jnp.bfloat16)
    value_low = value_sum.reshape(rows, D).astype(jnp.bfloat16)
    projected_grad = jnp.concatenate([query_low, key_low, value_low], axis=1)
    input_grad = jnp.einsum(
        "rd,re->de", hidden_in, projected_grad, preferred_element_type=jnp.float32
    )
    query_bias_grad = jnp.sum(query_low.astype(jnp.float32), axis=0)
    value_bias_grad = jnp.sum(value_low.astype(jnp.float32), axis=0)
    hidden_in_grad = jnp.einsum(
        "re,de->rd", projected_grad, input_weight, preferred_element_type=jnp.float32
    )
    resid_part, first_gain_grad = first_back(hidden_in_grad)
    residual_grad = (middle_grad + resid_part).astype(jnp.bfloat16)
    input_part, output_part, up_part, down_part = (
        lax.psum_scatter(input_grad, ("bucket", "blk"), scatter_dimension=0, tiled=True),
        lax.psum_scatter(output_grad, ("bucket", "blk"), scatter_dimension=0, tiled=True),
        lax.psum_scatter(up_grad, ("bucket", "blk"), scatter_dimension=0, tiled=True),
        lax.psum_scatter(down_grad, ("bucket", "blk"), scatter_dimension=0, tiled=True),
    )
    (
        first_sum,
        query_sum_bias,
        value_sum_bias,
        output_sum_bias,
        second_sum,
        up_sum_bias,
        down_sum_bias,
    ) = lax.psum(
        (
            first_gain_grad,
            query_bias_grad,
            value_bias_grad,
            output_bias_grad,
            second_gain_grad,
            up_bias_grad,
            down_bias_grad,
        ),
        ("bucket", "blk"),
    )
    mean_norms = stat_sums / valid_count
    return (
        residual_out,
        residual_grad,
        first_sum,
        input_part,
        query_sum_bias,
        value_sum_bias,
        output_part,
        output_sum_bias,
        second_sum,
        up_part,
        up_sum_bias,
        down_part,
        down_sum_bias,
        mean_norms,
    )


def solution(mesh):
    placed = (
        P(("bucket", "blk"), None),
        P(("bucket", "blk"), None),
        P(),
        P(),
        P(),
        P(),
        P(),
        P(),
        P(),
        P(),
        P(),
        P(),
        P(),
        P(),
        P("bucket", None),
        P(),
    )
    return jax.shard_map(
        body,
        mesh=mesh,
        in_specs=placed,
        out_specs=(
            P(("bucket", "blk"), None),
            P(("bucket", "blk"), None),
            P(),
            P(("bucket", "blk"), None),
            P(),
            P(),
            P(("bucket", "blk"), None),
            P(),
            P(),
            P(("bucket", "blk"), None),
            P(),
            P(("bucket", "blk"), None),
            P(),
            P(),
        ),
        check_vma=False,
    )
```

profile of v0, /device:TPU:0, one launch (start us, length us, event | category | flops | bytes accessed | tf_op | source)
XLA Modules:
  0.0 704.5 jit_solution(15844986021589594006)
XLA Ops:
  35.0 2.6 and_select_fusion.9
  40.1 2.6 and_select_fusion.7
  42.7 5.5 fusion.105
  48.3 4.0 copy.59
  52.2 24.6 %all-gather.7.cloned.1.call-done = bf16[1280,768]{1,0:T(8,128)(2,1)} async-done(((bf16[160,768]{1,0:T(8,128)(2,1)}), bf16[1280,768]{1,0:T(8,128)(2,1)}) %all-gather.7.cloned.1.call-update) | async-done | bytes 1966096 | tf_op jit(solution)/shard_map/all_gather | solution.py:98
  76.8 4.0 copy.58
  80.8 48.1 %while.45 = (s32[]{:T(128)}, f32[12,160]{1,0:T(8,128)S(1)}, f32[12,160]{1,0:T(8,128)}, f32[12,160,64]{1,2,0:T(8,128)}, s32[2,640]{1,0:T(2,128)}, /*index=5*/s32[...) while((s32[]{:T(128)}, f32[12,160]{1,0:T(8,128)S(1)}, ...), condition=%wide.region_5.6_spmd.clone.clone.clone, body=%wide.region_2.5_spmd.clone.clone.clone.sunk | while | flops 331336640 | bytes 43951400 | solution.py:128
  80.8 2.6 and_select_fusion.13
  89.5 2.7 constant_dynamic-slice_fusion.13
  92.2 3.8 fusion.167
  96.7 3.6 fusion.168
  101.0 3.7 fusion.170
  104.7 2.6 and_select_fusion.13
  113.4 2.7 constant_dynamic-slice_fusion.13
  116.1 3.8 fusion.167
  120.7 3.6 fusion.168
  124.9 3.9 fusion.170
  139.2 7.2 %convert_reduce_fusion = (f32[3072]{0:T(1024)}, bf16[160,3072]{1,0:T(8,128)(2,1)S(1)}, f32[160,3072]{1,0:T(8,128)}) fusion(f32[160,3072]{1,0:T(8,128)} %fusion.105, f32[3072]{0:T(1024)} %param.32, bf16[768,3072]{1,0:T(8,128)(2,1)} %param.31, f32[768]{0:T(1024)S(1)} %copy-done.31, f32[160]{0:T(256)S(1)} %get-tuple-element.885, f32[160,1]{1,0:T(8,128)} %copy.60, ...), kind=kOutput, calls=%fused_computation.97 | convolution fusion | flops 766768128 | bytes 10153600 | tf_op jit(solution)/shard_map/dot_general | solution.py:147
  146.4 5.2 multiply_reduce_fusion
  155.3 2.9 fusion.106
  158.5 7.1 %fusion.97 = f32[3072,767]{1,0:T(8,128)} fusion(bf16[160,767]{1,0:T(8,128)(2,1)} %param.23, f32[160,3072]{1,0:T(8,128)} %get-tuple-element.893), kind=kOutput, calls=%fused_computation.175 | convolution fusion | flops 758415360 | bytes 11636416 | tf_op jit(solution)/shard_map/rf,rc->fc/dot_general | solution.py:155
  165.6 6.5 fusion.89
  179.9 9.2 %all-gather.1 = f32[8,160,12]{1,2,0:T(8,128)S(1)} all-gather(f32[1,160,12]{1,2,0:T(8,128)S(1)} %bitcast.224), channel_id=1, replica_groups=mesh['bucket'=4,'blk'=8] {'blk'}, dimensions={0}, use_global_device_ids=true | all-gather | bytes 69120 | tf_op jit(solution)/shard_map/all_gather | solution.py:220
  191.5 8.4 %all-gather = f32[8,160,12]{1,2,0:T(8,128)S(1)} all-gather(f32[1,160,12]{1,2,0:T(8,128)} %bitcast.225), channel_id=1, replica_groups=mesh['bucket'=4,'blk'=8] {'blk'}, dimensions={0}, use_global_device_ids=true | all-gather | bytes 69120 | tf_op jit(solution)/shard_map/all_gather | solution.py:219
  202.2 39.1 %while.46 = (s32[]{:T(128)}, f32[160,12,64]{0,2,1:T(8,128)}, bf16[2,640,768]{1,2,0:T(8,128)(2,1)}, s32[2,640]{1,0:T(2,128)S(1)}, s32[2,640]{1,0:T(2,128)}, /*ind...) while((s32[]{:T(128)}, f32[160,12,64]{0,2,1:T(8,128)}, ...), condition=%wide.region_10.11_spmd.clone.clone.clone, body=%wide.region_9.10_spmd.clone.clone.clone.sunk | while | flops 481240640 | bytes 23345884 | solution.py:208
  209.1 2.6 constant_dynamic-slice_fusion.14
  211.7 3.1 fusion.177
  214.9 6.7 fusion.178
  231.0 3.1 fusion.177
  234.1 7.2 %fusion.178 = f32[160,12,64]{0,2,1:T(8,128)} fusion(bf16[640,12,64]{0,2,1:T(8,128)(2,1)} %bitcast.198, f32[12,640,160]{1,2,0:T(8,128)} %fusion.177, f32[12,160]{1,0:T(8,128)} %get-tuple-element.1362, f32[12,160]{1,0:T(8,128)} %get-tuple-element.1359, pred[160,640]{1,0:T(8,128)(4,1)} %compare_and_fusion.7, bf16[640,12,64]{0,2,1:T(8,128)(2,1)} %bitcast.204, ...), kind=kOutput, calls=%fused_computation.42.clone.1 | convolution fusion | flops 323543040 | bytes 8227841 | tf_op jit(solution)/shard_map/while/body/eval_jaxpr/hqk,khd->qhd/dot_general | solution.py:203
  243.9 69.2 %while.47 = (s32[]{:T(128)}, f32[160,12,64]{0,2,1:T(8,128)}, f32[160,12,64]{0,2,1:T(8,128)}, bf16[2,640,768]{2,1,0:T(8,128)(2,1)}, s32[2,640]{1,0:T(2,128)S(1)},...) while((s32[]{:T(128)}, f32[160,12,64]{0,2,1:T(8,128)}, ...), condition=%wide.region_12.13_spmd.clone.clone.clone, body=%wide.region_11.12_spmd.clone.clone.clone.sunk | while | flops 644917248 | bytes 29792240 | solution.py:266
  245.2 2.6 and_select_fusion.15
  252.0 2.9 constant_dynamic-slice_fusion.15
  257.1 4.4 fusion.186
  265.9 5.0 fusion.188
  271.5 6.4 fusion.187
  279.2 2.6 and_select_fusion.15
  286.0 2.9 constant_dynamic-slice_fusion.15
  291.1 4.4 fusion.186
  299.9 5.6 fusion.188
  306.1 7.0 fusion.187
  317.3 4.2 fusion.84
  325.3 5.3 fusion.78
  331.3 3.7 multiply_reduce_fusion.1
  336.3 43.9 %all-reduce = (f32[768]{0:T(1024)}, f32[768]{0:T(1024)}, f32[768]{0:T(1024)}, f32[767]{0:T(1024)}, f32[768]{0:T(1024)}, /*index=5*/f32[3072]{0:T(1024)}, f32[767]{0:T(1024)}, f32[2]{0:T(128)S(1)}) all-reduce(f32[768]{0:T(1024)S(1)} %copy-done.47, f32[768]{0:T(1024)} %reduce_sum.195, ...), channel_id=1, replica_groups=mesh['bucket'=4,'blk'=8] {'bucket','blk'}, use_global_device_ids=true, to_apply=%region_15.16 | all-reduce | flops 7680 | bytes 61440 | tf_op jit(solution)/shard_map/psum | solution.py:307
  381.3 49.8 %reduce-scatter.11.cloned.1.call-done = f32[96,767]{1,0:T(8,128)} async-done(((f32[3072,767]{1,0:T(8,128)}), f32[96,767]{1,0:T(8,128)}) %reduce-scatter.11.cloned.1.call-update) | async-done | bytes 294544 | tf_op jit(solution)/shard_map/reduce_scatter | solution.py:297
  431.1 140.9 %reduce-scatter.9.cloned.1.call-done = f32[24,3072]{1,0:T(8,128)} async-done(((f32[768,3072]{1,0:T(8,128)}), f32[24,3072]{1,0:T(8,128)}) %reduce-scatter.9.cloned.1.call-update) | async-done | bytes 294928 | tf_op jit(solution)/shard_map/reduce_scatter | solution.py:296
  572.0 125.6 %reduce-scatter.5.cloned.1.call-done = f32[24,2304]{1,0:T(8,128)} async-done(((f32[768,2304]{1,0:T(8,128)}), f32[24,2304]{1,0:T(8,128)}) %reduce-scatter.5.cloned.1.call-update) | async-done | bytes 221200 | tf_op jit(solution)/shard_map/reduce_scatter | solution.py:294
  (245 shorter events, 124.5 us)
Async XLA Ops:
  7.2 5.6 copy-start
  7.2 41.1 %all-gather.9.cloned.1.call-start = ((), (), s32[]{:S(2)}) async-start(), calls=%async_computation.5 | async-start | bytes 2211840 | tf_op jit(solution)/shard_map/all_gather | solution.py:99
  12.8 3.1 copy-start.45
  12.8 3.1 copy-start.46
  16.8 60.0 %all-gather.7.cloned.1.call-start = ((), (), s32[]{:S(2)}) async-start(), calls=%async_computation.4 | async-start | bytes 2211840 | tf_op jit(solution)/shard_map/all_gather | solution.py:98
  18.6 225.3 %all-gather.11.cloned.1.call-start = ((), (), s32[]{:S(2)}) async-start(), calls=%async_computation.6 | async-start | bytes 2211840 | tf_op jit(solution)/shard_map/all_gather | solution.py:225
  19.3 224.5 %all-gather.13.cloned.1.call-start = ((), (), s32[]{:S(2)}) async-start(), calls=%async_computation.7 | async-start | bytes 2211840 | tf_op jit(solution)/shard_map/all_gather | solution.py:226
  88.5 3.7 copy-start.3
  89.5 6.5 copy-start.5
  96.7 3.6 copy-start.26
  96.7 4.3 copy-start.1
  96.7 4.3 copy-start.6
  112.5 3.7 copy-start.3
  113.4 6.5 copy-start.5
  120.6 3.6 copy-start.26
  120.6 4.3 copy-start.1
  120.6 4.3 copy-start.6
  130.2 4.5 copy-start.29
  130.2 7.8 %copy-start.40 = (f32[160]{0:T(256)S(1)}, f32[160]{0:T(256)}, u32[]{:S(2)}) copy-start(f32[160]{0:T(256)} %copy-done.39) | copy-start | bytes 1924
  130.2 7.8 %copy-start.42 = (s32[160]{0:T(256)S(1)}, s32[160]{0:T(256)}, u32[]{:S(2)}) copy-start(s32[160]{0:T(256)} %reshape.496) | copy-start | bytes 1924
  130.2 9.0 %copy-start.31 = (f32[768]{0:T(1024)S(1)}, f32[768]{0:T(1024)}, u32[]{:S(2)}) copy-start(f32[768]{0:T(1024)} %param.30) | copy-start | bytes 9220
  139.2 7.2 %copy-start.9 = (f32[160,767]{1,0:T(8,128)S(1)}, f32[160,767]{1,0:T(8,128)}, u32[]{:S(2)}) copy-start(f32[160,767]{1,0:T(8,128)} %get-tuple-element.892) | copy-start | bytes 1472644
  139.2 7.2 %copy-start.24 = (f32[160,1]{1,0:T(8,128)S(1)}, f32[160,1]{1,0:T(8,128)}, u32[]{:S(2)}) copy-start(f32[160,1]{1,0:T(8,128)} %copy.60) | copy-start | bytes 1924
  146.4 5.2 copy-start.25
  146.4 6.1 copy-start.14
  155.3 226.0 %reduce-scatter.7.cloned.1.call-start = ((), (), s32[]{:S(2)}) async-start(), calls=%async_computation.9 | async-start | bytes 2433024 | tf_op jit(solution)/shard_map/reduce_scatter | solution.py:295
  158.3 272.8 %reduce-scatter.11.cloned.1.call-start = ((), (), s32[]{:S(2)}) async-start(), calls=%async_computation.11 | async-start | bytes 9732096 | tf_op jit(solution)/shard_map/reduce_scatter | solution.py:297
  165.6 406.5 %reduce-scatter.9.cloned.1.call-start = ((), (), s32[]{:S(2)}) async-start(), calls=%async_computation.10 | async-start | bytes 9732096 | tf_op jit(solution)/shard_map/reduce_scatter | solution.py:296
  172.2 30.0 %copy-start.28 = (s32[2,640]{1,0:T(2,128)S(1)}, s32[2,640]{1,0:T(2,128)}, u32[]{:S(2)}) copy-start(s32[2,640]{1,0:T(2,128)} %get-tuple-element.1401) | copy-start | bytes 15364
  172.2 525.4 %reduce-scatter.5.cloned.1.call-start = ((), (), s32[]{:S(2)}) async-start(), calls=%async_computation.8 | async-start | bytes 7299072 | tf_op jit(solution)/shard_map/reduce_scatter | solution.py:294
  207.5 4.2 copy-start.4
  211.7 3.1 copy-start.2
  226.8 4.2 copy-start.4
  231.0 3.1 copy-start.2
  265.9 5.0 copy-start.17
  299.9 5.6 copy-start.17
  313.1 4.2 copy-start.7
  313.1 4.2 copy-start.19
  313.1 4.2 copy-start.21
  313.1 4.2 copy-start.30
  313.1 4.2 copy-start.37
  325.3 5.3 copy-start.35
  331.3 3.7 copy-start.41
  331.3 3.8 copy-start.8
  331.3 3.8 copy-start.20
  331.3 4.1 copy-start.12
  331.3 4.1 copy-start.15
  331.3 4.1 copy-start.44
  (18 other events, 18.8 us)
Sparse Core Ops, SparseCore 0:
  16.9 30.1 all-gather.8
  49.5 27.2 all-gather.6
  78.7 27.3 all-gather.10
  155.4 27.4 all-gather.12
  188.6 99.0 reduce-scatter.6
  295.1 136.0 reduce-scatter.10
  437.6 134.4 reduce-scatter.8
  579.2 118.3 reduce-scatter.4
where the time goes:
time: 707 us; the launch traced here: 704 us
  waiting for transfers between devices  342 us (48%)
  matrix products  121 us (17%)
  local copies, waits for them, and re-layouts  91.8 us (13%)
  other arithmetic  70.3 us (10%)
  blocking collectives  61.5 us (9%)
  between operations  17.1 us (2%)
    reduce_scatter x1, waiting for transfers between devices, body(): lax.psum_scatter(up_grad, ('bucket', 'blk'), scatter_dimension=0, tiled=T...  141 us
    reduce_scatter x1, waiting for transfers between devices, body(): lax.psum_scatter(input_grad, ('bucket', 'blk'), scatter_dimension=0, tile...  126 us
    reduce_scatter x1, waiting for transfers between devices, body(): lax.psum_scatter(down_grad, ('bucket', 'blk'), scatter_dimension=0, tiled...  49.8 us
    psum x1, blocking collectives, body(): lax.psum((first_gain_grad, query_bias_grad, value_bias_grad, output_bias_...  43.9 us
    dynamic_slice x16, local copies, waits for them, and re-layouts, body(): lax.scan(forward_advance, state, (key_piece.reshape(number, width, D), va...  30.8 us
    all_gather x1, waiting for transfers between devices, body(): key_piece = lax.all_gather(keys, 'blk', axis=0, tiled=True)  24.6 us
    select_n x8, other arithmetic, documents_of(): return jnp.where(first_in, 0, jnp.where(second_in, 1, -1)).astype(jnp.int32)  20.8 us
  transfers between devices with their start and end apart: 8, of which 4 were waited for; matrix products, arithmetic and copies ran while one was open for 38% of the time, Pallas kernels for 0%

commit v1 on v0

--- a/solution.py
+++ b/solution.py
@@ -1,6 +1,8 @@
 import jax
 import jax.numpy as jnp
 from jax import lax
+from jax.experimental import pallas as pl
+from jax.experimental.pallas import tpu as pltpu
 from jax.sharding import PartitionSpec as P
 
 D = 768
@@ -51,7 +53,7 @@
     return (shards // width, width * unit)
 
 
-def body(
+def general_body(
     residual_in,
     out_cotangent,
     first_gain,
@@ -335,6 +337,510 @@
     )
 
 
+DC = 767
+SPLIT = 192
+FF = 3072
+low = jnp.bfloat16
+wide = jnp.float32
+VMEM=pl.BlockSpec(memory_space=pltpu.VMEM); SMEM=pl.BlockSpec(memory_space=pltpu.SMEM)
+
+def call(kernel, outs, ins, scratch=(), flops=1_000_000, name=None):
+    shapes=[jax.ShapeDtypeStruct(s,d) for s,d in outs]
+    return pl.pallas_call(kernel, out_shape=shapes, in_specs=[SMEM]+[VMEM]*(len(ins)-1), out_specs=[VMEM]*len(outs), scratch_shapes=list(scratch),
+      compiler_params=pltpu.CompilerParams(vmem_limit_bytes=60*1024*1024), name=name,
+      cost_estimate=pl.CostEstimate(flops=flops,bytes_accessed=sum(x.size*x.dtype.itemsize for x in ins),transcendentals=0))(*ins)
+
+def full_of(x):
+    rows=x.shape[0]
+    wide_x=jnp.concatenate([x,jnp.zeros((rows,1),x.dtype)],axis=1)
+    last=lax.broadcasted_iota(jnp.int32,(rows,D),1)==D-1
+    return jnp.where(last,-jnp.sum(x,axis=1,keepdims=True),wide_x)
+
+def entry_kernel(ids,resid,cot,gain,weight,qbias,vbias,s0,s1,s2,s3,pair,root_out,buf):
+    me=ids[0]
+    full=full_of(resid[...].astype(wide))
+    root=jnp.sqrt(jnp.mean(full*full,axis=1,keepdims=True)+epsilon)
+    root_out[...]=root
+    hidden=(full/root*gain[...]).astype(low)
+    pair[:160,:]=hidden
+    pair[160:,:]=jnp.concatenate([cot[...].astype(wide),jnp.zeros((160,1),wide)],axis=1).astype(low)
+    for i in range(3):
+        p=jnp.dot(hidden,weight[:,i*D:(i+1)*D],preferred_element_type=wide)
+        if i==0: p=(p+qbias[...])*0.125
+        if i==2: p=p+vbias[...]
+        for j in range(4):
+            piece=p[:,j*SPLIT:(j+1)*SPLIT]
+            buf[j^me,i*80:(i+1)*80,:]=jnp.concatenate([piece[:80],piece[80:]],axis=1).astype(low)
+    for r,s in enumerate((s0,s1,s2,s3)):
+        s[...]=buf[r]
+
+def nt(a,b): return lax.dot_general(a,b,(((1,),(1,)),((),())),preferred_element_type=wide)
+def tn(a,b): return lax.dot_general(a,b,(((0,),(0,)),((),())),preferred_element_type=wide)
+
+def push_kernel(ids,cot,weight,out):
+    for i in range(4):
+        out[:,i*D:(i+1)*D]=nt(cot[...],weight[i*D:(i+1)*D,:])
+
+def assemble_kernel(ids,p0,p1,p2,p3,query,both):
+    for r,p in enumerate((p0,p1,p2,p3)):
+        for i in range(3):
+            piece=p[i*80:(i+1)*80,:].astype(wide)
+            two=jnp.concatenate([piece[:,:SPLIT],piece[:,SPLIT:]],axis=0).astype(low)
+            rows=slice(r*160,(r+1)*160)
+            if i==0: query[rows,:]=two
+            elif i==1: both[rows,:SPLIT]=two
+            else: both[rows,SPLIT:]=two
+
+def head_mask(x,h):
+    lane=lax.broadcasted_iota(jnp.int32,x.shape,1)
+    return jnp.where((lane>=h*64)&(lane<(h+1)*64),x,jnp.zeros_like(x))
+
+def span_of(ids,chip,core,half):
+    return ids[8+chip*4+core*2+half]
+
+def limits(ids,chip,core,half):
+    place=span_of(ids,chip,core,half)*80+lax.broadcasted_iota(jnp.int32,(80,1),0)
+    first=(place>=ids[3])&(place<ids[5])
+    second=(place>=ids[4])&(place<ids[6])
+    return jnp.where(first,ids[3],ids[4]),jnp.where(first|second,place,-1)
+
+def forward_kernel(ids,query,own,sib,chance,attended,mixed,b0,b1,b2,b3,keys,vals):
+    keys[:640,:]=own[:,:SPLIT]
+    keys[640:,:]=sib[:,:SPLIT]
+    v=jnp.concatenate([own[:,SPLIT:].astype(wide),sib[:,SPLIT:].astype(wide)],axis=0)
+    for h in range(3): vals[h]=head_mask(v,h).astype(low)
+    me=ids[0]; core=ids[2]
+    lane=lax.broadcasted_iota(jnp.int32,(1,1280),1)
+    place=lane
+    for blk in range(16):
+        chip=(blk%8)//2^me
+        other=core^(blk//8)
+        place=jnp.where((lane>=blk*80)&(lane<(blk+1)*80),lane+(span_of(ids,chip,other,blk%2)-blk)*80,place)
+    for r,b in enumerate((b0,b1,b2,b3)):
+        rows=slice(r*160,(r+1)*160)
+        q=query[rows,:].astype(wide)
+        l0,h0=limits(ids,r^me,core,0)
+        l1,h1=limits(ids,r^me,core,1)
+        lo=jnp.concatenate([l0,l1],axis=0); hi=jnp.concatenate([h0,h1],axis=0)
+        allowed=(place>=lo)&(place<=hi)
+        acc=jnp.zeros((160,SPLIT),wide)
+        for h in range(3):
+            s=nt(head_mask(q,h).astype(low),keys[...])
+            s=jnp.where(allowed,s,-1e30)
+            peak=jnp.max(s,axis=1,keepdims=True)
+            w=jnp.exp(s-peak)
+            total=jnp.sum(w,axis=1,keepdims=True)
+            p=(w*jnp.where(hi>=0,1.0/total,0.0)).astype(low)
+            chance[h,rows,:]=p
+            acc=acc+jnp.dot(p,vals[h],preferred_element_type=wide)
+        attended[rows,:]=acc
+        mixed[rows,:]=acc.astype(low)
+        b[...]=jnp.concatenate([acc[:80],acc[80:]],axis=1).astype(low)
+
+def middle_kernel(ids,p0,p1,p2,p3,out_weight,out_bias,resid,root_in,cot,gain,up_weight,up_bias,push,
+                  m0,m1,m2,m3,active,branch_own,middle,middle_grad,vector,buf):
+    me=ids[0]
+    branch=out_bias[...]
+    for r,p in enumerate((p0,p1,p2,p3)):
+        piece=p[...].astype(wide)
+        two=jnp.concatenate([piece[:,:SPLIT],piece[:,SPLIT:]],axis=0).astype(low)
+        w=out_weight[pl.ds(pl.multiple_of((me^r)*SPLIT,SPLIT),SPLIT),:]
+        branch=branch+jnp.dot(two,w,preferred_element_type=wide)
+    mid=resid[...].astype(wide)+branch
+    middle[...]=mid
+    full=full_of(mid)
+    root=jnp.sqrt(jnp.mean(full*full,axis=1,keepdims=True)+epsilon)
+    n=full/root
+    hidden=(n*gain[...]).astype(low)
+    for r in range(4): buf[r,0:160,:]=hidden
+    e=jnp.zeros((160,D),wide)
+    c=0.7978845608028654
+    up_sums=[]
+    for blk in range(4):
+        cols=slice(blk*D,(blk+1)*D)
+        u=jnp.dot(hidden,up_weight[:,cols],preferred_element_type=wide)+up_bias[:,cols]
+        t=jnp.tanh(c*(u+0.044715*u*u*u))
+        act=0.5*u*(1.0+t)
+        slope=0.5*(1.0+t)+0.5*u*(1.0-t*t)*(c*(1.0+3*0.044715*u*u))
+        active[:,cols]=act.astype(low)
+        for j in range(4):
+            buf[j^me,160:320,blk*SPLIT:(blk+1)*SPLIT]=act[:,j*SPLIT:(j+1)*SPLIT].astype(low)
+        g=(push[:,cols]*slope).astype(low)
+        buf[blk^me,320:480,:]=g
+        up_sums.append(jnp.sum(g.astype(wide),axis=0,keepdims=True))
+        e=e+nt(g,up_weight[:,cols])
+    for r,m in enumerate((m0,m1,m2,m3)): m[...]=buf[r]
+    gain_sum=jnp.sum(e*n,axis=0,keepdims=True)
+    eg=e*gain[...]
+    f=(eg-n*jnp.mean(eg*n,axis=1,keepdims=True))/root
+    cot_wide=jnp.concatenate([cot[...].astype(wide),jnp.zeros((160,1),wide)],axis=1)
+    lane=lax.broadcasted_iota(jnp.int32,(160,D),1)
+    last=jnp.sum(jnp.where(lane==D-1,f,0.0),axis=1,keepdims=True)
+    grad=jnp.where(lane==D-1,0.0,cot_wide+f-last)
+    middle_grad[...]=grad
+    grad_low=grad.astype(low)
+    branch_own[...]=grad_low
+    ends=[limits(ids,me,ids[2],half)[1] for half in range(2)]
+    valid=jnp.where(jnp.concatenate(ends,axis=0)>=0,1.0,0.0)
+    one=jnp.sum(valid*root_in[...],axis=0,keepdims=True)
+    two=jnp.sum(valid*root,axis=0,keepdims=True)
+    row=lax.broadcasted_iota(jnp.int32,(1,D),1)
+    stats=jnp.where(row==0,one,jnp.where(row==1,two,0.0))
+    zero=jnp.zeros((1,D),wide)
+    vector[...]=jnp.concatenate([zero,zero,zero,jnp.sum(grad_low.astype(wide),axis=0,keepdims=True),gain_sum]+up_sums+
+       [jnp.sum(cot_wide,axis=0,keepdims=True),stats]+[zero]*5,axis=0)
+
+def closing_kernel(ids,active,weight,middle,bias,out):
+    acc=middle[...]+bias[...]
+    for i in range(4):
+        acc=acc+jnp.dot(active[:,i*D:(i+1)*D],weight[i*D:(i+1)*D,:],preferred_element_type=wide)
+    out[...]=acc.astype(low)
+
+def backward_kernel(ids,b0,b1,b2,b3,out_weight,query,own,sib,chance,attended,query_grad,both_grad,away,keys,vals,grads,slopes):
+    me=ids[0]
+    w=out_weight[pl.ds(pl.multiple_of(me*SPLIT,SPLIT),SPLIT),:].astype(wide)
+    w=jnp.concatenate([w,jnp.zeros((SPLIT,1),wide)],axis=1).astype(low)
+    for r,b in enumerate((b0,b1,b2,b3)):
+        grads[r*160:(r+1)*160,:]=nt(b[...],w).astype(low)
+    k=jnp.concatenate([own[:,:SPLIT],sib[:,:SPLIT]],axis=0).astype(wide)
+    for h in range(3): keys[h]=head_mask(k,h).astype(low)
+    vals[:640,:]=own[:,SPLIT:].astype(wide).astype(low)
+    vals[640:,:]=sib[:,SPLIT:].astype(wide).astype(low)
+    dq=jnp.zeros((640,SPLIT),wide)
+    dk=jnp.zeros((1280,SPLIT),wide)
+    dv=jnp.zeros((1280,SPLIT),wide)
+    g=grads[...].astype(wide)
+    q=query[...].astype(wide)
+    for h in range(3):
+        gh=head_mask(g,h)
+        gl=gh.astype(low)
+        delta=jnp.sum(gh*attended[...],axis=1,keepdims=True)
+        for r in range(4):
+            rows=slice(r*160,(r+1)*160)
+            push=nt(gl[rows,:],vals[...])
+            slopes[rows,:]=(chance[h,rows,:].astype(wide)*(push-delta[rows,:])).astype(low)
+        dq=dq+jnp.dot(slopes[...],keys[h],preferred_element_type=wide)
+        dk=dk+tn(slopes[...],head_mask(q,h).astype(low))
+        dv=dv+tn(chance[h],gl)
+    query_grad[...]=(dq*0.125).astype(low)
+    both_grad[:,:SPLIT]=dk[:640]
+    both_grad[:,SPLIT:]=dv[:640]
+    away[:,:SPLIT]=dk[640:].astype(low)
+    away[:,SPLIT:]=dv[640:].astype(low)
+
+def split_pair(x):
+    hi=x.astype(low)
+    return hi,(x-hi.astype(wide)).astype(low)
+
+def input_grad_kernel(ids,query_grad,both_grad,arrived,p0,p1,p2,p3,weight,gain,vector,
+                      h0,h1,h2,h3,keep,send,hidden,heads,buf):
+    me=ids[0]; bucket=ids[1]; core=ids[2]
+    both=both_grad[...]+arrived[...].astype(wide)
+    parts=[query_grad[...].astype(wide),both[:,:SPLIT],both[:,SPLIT:]]
+    parts=[p.astype(low).astype(wide) for p in parts]
+    for r,(p,h) in enumerate(zip((p0,p1,p2,p3),(h0,h1,h2,h3))):
+        hidden[r*160:(r+1)*160,:]=p[:160,:]
+        for i in range(3):
+            piece=parts[i][r*160:(r+1)*160]
+            h[i*80:(i+1)*80,:]=jnp.concatenate([piece[:80],piece[80:]],axis=1).astype(low)
+    heads[...]=jnp.concatenate(parts,axis=1).astype(low)
+    grad=tn(hidden[...],heads[...])
+    parts_grad=[grad[:,i*SPLIT:(i+1)*SPLIT] for i in range(3)]
+    product=jnp.zeros((D,SPLIT),wide)
+    for i in range(3):
+        w=jnp.zeros((D,SPLIT),wide)
+        for j in range(4):
+            w=jnp.where(me==j,weight[:,i*D+j*SPLIT:i*D+(j+1)*SPLIT].astype(wide),w)
+        product=product+w*parts_grad[i]
+    gain_row=lax.dot_general(jnp.ones((8,SPLIT),wide),product,(((1,),(1,)),((),())),precision=lax.Precision.HIGHEST,preferred_element_type=wide)[0:1]/gain[...]
+    lane=lax.broadcasted_iota(jnp.int32,(1,D),1)
+    mine=(lane>=me*SPLIT)&(lane<(me+1)*SPLIT)
+    def column_sum(x):
+        s=jnp.sum(x,axis=0,keepdims=True)
+        return jnp.where(mine,jnp.concatenate([s]*4,axis=1),0.0)
+    total=vector[...]
+    row=lax.broadcasted_iota(jnp.int32,(16,D),0)
+    total=total+jnp.where(row==0,gain_row,0.0)+jnp.where(row==1,column_sum(parts[0]),0.0)+jnp.where(row==2,column_sum(parts[2]),0.0)
+    for b in range(4):
+        for c in range(2):
+            block=jnp.concatenate([jnp.concatenate([parts_grad[i][b*192+j*48+c*24:b*192+j*48+c*24+24] for j in range(4)],axis=1) for i in range(3)]+[jnp.zeros((8,D),wide)],axis=0)
+            buf[c^core,(b-bucket)&3]=block.astype(low)
+    keep[...]=buf[0]
+    hi,lo=split_pair(total)
+    for d in range(4): send[d*80:(d+1)*80,:]=buf[1,d]
+    send[320:336,:]=hi
+    send[336:352,:]=lo
+
+def input_bucket_kernel(ids,keep,send,arrived,z0,z1,z2,z3):
+    total=(send[320:336,:].astype(wide)+send[336:352,:].astype(wide))+(arrived[320:336,:].astype(wide)+arrived[336:352,:].astype(wide))
+    hi,lo=split_pair(total)
+    for d,z in enumerate((z0,z1,z2,z3)):
+        z[0:80,:]=(keep[d].astype(wide)+arrived[d*80:(d+1)*80,:].astype(wide)).astype(low)
+        z[80:96,:]=hi
+        z[96:112,:]=lo
+
+def weight_grad_kernel(ids,m0,m1,m2,m3,p0,p1,p2,p3,b0,b1,b2,b3,mixed,keep,send,left,right,buf):
+    bucket=ids[1]; core=ids[2]
+    def grad(lefts,rights):
+        n=lefts[0].shape[1]
+        for r in range(4):
+            rows=slice(r*160,(r+1)*160)
+            left[rows,:n]=lefts[r]
+            right[rows,:]=rights[r]
+        return tn(left[:,:n],right[...])
+    ms=(m0,m1,m2,m3); ps=(p0,p1,p2,p3); bs=(b0,b1,b2,b3)
+    down=grad([m[160:320,:] for m in ms],[p[160:320,:] for p in ps])
+    for b in range(4):
+        for c in range(2):
+            buf[c^core,(b-bucket)&3,0:96,:]=down[b*192+c*96:b*192+(c+1)*96].astype(low)
+    up=grad([m[0:160,:] for m in ms],[m[320:480,:] for m in ms])
+    for r in range(4): right[r*160:(r+1)*160,:]=bs[r][...]
+    out=tn(mixed[...],right[...])
+    for b in range(4):
+        for c in range(2):
+            block=[up[b*192+j*48+c*24:b*192+j*48+c*24+24] for j in range(4)]+[out[b*48+c*24:b*48+c*24+24],jnp.zeros((8,D),wide)]
+            buf[c^core,(b-bucket)&3,96:224,:]=jnp.concatenate(block,axis=0).astype(low)
+    keep[...]=buf[0]
+    send[...]=buf[1]
+
+def bucket_kernel(ids,keep,arrived,z0,z1,z2,z3):
+    for d,z in enumerate((z0,z1,z2,z3)):
+        z[...]=(keep[d].astype(wide)+arrived[d].astype(wide)).astype(low)
+
+def weight_sum_kernel(ids,z0,z1,z2,z3,down,up,out):
+    total=z0[...].astype(wide)+z1[...].astype(wide)+z2[...].astype(wide)+z3[...].astype(wide)
+    down[...]=total[0:96,:DC]
+    up[...]=total[96:192]
+    out[...]=total[192:216]
+
+def final_send_kernel(ids,z0,z1,z2,z3,up,f0,f1,f2,f3,buf,vec):
+    me=ids[0]; bucket=ids[1]
+    zs=(z0,z1,z2,z3)
+    total=sum(z[0:72,:].astype(wide) for z in zs)
+    for d,z in enumerate(zs):
+        vec[(bucket-d)&3]=z[80:96,:].astype(wide)+z[96:112,:].astype(wide)
+    hi,lo=split_pair(vec[0]+vec[1]+vec[2]+vec[3])
+    pad8=jnp.zeros((8,D),wide); padl=jnp.zeros((24,D-3*SPLIT),wide)
+    for j in range(4):
+        ins=jnp.concatenate([total[i*24:(i+1)*24,j*SPLIT:(j+1)*SPLIT] for i in range(3)]+[padl],axis=1)
+        block=jnp.concatenate([up[j*24:(j+1)*24,:],pad8,ins,pad8],axis=0)
+        buf[j^me]=block.astype(low)
+    for r,f in enumerate((f0,f1,f2,f3)):
+        f[0:16,:]=hi
+        f[16:32,:]=lo
+        f[32:96,:]=buf[r]
+
+def final_kernel(ids,f0,f1,f2,f3,in_total,up_total,first,query,value,output,second,up_bias,down,stats,buf):
+    me=ids[0]
+    for r,f in enumerate((f0,f1,f2,f3)):
+        buf[r^me]=f[...].astype(wide)
+    total=buf[0,0:16]+buf[0,16:32]
+    for j in (1,2,3): total=total+(buf[j,0:16]+buf[j,16:32])
+    first[...]=total[0]
+    query[...]=total[1]
+    value[...]=total[2]
+    output[...]=total[3,:DC]
+    second[...]=total[4]
+    for i in range(4): up_bias[i*D:(i+1)*D]=total[5+i]
+    down[...]=total[9,:DC]
+    stats[...]=total[10,:2]/ids[7].astype(wide)
+    for j in range(4): up_total[:,j*D:(j+1)*D]=buf[j,32:56,:]
+    for i in range(3):
+        in_total[:,i*D:(i+1)*D]=jnp.concatenate([buf[j,64:88,i*SPLIT:(i+1)*SPLIT] for j in range(4)],axis=1)
+
+def home_kernel(ids,h0,h1,h2,h3,weight,resid,gain,middle_grad,out,buf):
+    me=ids[0]
+    for r,h in enumerate((h0,h1,h2,h3)): buf[r^me]=h[...]
+    e=jnp.zeros((160,D),wide)
+    for i in range(3):
+        cols=[]
+        for j in range(4):
+            piece=buf[j,i*80:(i+1)*80,:].astype(wide)
+            cols.append(jnp.concatenate([piece[:,:SPLIT],piece[:,SPLIT:]],axis=0))
+        g=jnp.concatenate(cols,axis=1).astype(low)
+        e=e+nt(g,weight[:,i*D:(i+1)*D])
+    full=full_of(resid[...].astype(wide))
+    root=jnp.sqrt(jnp.mean(full*full,axis=1,keepdims=True)+epsilon)
+    n=full/root
+    eg=e*gain[...]
+    f=(eg-n*jnp.mean(eg*n,axis=1,keepdims=True))/root
+    lane=lax.broadcasted_iota(jnp.int32,(160,D),1)
+    last=jnp.sum(jnp.where(lane==D-1,f,0.0),axis=1,keepdims=True)
+    out[...]=(middle_grad[...]+f-last)[:,:DC].astype(low)
+
+def swap_chip(block, step):
+    return lax.ppermute(block, "blk", [(k, k ^ (2 * step)) for k in range(8)])
+
+
+def swap_core(block):
+    return lax.ppermute(block, "blk", [(k, k ^ 1) for k in range(8)])
+
+
+def shift_bucket(block, step):
+    return lax.ppermute(block, "bucket", [(b, (b + step) % 4) for b in range(4)])
+
+
+def exchange(blocks):
+    got = {r: swap_chip(blocks[r], r) for r in (3, 1, 2)}
+    return [blocks[0], got[1], got[2], got[3]]
+
+
+def over_buckets(blocks):
+    return [blocks[0]] + [shift_bucket(blocks[d], d) for d in (1, 2, 3)]
+
+
+def body(
+    residual_in,
+    out_cotangent,
+    first_gain,
+    input_weight,
+    query_bias,
+    value_bias,
+    output_weight,
+    output_bias,
+    second_gain,
+    up_weight,
+    up_bias,
+    down_weight,
+    down_bias,
+    lengths,
+    offsets,
+    span_order,
+):
+    index = lax.axis_index("blk")
+    bucket = lax.axis_index("bucket")
+    own_lengths = lax.dynamic_slice_in_dim(lengths, bucket, 1, 0)[0]
+    starts = offsets[0]
+    scalars = [index // 2, bucket, index % 2, starts[0], starts[1]]
+    scalars += [starts[0] + own_lengths[0], starts[1] + own_lengths[1], jnp.sum(lengths)]
+    ids = jnp.concatenate([jnp.stack(scalars).astype(jnp.int32), span_order, jnp.zeros((8,), jnp.int32)])
+    gain_one = first_gain[None]
+    gain_two = second_gain[None]
+
+    packed = ((240, 384), low)
+    s0, s1, s2, s3, pair, root_one = call(
+        entry_kernel,
+        [packed] * 4 + [((320, D), low), ((160, 1), wide)],
+        [ids, residual_in, out_cotangent, gain_one, input_weight, query_bias[None], value_bias[None]],
+        [pltpu.VMEM((4, 240, 384), low)],
+        flops=2 * 160 * D * 3 * D,
+    )
+    got = exchange([s0, s1, s2, s3])
+    (push,) = call(
+        push_kernel, [((160, FF), wide)], [ids, out_cotangent, down_weight], flops=2 * 160 * D * FF
+    )
+    query, own_both = call(assemble_kernel, [((640, SPLIT), low), ((640, 2 * SPLIT), low)], [ids] + got)
+    sib_both = swap_core(own_both)
+    pairs = exchange([pair] * 4)
+    backed = ((80, 384), low)
+    chance, attended, mixed, b0, b1, b2, b3 = call(
+        forward_kernel,
+        [((3, 640, 1280), low), ((640, SPLIT), wide), ((640, SPLIT), low)] + [backed] * 4,
+        [ids, query, own_both, sib_both],
+        [pltpu.VMEM((1280, SPLIT), low), pltpu.VMEM((3, 1280, SPLIT), low)],
+        flops=4 * 12 * 160 * 1280 * 256,
+    )
+    back = exchange([b0, b1, b2, b3])
+    late = ((480, D), low)
+    m0, m1, m2, m3, active, branch_own, middle, middle_grad, vector = call(
+        middle_kernel,
+        [late] * 4
+        + [((160, FF), low), ((160, D), low), ((160, DC), wide), ((160, D), wide), ((16, D), wide)],
+        [ids]
+        + back
+        + [output_weight, output_bias[None], residual_in, root_one, out_cotangent, gain_two]
+        + [up_weight, up_bias[None], push],
+        [pltpu.VMEM((4, 480, D), low)],
+        flops=2 * 160 * D * (D + 2 * FF),
+    )
+    branches = exchange([branch_own] * 4)
+    lates = exchange([m0, m1, m2, m3])
+    (residual_out,) = call(
+        closing_kernel,
+        [((160, DC), low)],
+        [ids, active, down_weight, middle, down_bias[None]],
+        flops=2 * 160 * D * FF,
+    )
+    query_grad, both_grad, away = call(
+        backward_kernel,
+        [((640, SPLIT), low), ((640, 2 * SPLIT), wide), ((640, 2 * SPLIT), low)],
+        [ids] + branches + [output_weight, query, own_both, sib_both, chance, attended],
+        [
+            pltpu.VMEM((3, 1280, SPLIT), low),
+            pltpu.VMEM((1280, SPLIT), low),
+            pltpu.VMEM((640, SPLIT), low),
+            pltpu.VMEM((640, 1280), low),
+        ],
+        flops=10 * 12 * 160 * 1280 * 256,
+    )
+    arrived = swap_core(away)
+    h0, h1, h2, h3, in_keep, in_send = call(
+        input_grad_kernel,
+        [packed] * 4 + [((4, 80, D), low), ((352, D), low)],
+        [ids, query_grad, both_grad, arrived] + pairs + [input_weight, gain_one, vector],
+        [
+            pltpu.VMEM((640, D), low),
+            pltpu.VMEM((640, 3 * SPLIT), low),
+            pltpu.VMEM((2, 4, 80, D), low),
+        ],
+        flops=2 * 640 * D * 3 * SPLIT,
+    )
+    home = exchange([h0, h1, h2, h3])
+    keep, send = call(
+        weight_grad_kernel,
+        [((4, 224, D), low)] * 2,
+        [ids] + lates + pairs + branches + [mixed],
+        [pltpu.VMEM((640, D), low), pltpu.VMEM((640, D), low), pltpu.VMEM((2, 4, 224, D), low)],
+        flops=2 * 640 * D * (2 * D + SPLIT),
+    )
+    z = call(bucket_kernel, [((224, D), low)] * 4, [ids, keep, swap_core(send)])
+    down_total, up_sum, out_sum = call(
+        weight_sum_kernel,
+        [((96, DC), wide), ((96, D), wide), ((24, D), wide)],
+        [ids] + over_buckets(z),
+    )
+    turned = [(b * 8 + j * 2 + c, j * 8 + b * 2 + c) for b in range(4) for j in range(4) for c in range(2)]
+    out_total = lax.ppermute(out_sum, ("bucket", "blk"), turned)[:, :DC]
+    z = call(input_bucket_kernel, [((112, D), low)] * 4, [ids, in_keep, in_send, swap_core(in_send)])
+    finals = call(
+        final_send_kernel,
+        [((96, D), low)] * 4,
+        [ids] + over_buckets(z) + [up_sum],
+        [pltpu.VMEM((4, 64, D), low), pltpu.VMEM((4, 16, D), wide)],
+    )
+    in_total, up_total, first, query_sum, value_sum, output, second, up_sum_bias, down, stats = call(
+        final_kernel,
+        [((24, 3 * D), wide), ((24, FF), wide)]
+        + [((D,), wide)] * 3
+        + [((DC,), wide), ((D,), wide), ((FF,), wide), ((DC,), wide), ((2,), wide)],
+        [ids] + exchange(finals),
+        [pltpu.VMEM((4, 96, D), wide)],
+    )
+    (residual_grad,) = call(
+        home_kernel,
+        [((160, DC), low)],
+        [ids] + home + [input_weight, residual_in, gain_one, middle_grad],
+        [pltpu.VMEM((4, 240, 384), low)],
+        flops=2 * 160 * D * 3 * D,
+    )
+    return (
+        residual_out,
+        residual_grad,
+        first,
+        in_total,
+        query_sum,
+        value_sum,
+        out_total,
+        output,
+        second,
+        up_total,
+        up_sum_bias,
+        down_total,
+        down,
+        stats,
+    )
+
+
 def solution(mesh):
     placed = (
         P(("bucket", "blk"), None),
@@ -355,7 +861,7 @@
         P(),
     )
     return jax.shard_map(
-        body,
+        body if dict(mesh.shape) == {"bucket": 4, "blk": 8} else general_body,
         mesh=mesh,
         in_specs=placed,
         out_specs=(

time: 707 us -> 225 us (0.32)
  waiting for transfers between devices: 342 us -> 72.9 us
  matrix products: 121 us -> 0 us
  Pallas kernels: 0 us -> 81.8 us
  local copies, waits for them, and re-layouts: 91.8 us -> 20.2 us
  other arithmetic: 70.3 us -> 1.32 us
  blocking collectives: 61.5 us -> 0 us
  starting transfers between devices: 0.51 us -> 43.1 us
  between operations: 17.1 us -> 3.49 us
    reduce_scatter x4 -> x0, waiting for transfers between devices: 316 us -> none  [the longest x1 141 us: body(): lax.psum_scatter(up_grad, ('bucket', 'blk'), scatter_dimension=0, tiled=T...]
    dot_general x26 -> x0, matrix products: 121 us -> none  [the longest x2 13.9 us: query_advance(): jnp.einsum('hqk,khd->qhd', slope, block_keys, preferred_element_type=jnp....]
    pallas_call x0 -> x15, Pallas kernels: none -> 81.8 us  [call(): pl.pallas_call(kernel, out_shape=shapes, in_specs=[SMEM] + [VMEM] * (len(...]
    ppermute x0 -> x32, waiting for transfers between devices: none -> 72.9 us  [the longest x21 47.6 us: swap_chip(): return lax.ppermute(block, 'blk', [(k, k ^ 2 * step) for k in range(8)])]
    psum x1 -> x0, blocking collectives: 43.9 us -> none  [body(): lax.psum((first_gain_grad, query_bias_grad, value_bias_grad, output_bias_...]
    ppermute x0 -> x32, starting transfers between devices: none -> 43.1 us  [the longest x21 26 us: swap_chip(): return lax.ppermute(block, 'blk', [(k, k ^ 2 * step) for k in range(8)])]
    dynamic_slice x23 -> x1, local copies, waits for them, and re-layouts: 37.1 us -> 0.75 us  [body(): own_lengths = lax.dynamic_slice_in_dim(lengths, bucket, 1, 0)[0]]
    all_gather x4 -> x0, waiting for transfers between devices: 24.6 us -> none  [the longest x1 24.6 us: body(): key_piece = lax.all_gather(keys, 'blk', axis=0, tiled=True)]
  transfers between devices with their start and end apart: 8 -> 32, of which waited for: 4 -> 8; matrix products, arithmetic and copies ran while one was open for 38% -> 1% of each run, Pallas kernels for 0% -> 30%
where the time goes in v1:
time: 225 us; the launch traced here: 223 us
  Pallas kernels  81.8 us (36%)
  waiting for transfers between devices  72.9 us (32%)
  starting transfers between devices  43.1 us (19%)
  local copies, waits for them, and re-layouts  20.2 us (9%)
  between operations  3.49 us (2%)
    pallas_call x15, Pallas kernels, call(): pl.pallas_call(kernel, out_shape=shapes, in_specs=[SMEM] + [VMEM] * (len(...  81.8 us
    ppermute x21, waiting for transfers between devices, swap_chip(): return lax.ppermute(block, 'blk', [(k, k ^ 2 * step) for k in range(8)])  47.6 us
    ppermute x21, starting transfers between devices, swap_chip(): return lax.ppermute(block, 'blk', [(k, k ^ 2 * step) for k in range(8)])  26 us
    ppermute x6, waiting for transfers between devices, shift_bucket(): lax.ppermute(block, 'bucket', [(b, (b + step) % 4) for b in range(4)])  23.7 us
    ppermute x6, starting transfers between devices, shift_bucket(): lax.ppermute(block, 'bucket', [(b, (b + step) % 4) for b in range(4)])  14.6 us
    unnamed x75, local copies, waits for them, and re-layouts  8.8 us
  transfers between devices with their start and end apart: 32, of which 8 were waited for; matrix products, arithmetic and copies ran while one was open for 1% of the time, Pallas kernels for 30%

profile of v1, /device:TPU:0, one launch (start us, length us, event | category | flops | bytes accessed | tf_op | source)
XLA Modules:
  0.0 222.8 jit_solution(16371391154179067069)
XLA Ops:
  0.7 1.3 fusion.1
  2.0 1.3 reduce_sum.9
  4.6 1.3 broadcast_in_dim.21.gain
  5.8 1.3 broadcast_in_dim.22.qbias
  7.1 1.3 broadcast_in_dim.23.vbias
  11.0 3.3 %concatenate.3.ids = s32[32]{0:T(128)} concatenate(s32[1]{0:T(128)} %bitcast, s32[1]{0:T(128)} %bitcast.1, s32[1]{0:T(128)} %bitcast.2, s32[1]{0:T(128)} %bitcast.3, s32[1]{0:T(128)} %bitcast.4, s32[1]{0:T(128)} %bitcast.5, s32[1]{0:T(128)} %bitcast.6, s32[1]{0:T(128)} %bitcast.7, s32[16]{0:T(128)} %param.31, s32[8]{0:T(128)S(1)} %broadcast.5), dimensions={0} | concatenate | bytes 256 | tf_op jit(solution)/shard_map/concatenate | solution.py:716
  14.2 4.2 %shard_map.263 = (bf16[240,384]{1,0:T(8,128)(2,1)}, bf16[240,384]{1,0:T(8,128)(2,1)}, bf16[240,384]{1,0:T(8,128)(2,1)}, bf16[240,384]{1,0:T(8,128)(2,1)}, bf16[320,768]{1,0:T(8,128)(2,1)}, /*index=5*/f32[160,1]{1,0:T(8,128)}) custom-call(s32[32]{0:T(128)} %concatenate.3.ids, bf16[160,767]{1,0:T(8,128)(2,1)} %resid.5, bf16[160,767]{1,0:T(8,128)(2,1)} %cot.5, ...), custom_call_target="tpu_custom_call" | custom-call | flops 566231040 | bytes 4039168 | tf_op jit(solution)/shard_map/pallas_call | solution.py:349
  18.4 2.9 %collective-permute-start = (bf16[240,384]{1,0:T(8,128)(2,1)}, bf16[240,384]{1,0:T(8,128)(2,1)S(1)}, u32[]{:S(2)}, u32[]{:S(2)}) collective-permute-start(bf16[240,384]{1,0:T(8,128)(2,1)} %get-tuple-element.75), channel_id=1, source_target_pairs={{0,2},{1,3},{2,0},{3,1},{4,6},{5,7},{6,4},{7,5},{8,10},{9,11},{10,... | collective-permute-start | bytes 552968 | tf_op jit(solution)/shard_map/ppermute | solution.py:672
  21.4 1.5 collective-permute-start.1
  22.9 4.1 %collective-permute-done.p1 = bf16[240,384]{1,0:T(8,128)(2,1)S(1)} collective-permute-done((bf16[240,384]{1,0:T(8,128)(2,1)}, bf16[240,384]{1,0:T(8,128)(2,1)S(1)}, u32[]{:S(2)}, u32[]{:S(2)}) %collective-permute-start) | collective-permute-done | bytes 184352 | tf_op jit(solution)/shard_map/ppermute | solution.py:672
  27.1 4.6 %collective-permute-done.1.p2 = bf16[240,384]{1,0:T(8,128)(2,1)S(1)} collective-permute-done((bf16[240,384]{1,0:T(8,128)(2,1)}, bf16[240,384]{1,0:T(8,128)(2,1)S(1)}, u32[]{:S(2)}, u32[]{:S(2)}) %collective-permute-start.1) | collective-permute-done | bytes 184352 | tf_op jit(solution)/shard_map/ppermute | solution.py:672
  32.4 2.5 %shard_map.264 = (bf16[640,192]{1,0:T(8,128)(2,1)}, bf16[640,384]{1,0:T(8,128)(2,1)}) custom-call(s32[32]{0:T(128)} %concatenate.3.ids, bf16[240,384]{1,0:T(8,128)(2,1)} %get-tuple-element.74.p0, bf16[240,384]{1,0:T(8,128)(2,1)} %copy-done.10, bf16[240,384]{1,0:T(8,128)(2,1)} %copy-done.11, bf16[240,384]{1,0:T(8,128)(2,1)} %copy-done.12), custom_call_target="tpu_custom_call" | custom-call | flops 1000000 | bytes 737408 | tf_op jit(solution)/shard_map/pallas_call | solution.py:349
  34.8 1.2 collective-permute-start.11
  38.9 11.1 %shard_map.265 = (bf16[3,640,1280]{2,1,0:T(8,128)(2,1)}, f32[640,192]{1,0:T(8,128)}, bf16[640,192]{1,0:T(8,128)(2,1)}, bf16[80,384]{1,0:T(8,128)(2,1)}, bf16[80,...) custom-call(s32[32]{0:T(128)} %concatenate.3.ids, bf16[640,192]{1,0:T(8,128)(2,1)} %get-tuple-element.78.query, ...), custom_call_target="tpu_custom_call" | custom-call | flops 2516582400 | bytes 1228928 | tf_op jit(solution)/shard_map/pallas_call | solution.py:349
  50.0 1.5 collective-permute-start.4
  52.0 1.5 collective-permute-start.6
  53.5 5.4 %shard_map.266.push = f32[160,3072]{1,0:T(8,128)} custom-call(s32[32]{0:T(128)} %concatenate.3.ids, bf16[160,767]{1,0:T(8,128)(2,1)} %cot.5, bf16[3072,767]{1,0:T(8,128)(2,1)} %weight.7), custom_call_target="tpu_custom_call" | custom-call | flops 754974720 | bytes 4958016 | tf_op jit(solution)/shard_map/pallas_call | solution.py:349
  58.9 1.5 collective-permute-start.13
  61.1 10.6 %shard_map.267 = (bf16[480,768]{1,0:T(8,128)(2,1)}, bf16[480,768]{1,0:T(8,128)(2,1)}, bf16[480,768]{1,0:T(8,128)(2,1)}, bf16[480,768]{1,0:T(8,128)(2,1)}, bf16[1...) custom-call(s32[32]{0:T(128)} %concatenate.3.ids, ...), custom_call_target="tpu_custom_call" | custom-call | flops 1698693120 | bytes 8618620 | tf_op jit(solution)/shard_map/pallas_call | solution.py:349
  71.7 1.2 collective-permute-start.21
  73.8 1.4 collective-permute-start.23
  75.2 1.2 collective-permute-start.7
  77.3 33.0 %collective-permute-done.7.b1 = bf16[160,768]{1,0:T(8,128)(2,1)S(1)} collective-permute-done((bf16[160,768]{1,0:T(8,128)(2,1)}, bf16[160,768]{1,0:T(8,128)(2,1)S(1)}, u32[]{:S(2)}, u32[]{:S(2)}) %collective-permute-start.7) | collective-permute-done | bytes 245792 | tf_op jit(solution)/shard_map/ppermute | solution.py:672
  110.3 1.5 collective-permute-start.9
  111.8 5.8 %collective-permute-done.9.b3 = bf16[160,768]{1,0:T(8,128)(2,1)S(1)} collective-permute-done((bf16[160,768]{1,0:T(8,128)(2,1)}, bf16[160,768]{1,0:T(8,128)(2,1)S(1)}, u32[]{:S(2)}, u32[]{:S(2)}) %collective-permute-start.9) | collective-permute-done | bytes 245792 | tf_op jit(solution)/shard_map/ppermute | solution.py:672
  118.8 6.8 %shard_map.273 = (bf16[4,224,768]{2,1,0:T(8,128)(2,1)}, bf16[4,224,768]{2,1,0:T(8,128)(2,1)}) custom-call(s32[32]{0:T(128)} %concatenate.3.ids, bf16[480,768]{1,0:T(8,128)(2,1)} %get-tuple-element.106.m0, bf16[480,768]{1,0:T(8,128)(2,1)} %copy-done.28, bf16[480,768]{1,0:T(8,128)(2,1)} %copy-done.29, bf16[480,768]{1,0:T(8,128)(2,1)} %collective-permute-done.23.m3, ...), custom_call_target="tpu_custom_call" | custom-call | flops 1698693120 | bytes 6144128 | tf_op jit(solution)/shard_map/pallas_call | solution.py:349
  125.6 13.1 %shard_map.269 = (bf16[640,192]{1,0:T(8,128)(2,1)}, f32[640,384]{1,0:T(8,128)}, bf16[640,384]{1,0:T(8,128)(2,1)}) custom-call(s32[32]{0:T(128)} %concatenate.3.ids, bf16[160,768]{1,0:T(8,128)(2,1)} %get-tuple-element.87.b0, bf16[160,768]{1,0:T(8,128)(2,1)} %copy-done.31, bf16[160,768]{1,0:T(8,128)(2,1)} %copy-done.32, bf16[160,768]{1,0:T(8,128)(2,1)} %copy-done.33, ...), custom_call_target="tpu_custom_call" | custom-call | flops 6291456000 | bytes 8796800 | tf_op jit(solution)/shard_map/pallas_call | solution.py:349
  139.2 1.7 collective-permute-done.10.arrived
  141.7 7.1 %shard_map.270 = (bf16[240,384]{1,0:T(8,128)(2,1)}, bf16[240,384]{1,0:T(8,128)(2,1)}, bf16[240,384]{1,0:T(8,128)(2,1)}, bf16[240,384]{1,0:T(8,128)(2,1)}, bf16[4...) custom-call(s32[32]{0:T(128)} %concatenate.3.ids, bf16[640,192]{1,0:T(8,128)(2,1)} %get-tuple-element.90.query_grad, ...), custom_call_target="tpu_custom_call" | custom-call | flops 566231040 | bytes 7277696 | tf_op jit(solution)/shard_map/pallas_call | solution.py:349
  150.3 3.0 %shard_map.274 = (bf16[224,768]{1,0:T(8,128)(2,1)}, bf16[224,768]{1,0:T(8,128)(2,1)}, bf16[224,768]{1,0:T(8,128)(2,1)}, bf16[224,768]{1,0:T(8,128)(2,1)}) custom-call(s32[32]{0:T(128)} %concatenate.3.ids, bf16[4,224,768]{2,1,0:T(8,128)(2,1)} %get-tuple-element.111.keep, bf16[4,224,768]{2,1,0:T(8,128)(2,1)} %copy-done), custom_call_target="tpu_custom_call" | custom-call | flops 1000000 | bytes 2752640 | tf_op jit(solution)/shard_map/pallas_call | solution.py:349
  153.3 1.6 collective-permute-start.25
  154.9 2.6 %collective-permute-start.26 = (bf16[224,768]{1,0:T(8,128)(2,1)}, bf16[224,768]{1,0:T(8,128)(2,1)S(1)}, u32[]{:S(2)}, u32[]{:S(2)}) collective-permute-start(bf16[224,768]{1,0:T(8,128)(2,1)} %get-tuple-element.115), channel_id=1, source_target_pairs={{0,16},{8,24},{16,0},{24,8},{1,17},{9,25},{17,1},{25,9},{2,18},{10... | collective-permute-start | bytes 1032200 | tf_op jit(solution)/shard_map/ppermute | solution.py:680
  157.5 1.4 collective-permute-start.27
  159.7 2.3 %shard_map.272 = (bf16[112,768]{1,0:T(8,128)(2,1)}, bf16[112,768]{1,0:T(8,128)(2,1)}, bf16[112,768]{1,0:T(8,128)(2,1)}, bf16[112,768]{1,0:T(8,128)(2,1)}) custom-call(s32[32]{0:T(128)} %concatenate.3.ids, bf16[4,80,768]{2,1,0:T(8,128)(2,1)} %get-tuple-element.100.keep, bf16[352,768]{1,0:T(8,128)(2,1)} %get-tuple-element.101.send, bf16[352,768]{1,0:T(8,128)(2,1)} %copy-done.1), custom_call_target="tpu_custom_call" | custom-call | flops 1000000 | bytes 1572992 | tf_op jit(solution)/shard_map/pallas_call | solution.py:349
  162.6 1.2 collective-permute-start.14
  163.8 20.3 %collective-permute-done.18.z1 = bf16[112,768]{1,0:T(8,128)(2,1)S(1)} collective-permute-done((bf16[112,768]{1,0:T(8,128)(2,1)}, bf16[112,768]{1,0:T(8,128)(2,1)S(1)}, u32[]{:S(2)}, u32[]{:S(2)}) %collective-permute-start.18) | collective-permute-done | bytes 172064 | tf_op jit(solution)/shard_map/ppermute | solution.py:680
  184.1 7.9 %collective-permute-start.19 = (bf16[112,768]{1,0:T(8,128)(2,1)}, bf16[112,768]{1,0:T(8,128)(2,1)S(1)}, u32[]{:S(2)}, u32[]{:S(2)}) collective-permute-start(bf16[112,768]{1,0:T(8,128)(2,1)} %get-tuple-element.104), channel_id=1, source_target_pairs={{0,16},{8,24},{16,0},{24,8},{1,17},{9,25},{17,1},{25,9},{2,18},{10... | collective-permute-start | bytes 516104 | tf_op jit(solution)/shard_map/ppermute | solution.py:680
  192.6 1.6 collective-permute-start.15
  194.2 1.2 collective-permute-start.16
  195.3 2.2 shard_map.275
  197.5 2.7 %collective-permute-done.19.z2 = bf16[112,768]{1,0:T(8,128)(2,1)S(1)} collective-permute-done((bf16[112,768]{1,0:T(8,128)(2,1)}, bf16[112,768]{1,0:T(8,128)(2,1)S(1)}, u32[]{:S(2)}, u32[]{:S(2)}) %collective-permute-start.19) | collective-permute-done | bytes 172064 | tf_op jit(solution)/shard_map/ppermute | solution.py:680
  201.5 2.3 %shard_map.276 = (bf16[96,768]{1,0:T(8,128)(2,1)}, bf16[96,768]{1,0:T(8,128)(2,1)}, bf16[96,768]{1,0:T(8,128)(2,1)}, bf16[96,768]{1,0:T(8,128)(2,1)}) custom-call(s32[32]{0:T(128)} %concatenate.3.ids, bf16[112,768]{1,0:T(8,128)(2,1)} %get-tuple-element.102.z0, bf16[112,768]{1,0:T(8,128)(2,1)} %copy-done.16, bf16[112,768]{1,0:T(8,128)(2,1)} %copy-done.17, ...), custom_call_target="tpu_custom_call" | custom-call | flops 1000000 | bytes 983168 | tf_op jit(solution)/shard_map/pallas_call | solution.py:349
  203.8 1.2 collective-permute-start.28
  205.9 1.4 collective-permute-start.30
  207.9 1.5 collective-permute-start.31
  209.4 4.4 %shard_map.268 = bf16[160,767]{1,0:T(8,128)(2,1)} custom-call(s32[32]{0:T(128)} %concatenate.3.ids, bf16[160,3072]{1,0:T(8,128)(2,1)} %get-tuple-element.85.active, bf16[3072,767]{1,0:T(8,128)(2,1)} %weight.7, f32[160,767]{1,0:T(8,128)} %get-tuple-element.86.middle, f32[1,767]{1,0:T(1,128)} %broadcast_in_dim.27.bias), custom_call_target="tpu_custom_call" | custom-call | flops 754974720 | bytes 6189564 | tf_op jit(solution)/shard_map/pallas_call | solution.py:349
  214.5 4.8 %shard_map.271 = bf16[160,767]{1,0:T(8,128)(2,1)} custom-call(s32[32]{0:T(128)} %concatenate.3.ids, bf16[240,384]{1,0:T(8,128)(2,1)} %get-tuple-element.95.h0, bf16[240,384]{1,0:T(8,128)(2,1)} %copy-done.13, bf16[240,384]{1,0:T(8,128)(2,1)} %copy-done.14, bf16[240,384]{1,0:T(8,128)(2,1)} %copy-done.15, bf16[768,2304]{1,0:T(8,128)(2,1)} %weight.9, ...), custom_call_target="tpu_custom_call" | custom-call | flops 566231040 | bytes 5016384 | tf_op jit(solution)/shard_map/pallas_call | solution.py:349
  220.0 2.1 shard_map.277
  (118 shorter events, 18.7 us)
Async XLA Ops:
  14.2 22.7 %copy-start.25 = (f32[767]{0:T(1024)S(1)}, f32[767]{0:T(1024)}, u32[]{:S(2)}) copy-start(f32[767]{0:T(1024)} %param.23) | copy-start | bytes 9208
  14.2 23.2 %copy-start.26 = (f32[768]{0:T(1024)S(1)}, f32[768]{0:T(1024)}, u32[]{:S(2)}) copy-start(f32[768]{0:T(1024)} %param.24) | copy-start | bytes 9220
  18.4 8.6 %collective-permute-start = (bf16[240,384]{1,0:T(8,128)(2,1)}, bf16[240,384]{1,0:T(8,128)(2,1)S(1)}, u32[]{:S(2)}, u32[]{:S(2)}) collective-permute-start(bf16[240,384]{1,0:T(8,128)(2,1)} %get-tuple-element.75), channel_id=1, source_target_pairs={{0,2},{1,3},{2,0},{3,1},{4,6},{5,7},{6,4},{7,5},{8,10},{9,11},{10,... | collective-permute-start | bytes 552968 | tf_op jit(solution)/shard_map/ppermute | solution.py:672
  21.4 10.3 %collective-permute-start.1 = (bf16[240,384]{1,0:T(8,128)(2,1)}, bf16[240,384]{1,0:T(8,128)(2,1)S(1)}, u32[]{:S(2)}, u32[]{:S(2)}) collective-permute-start(bf16[240,384]{1,0:T(8,128)(2,1)} %get-tuple-element.76), channel_id=1, source_target_pairs={{0,4},{1,5},{2,6},{3,7},{4,0},{5,1},{6,2},{7,3},{8,12},{9,13},{10,... | collective-permute-start | bytes 552968 | tf_op jit(solution)/shard_map/ppermute | solution.py:672
  22.9 8.7 %collective-permute-start.2 = (bf16[240,384]{1,0:T(8,128)(2,1)}, bf16[240,384]{1,0:T(8,128)(2,1)S(1)}, u32[]{:S(2)}, u32[]{:S(2)}) collective-permute-start(bf16[240,384]{1,0:T(8,128)(2,1)} %get-tuple-element.77), channel_id=1, source_target_pairs={{0,6},{1,7},{2,4},{3,5},{4,2},{5,3},{6,0},{7,1},{8,14},{9,15},{10,... | collective-permute-start | bytes 552968 | tf_op jit(solution)/shard_map/ppermute | solution.py:672
  27.1 4.6 %copy-start.10 = (bf16[240,384]{1,0:T(8,128)(2,1)}, bf16[240,384]{1,0:T(8,128)(2,1)S(1)}, u32[]{:S(2)}) copy-start(bf16[240,384]{1,0:T(8,128)(2,1)S(1)} %collective-permute-done.p1) | copy-start | bytes 552964
  34.8 3.2 %collective-permute-start.3 = (bf16[640,384]{1,0:T(8,128)(2,1)}, bf16[640,384]{1,0:T(8,128)(2,1)S(1)}, u32[]{:S(2)}, u32[]{:S(2)}) collective-permute-start(bf16[640,384]{1,0:T(8,128)(2,1)} %get-tuple-element.79.own), channel_id=1, source_target_pairs={{0,1},{1,0},{2,3},{3,2},{4,5},{5,4},{6,7},{7,6},{8,9},{9,8},{10,11... | collective-permute-start | bytes 1474568 | tf_op jit(solution)/shard_map/ppermute | solution.py:676
  34.8 38.9 %collective-permute-start.11 = (bf16[320,768]{1,0:T(8,128)(2,1)}, bf16[320,768]{1,0:T(8,128)(2,1)S(1)}, u32[]{:S(2)}, u32[]{:S(2)}) collective-permute-start(bf16[320,768]{1,0:T(8,128)(2,1)} %get-tuple-element.93.p0), channel_id=1, source_target_pairs={{0,2},{1,3},{2,0},{3,1},{4,6},{5,7},{6,4},{7,5},{8,10},{9,11},{10,... | collective-permute-start | bytes 1474568 | tf_op jit(solution)/shard_map/ppermute | solution.py:672
  36.0 39.2 %collective-permute-start.12 = (bf16[320,768]{1,0:T(8,128)(2,1)}, bf16[320,768]{1,0:T(8,128)(2,1)S(1)}, u32[]{:S(2)}, u32[]{:S(2)}) collective-permute-start(bf16[320,768]{1,0:T(8,128)(2,1)} %get-tuple-element.93.p0), channel_id=1, source_target_pairs={{0,4},{1,5},{2,6},{3,7},{4,0},{5,1},{6,2},{7,3},{8,12},{9,13},{10,... | collective-permute-start | bytes 1474568 | tf_op jit(solution)/shard_map/ppermute | solution.py:672
  50.0 8.9 %collective-permute-start.4 = (bf16[80,384]{1,0:T(8,128)(2,1)}, bf16[80,384]{1,0:T(8,128)(2,1)S(1)}, u32[]{:S(2)}, u32[]{:S(2)}) collective-permute-start(bf16[80,384]{1,0:T(8,128)(2,1)} %get-tuple-element.81), channel_id=1, source_target_pairs={{0,2},{1,3},{2,0},{3,1},{4,6},{5,7},{6,4},{7,5},{8,10},{9,11},{10,... | collective-permute-start | bytes 184328 | tf_op jit(solution)/shard_map/ppermute | solution.py:672
  51.5 8.9 %collective-permute-start.5 = (bf16[80,384]{1,0:T(8,128)(2,1)}, bf16[80,384]{1,0:T(8,128)(2,1)S(1)}, u32[]{:S(2)}, u32[]{:S(2)}) collective-permute-start(bf16[80,384]{1,0:T(8,128)(2,1)} %get-tuple-element.82), channel_id=1, source_target_pairs={{0,4},{1,5},{2,6},{3,7},{4,0},{5,1},{6,2},{7,3},{8,12},{9,13},{10,... | collective-permute-start | bytes 184328 | tf_op jit(solution)/shard_map/ppermute | solution.py:672
  52.0 6.9 %copy-start.2 = (bf16[320,768]{1,0:T(8,128)(2,1)S(1)}, bf16[320,768]{1,0:T(8,128)(2,1)}, u32[]{:S(2)}) copy-start(bf16[320,768]{1,0:T(8,128)(2,1)} %get-tuple-element.93.p0) | copy-start | bytes 1474564
  52.0 8.4 %collective-permute-start.6 = (bf16[80,384]{1,0:T(8,128)(2,1)}, bf16[80,384]{1,0:T(8,128)(2,1)S(1)}, u32[]{:S(2)}, u32[]{:S(2)}) collective-permute-start(bf16[80,384]{1,0:T(8,128)(2,1)} %get-tuple-element.83), channel_id=1, source_target_pairs={{0,6},{1,7},{2,4},{3,5},{4,2},{5,3},{6,0},{7,1},{8,14},{9,15},{10,... | collective-permute-start | bytes 184328 | tf_op jit(solution)/shard_map/ppermute | solution.py:672
  58.9 17.5 %collective-permute-start.13 = (bf16[320,768]{1,0:T(8,128)(2,1)S(1)}, bf16[320,768]{1,0:T(8,128)(2,1)S(1)}, u32[]{:S(2)}, u32[]{:S(2)}) collective-permute-start(bf16[320,768]{1,0:T(8,128)(2,1)S(1)} %copy-done.2), channel_id=1, source_target_pairs={{0,6},{1,7},{2,4},{3,5},{4,2},{5,3},{6,0},{7,1},{8,14},{9,15},{10,... | collective-permute-start | bytes 1474568 | tf_op jit(solution)/shard_map/ppermute | solution.py:672
  71.7 45.9 %collective-permute-start.21 = (bf16[480,768]{1,0:T(8,128)(2,1)}, bf16[480,768]{1,0:T(8,128)(2,1)S(1)}, u32[]{:S(2)}, u32[]{:S(2)}) collective-permute-start(bf16[480,768]{1,0:T(8,128)(2,1)} %get-tuple-element.107), channel_id=1, source_target_pairs={{0,2},{1,3},{2,0},{3,1},{4,6},{5,7},{6,4},{7,5},{8,10},{9,11},{10,... | collective-permute-start | bytes 2211848 | tf_op jit(solution)/shard_map/ppermute | solution.py:672
  72.9 44.7 %collective-permute-start.22 = (bf16[480,768]{1,0:T(8,128)(2,1)}, bf16[480,768]{1,0:T(8,128)(2,1)S(1)}, u32[]{:S(2)}, u32[]{:S(2)}) collective-permute-start(bf16[480,768]{1,0:T(8,128)(2,1)} %get-tuple-element.108), channel_id=1, source_target_pairs={{0,4},{1,5},{2,6},{3,7},{4,0},{5,1},{6,2},{7,3},{8,12},{9,13},{10,... | collective-permute-start | bytes 2211848 | tf_op jit(solution)/shard_map/ppermute | solution.py:672
  73.8 43.8 %copy-start.3 = (bf16[320,768]{1,0:T(8,128)(2,1)}, bf16[320,768]{1,0:T(8,128)(2,1)S(1)}, u32[]{:S(2)}) copy-start(bf16[320,768]{1,0:T(8,128)(2,1)S(1)} %collective-permute-done.11.p1) | copy-start | bytes 1474564
  73.8 43.8 %collective-permute-start.23 = (bf16[480,768]{1,0:T(8,128)(2,1)}, bf16[480,768]{1,0:T(8,128)(2,1)}, u32[]{:S(2)}, u32[]{:S(2)}) collective-permute-start(bf16[480,768]{1,0:T(8,128)(2,1)} %get-tuple-element.109), channel_id=1, source_target_pairs={{0,6},{1,7},{2,4},{3,5},{4,2},{5,3},{6,0},{7,1},{8,14},{9,15},{10,... | collective-permute-start | bytes 2211848 | tf_op jit(solution)/shard_map/ppermute | solution.py:672
  75.2 42.4 %copy-start.4 = (bf16[320,768]{1,0:T(8,128)(2,1)}, bf16[320,768]{1,0:T(8,128)(2,1)S(1)}, u32[]{:S(2)}) copy-start(bf16[320,768]{1,0:T(8,128)(2,1)S(1)} %collective-permute-done.12.p2) | copy-start | bytes 1474564
  75.2 35.0 %collective-permute-start.7 = (bf16[160,768]{1,0:T(8,128)(2,1)}, bf16[160,768]{1,0:T(8,128)(2,1)S(1)}, u32[]{:S(2)}, u32[]{:S(2)}) collective-permute-start(bf16[160,768]{1,0:T(8,128)(2,1)} %get-tuple-element.87.b0), channel_id=1, source_target_pairs={{0,2},{1,3},{2,0},{3,1},{4,6},{5,7},{6,4},{7,5},{8,10},{9,11},{10,... | collective-permute-start | bytes 737288 | tf_op jit(solution)/shard_map/ppermute | solution.py:672
  76.4 41.2 %copy-start.5 = (bf16[320,768]{1,0:T(8,128)(2,1)}, bf16[320,768]{1,0:T(8,128)(2,1)S(1)}, u32[]{:S(2)}) copy-start(bf16[320,768]{1,0:T(8,128)(2,1)S(1)} %collective-permute-done.13.p3) | copy-start | bytes 1474564
  76.4 35.4 %collective-permute-start.8 = (bf16[160,768]{1,0:T(8,128)(2,1)}, bf16[160,768]{1,0:T(8,128)(2,1)S(1)}, u32[]{:S(2)}, u32[]{:S(2)}) collective-permute-start(bf16[160,768]{1,0:T(8,128)(2,1)} %get-tuple-element.87.b0), channel_id=1, source_target_pairs={{0,4},{1,5},{2,6},{3,7},{4,0},{5,1},{6,2},{7,3},{8,12},{9,13},{10,... | collective-permute-start | bytes 737288 | tf_op jit(solution)/shard_map/ppermute | solution.py:672
  110.3 7.4 %copy-start.31 = (bf16[160,768]{1,0:T(8,128)(2,1)}, bf16[160,768]{1,0:T(8,128)(2,1)S(1)}, u32[]{:S(2)}) copy-start(bf16[160,768]{1,0:T(8,128)(2,1)S(1)} %collective-permute-done.7.b1) | copy-start | bytes 737284
  110.3 7.3 %collective-permute-start.9 = (bf16[160,768]{1,0:T(8,128)(2,1)}, bf16[160,768]{1,0:T(8,128)(2,1)S(1)}, u32[]{:S(2)}, u32[]{:S(2)}) collective-permute-start(bf16[160,768]{1,0:T(8,128)(2,1)} %get-tuple-element.87.b0), channel_id=1, source_target_pairs={{0,6},{1,7},{2,4},{3,5},{4,2},{5,3},{6,0},{7,1},{8,14},{9,15},{10,... | collective-permute-start | bytes 737288 | tf_op jit(solution)/shard_map/ppermute | solution.py:672
  111.8 5.9 %copy-start.32 = (bf16[160,768]{1,0:T(8,128)(2,1)}, bf16[160,768]{1,0:T(8,128)(2,1)S(1)}, u32[]{:S(2)}) copy-start(bf16[160,768]{1,0:T(8,128)(2,1)S(1)} %collective-permute-done.8.b2) | copy-start | bytes 737284
  125.6 23.6 %collective-permute-start.24 = (bf16[4,224,768]{2,1,0:T(8,128)(2,1)}, bf16[4,224,768]{2,1,0:T(8,128)(2,1)S(1)}, u32[]{:S(2)}, u32[]{:S(2)}) collective-permute-start(bf16[4,224,768]{2,1,0:T(8,128)(2,1)} %get-tuple-element.112), channel_id=1, source_target_pairs={{0,1},{1,0},{2,3},{3,2},{4,5},{5,4},{6,7},{7,6},{8,9},{9,8},{10,11... | collective-permute-start | bytes 4128776 | tf_op jit(solution)/shard_map/ppermute | solution.py:676
  138.7 2.2 collective-permute-start.10
  148.8 10.0 %collective-permute-start.17 = (bf16[352,768]{1,0:T(8,128)(2,1)}, bf16[352,768]{1,0:T(8,128)(2,1)S(1)}, u32[]{:S(2)}, u32[]{:S(2)}) collective-permute-start(bf16[352,768]{1,0:T(8,128)(2,1)} %get-tuple-element.101.send), channel_id=1, source_target_pairs={{0,1},{1,0},{2,3},{3,2},{4,5},{5,4},{6,7},{7,6},{8,9},{9,8},{10,11... | collective-permute-start | bytes 1622024 | tf_op jit(solution)/shard_map/ppermute | solution.py:676
  150.3 12.3 %copy-start.36 = (bf16[240,384]{1,0:T(8,128)(2,1)S(1)}, bf16[240,384]{1,0:T(8,128)(2,1)}, u32[]{:S(2)}) copy-start(bf16[240,384]{1,0:T(8,128)(2,1)} %get-tuple-element.96) | copy-start | bytes 552964
  150.3 42.3 %copy-start.35 = (bf16[240,384]{1,0:T(8,128)(2,1)S(1)}, bf16[240,384]{1,0:T(8,128)(2,1)}, u32[]{:S(2)}) copy-start(bf16[240,384]{1,0:T(8,128)(2,1)} %get-tuple-element.97) | copy-start | bytes 552964
  150.3 43.9 %copy-start.34 = (bf16[240,384]{1,0:T(8,128)(2,1)S(1)}, bf16[240,384]{1,0:T(8,128)(2,1)}, u32[]{:S(2)}) copy-start(bf16[240,384]{1,0:T(8,128)(2,1)} %get-tuple-element.98) | copy-start | bytes 552964
  153.3 38.7 %collective-permute-start.25 = (bf16[224,768]{1,0:T(8,128)(2,1)}, bf16[224,768]{1,0:T(8,128)(2,1)S(1)}, u32[]{:S(2)}, u32[]{:S(2)}) collective-permute-start(bf16[224,768]{1,0:T(8,128)(2,1)} %get-tuple-element.114), channel_id=1, source_target_pairs={{0,8},{8,16},{16,24},{24,0},{1,9},{9,17},{17,25},{25,1},{2,10},{10... | collective-permute-start | bytes 1032200 | tf_op jit(solution)/shard_map/ppermute | solution.py:680
  154.9 37.7 %collective-permute-start.26 = (bf16[224,768]{1,0:T(8,128)(2,1)}, bf16[224,768]{1,0:T(8,128)(2,1)S(1)}, u32[]{:S(2)}, u32[]{:S(2)}) collective-permute-start(bf16[224,768]{1,0:T(8,128)(2,1)} %get-tuple-element.115), channel_id=1, source_target_pairs={{0,16},{8,24},{16,0},{24,8},{1,17},{9,25},{17,1},{25,9},{2,18},{10... | collective-permute-start | bytes 1032200 | tf_op jit(solution)/shard_map/ppermute | solution.py:680
  157.5 36.7 %collective-permute-start.27 = (bf16[224,768]{1,0:T(8,128)(2,1)}, bf16[224,768]{1,0:T(8,128)(2,1)S(1)}, u32[]{:S(2)}, u32[]{:S(2)}) collective-permute-start(bf16[224,768]{1,0:T(8,128)(2,1)} %get-tuple-element.116), channel_id=1, source_target_pairs={{0,24},{8,0},{16,8},{24,16},{1,25},{9,1},{17,9},{25,17},{2,26},{10... | collective-permute-start | bytes 1032200 | tf_op jit(solution)/shard_map/ppermute | solution.py:680
  159.7 47.7 %copy-start.27 = (f32[767]{0:T(1024)S(1)}, f32[767]{0:T(1024)}, u32[]{:S(2)}) copy-start(f32[767]{0:T(1024)} %param.28) | copy-start | bytes 9208
  161.9 22.2 %collective-permute-start.18 = (bf16[112,768]{1,0:T(8,128)(2,1)}, bf16[112,768]{1,0:T(8,128)(2,1)S(1)}, u32[]{:S(2)}, u32[]{:S(2)}) collective-permute-start(bf16[112,768]{1,0:T(8,128)(2,1)} %get-tuple-element.103), channel_id=1, source_target_pairs={{0,8},{8,16},{16,24},{24,0},{1,9},{9,17},{17,25},{25,1},{2,10},{10... | collective-permute-start | bytes 516104 | tf_op jit(solution)/shard_map/ppermute | solution.py:680
  162.6 43.3 %collective-permute-start.14 = (bf16[240,384]{1,0:T(8,128)(2,1)S(1)}, bf16[240,384]{1,0:T(8,128)(2,1)S(1)}, u32[]{:S(2)}, u32[]{:S(2)}) collective-permute-start(bf16[240,384]{1,0:T(8,128)(2,1)S(1)} %copy-done.36), channel_id=1, source_target_pairs={{0,2},{1,3},{2,0},{3,1},{4,6},{5,7},{6,4},{7,5},{8,10},{9,11},{10,... | collective-permute-start | bytes 552968 | tf_op jit(solution)/shard_map/ppermute | solution.py:672
  184.1 16.8 %copy-start.16 = (bf16[112,768]{1,0:T(8,128)(2,1)}, bf16[112,768]{1,0:T(8,128)(2,1)S(1)}, u32[]{:S(2)}) copy-start(bf16[112,768]{1,0:T(8,128)(2,1)S(1)} %collective-permute-done.18.z1) | copy-start | bytes 516100
  184.1 16.1 %collective-permute-start.19 = (bf16[112,768]{1,0:T(8,128)(2,1)}, bf16[112,768]{1,0:T(8,128)(2,1)S(1)}, u32[]{:S(2)}, u32[]{:S(2)}) collective-permute-start(bf16[112,768]{1,0:T(8,128)(2,1)} %get-tuple-element.104), channel_id=1, source_target_pairs={{0,16},{8,24},{16,0},{24,8},{1,17},{9,25},{17,1},{25,9},{2,18},{10... | collective-permute-start | bytes 516104 | tf_op jit(solution)/shard_map/ppermute | solution.py:680
  192.0 8.8 %collective-permute-start.20 = (bf16[112,768]{1,0:T(8,128)(2,1)}, bf16[112,768]{1,0:T(8,128)(2,1)S(1)}, u32[]{:S(2)}, u32[]{:S(2)}) collective-permute-start(bf16[112,768]{1,0:T(8,128)(2,1)} %get-tuple-element.105), channel_id=1, source_target_pairs={{0,24},{8,0},{16,8},{24,16},{1,25},{9,1},{17,9},{25,17},{2,26},{10... | collective-permute-start | bytes 516104 | tf_op jit(solution)/shard_map/ppermute | solution.py:680
  192.6 15.3 %collective-permute-start.15 = (bf16[240,384]{1,0:T(8,128)(2,1)S(1)}, bf16[240,384]{1,0:T(8,128)(2,1)S(1)}, u32[]{:S(2)}, u32[]{:S(2)}) collective-permute-start(bf16[240,384]{1,0:T(8,128)(2,1)S(1)} %copy-done.35), channel_id=1, source_target_pairs={{0,4},{1,5},{2,6},{3,7},{4,0},{5,1},{6,2},{7,3},{8,12},{9,13},{10,... | collective-permute-start | bytes 552968 | tf_op jit(solution)/shard_map/ppermute | solution.py:672
  194.2 19.6 %collective-permute-start.16 = (bf16[240,384]{1,0:T(8,128)(2,1)S(1)}, bf16[240,384]{1,0:T(8,128)(2,1)S(1)}, u32[]{:S(2)}, u32[]{:S(2)}) collective-permute-start(bf16[240,384]{1,0:T(8,128)(2,1)S(1)} %copy-done.34), channel_id=1, source_target_pairs={{0,6},{1,7},{2,4},{3,5},{4,2},{5,3},{6,0},{7,1},{8,14},{9,15},{10,... | collective-permute-start | bytes 552968 | tf_op jit(solution)/shard_map/ppermute | solution.py:672
  203.8 15.5 %collective-permute-start.28 = (bf16[96,768]{1,0:T(8,128)(2,1)}, bf16[96,768]{1,0:T(8,128)(2,1)S(1)}, u32[]{:S(2)}, u32[]{:S(2)}) collective-permute-start(bf16[96,768]{1,0:T(8,128)(2,1)} %get-tuple-element.119), channel_id=1, source_target_pairs={{0,2},{1,3},{2,0},{3,1},{4,6},{5,7},{6,4},{7,5},{8,10},{9,11},{10,... | collective-permute-start | bytes 442376 | tf_op jit(solution)/shard_map/ppermute | solution.py:672
  205.0 14.3 %collective-permute-start.29 = (bf16[96,768]{1,0:T(8,128)(2,1)}, bf16[96,768]{1,0:T(8,128)(2,1)S(1)}, u32[]{:S(2)}, u32[]{:S(2)}) collective-permute-start(bf16[96,768]{1,0:T(8,128)(2,1)} %get-tuple-element.120), channel_id=1, source_target_pairs={{0,4},{1,5},{2,6},{3,7},{4,0},{5,1},{6,2},{7,3},{8,12},{9,13},{10,... | collective-permute-start | bytes 442376 | tf_op jit(solution)/shard_map/ppermute | solution.py:672
  205.9 7.9 %copy-start.13 = (bf16[240,384]{1,0:T(8,128)(2,1)}, bf16[240,384]{1,0:T(8,128)(2,1)S(1)}, u32[]{:S(2)}) copy-start(bf16[240,384]{1,0:T(8,128)(2,1)S(1)} %collective-permute-done.14.h1) | copy-start | bytes 552964
  205.9 13.4 %collective-permute-start.30 = (bf16[96,768]{1,0:T(8,128)(2,1)}, bf16[96,768]{1,0:T(8,128)(2,1)S(1)}, u32[]{:S(2)}, u32[]{:S(2)}) collective-permute-start(bf16[96,768]{1,0:T(8,128)(2,1)} %get-tuple-element.121), channel_id=1, source_target_pairs={{0,6},{1,7},{2,4},{3,5},{4,2},{5,3},{6,0},{7,1},{8,14},{9,15},{10,... | collective-permute-start | bytes 442376 | tf_op jit(solution)/shard_map/ppermute | solution.py:672
  207.9 5.9 %copy-start.14 = (bf16[240,384]{1,0:T(8,128)(2,1)}, bf16[240,384]{1,0:T(8,128)(2,1)S(1)}, u32[]{:S(2)}) copy-start(bf16[240,384]{1,0:T(8,128)(2,1)S(1)} %collective-permute-done.15.h2) | copy-start | bytes 552964
  207.9 11.4 %collective-permute-start.31 = (f32[24,768]{1,0:T(8,128)}, f32[24,768]{1,0:T(8,128)S(1)}, u32[]{:S(2)}, u32[]{:S(2)}) collective-permute-start(f32[24,768]{1,0:T(8,128)} %get-tuple-element.126), channel_id=1, source_target_pairs={{0,0},{1,1},{2,8},{3,9},{4,16},{5,17},{6,24},{7,25},{8,2},{9,3},{1... | collective-permute-start | bytes 221192 | tf_op jit(solution)/shard_map/ppermute | solution.py:803
  (21 other events, 21.9 us)

commit v2 on v0

--- a/solution.py
+++ b/solution.py
@@ -1,6 +1,8 @@
 import jax
 import jax.numpy as jnp
 from jax import lax
+from jax.experimental import pallas as pl
+from jax.experimental.pallas import tpu as pltpu
 from jax.sharding import PartitionSpec as P
 
 D = 768
@@ -51,7 +53,7 @@
     return (shards // width, width * unit)
 
 
-def body(
+def general_body(
     residual_in,
     out_cotangent,
     first_gain,
@@ -335,6 +337,645 @@
     )
 
 
+DC = 767
+SPLIT = 192
+FF = 3072
+low = jnp.bfloat16
+wide = jnp.float32
+VMEM = pl.BlockSpec(memory_space=pltpu.VMEM)
+SMEM = pl.BlockSpec(memory_space=pltpu.SMEM)
+
+def padded_bytes(shape, dtype):
+    shape = (1, 1) + tuple(shape)
+    size = jnp.dtype(dtype).itemsize
+    rows, lanes = -(-shape[-2] // 16) * 16, -(-shape[-1] // 128) * 128
+    for d in shape[:-2]:
+        rows = rows * d
+    return rows * lanes * size
+
+
+def call(kernel, outs, ins, scratch=(), extra=8, small=0):
+    shapes = [jax.ShapeDtypeStruct(s, d) for s, d in outs]
+    held = [(s, d) for s, d in outs] + [(x.shape, x.dtype) for x in ins[small:]]
+    held += [(s.shape, s.dtype) for s in scratch]
+    limit = sum(padded_bytes(s, d) for s, d in held) + extra * 1024 * 1024
+    return pl.pallas_call(
+        kernel,
+        out_shape=shapes,
+        in_specs=[SMEM] * small + [VMEM] * (len(ins) - small),
+        out_specs=[VMEM] * len(outs),
+        scratch_shapes=list(scratch),
+        compiler_params=pltpu.CompilerParams(vmem_limit_bytes=min(limit, 60 * 1024 * 1024)),
+        cost_estimate=pl.CostEstimate(
+            flops=1000,
+            bytes_accessed=1000,
+            transcendentals=0,
+        ),
+    )(*ins)
+
+
+def here():
+    index = lax.axis_index("blk")
+    return index // 2, lax.axis_index("bucket"), index % 2
+
+
+def full_of(x):
+    rows=x.shape[0]
+    wide_x=jnp.concatenate([x,jnp.zeros((rows,1),x.dtype)],axis=1)
+    last=lax.broadcasted_iota(jnp.int32,(rows,D),1)==D-1
+    return jnp.where(last,-jnp.sum(x,axis=1,keepdims=True),wide_x)
+
+def row(ref):
+    return ref[...].reshape(1, ref.shape[0])
+
+
+def nt(a, b):
+    return lax.dot_general(a, b, (((1,), (1,)), ((), ())), preferred_element_type=wide)
+
+
+def tn(a, b):
+    return lax.dot_general(a, b, (((0,), (0,)), ((), ())), preferred_element_type=wide)
+
+
+def packed(x):
+    half = x.shape[0] // 2
+    return jnp.concatenate([x[:half], x[half:]], axis=1).astype(low)
+
+
+def unpacked(x):
+    x = x.astype(wide)
+    half = x.shape[1] // 2
+    return jnp.concatenate([x[:, :half], x[:, half:]], axis=0)
+
+
+def split_pair(x):
+    hi = x.astype(low)
+    return hi, (x - hi.astype(wide)).astype(low)
+
+
+def head_mask(x, h):
+    lane = lax.broadcasted_iota(jnp.int32, x.shape, 1)
+    return jnp.where((lane >= h * 64) & (lane < (h + 1) * 64), x, jnp.zeros_like(x))
+
+
+def limits(spans, offsets, lengths, bucket, chip, core, half):
+    place = spans[chip * 4 + core * 2 + half] * 80 + lax.broadcasted_iota(jnp.int32, (80, 1), 0)
+    one, two = offsets[0, 0], offsets[0, 1]
+    first = (place >= one) & (place < one + lengths[bucket, 0])
+    second = (place >= two) & (place < two + lengths[bucket, 1])
+    return jnp.where(first, one, two), jnp.where(first | second, place, -1)
+
+
+def entry_kernel(resid, gain, weight, qbias, vbias, s0, s1, s2, s3, hidden_out, root_out, buf):
+    me = here()[0]
+    full = full_of(resid[...].astype(wide))
+    root = jnp.sqrt(jnp.mean(full * full, axis=1, keepdims=True) + epsilon)
+    root_out[...] = root
+    hidden = (full / root * row(gain)).astype(low)
+    hidden_out[...] = hidden
+    for i in range(3):
+        p = jnp.dot(hidden, weight[:, i * D : (i + 1) * D], preferred_element_type=wide)
+        if i == 0:
+            p = (p + row(qbias)) * 0.125
+        if i == 2:
+            p = p + row(vbias)
+        for j in range(4):
+            buf[j ^ me, i * 80 : (i + 1) * 80, :] = packed(p[:, j * SPLIT : (j + 1) * SPLIT])
+    for r, s in enumerate((s0, s1, s2, s3)):
+        s[...] = buf[r]
+
+
+def push_kernel(cot, weight, out):
+    for i in range(4):
+        out[:, i * D : (i + 1) * D] = nt(cot[...], weight[i * D : (i + 1) * D, :])
+
+
+def columns_kernel(weight, out):
+    me = here()[0]
+    for j in range(4):
+
+        @pl.when(me == j)
+        def _():
+            for i in range(3):
+                piece = weight[:, i * D + j * SPLIT : i * D + (j + 1) * SPLIT].astype(wide)
+                out[:, i * SPLIT : (i + 1) * SPLIT] = piece.astype(low)
+
+
+def assemble_kernel(p0, p1, p2, p3, query, both):
+    for r, p in enumerate((p0, p1, p2, p3)):
+        rows = slice(r * 160, (r + 1) * 160)
+        query[rows, :] = unpacked(p[0:80, :]).astype(low)
+        both[rows, :SPLIT] = unpacked(p[80:160, :]).astype(low)
+        both[rows, SPLIT:] = unpacked(p[160:240, :]).astype(low)
+
+
+def forward_kernel(
+    spans, offsets, lengths, query, own, sib, chance, attended, b0, b1, b2, b3, keys, vals, scores
+):
+    me, bucket, core = here()
+    keys[:640, :] = own[:, :SPLIT]
+    keys[640:, :] = sib[:, :SPLIT]
+    v = jnp.concatenate([own[:, SPLIT:].astype(wide), sib[:, SPLIT:].astype(wide)], axis=0)
+    for h in range(3):
+        vals[h] = head_mask(v, h).astype(low)
+    lane = lax.broadcasted_iota(jnp.int32, (1, 1280), 1)
+    place = lane
+    for blk in range(16):
+        chip = ((blk % 8) // 2) ^ me
+        span = spans[chip * 4 + (core ^ (blk // 8)) * 2 + blk % 2]
+        place = jnp.where((lane >= blk * 80) & (lane < (blk + 1) * 80), lane + (span - blk) * 80, place)
+    q = query[...].astype(wide)
+    for h in range(3):
+        scores[...] = nt(head_mask(q, h).astype(low), keys[...])
+        for blk in range(8):
+            rows = slice(blk * 80, (blk + 1) * 80)
+            lo, hi = limits(spans, offsets, lengths, bucket, (blk // 2) ^ me, core, blk % 2)
+            s = jnp.where((place >= lo) & (place <= hi), scores[rows, :], masked_value)
+            peak = jnp.max(s, axis=1, keepdims=True)
+            w = jnp.exp(s - peak)
+            total = jnp.sum(w, axis=1, keepdims=True)
+            chance[h, rows, :] = (w * jnp.where(hi >= 0, 1.0 / total, 0.0)).astype(low)
+        part = jnp.dot(chance[h], vals[h], preferred_element_type=wide)
+        if h == 0:
+            attended[...] = part
+        else:
+            attended[...] += part
+    acc = attended[...]
+    for r, b in enumerate((b0, b1, b2, b3)):
+        b[...] = packed(acc[r * 160 : (r + 1) * 160])
+
+
+def middle_kernel(
+    spans, offsets, lengths, p0, p1, p2, p3, out_weight, out_bias, resid, root_in, cot, gain, up_weight, up_bias, push,
+    d0, d1, d2, d3, a0, a1, a2, a3, n0, n1, n2, n3, branch_own, middle, middle_grad, vector, dbuf, abuf, nbuf,
+):
+    me, bucket, core = here()
+    branch = row(out_bias)
+    for r, p in enumerate((p0, p1, p2, p3)):
+        w = out_weight[pl.ds(pl.multiple_of((me ^ r) * SPLIT, SPLIT), SPLIT), :]
+        branch = branch + jnp.dot(unpacked(p[...]).astype(low), w, preferred_element_type=wide)
+    mid = resid[...].astype(wide) + branch
+    middle[...] = mid
+    full = full_of(mid)
+    root = jnp.sqrt(jnp.mean(full * full, axis=1, keepdims=True) + epsilon)
+    n = full / root
+    hidden = (n * row(gain)).astype(low)
+    for r in range(4):
+        nbuf[r, 0:160, :] = hidden
+    e = jnp.zeros((160, D), wide)
+    c = 0.7978845608028654
+    up_sums = []
+    for blk in range(4):
+        cols = slice(blk * D, (blk + 1) * D)
+        u = jnp.dot(hidden, up_weight[:, cols], preferred_element_type=wide) + up_bias[cols].reshape(1, D)
+        t = jnp.tanh(c * (u + 0.044715 * u * u * u))
+        abuf[blk ^ bucket] = (0.5 * u * (1.0 + t)).astype(low)
+        slope = 0.5 * (1.0 + t) + 0.5 * u * (1.0 - t * t) * (c * (1.0 + 3 * 0.044715 * u * u))
+        g = (push[:, cols] * slope).astype(low)
+        nbuf[blk ^ me, 160:320, :] = g
+        up_sums.append(jnp.sum(g.astype(wide), axis=0, keepdims=True))
+        e = e + nt(g, up_weight[:, cols])
+    gain_sum = jnp.sum(e * n, axis=0, keepdims=True)
+    eg = e * row(gain)
+    f = (eg - n * jnp.mean(eg * n, axis=1, keepdims=True)) / root
+    cot_wide = jnp.concatenate([cot[...].astype(wide), jnp.zeros((160, 1), wide)], axis=1)
+    lane = lax.broadcasted_iota(jnp.int32, (160, D), 1)
+    last = jnp.sum(jnp.where(lane == D - 1, f, 0.0), axis=1, keepdims=True)
+    grad = jnp.where(lane == D - 1, 0.0, cot_wide + f - last)
+    middle_grad[...] = grad
+    grad_low = grad.astype(low)
+    grad_wide = grad_low.astype(wide)
+    branch_own[...] = grad_low
+    back = nt(grad_wide[:, :DC].astype(low), out_weight[...])
+    for j in range(4):
+        dbuf[j ^ me] = packed(back[:, j * SPLIT : (j + 1) * SPLIT])
+    for r in range(4):
+        (d0, d1, d2, d3)[r][...] = dbuf[r]
+        (a0, a1, a2, a3)[r][...] = abuf[r]
+        (n0, n1, n2, n3)[r][...] = nbuf[r]
+    ends = [limits(spans, offsets, lengths, bucket, me, core, half)[1] for half in range(2)]
+    valid = jnp.where(jnp.concatenate(ends, axis=0) >= 0, 1.0, 0.0)
+    one = jnp.sum(valid * root_in[...], axis=0, keepdims=True)
+    two = jnp.sum(valid * root, axis=0, keepdims=True)
+    at = lax.broadcasted_iota(jnp.int32, (1, D), 1)
+    stats = jnp.where(at == 0, one, jnp.where(at == 1, two, 0.0))
+    zero = jnp.zeros((1, D), wide)
+    sums = [zero, zero, zero, jnp.sum(grad_wide, axis=0, keepdims=True), gain_sum] + up_sums
+    sums += [jnp.sum(cot_wide, axis=0, keepdims=True), stats] + [zero] * 5
+    vector[...] = jnp.concatenate(sums, axis=0)
+
+
+def closing_kernel(a0, a1, a2, a3, weight, middle, bias, out):
+    bucket = here()[1]
+    acc = middle[...] + row(bias)
+    for d, a in enumerate((a0, a1, a2, a3)):
+        w = weight[pl.ds(pl.multiple_of((bucket ^ d) * D, D), D), :]
+        acc = acc + jnp.dot(a[...], w, preferred_element_type=wide)
+    out[...] = acc.astype(low)
+
+
+def backward_kernel(
+    d0, d1, d2, d3, query, own, sib, chance, attended, query_grad, both_grad, away_one, away_two, keys, vals, grads, slopes
+):
+    for r, d in enumerate((d0, d1, d2, d3)):
+        grads[r * 160 : (r + 1) * 160, :] = unpacked(d[...]).astype(low)
+    k = jnp.concatenate([own[:, :SPLIT], sib[:, :SPLIT]], axis=0).astype(wide)
+    for h in range(3):
+        keys[h] = head_mask(k, h).astype(low)
+    vals[:640, :] = own[:, SPLIT:].astype(wide).astype(low)
+    vals[640:, :] = sib[:, SPLIT:].astype(wide).astype(low)
+    dq = jnp.zeros((640, SPLIT), wide)
+    dk = jnp.zeros((1280, SPLIT), wide)
+    dv = jnp.zeros((1280, SPLIT), wide)
+    g = grads[...].astype(wide)
+    q = query[...].astype(wide)
+    for h in range(3):
+        gh = head_mask(g, h)
+        gl = gh.astype(low)
+        delta = jnp.sum(gh * attended[...], axis=1, keepdims=True)
+        for r in range(4):
+            rows = slice(r * 160, (r + 1) * 160)
+            push = nt(gl[rows, :], vals[...])
+            slopes[rows, :] = (chance[h, rows, :].astype(wide) * (push - delta[rows, :])).astype(low)
+        dq = dq + jnp.dot(slopes[...], keys[h], preferred_element_type=wide)
+        dk = dk + tn(slopes[...], head_mask(q, h).astype(low))
+        dv = dv + tn(chance[h], gl)
+    query_grad[...] = (dq * 0.125).astype(low)
+    both_grad[:, :SPLIT] = dk[:640]
+    both_grad[:, SPLIT:] = dv[:640]
+    away_one[:, :SPLIT] = dk[640:960].astype(low)
+    away_one[:, SPLIT:] = dv[640:960].astype(low)
+    away_two[:, :SPLIT] = dk[960:].astype(low)
+    away_two[:, SPLIT:] = dv[960:].astype(low)
+
+
+def late_kernel(
+    query_grad, both_grad, arrive_one, arrive_two, i0, i1, i2, i3, a0, a1, a2, a3, c0, c1, c2, c3, p0, p1, p2, p3, branch_own, columns, gain, vector,
+    h0, h1, h2, h3, keep_x, keep_z, send, left, right, heads, xbuf, zbuf, obuf,
+):
+    me, bucket, core = here()
+    arrived = jnp.concatenate([arrive_one[...].astype(wide), arrive_two[...].astype(wide)], axis=0)
+    both = both_grad[...] + arrived
+    parts = [query_grad[...].astype(wide), both[:, :SPLIT], both[:, SPLIT:]]
+    parts = [p.astype(low).astype(wide) for p in parts]
+    for r, h in enumerate((h0, h1, h2, h3)):
+        left[r * 160 : (r + 1) * 160, :] = (i0, i1, i2, i3)[r][...]
+        for i in range(3):
+            h[i * 80 : (i + 1) * 80, :] = packed(parts[i][r * 160 : (r + 1) * 160])
+    heads[...] = jnp.concatenate(parts, axis=1).astype(low)
+    grad = tn(left[...], heads[...])
+    sums = jnp.sum(grad * columns[...].astype(wide), axis=1, keepdims=True)
+    gain_row = jnp.transpose(jnp.broadcast_to(sums, (D, 128)))[0:1] / row(gain)
+    lane = lax.broadcasted_iota(jnp.int32, (1, D), 1)
+    mine = (lane >= me * SPLIT) & (lane < (me + 1) * SPLIT)
+
+    def column_sum(x):
+        s = jnp.sum(x, axis=0, keepdims=True)
+        return jnp.where(mine, jnp.concatenate([s] * 4, axis=1), 0.0)
+
+    at = lax.broadcasted_iota(jnp.int32, (16, D), 0)
+    total = vector[...] + jnp.where(at == 0, gain_row, 0.0)
+    total = total + jnp.where(at == 1, column_sum(parts[0]), 0.0)
+    total = total + jnp.where(at == 2, column_sum(parts[2]), 0.0)
+    thirds = [grad[:, i * SPLIT : (i + 1) * SPLIT] for i in range(3)]
+    for b in range(4):
+        for c in range(2):
+            block = []
+            for part in thirds:
+                starts = [b * 192 + j * 48 + c * 24 for j in range(4)]
+                block.append(jnp.concatenate([part[s : s + 24] for s in starts], axis=1))
+            block.append(jnp.zeros((8, D), wide))
+            zbuf[c ^ core, b ^ bucket] = jnp.concatenate(block, axis=0).astype(low)
+    for d in range(4):
+        cot = (c0, c1, c2, c3)[d][...].astype(wide)
+        right[d * 160 : (d + 1) * 160, :] = jnp.concatenate([cot, jnp.zeros((160, 1), wide)], axis=1).astype(low)
+        left[d * 160 : (d + 1) * 160, :] = (a0, a1, a2, a3)[d][...]
+    down = tn(left[...], right[...])
+    for j in range(4):
+        for c in range(2):
+            s = j * 192 + c * 96
+            xbuf[c ^ core, j ^ me, 0:96, :] = down[s : s + 96].astype(low)
+    for r, p in enumerate((p0, p1, p2, p3)):
+        out = tn(unpacked(p[...]).astype(low), branch_own[...])
+        for j in range(4):
+            for c in range(2):
+                s = j * 48 + c * 24
+                obuf[c ^ core, j ^ me, me ^ r ^ bucket] = out[s : s + 24]
+    for c in range(2):
+        for r in range(4):
+            xbuf[c, r, 96:192, :] = jnp.concatenate([obuf[c, r, d] for d in range(4)], axis=0).astype(low)
+    keep_x[...] = xbuf[0]
+    keep_z[...] = zbuf[0]
+    for r in range(4):
+        send[r * 192 : (r + 1) * 192, :] = xbuf[1, r]
+        send[768 + r * 80 : 848 + r * 80, :] = zbuf[1, r]
+    hi, lo = split_pair(total)
+    send[1088:1104, :] = hi
+    send[1104:1120, :] = lo
+
+
+def late_sum_kernel(keep_x, keep_z, send, arrived, h0, h1, h2, h3, x0, x1, x2, x3, z0, z1, z2, z3):
+    own = send[1088:1104, :].astype(wide) + send[1104:1120, :].astype(wide)
+    hi, lo = split_pair(own + (arrived[1088:1104, :].astype(wide) + arrived[1104:1120, :].astype(wide)))
+    for r in range(4):
+        x, z, h = (x0, x1, x2, x3)[r], (z0, z1, z2, z3)[r], (h0, h1, h2, h3)[r]
+        x[0:192, :] = (keep_x[r].astype(wide) + arrived[r * 192 : (r + 1) * 192, :].astype(wide)).astype(low)
+        x[192:272, 0:384] = h[0:80, :]
+        x[192:272, 384:768] = h[80:160, :]
+        x[272:352, 0:384] = h[160:240, :]
+        x[272:352, 384:768] = jnp.zeros((80, 384), low)
+        came = arrived[768 + r * 80 : 848 + r * 80, :].astype(wide)
+        z[0:80, :] = (keep_z[r].astype(wide) + came).astype(low)
+        z[80:96, :] = hi
+        z[96:112, :] = lo
+
+
+def up_grad_kernel(n0, n1, n2, n3, keep, send, left, right, buf):
+    me, bucket, core = here()
+    for r in range(4):
+        rows = slice(r * 160, (r + 1) * 160)
+        n = (n0, n1, n2, n3)[r]
+        left[rows, :] = n[0:160, :]
+        right[rows, :] = n[160:320, :]
+    up = tn(left[...], right[...])
+    for b in range(4):
+        for c in range(2):
+            starts = [b * 192 + j * 48 + c * 24 for j in range(4)]
+            block = jnp.concatenate([up[s : s + 24] for s in starts], axis=0)
+            buf[c ^ core, b ^ bucket] = block.astype(low)
+    keep[...] = buf[0]
+    send[...] = buf[1]
+
+
+def up_sum_kernel(keep, arrived, z0, z1, z2, z3):
+    for d, z in enumerate((z0, z1, z2, z3)):
+        z[...] = (keep[d].astype(wide) + arrived[d].astype(wide)).astype(low)
+
+
+def final_send_kernel(z0, z1, z2, z3, w0, w1, w2, w3, f0, f1, f2, f3, buf, vec):
+    me, bucket, core = here()
+    zs = (z0, z1, z2, z3)
+    ins = sum(z[0:72, :].astype(wide) for z in zs)
+    ups = sum(w[...].astype(wide) for w in (w0, w1, w2, w3))
+    for d, z in enumerate(zs):
+        vec[bucket ^ d] = z[80:96, :].astype(wide) + z[96:112, :].astype(wide)
+    hi, lo = split_pair(vec[0] + vec[1] + vec[2] + vec[3])
+    pad = jnp.zeros((8, D), wide)
+    rest = jnp.zeros((24, SPLIT), wide)
+    for j in range(4):
+        lanes = slice(j * SPLIT, (j + 1) * SPLIT)
+        wide_rows = [ins[i * 24 : (i + 1) * 24, lanes] for i in range(3)] + [rest]
+        block = [ups[j * 24 : (j + 1) * 24], pad, jnp.concatenate(wide_rows, axis=1), pad]
+        buf[j ^ me] = jnp.concatenate(block, axis=0).astype(low)
+    for r, f in enumerate((f0, f1, f2, f3)):
+        f[0:16, :] = hi
+        f[16:32, :] = lo
+        f[32:96, :] = buf[r]
+
+
+def final_kernel(
+    lengths, f0, f1, f2, f3, in_total, up_total, first, query, value, output, second, up_bias, down, stats, buf
+):
+    me = here()[0]
+    for r, f in enumerate((f0, f1, f2, f3)):
+        buf[r ^ me] = f[...].astype(wide)
+    total = buf[0, 0:16] + buf[0, 16:32]
+    for j in (1, 2, 3):
+        total = total + (buf[j, 0:16] + buf[j, 16:32])
+    first[...] = total[0]
+    query[...] = total[1]
+    value[...] = total[2]
+    output[...] = total[3, :DC]
+    second[...] = total[4]
+    for i in range(4):
+        up_bias[i * D : (i + 1) * D] = total[5 + i]
+    down[...] = total[9, :DC]
+    count = lengths[0, 0] + lengths[0, 1]
+    for b in (1, 2, 3):
+        count = count + lengths[b, 0] + lengths[b, 1]
+    stats[...] = total[10, :2] / count.astype(wide)
+    for j in range(4):
+        up_total[:, j * D : (j + 1) * D] = buf[j, 32:56, :]
+    for i in range(3):
+        piece = jnp.concatenate([buf[j, 64:88, i * SPLIT : (i + 1) * SPLIT] for j in range(4)], axis=1)
+        in_total[:, i * D : (i + 1) * D] = piece
+
+
+def home_kernel(x0, x1, x2, x3, weight, resid, gain, middle_grad, out, buf):
+    me = here()[0]
+    for r, x in enumerate((x0, x1, x2, x3)):
+        buf[r ^ me, 0:80, :] = x[192:272, 0:384]
+        buf[r ^ me, 80:160, :] = x[192:272, 384:768]
+        buf[r ^ me, 160:240, :] = x[272:352, 0:384]
+    e = jnp.zeros((160, D), wide)
+    for i in range(3):
+        g = jnp.concatenate([unpacked(buf[j, i * 80 : (i + 1) * 80, :]) for j in range(4)], axis=1)
+        e = e + nt(g.astype(low), weight[:, i * D : (i + 1) * D])
+    full = full_of(resid[...].astype(wide))
+    root = jnp.sqrt(jnp.mean(full * full, axis=1, keepdims=True) + epsilon)
+    n = full / root
+    eg = e * row(gain)
+    f = (eg - n * jnp.mean(eg * n, axis=1, keepdims=True)) / root
+    lane = lax.broadcasted_iota(jnp.int32, (160, D), 1)
+    last = jnp.sum(jnp.where(lane == D - 1, f, 0.0), axis=1, keepdims=True)
+    out[...] = (middle_grad[...] + f - last)[:, :DC].astype(low)
+
+
+def down_sum_kernel(x0, x1, x2, x3, down_total, o0, o1, o2, o3):
+    total = x0[0:192, :].astype(wide)
+    for x in (x1, x2, x3):
+        total = total + x[0:192, :].astype(wide)
+    down_total[...] = total[0:96, :DC]
+    for d, o in enumerate((o0, o1, o2, o3)):
+        block = [total[96 + d * 24 : 120 + d * 24], jnp.zeros((8, D), wide)]
+        o[...] = jnp.concatenate(block, axis=0).astype(low)
+
+
+def out_sum_kernel(o0, o1, o2, o3, out_total):
+    total = o0[...].astype(wide) + o1[...].astype(wide) + o2[...].astype(wide) + o3[...].astype(wide)
+    out_total[...] = total[0:24, :DC]
+
+def swap_chip(block, step):
+    return lax.ppermute(block, "blk", [(k, k ^ (2 * step)) for k in range(8)])
+
+
+def swap_core(block):
+    return lax.ppermute(block, "blk", [(k, k ^ 1) for k in range(8)])
+
+
+def shift_bucket(block, step):
+    return lax.ppermute(block, "bucket", [(b, b ^ step) for b in range(4)])
+
+
+def exchange(blocks):
+    got = {r: swap_chip(blocks[r], r) for r in (3, 1, 2)}
+    return [blocks[0], got[1], got[2], got[3]]
+
+
+def over_buckets(blocks):
+    got = {d: shift_bucket(blocks[d], d) for d in (2, 1, 3)}
+    return [blocks[0], got[1], got[2], got[3]]
+
+
+def after(values, *others):
+    return lax.optimization_barrier((tuple(values), others))[0]
+
+
+def body(
+    residual_in,
+    out_cotangent,
+    first_gain,
+    input_weight,
+    query_bias,
+    value_bias,
+    output_weight,
+    output_bias,
+    second_gain,
+    up_weight,
+    up_bias,
+    down_weight,
+    down_bias,
+    lengths,
+    offsets,
+    span_order,
+):
+    where = [span_order, offsets, lengths]
+    packed_block = ((240, 2 * SPLIT), low)
+    token = ((160, D), low)
+    cots = over_buckets([out_cotangent] * 4)
+    s0, s1, s2, s3, hidden, root_one = call(
+        entry_kernel,
+        [packed_block] * 4 + [token, ((160, 1), wide)],
+        [residual_in, first_gain, input_weight, query_bias, value_bias],
+        [pltpu.VMEM((4, 240, 2 * SPLIT), low)],
+    )
+    got = exchange([s0, s1, s2, s3])
+    (push,) = call(push_kernel, [((160, FF), wide)], [out_cotangent, down_weight])
+    hiddens = exchange([hidden] * 4)
+    got = list(after(got, push, cots[1], cots[3]))
+    query, own_both = call(assemble_kernel, [((640, SPLIT), low), ((640, 2 * SPLIT), low)], got)
+    sib_both = swap_core(own_both)
+    backed = ((80, 2 * SPLIT), low)
+    chance, attended, b0, b1, b2, b3 = call(
+        forward_kernel,
+        [((3, 640, 1280), low), ((640, SPLIT), wide)] + [backed] * 4,
+        where + [query, own_both, sib_both],
+        [pltpu.VMEM((1280, SPLIT), low), pltpu.VMEM((3, 1280, SPLIT), low), pltpu.VMEM((640, 1280), wide)],
+        small=3,
+    )
+    back = exchange([b0, b1, b2, b3])
+    back = list(after(back, cots[2], *hiddens[1:]))
+    (columns,) = call(columns_kernel, [((D, 3 * SPLIT), low)], after([input_weight], b0))
+    outs = call(
+        middle_kernel,
+        [backed] * 4
+        + [token] * 4
+        + [((320, D), low)] * 4
+        + [token, ((160, DC), wide), ((160, D), wide), ((16, D), wide)],
+        where
+        + back
+        + [output_weight, output_bias, residual_in, root_one, out_cotangent, second_gain]
+        + [up_weight, up_bias, push],
+        [pltpu.VMEM((4, 80, 2 * SPLIT), low), pltpu.VMEM((4, 160, D), low), pltpu.VMEM((4, 320, D), low)],
+        small=3,
+    )
+    actives, lates = list(outs[4:8]), list(outs[8:12])
+    branch_own, middle, middle_grad, vector = outs[12:]
+    grads = exchange(outs[:4])
+    (residual_out,) = call(
+        closing_kernel,
+        [((160, DC), low)],
+        actives + [down_weight, middle, down_bias],
+    )
+    actives = over_buckets(actives)
+    lates = exchange(after(lates, grads[1]))
+    query_grad, both_grad, *away = call(
+        backward_kernel,
+        [((640, SPLIT), low), ((640, 2 * SPLIT), wide)] + [((320, 2 * SPLIT), low)] * 2,
+        grads + [query, own_both, sib_both, chance, attended],
+        [
+            pltpu.VMEM((3, 1280, SPLIT), low),
+            pltpu.VMEM((1280, SPLIT), low),
+            pltpu.VMEM((640, SPLIT), low),
+            pltpu.VMEM((640, 1280), low),
+        ],
+    )
+    arrived = [swap_core(x) for x in after(away, *actives[1:])]
+    arrived = list(after(arrived, lates[1], lates[2]))
+    outs = call(
+        late_kernel,
+        [packed_block] * 4 + [((4, 192, D), low), ((4, 80, D), low), ((1120, D), low)],
+        [query_grad, both_grad] + arrived + hiddens + actives + cots + back + [branch_own, columns, first_gain, vector],
+        [
+            pltpu.VMEM((640, D), low),
+            pltpu.VMEM((640, D), low),
+            pltpu.VMEM((640, 3 * SPLIT), low),
+            pltpu.VMEM((2, 4, 192, D), low),
+            pltpu.VMEM((2, 4, 80, D), low),
+            pltpu.VMEM((2, 4, 4, 24, D), wide),
+        ],
+    )
+    homes = list(outs[:4])
+    keep_x, keep_z, send = outs[4:]
+    outs = call(
+        late_sum_kernel,
+        [((352, D), low)] * 4 + [((112, D), low)] * 4,
+        [keep_x, keep_z, send, swap_core(send)] + homes,
+    )
+    in_z = over_buckets(outs[4:])
+    home = exchange(outs[:4])
+    keep, send = call(
+        up_grad_kernel,
+        [((4, 96, D), low)] * 2,
+        list(after(lates, *in_z[1:])),
+        [
+            pltpu.VMEM((640, D), low),
+            pltpu.VMEM((640, D), low),
+            pltpu.VMEM((2, 4, 96, D), low),
+        ],
+    )
+    up_z = over_buckets(call(up_sum_kernel, [((96, D), low)] * 4, [keep, swap_core(send)]))
+    down_total, *pieces = call(down_sum_kernel, [((96, DC), wide)] + [((32, D), low)] * 4, home)
+    (out_total,) = call(out_sum_kernel, [((24, DC), wide)], over_buckets(pieces))
+    (residual_grad,) = call(
+        home_kernel,
+        [((160, DC), low)],
+        home + [input_weight, residual_in, first_gain, middle_grad],
+        [pltpu.VMEM((4, 240, 2 * SPLIT), low)],
+    )
+    finals = call(
+        final_send_kernel,
+        [((96, D), low)] * 4,
+        in_z + up_z,
+        [pltpu.VMEM((4, 64, D), low), pltpu.VMEM((4, 16, D), wide)],
+    )
+    in_total, up_total, first, query_sum, value_sum, output, second, up_sum_bias, down, stats = call(
+        final_kernel,
+        [((24, 3 * D), wide), ((24, FF), wide)]
+        + [((D,), wide)] * 3
+        + [((DC,), wide), ((D,), wide), ((FF,), wide), ((DC,), wide), ((2,), wide)],
+        [lengths] + exchange(finals),
+        [pltpu.VMEM((4, 96, D), wide)],
+        small=1,
+    )
+    return (
+        residual_out,
+        residual_grad,
+        first,
+        in_total,
+        query_sum,
+        value_sum,
+        out_total,
+        output,
+        second,
+        up_total,
+        up_sum_bias,
+        down_total,
+        down,
+        stats,
+    )
+
+
 def solution(mesh):
     placed = (
         P(("bucket", "blk"), None),
@@ -355,7 +996,7 @@
         P(),
     )
     return jax.shard_map(
-        body,
+        body if dict(mesh.shape) == {"bucket": 4, "blk": 8} else general_body,
         mesh=mesh,
         in_specs=placed,
         out_specs=(

time: 707 us -> 152 us (0.21)
  waiting for transfers between devices: 342 us -> 46.3 us
  matrix products: 121 us -> 0 us
  local copies, waits for them, and re-layouts: 91.8 us -> 12.2 us
  other arithmetic: 70.3 us -> 0.01 us
  blocking collectives: 61.5 us -> 0 us
  starting transfers between devices: 0.51 us -> 52.8 us
  Pallas kernels: 0 us -> 38.8 us
  between operations: 17.1 us -> 1.13 us
    reduce_scatter x4 -> x0, waiting for transfers between devices: 316 us -> none  [the longest x1 141 us: body(): lax.psum_scatter(up_grad, ('bucket', 'blk'), scatter_dimension=0, tiled=T...]
    dot_general x26 -> x0, matrix products: 121 us -> none  [the longest x2 13.9 us: query_advance(): jnp.einsum('hqk,khd->qhd', slope, block_keys, preferred_element_type=jnp....]
    ppermute x0 -> x41, starting transfers between devices: none -> 52.8 us  [the longest x15 27.2 us: shift_bucket(): return lax.ppermute(block, 'bucket', [(b, b ^ step) for b in range(4)])]
    ppermute x0 -> x41, waiting for transfers between devices: none -> 46.3 us  [the longest x15 28.4 us: shift_bucket(): return lax.ppermute(block, 'bucket', [(b, b ^ step) for b in range(4)])]
    psum x1 -> x0, blocking collectives: 43.9 us -> none  [body(): lax.psum((first_gain_grad, query_bias_grad, value_bias_grad, output_bias_...]
    pallas_call x0 -> x17, Pallas kernels: none -> 38.8 us  [call(): pl.pallas_call(kernel, out_shape=shapes, in_specs=[SMEM] * small + [VMEM]...]
    dynamic_slice x23 -> x0, local copies, waits for them, and re-layouts: 37.1 us -> none  [the longest x16 30.8 us: body(): lax.scan(forward_advance, state, (key_piece.reshape(number, width, D), va...]
    all_gather x4 -> x0, waiting for transfers between devices: 24.6 us -> none  [the longest x1 24.6 us: body(): key_piece = lax.all_gather(keys, 'blk', axis=0, tiled=True)]
  transfers between devices with their start and end apart: 8 -> 41, of which waited for: 4 -> 16; matrix products, arithmetic and copies ran while one was open for 38% -> 1% of each run, Pallas kernels for 0% -> 17%
where the time goes in v2:
time: 152 us; the launch traced here: 151 us
  starting transfers between devices  52.8 us (35%)
  waiting for transfers between devices  46.3 us (30%)
  Pallas kernels  38.8 us (26%)
  local copies, waits for them, and re-layouts  12.2 us (8%)
    pallas_call x17, Pallas kernels, call(): pl.pallas_call(kernel, out_shape=shapes, in_specs=[SMEM] * small + [VMEM]...  38.8 us
    ppermute x15, waiting for transfers between devices, shift_bucket(): return lax.ppermute(block, 'bucket', [(b, b ^ step) for b in range(4)])  28.4 us
    ppermute x15, starting transfers between devices, shift_bucket(): return lax.ppermute(block, 'bucket', [(b, b ^ step) for b in range(4)])  27.2 us
    ppermute x21, starting transfers between devices, swap_chip(): return lax.ppermute(block, 'blk', [(k, k ^ 2 * step) for k in range(8)])  24.7 us
    ppermute x21, waiting for transfers between devices, swap_chip(): return lax.ppermute(block, 'blk', [(k, k ^ 2 * step) for k in range(8)])  15 us
    unnamed x55, local copies, waits for them, and re-layouts  12.2 us
  transfers between devices with their start and end apart: 41, of which 16 were waited for; matrix products, arithmetic and copies ran while one was open for 1% of the time, Pallas kernels for 17%

profile of v2, /device:TPU:0, one launch (start us, length us, event | category | flops | bytes accessed | tf_op | source)
XLA Modules:
  0.0 151.2 jit_solution(14974127581895974403)
XLA Ops:
  0.6 3.1 %collective-permute-start.3 = (bf16[160,767]{1,0:T(8,128)(2,1)}, bf16[160,767]{1,0:T(8,128)(2,1)S(1)}, u32[]{:S(2)}, u32[]{:S(2)}) collective-permute-start(bf16[160,767]{1,0:T(8,128)(2,1)} %c0.1), channel_id=1, source_target_pairs={{0,8},{8,0},{16,24},{24,16},{1,9},{9,1},{17,25},{25,17},{2,10},{10... | collective-permute-start | bytes 736328 | tf_op jit(solution)/shard_map/ppermute | solution.py:807
  3.7 2.5 %collective-permute-start.4 = (bf16[160,767]{1,0:T(8,128)(2,1)}, bf16[160,767]{1,0:T(8,128)(2,1)S(1)}, u32[]{:S(2)}, u32[]{:S(2)}) collective-permute-start(bf16[160,767]{1,0:T(8,128)(2,1)} %c0.1), channel_id=1, source_target_pairs={{0,24},{8,16},{16,8},{24,0},{1,25},{9,17},{17,9},{25,1},{2,26},{10... | collective-permute-start | bytes 736328 | tf_op jit(solution)/shard_map/ppermute | solution.py:807
  6.2 2.0 %copy-done = bf16[768,2304]{1,0:T(8,128)(2,1)S(1)} copy-done((bf16[768,2304]{1,0:T(8,128)(2,1)S(1)}, bf16[768,2304]{1,0:T(8,128)(2,1)}, u32[]{:S(2)}) %copy-start) | copy-done | bytes 3538968
  11.2 1.7 %shard_map.263 = (bf16[240,384]{1,0:T(8,128)(2,1)S(1)}, bf16[240,384]{1,0:T(8,128)(2,1)S(1)}, bf16[240,384]{1,0:T(8,128)(2,1)S(1)}, bf16[240,384]{1,0:T(8,128)(2...) custom-call(bf16[160,767]{1,0:T(8,128)(2,1)S(1)} %copy-done.4, f32[768]{0:T(1024)S(1)} %copy-done.15, ...), custom_call_target="tpu_custom_call" | custom-call | flops 1000 | bytes 1000 | tf_op jit(solution)/shard_map/pallas_call | solution.py:362
  12.9 1.5 collective-permute-start
  14.4 1.5 %collective-permute-start.1 = (bf16[240,384]{1,0:T(8,128)(2,1)S(1)}, bf16[240,384]{1,0:T(8,128)(2,1)S(1)}, u32[]{:S(2)}, u32[]{:S(2)}) collective-permute-start(bf16[240,384]{1,0:T(8,128)(2,1)S(1)} %get-tuple-element.111), channel_id=1, source_target_pairs={{0,4},{1,5},{2,6},{3,7},{4,0},{5,1},{6,2},{7,3},{8,12},{9,13},{10,... | collective-permute-start | bytes 552968 | tf_op jit(solution)/shard_map/ppermute | solution.py:799
  16.4 2.3 %copy-done.2 = bf16[3072,767]{1,0:T(8,128)(2,1)S(1)} copy-done((bf16[3072,767]{1,0:T(8,128)(2,1)S(1)}, bf16[3072,767]{1,0:T(8,128)(2,1)}, u32[]{:S(2)}) %copy-start.2) | copy-done | bytes 4712472
  18.7 1.7 %shard_map.264.push = f32[160,3072]{1,0:T(8,128)S(1)} custom-call(bf16[160,767]{1,0:T(8,128)(2,1)S(1)} %copy-done.6, bf16[3072,767]{1,0:T(8,128)(2,1)S(1)} %copy-done.2), custom_call_target="tpu_custom_call" | custom-call | flops 1000 | bytes 1000 | tf_op jit(solution)/shard_map/pallas_call | solution.py:362
  20.4 3.4 %collective-permute-done.1.p2 = bf16[240,384]{1,0:T(8,128)(2,1)S(1)} collective-permute-done((bf16[240,384]{1,0:T(8,128)(2,1)S(1)}, bf16[240,384]{1,0:T(8,128)(2,1)S(1)}, u32[]{:S(2)}, u32[]{:S(2)}) %collective-permute-start.1) | collective-permute-done | bytes 184352 | tf_op jit(solution)/shard_map/ppermute | solution.py:799
  25.1 1.2 collective-permute-start.10
  27.5 1.4 collective-permute-start.12
  30.7 7.0 %shard_map.266 = (bf16[3,640,1280]{2,1,0:T(8,128)(2,1)S(1)}, f32[640,192]{1,0:T(8,128)S(1)}, bf16[80,384]{1,0:T(8,128)(2,1)S(1)}, bf16[80,384]{1,0:T(8,128)(2,1)...) custom-call(s32[16]{0:T(128)S(1)} %copy-done.23, s32[1,2]{1,0:T(1,128)S(1)} %copy-done.24, ...), custom_call_target="tpu_custom_call" | custom-call | flops 1000 | bytes 1000 | tf_op jit(solution)/shard_map/pallas_call | solution.py:362
  37.7 1.3 collective-permute-start.6
  39.0 1.7 %collective-permute-done.9.c2 = bf16[160,767]{1,0:T(8,128)(2,1)} collective-permute-done((bf16[160,767]{1,0:T(8,128)(2,1)S(1)}, bf16[160,767]{1,0:T(8,128)(2,1)}, u32[]{:S(2)}, u32[]{:S(2)}) %collective-permute-start.9) | collective-permute-done | bytes 245472 | tf_op jit(solution)/shard_map/ppermute | solution.py:807
  41.5 1.4 collective-permute-start.8
  43.0 2.6 %collective-permute-done.7.p2 = bf16[80,384]{1,0:T(8,128)(2,1)S(1)} collective-permute-done((bf16[80,384]{1,0:T(8,128)(2,1)S(1)}, bf16[80,384]{1,0:T(8,128)(2,1)S(1)}, u32[]{:S(2)}, u32[]{:S(2)}) %collective-permute-start.7) | collective-permute-done | bytes 61472 | tf_op jit(solution)/shard_map/ppermute | solution.py:799
  46.7 2.3 %copy-done.3 = bf16[768,3072]{1,0:T(8,128)(2,1)S(1)} copy-done((bf16[768,3072]{1,0:T(8,128)(2,1)S(1)}, bf16[768,3072]{1,0:T(8,128)(2,1)}, u32[]{:S(2)}) %copy-start.3) | copy-done | bytes 4718616
  49.0 6.0 %shard_map.267 = (bf16[80,384]{1,0:T(8,128)(2,1)S(1)}, bf16[80,384]{1,0:T(8,128)(2,1)S(1)}, bf16[80,384]{1,0:T(8,128)(2,1)S(1)}, bf16[80,384]{1,0:T(8,128)(2,1)S...) custom-call(s32[16]{0:T(128)S(1)} %copy-done.23, ...), custom_call_target="tpu_custom_call" | custom-call | flops 1000 | bytes 1000 | tf_op jit(solution)/shard_map/pallas_call | solution.py:362
  55.0 1.6 %collective-permute-start.13 = (bf16[80,384]{1,0:T(8,128)(2,1)S(1)}, bf16[80,384]{1,0:T(8,128)(2,1)S(1)}, u32[]{:S(2)}, u32[]{:S(2)}) collective-permute-start(bf16[80,384]{1,0:T(8,128)(2,1)S(1)} %get-tuple-element.135), channel_id=1, source_target_pairs={{0,2},{1,3},{2,0},{3,1},{4,6},{5,7},{6,4},{7,5},{8,10},{9,11},{10,... | collective-permute-start | bytes 184328 | tf_op jit(solution)/shard_map/ppermute | solution.py:799
  57.1 1.5 collective-permute-start.15
  58.6 1.9 %collective-permute-start.17 = (bf16[160,768]{1,0:T(8,128)(2,1)S(1)}, bf16[160,768]{1,0:T(8,128)(2,1)S(1)}, u32[]{:S(2)}, u32[]{:S(2)}) collective-permute-start(bf16[160,768]{1,0:T(8,128)(2,1)S(1)} %get-tuple-element.131.a2), channel_id=1, source_target_pairs={{0,16},{8,24},{16,0},{24,8},{1,17},{9,25},{17,1},{25,9},{2,18},{10... | collective-permute-start | bytes 737288 | tf_op jit(solution)/shard_map/ppermute | solution.py:807
  60.5 2.5 %collective-permute-start.18 = (bf16[160,768]{1,0:T(8,128)(2,1)S(1)}, bf16[160,768]{1,0:T(8,128)(2,1)S(1)}, u32[]{:S(2)}, u32[]{:S(2)}) collective-permute-start(bf16[160,768]{1,0:T(8,128)(2,1)S(1)} %get-tuple-element.132.a3), channel_id=1, source_target_pairs={{0,24},{8,16},{16,8},{24,0},{1,25},{9,17},{17,9},{25,1},{2,26},{10... | collective-permute-start | bytes 737288 | tf_op jit(solution)/shard_map/ppermute | solution.py:807
  63.0 1.5 collective-permute-start.21
  65.0 8.2 %shard_map.269 = (bf16[640,192]{1,0:T(8,128)(2,1)S(1)}, f32[640,384]{1,0:T(8,128)S(1)}, bf16[320,384]{1,0:T(8,128)(2,1)S(1)}, bf16[320,384]{1,0:T(8,128)(2,1)S(1)}) custom-call(bf16[80,384]{1,0:T(8,128)(2,1)S(1)} %get-tuple-element.134.d0, bf16[80,384]{1,0:T(8,128)(2,1)S(1)} %collective-permute-done.13.d1, bf16[80,384]{1,0:T(8,128)(2,1)S(1)} %collective-permute-done.14.d2, ...), custom_call_target="tpu_custom_call" | custom-call | flops 1000 | bytes 1000 | tf_op jit(solution)/shard_map/pallas_call | solution.py:362
  73.2 4.4 %collective-permute-done.17.a2 = bf16[160,768]{1,0:T(8,128)(2,1)S(1)} collective-permute-done((bf16[160,768]{1,0:T(8,128)(2,1)S(1)}, bf16[160,768]{1,0:T(8,128)(2,1)S(1)}, u32[]{:S(2)}, u32[]{:S(2)}) %collective-permute-start.17) | collective-permute-done | bytes 245792 | tf_op jit(solution)/shard_map/ppermute | solution.py:807
  79.6 4.4 %shard_map.271 = (bf16[240,384]{1,0:T(8,128)(2,1)S(1)}, bf16[240,384]{1,0:T(8,128)(2,1)S(1)}, bf16[240,384]{1,0:T(8,128)(2,1)S(1)}, bf16[240,384]{1,0:T(8,128)(2...) custom-call(bf16[640,192]{1,0:T(8,128)(2,1)S(1)} %get-tuple-element.140.qu, ...), custom_call_target="tpu_custom_call" | custom-call | flops 1000 | bytes 1000 | tf_op jit(solution)/shard_map/pallas_call | solution.py:362
  84.3 1.5 %collective-permute-start.30 = (bf16[320,768]{1,0:T(8,128)(2,1)S(1)}, bf16[320,768]{1,0:T(8,128)(2,1)S(1)}, u32[]{:S(2)}, u32[]{:S(2)}) collective-permute-start(bf16[320,768]{1,0:T(8,128)(2,1)S(1)} %get-tuple-element.174), channel_id=1, source_target_pairs={{0,6},{1,7},{2,4},{3,5},{4,2},{5,3},{6,0},{7,1},{8,14},{9,15},{10,... | collective-permute-start | bytes 1474568 | tf_op jit(solution)/shard_map/ppermute | solution.py:799
  85.8 1.9 %collective-permute-done.23.arrived = bf16[1120,768]{1,0:T(8,128)(2,1)S(1)} collective-permute-done((bf16[1120,768]{1,0:T(8,128)(2,1)S(1)}, bf16[1120,768]{1,0:T(8,128)(2,1)S(1)}, u32[]{:S(2)}, u32[]{:S(2)}) %collective-permute-start.23) | collective-permute-done | bytes 1720352 | tf_op jit(solution)/shard_map/ppermute | solution.py:803
  88.2 3.8 %collective-permute-start.27 = (bf16[112,768]{1,0:T(8,128)(2,1)S(1)}, bf16[112,768]{1,0:T(8,128)(2,1)S(1)}, u32[]{:S(2)}, u32[]{:S(2)}) collective-permute-start(bf16[112,768]{1,0:T(8,128)(2,1)S(1)} %get-tuple-element.170), channel_id=1, source_target_pairs={{0,8},{8,0},{16,24},{24,16},{1,9},{9,1},{17,25},{25,17},{2,10},{10... | collective-permute-start | bytes 516104 | tf_op jit(solution)/shard_map/ppermute | solution.py:807
  92.3 2.1 %collective-permute-start.29 = (bf16[112,768]{1,0:T(8,128)(2,1)S(1)}, bf16[112,768]{1,0:T(8,128)(2,1)S(1)}, u32[]{:S(2)}, u32[]{:S(2)}) collective-permute-start(bf16[112,768]{1,0:T(8,128)(2,1)S(1)} %get-tuple-element.172), channel_id=1, source_target_pairs={{0,24},{8,16},{16,8},{24,0},{1,25},{9,17},{17,9},{25,1},{2,26},{10... | collective-permute-start | bytes 516104 | tf_op jit(solution)/shard_map/ppermute | solution.py:807
  94.5 4.2 %collective-permute-done.30.n3 = bf16[320,768]{1,0:T(8,128)(2,1)S(1)} collective-permute-done((bf16[320,768]{1,0:T(8,128)(2,1)S(1)}, bf16[320,768]{1,0:T(8,128)(2,1)S(1)}, u32[]{:S(2)}, u32[]{:S(2)}) %collective-permute-start.30) | collective-permute-done | bytes 491552 | tf_op jit(solution)/shard_map/ppermute | solution.py:799
  99.4 8.1 %collective-permute-done.28.z2 = bf16[112,768]{1,0:T(8,128)(2,1)S(1)} collective-permute-done((bf16[112,768]{1,0:T(8,128)(2,1)S(1)}, bf16[112,768]{1,0:T(8,128)(2,1)S(1)}, u32[]{:S(2)}, u32[]{:S(2)}) %collective-permute-start.28) | collective-permute-done | bytes 172064 | tf_op jit(solution)/shard_map/ppermute | solution.py:807
  107.6 1.2 shard_map.274
  108.9 1.5 %collective-permute-start.24 = (bf16[352,768]{1,0:T(8,128)(2,1)S(1)}, bf16[352,768]{1,0:T(8,128)(2,1)S(1)}, u32[]{:S(2)}, u32[]{:S(2)}) collective-permute-start(bf16[352,768]{1,0:T(8,128)(2,1)S(1)} %get-tuple-element.165), channel_id=1, source_target_pairs={{0,2},{1,3},{2,0},{3,1},{4,6},{5,7},{6,4},{7,5},{8,10},{9,11},{10,... | collective-permute-start | bytes 1622024 | tf_op jit(solution)/shard_map/ppermute | solution.py:799
  111.0 1.5 collective-permute-start.26
  112.6 3.3 %collective-permute-start.32 = (bf16[96,768]{1,0:T(8,128)(2,1)S(1)}, bf16[96,768]{1,0:T(8,128)(2,1)S(1)}, u32[]{:S(2)}, u32[]{:S(2)}) collective-permute-start(bf16[96,768]{1,0:T(8,128)(2,1)S(1)} %get-tuple-element.182), channel_id=1, source_target_pairs={{0,8},{8,0},{16,24},{24,16},{1,9},{9,1},{17,25},{25,17},{2,10},{10... | collective-permute-start | bytes 442376 | tf_op jit(solution)/shard_map/ppermute | solution.py:807
  116.1 4.9 %collective-permute-done.32.w1 = bf16[96,768]{1,0:T(8,128)(2,1)S(1)} collective-permute-done((bf16[96,768]{1,0:T(8,128)(2,1)S(1)}, bf16[96,768]{1,0:T(8,128)(2,1)S(1)}, u32[]{:S(2)}, u32[]{:S(2)}) %collective-permute-start.32) | collective-permute-done | bytes 147488 | tf_op jit(solution)/shard_map/ppermute | solution.py:807
  121.0 2.0 %collective-permute-start.34 = (bf16[96,768]{1,0:T(8,128)(2,1)S(1)}, bf16[96,768]{1,0:T(8,128)(2,1)S(1)}, u32[]{:S(2)}, u32[]{:S(2)}) collective-permute-start(bf16[96,768]{1,0:T(8,128)(2,1)S(1)} %get-tuple-element.184), channel_id=1, source_target_pairs={{0,24},{8,16},{16,8},{24,0},{1,25},{9,17},{17,9},{25,1},{2,26},{10... | collective-permute-start | bytes 442376 | tf_op jit(solution)/shard_map/ppermute | solution.py:807
  123.1 6.1 %collective-permute-done.33.w2 = bf16[96,768]{1,0:T(8,128)(2,1)S(1)} collective-permute-done((bf16[96,768]{1,0:T(8,128)(2,1)S(1)}, bf16[96,768]{1,0:T(8,128)(2,1)S(1)}, u32[]{:S(2)}, u32[]{:S(2)}) %collective-permute-start.33) | collective-permute-done | bytes 147488 | tf_op jit(solution)/shard_map/ppermute | solution.py:807
  129.5 1.6 %collective-permute-start.35 = (bf16[96,768]{1,0:T(8,128)(2,1)S(1)}, bf16[96,768]{1,0:T(8,128)(2,1)S(1)}, u32[]{:S(2)}, u32[]{:S(2)}) collective-permute-start(bf16[96,768]{1,0:T(8,128)(2,1)S(1)} %get-tuple-element.186), channel_id=1, source_target_pairs={{0,2},{1,3},{2,0},{3,1},{4,6},{5,7},{6,4},{7,5},{8,10},{9,11},{10,... | collective-permute-start | bytes 442376 | tf_op jit(solution)/shard_map/ppermute | solution.py:799
  131.5 1.5 collective-permute-start.37
  133.0 3.7 %collective-permute-done.25.x2 = bf16[352,768]{1,0:T(8,128)(2,1)S(1)} collective-permute-done((bf16[352,768]{1,0:T(8,128)(2,1)S(1)}, bf16[352,768]{1,0:T(8,128)(2,1)S(1)}, u32[]{:S(2)}, u32[]{:S(2)}) %collective-permute-start.25) | collective-permute-done | bytes 540704 | tf_op jit(solution)/shard_map/ppermute | solution.py:799
  137.6 3.2 %collective-permute-start.38 = (bf16[32,768]{1,0:T(8,128)(2,1)S(1)}, bf16[32,768]{1,0:T(8,128)(2,1)S(1)}, u32[]{:S(2)}, u32[]{:S(2)}) collective-permute-start(bf16[32,768]{1,0:T(8,128)(2,1)S(1)} %get-tuple-element.194), channel_id=1, source_target_pairs={{0,8},{8,0},{16,24},{24,16},{1,9},{9,1},{17,25},{25,17},{2,10},{10... | collective-permute-start | bytes 147464 | tf_op jit(solution)/shard_map/ppermute | solution.py:807
  140.7 2.1 %collective-permute-done.38.o1 = bf16[32,768]{1,0:T(8,128)(2,1)S(1)} collective-permute-done((bf16[32,768]{1,0:T(8,128)(2,1)S(1)}, bf16[32,768]{1,0:T(8,128)(2,1)S(1)}, u32[]{:S(2)}, u32[]{:S(2)}) %collective-permute-start.38) | collective-permute-done | bytes 49184 | tf_op jit(solution)/shard_map/ppermute | solution.py:807
  142.8 1.8 %collective-permute-start.40 = (bf16[32,768]{1,0:T(8,128)(2,1)S(1)}, bf16[32,768]{1,0:T(8,128)(2,1)S(1)}, u32[]{:S(2)}, u32[]{:S(2)}) collective-permute-start(bf16[32,768]{1,0:T(8,128)(2,1)S(1)} %get-tuple-element.196), channel_id=1, source_target_pairs={{0,24},{8,16},{16,8},{24,0},{1,25},{9,17},{17,9},{25,1},{2,26},{10... | collective-permute-start | bytes 147464 | tf_op jit(solution)/shard_map/ppermute | solution.py:807
  144.6 1.7 %shard_map.268 = bf16[160,767]{1,0:T(8,128)(2,1)} custom-call(bf16[160,768]{1,0:T(8,128)(2,1)S(1)} %get-tuple-element.129.a0, bf16[160,768]{1,0:T(8,128)(2,1)S(1)} %get-tuple-element.130.a1, bf16[160,768]{1,0:T(8,128)(2,1)S(1)} %get-tuple-element.131.a2, bf16[160,768]{1,0:T(8,128)(2,1)S(1)} %get-tuple-element.132.a3, bf16[3072,767]{1,0:T(8,128)(2,1)S(1)} %bitcast.1, ...), custom_call_target="tpu_custom_call" | custom-call | flops 1000 | bytes 1000 | tf_op jit(solution)/shard_map/pallas_call | solution.py:362
  146.3 2.3 %shard_map.273 = bf16[160,767]{1,0:T(8,128)(2,1)} custom-call(bf16[352,768]{1,0:T(8,128)(2,1)S(1)} %get-tuple-element.164.x0, bf16[352,768]{1,0:T(8,128)(2,1)S(1)} %collective-permute-done.24.x1, bf16[352,768]{1,0:T(8,128)(2,1)S(1)} %collective-permute-done.25.x2, bf16[352,768]{1,0:T(8,128)(2,1)S(1)} %collective-permute-done.26.x3, ...), custom_call_target="tpu_custom_call" | custom-call | flops 1000 | bytes 1000 | tf_op jit(solution)/shard_map/pallas_call | solution.py:362
  149.5 1.5 %shard_map.277 = (f32[24,2304]{1,0:T(8,128)}, f32[24,3072]{1,0:T(8,128)}, f32[768]{0:T(1024)}, f32[768]{0:T(1024)}, f32[768]{0:T(1024)}, /*index=5*/f32[767]{0:T...) custom-call(s32[4,2]{1,0:T(4,128)S(1)} %copy.31.lengths, bf16[96,768]{1,0:T(8,128)(2,1)S(1)} %get-tuple-element.185.f0, ...), custom_call_target="tpu_custom_call" | custom-call | flops 1000 | bytes 1000 | tf_op jit(solution)/shard_map/pallas_call | solution.py:362
  (107 shorter events, 17.9 us)
Async XLA Ops:
  0.6 23.2 %collective-permute-start.3 = (bf16[160,767]{1,0:T(8,128)(2,1)}, bf16[160,767]{1,0:T(8,128)(2,1)S(1)}, u32[]{:S(2)}, u32[]{:S(2)}) collective-permute-start(bf16[160,767]{1,0:T(8,128)(2,1)} %c0.1), channel_id=1, source_target_pairs={{0,8},{8,0},{16,24},{24,16},{1,9},{9,1},{17,25},{25,17},{2,10},{10... | collective-permute-start | bytes 736328 | tf_op jit(solution)/shard_map/ppermute | solution.py:807
  3.7 20.1 %collective-permute-start.4 = (bf16[160,767]{1,0:T(8,128)(2,1)}, bf16[160,767]{1,0:T(8,128)(2,1)S(1)}, u32[]{:S(2)}, u32[]{:S(2)}) collective-permute-start(bf16[160,767]{1,0:T(8,128)(2,1)} %c0.1), channel_id=1, source_target_pairs={{0,24},{8,16},{16,8},{24,0},{1,25},{9,17},{17,9},{25,1},{2,26},{10... | collective-permute-start | bytes 736328 | tf_op jit(solution)/shard_map/ppermute | solution.py:807
  12.9 7.6 %collective-permute-start = (bf16[240,384]{1,0:T(8,128)(2,1)S(1)}, bf16[240,384]{1,0:T(8,128)(2,1)S(1)}, u32[]{:S(2)}, u32[]{:S(2)}) collective-permute-start(bf16[240,384]{1,0:T(8,128)(2,1)S(1)} %get-tuple-element.110), channel_id=1, source_target_pairs={{0,2},{1,3},{2,0},{3,1},{4,6},{5,7},{6,4},{7,5},{8,10},{9,11},{10,... | collective-permute-start | bytes 552968 | tf_op jit(solution)/shard_map/ppermute | solution.py:799
  14.4 9.5 %collective-permute-start.1 = (bf16[240,384]{1,0:T(8,128)(2,1)S(1)}, bf16[240,384]{1,0:T(8,128)(2,1)S(1)}, u32[]{:S(2)}, u32[]{:S(2)}) collective-permute-start(bf16[240,384]{1,0:T(8,128)(2,1)S(1)} %get-tuple-element.111), channel_id=1, source_target_pairs={{0,4},{1,5},{2,6},{3,7},{4,0},{5,1},{6,2},{7,3},{8,12},{9,13},{10,... | collective-permute-start | bytes 552968 | tf_op jit(solution)/shard_map/ppermute | solution.py:799
  15.9 8.0 %collective-permute-start.2 = (bf16[240,384]{1,0:T(8,128)(2,1)S(1)}, bf16[240,384]{1,0:T(8,128)(2,1)S(1)}, u32[]{:S(2)}, u32[]{:S(2)}) collective-permute-start(bf16[240,384]{1,0:T(8,128)(2,1)S(1)} %get-tuple-element.112), channel_id=1, source_target_pairs={{0,6},{1,7},{2,4},{3,5},{4,2},{5,3},{6,0},{7,1},{8,14},{9,15},{10,... | collective-permute-start | bytes 552968 | tf_op jit(solution)/shard_map/ppermute | solution.py:799
  20.4 26.2 %copy-start.5 = (bf16[160,767]{1,0:T(8,128)(2,1)S(1)}, bf16[160,767]{1,0:T(8,128)(2,1)}, u32[]{:S(2)}) copy-start(bf16[160,767]{1,0:T(8,128)(2,1)} %resid.5) | copy-start | bytes 736324
  20.4 26.2 %copy-start.17 = (f32[3072]{0:T(1024)S(1)}, f32[3072]{0:T(1024)}, u32[]{:S(2)}) copy-start(f32[3072]{0:T(1024)} %up_bias.1) | copy-start | bytes 36868
  20.4 26.2 %copy-start.20 = (f32[767]{0:T(1024)S(1)}, f32[767]{0:T(1024)}, u32[]{:S(2)}) copy-start(f32[767]{0:T(1024)} %out_bias.1) | copy-start | bytes 9208
  20.4 26.2 %copy-start.21 = (f32[768]{0:T(1024)S(1)}, f32[768]{0:T(1024)}, u32[]{:S(2)}) copy-start(f32[768]{0:T(1024)} %gain.5) | copy-start | bytes 9220
  25.1 4.7 %collective-permute-start.5 = (bf16[640,384]{1,0:T(8,128)(2,1)S(1)}, bf16[640,384]{1,0:T(8,128)(2,1)S(1)}, u32[]{:S(2)}, u32[]{:S(2)}) collective-permute-start(bf16[640,384]{1,0:T(8,128)(2,1)S(1)} %get-tuple-element.118.own), channel_id=1, source_target_pairs={{0,1},{1,0},{2,3},{3,2},{4,5},{5,4},{6,7},{7,6},{8,9},{9,8},{10,11... | collective-permute-start | bytes 1474568 | tf_op jit(solution)/shard_map/ppermute | solution.py:803
  25.1 16.4 %collective-permute-start.10 = (bf16[160,768]{1,0:T(8,128)(2,1)}, bf16[160,768]{1,0:T(8,128)(2,1)}, u32[]{:S(2)}, u32[]{:S(2)}) collective-permute-start(bf16[160,768]{1,0:T(8,128)(2,1)} %get-tuple-element.123.i0), channel_id=1, source_target_pairs={{0,2},{1,3},{2,0},{3,1},{4,6},{5,7},{6,4},{7,5},{8,10},{9,11},{10,... | collective-permute-start | bytes 737288 | tf_op jit(solution)/shard_map/ppermute | solution.py:799
  26.3 14.4 %collective-permute-start.9 = (bf16[160,767]{1,0:T(8,128)(2,1)S(1)}, bf16[160,767]{1,0:T(8,128)(2,1)}, u32[]{:S(2)}, u32[]{:S(2)}) collective-permute-start(bf16[160,767]{1,0:T(8,128)(2,1)S(1)} %copy-done.6), channel_id=1, source_target_pairs={{0,16},{8,24},{16,0},{24,8},{1,17},{9,25},{17,1},{25,9},{2,18},{10... | collective-permute-start | bytes 736328 | tf_op jit(solution)/shard_map/ppermute | solution.py:807
  26.7 16.2 %collective-permute-start.11 = (bf16[160,768]{1,0:T(8,128)(2,1)}, bf16[160,768]{1,0:T(8,128)(2,1)}, u32[]{:S(2)}, u32[]{:S(2)}) collective-permute-start(bf16[160,768]{1,0:T(8,128)(2,1)} %get-tuple-element.123.i0), channel_id=1, source_target_pairs={{0,4},{1,5},{2,6},{3,7},{4,0},{5,1},{6,2},{7,3},{8,12},{9,13},{10,... | collective-permute-start | bytes 737288 | tf_op jit(solution)/shard_map/ppermute | solution.py:799
  27.5 15.4 %collective-permute-start.12 = (bf16[160,768]{1,0:T(8,128)(2,1)}, bf16[160,768]{1,0:T(8,128)(2,1)}, u32[]{:S(2)}, u32[]{:S(2)}) collective-permute-start(bf16[160,768]{1,0:T(8,128)(2,1)} %get-tuple-element.123.i0), channel_id=1, source_target_pairs={{0,6},{1,7},{2,4},{3,5},{4,2},{5,3},{6,0},{7,1},{8,14},{9,15},{10,... | collective-permute-start | bytes 737288 | tf_op jit(solution)/shard_map/ppermute | solution.py:799
  37.7 5.2 %collective-permute-start.6 = (bf16[80,384]{1,0:T(8,128)(2,1)S(1)}, bf16[80,384]{1,0:T(8,128)(2,1)S(1)}, u32[]{:S(2)}, u32[]{:S(2)}) collective-permute-start(bf16[80,384]{1,0:T(8,128)(2,1)S(1)} %get-tuple-element.120), channel_id=1, source_target_pairs={{0,2},{1,3},{2,0},{3,1},{4,6},{5,7},{6,4},{7,5},{8,10},{9,11},{10,... | collective-permute-start | bytes 184328 | tf_op jit(solution)/shard_map/ppermute | solution.py:799
  40.7 4.9 %collective-permute-start.7 = (bf16[80,384]{1,0:T(8,128)(2,1)S(1)}, bf16[80,384]{1,0:T(8,128)(2,1)S(1)}, u32[]{:S(2)}, u32[]{:S(2)}) collective-permute-start(bf16[80,384]{1,0:T(8,128)(2,1)S(1)} %get-tuple-element.121), channel_id=1, source_target_pairs={{0,4},{1,5},{2,6},{3,7},{4,0},{5,1},{6,2},{7,3},{8,12},{9,13},{10,... | collective-permute-start | bytes 184328 | tf_op jit(solution)/shard_map/ppermute | solution.py:799
  41.5 5.1 %collective-permute-start.8 = (bf16[80,384]{1,0:T(8,128)(2,1)S(1)}, bf16[80,384]{1,0:T(8,128)(2,1)S(1)}, u32[]{:S(2)}, u32[]{:S(2)}) collective-permute-start(bf16[80,384]{1,0:T(8,128)(2,1)S(1)} %get-tuple-element.122), channel_id=1, source_target_pairs={{0,6},{1,7},{2,4},{3,5},{4,2},{5,3},{6,0},{7,1},{8,14},{9,15},{10,... | collective-permute-start | bytes 184328 | tf_op jit(solution)/shard_map/ppermute | solution.py:799
  55.0 5.4 %collective-permute-start.13 = (bf16[80,384]{1,0:T(8,128)(2,1)S(1)}, bf16[80,384]{1,0:T(8,128)(2,1)S(1)}, u32[]{:S(2)}, u32[]{:S(2)}) collective-permute-start(bf16[80,384]{1,0:T(8,128)(2,1)S(1)} %get-tuple-element.135), channel_id=1, source_target_pairs={{0,2},{1,3},{2,0},{3,1},{4,6},{5,7},{6,4},{7,5},{8,10},{9,11},{10,... | collective-permute-start | bytes 184328 | tf_op jit(solution)/shard_map/ppermute | solution.py:799
  56.6 6.4 %collective-permute-start.14 = (bf16[80,384]{1,0:T(8,128)(2,1)S(1)}, bf16[80,384]{1,0:T(8,128)(2,1)S(1)}, u32[]{:S(2)}, u32[]{:S(2)}) collective-permute-start(bf16[80,384]{1,0:T(8,128)(2,1)S(1)} %get-tuple-element.136), channel_id=1, source_target_pairs={{0,4},{1,5},{2,6},{3,7},{4,0},{5,1},{6,2},{7,3},{8,12},{9,13},{10,... | collective-permute-start | bytes 184328 | tf_op jit(solution)/shard_map/ppermute | solution.py:799
  57.1 7.4 %collective-permute-start.15 = (bf16[80,384]{1,0:T(8,128)(2,1)S(1)}, bf16[80,384]{1,0:T(8,128)(2,1)S(1)}, u32[]{:S(2)}, u32[]{:S(2)}) collective-permute-start(bf16[80,384]{1,0:T(8,128)(2,1)S(1)} %get-tuple-element.137), channel_id=1, source_target_pairs={{0,6},{1,7},{2,4},{3,5},{4,2},{5,3},{6,0},{7,1},{8,14},{9,15},{10,... | collective-permute-start | bytes 184328 | tf_op jit(solution)/shard_map/ppermute | solution.py:799
  58.6 14.6 %collective-permute-start.16 = (bf16[160,768]{1,0:T(8,128)(2,1)S(1)}, bf16[160,768]{1,0:T(8,128)(2,1)S(1)}, u32[]{:S(2)}, u32[]{:S(2)}) collective-permute-start(bf16[160,768]{1,0:T(8,128)(2,1)S(1)} %get-tuple-element.130.a1), channel_id=1, source_target_pairs={{0,8},{8,0},{16,24},{24,16},{1,9},{9,1},{17,25},{25,17},{2,10},{10... | collective-permute-start | bytes 737288 | tf_op jit(solution)/shard_map/ppermute | solution.py:807
  58.6 19.1 %collective-permute-start.17 = (bf16[160,768]{1,0:T(8,128)(2,1)S(1)}, bf16[160,768]{1,0:T(8,128)(2,1)S(1)}, u32[]{:S(2)}, u32[]{:S(2)}) collective-permute-start(bf16[160,768]{1,0:T(8,128)(2,1)S(1)} %get-tuple-element.131.a2), channel_id=1, source_target_pairs={{0,16},{8,24},{16,0},{24,8},{1,17},{9,25},{17,1},{25,9},{2,18},{10... | collective-permute-start | bytes 737288 | tf_op jit(solution)/shard_map/ppermute | solution.py:807
  60.5 17.2 %collective-permute-start.18 = (bf16[160,768]{1,0:T(8,128)(2,1)S(1)}, bf16[160,768]{1,0:T(8,128)(2,1)S(1)}, u32[]{:S(2)}, u32[]{:S(2)}) collective-permute-start(bf16[160,768]{1,0:T(8,128)(2,1)S(1)} %get-tuple-element.132.a3), channel_id=1, source_target_pairs={{0,24},{8,16},{16,8},{24,0},{1,25},{9,17},{17,9},{25,1},{2,26},{10... | collective-permute-start | bytes 737288 | tf_op jit(solution)/shard_map/ppermute | solution.py:807
  63.0 16.6 %collective-permute-start.21 = (bf16[320,768]{1,0:T(8,128)(2,1)S(1)}, bf16[320,768]{1,0:T(8,128)(2,1)S(1)}, u32[]{:S(2)}, u32[]{:S(2)}) collective-permute-start(bf16[320,768]{1,0:T(8,128)(2,1)S(1)} %get-tuple-element.150), channel_id=1, source_target_pairs={{0,2},{1,3},{2,0},{3,1},{4,6},{5,7},{6,4},{7,5},{8,10},{9,11},{10,... | collective-permute-start | bytes 1474568 | tf_op jit(solution)/shard_map/ppermute | solution.py:799
  64.5 15.1 %collective-permute-start.22 = (bf16[320,768]{1,0:T(8,128)(2,1)S(1)}, bf16[320,768]{1,0:T(8,128)(2,1)S(1)}, u32[]{:S(2)}, u32[]{:S(2)}) collective-permute-start(bf16[320,768]{1,0:T(8,128)(2,1)S(1)} %get-tuple-element.151), channel_id=1, source_target_pairs={{0,4},{1,5},{2,6},{3,7},{4,0},{5,1},{6,2},{7,3},{8,12},{9,13},{10,... | collective-permute-start | bytes 1474568 | tf_op jit(solution)/shard_map/ppermute | solution.py:799
  77.7 1.6 %collective-permute-start.19 = (bf16[320,384]{1,0:T(8,128)(2,1)S(1)}, bf16[320,384]{1,0:T(8,128)(2,1)S(1)}, u32[]{:S(2)}, u32[]{:S(2)}) collective-permute-start(bf16[320,384]{1,0:T(8,128)(2,1)S(1)} %get-tuple-element.144), channel_id=1, source_target_pairs={{0,1},{1,0},{2,3},{3,2},{4,5},{5,4},{6,7},{7,6},{8,9},{9,8},{10,11... | collective-permute-start | bytes 737288 | tf_op jit(solution)/shard_map/ppermute | solution.py:803
  77.7 1.9 %collective-permute-start.20 = (bf16[320,384]{1,0:T(8,128)(2,1)S(1)}, bf16[320,384]{1,0:T(8,128)(2,1)S(1)}, u32[]{:S(2)}, u32[]{:S(2)}) collective-permute-start(bf16[320,384]{1,0:T(8,128)(2,1)S(1)} %get-tuple-element.145), channel_id=1, source_target_pairs={{0,1},{1,0},{2,3},{3,2},{4,5},{5,4},{6,7},{7,6},{8,9},{9,8},{10,11... | collective-permute-start | bytes 737288 | tf_op jit(solution)/shard_map/ppermute | solution.py:803
  79.6 65.0 %slice-start = ((s8[4718592]{0:T(1024)(128)(4,1)}), s8[4194304]{0:T(1024)(128)(4,1)S(1)}, s32[]{:S(2)}) async-start(s8[4718592]{0:T(1024)(128)(4,1)} %bitcast), calls=%async_computation | async-start | bytes 8388608
  84.1 3.7 %collective-permute-start.23 = (bf16[1120,768]{1,0:T(8,128)(2,1)S(1)}, bf16[1120,768]{1,0:T(8,128)(2,1)S(1)}, u32[]{:S(2)}, u32[]{:S(2)}) collective-permute-start(bf16[1120,768]{1,0:T(8,128)(2,1)S(1)} %get-tuple-element.159.send), channel_id=1, source_target_pairs={{0,1},{1,0},{2,3},{3,2},{4,5},{5,4},{6,7},{7,6},{8,9},{9,8},{10,11... | collective-permute-start | bytes 5160968 | tf_op jit(solution)/shard_map/ppermute | solution.py:803
  84.3 14.4 %collective-permute-start.30 = (bf16[320,768]{1,0:T(8,128)(2,1)S(1)}, bf16[320,768]{1,0:T(8,128)(2,1)S(1)}, u32[]{:S(2)}, u32[]{:S(2)}) collective-permute-start(bf16[320,768]{1,0:T(8,128)(2,1)S(1)} %get-tuple-element.174), channel_id=1, source_target_pairs={{0,6},{1,7},{2,4},{3,5},{4,2},{5,3},{6,0},{7,1},{8,14},{9,15},{10,... | collective-permute-start | bytes 1474568 | tf_op jit(solution)/shard_map/ppermute | solution.py:799
  87.7 56.9 %slice-start.1 = ((s8[4718592]{0:T(1024)(128)(4,1)}), s8[524288]{0:T(1024)(128)(4,1)S(1)}, s32[]{:S(2)}) async-start(s8[4718592]{0:T(1024)(128)(4,1)} %bitcast), calls=%async_computation.1 | async-start | bytes 1048576
  88.2 11.2 %collective-permute-start.27 = (bf16[112,768]{1,0:T(8,128)(2,1)S(1)}, bf16[112,768]{1,0:T(8,128)(2,1)S(1)}, u32[]{:S(2)}, u32[]{:S(2)}) collective-permute-start(bf16[112,768]{1,0:T(8,128)(2,1)S(1)} %get-tuple-element.170), channel_id=1, source_target_pairs={{0,8},{8,0},{16,24},{24,16},{1,9},{9,1},{17,25},{25,17},{2,10},{10... | collective-permute-start | bytes 516104 | tf_op jit(solution)/shard_map/ppermute | solution.py:807
  92.1 15.5 %collective-permute-start.28 = (bf16[112,768]{1,0:T(8,128)(2,1)S(1)}, bf16[112,768]{1,0:T(8,128)(2,1)S(1)}, u32[]{:S(2)}, u32[]{:S(2)}) collective-permute-start(bf16[112,768]{1,0:T(8,128)(2,1)S(1)} %get-tuple-element.171), channel_id=1, source_target_pairs={{0,16},{8,24},{16,0},{24,8},{1,17},{9,25},{17,1},{25,9},{2,18},{10... | collective-permute-start | bytes 516104 | tf_op jit(solution)/shard_map/ppermute | solution.py:807
  92.3 15.2 %collective-permute-start.29 = (bf16[112,768]{1,0:T(8,128)(2,1)S(1)}, bf16[112,768]{1,0:T(8,128)(2,1)S(1)}, u32[]{:S(2)}, u32[]{:S(2)}) collective-permute-start(bf16[112,768]{1,0:T(8,128)(2,1)S(1)} %get-tuple-element.172), channel_id=1, source_target_pairs={{0,24},{8,16},{16,8},{24,0},{1,25},{9,17},{17,9},{25,1},{2,26},{10... | collective-permute-start | bytes 516104 | tf_op jit(solution)/shard_map/ppermute | solution.py:807
  108.8 3.6 %collective-permute-start.31 = (bf16[4,96,768]{2,1,0:T(8,128)(2,1)S(1)}, bf16[4,96,768]{2,1,0:T(8,128)(2,1)S(1)}, u32[]{:S(2)}, u32[]{:S(2)}) collective-permute-start(bf16[4,96,768]{2,1,0:T(8,128)(2,1)S(1)} %get-tuple-element.180), channel_id=1, source_target_pairs={{0,1},{1,0},{2,3},{3,2},{4,5},{5,4},{6,7},{7,6},{8,9},{9,8},{10,11... | collective-permute-start | bytes 1769480 | tf_op jit(solution)/shard_map/ppermute | solution.py:803
  108.9 22.7 %collective-permute-start.24 = (bf16[352,768]{1,0:T(8,128)(2,1)S(1)}, bf16[352,768]{1,0:T(8,128)(2,1)S(1)}, u32[]{:S(2)}, u32[]{:S(2)}) collective-permute-start(bf16[352,768]{1,0:T(8,128)(2,1)S(1)} %get-tuple-element.165), channel_id=1, source_target_pairs={{0,2},{1,3},{2,0},{3,1},{4,6},{5,7},{6,4},{7,5},{8,10},{9,11},{10,... | collective-permute-start | bytes 1622024 | tf_op jit(solution)/shard_map/ppermute | solution.py:799
  110.4 26.4 %collective-permute-start.25 = (bf16[352,768]{1,0:T(8,128)(2,1)S(1)}, bf16[352,768]{1,0:T(8,128)(2,1)S(1)}, u32[]{:S(2)}, u32[]{:S(2)}) collective-permute-start(bf16[352,768]{1,0:T(8,128)(2,1)S(1)} %get-tuple-element.166), channel_id=1, source_target_pairs={{0,4},{1,5},{2,6},{3,7},{4,0},{5,1},{6,2},{7,3},{8,12},{9,13},{10,... | collective-permute-start | bytes 1622024 | tf_op jit(solution)/shard_map/ppermute | solution.py:799
  111.0 25.8 %collective-permute-start.26 = (bf16[352,768]{1,0:T(8,128)(2,1)S(1)}, bf16[352,768]{1,0:T(8,128)(2,1)S(1)}, u32[]{:S(2)}, u32[]{:S(2)}) collective-permute-start(bf16[352,768]{1,0:T(8,128)(2,1)S(1)} %get-tuple-element.167), channel_id=1, source_target_pairs={{0,6},{1,7},{2,4},{3,5},{4,2},{5,3},{6,0},{7,1},{8,14},{9,15},{10,... | collective-permute-start | bytes 1622024 | tf_op jit(solution)/shard_map/ppermute | solution.py:799
  112.6 32.0 %copy-start.22 = (f32[767]{0:T(1024)S(1)}, f32[767]{0:T(1024)}, u32[]{:S(2)}) copy-start(f32[767]{0:T(1024)} %bias.1) | copy-start | bytes 9208
  112.6 8.5 %collective-permute-start.32 = (bf16[96,768]{1,0:T(8,128)(2,1)S(1)}, bf16[96,768]{1,0:T(8,128)(2,1)S(1)}, u32[]{:S(2)}, u32[]{:S(2)}) collective-permute-start(bf16[96,768]{1,0:T(8,128)(2,1)S(1)} %get-tuple-element.182), channel_id=1, source_target_pairs={{0,8},{8,0},{16,24},{24,16},{1,9},{9,1},{17,25},{25,17},{2,10},{10... | collective-permute-start | bytes 442376 | tf_op jit(solution)/shard_map/ppermute | solution.py:807
  115.8 13.4 %collective-permute-start.33 = (bf16[96,768]{1,0:T(8,128)(2,1)S(1)}, bf16[96,768]{1,0:T(8,128)(2,1)S(1)}, u32[]{:S(2)}, u32[]{:S(2)}) collective-permute-start(bf16[96,768]{1,0:T(8,128)(2,1)S(1)} %get-tuple-element.183), channel_id=1, source_target_pairs={{0,16},{8,24},{16,0},{24,8},{1,17},{9,25},{17,1},{25,9},{2,18},{10... | collective-permute-start | bytes 442376 | tf_op jit(solution)/shard_map/ppermute | solution.py:807
  121.0 8.2 %collective-permute-start.34 = (bf16[96,768]{1,0:T(8,128)(2,1)S(1)}, bf16[96,768]{1,0:T(8,128)(2,1)S(1)}, u32[]{:S(2)}, u32[]{:S(2)}) collective-permute-start(bf16[96,768]{1,0:T(8,128)(2,1)S(1)} %get-tuple-element.184), channel_id=1, source_target_pairs={{0,24},{8,16},{16,8},{24,0},{1,25},{9,17},{17,9},{25,1},{2,26},{10... | collective-permute-start | bytes 442376 | tf_op jit(solution)/shard_map/ppermute | solution.py:807
  129.5 20.0 %collective-permute-start.35 = (bf16[96,768]{1,0:T(8,128)(2,1)S(1)}, bf16[96,768]{1,0:T(8,128)(2,1)S(1)}, u32[]{:S(2)}, u32[]{:S(2)}) collective-permute-start(bf16[96,768]{1,0:T(8,128)(2,1)S(1)} %get-tuple-element.186), channel_id=1, source_target_pairs={{0,2},{1,3},{2,0},{3,1},{4,6},{5,7},{6,4},{7,5},{8,10},{9,11},{10,... | collective-permute-start | bytes 442376 | tf_op jit(solution)/shard_map/ppermute | solution.py:799
  131.1 18.4 %collective-permute-start.36 = (bf16[96,768]{1,0:T(8,128)(2,1)S(1)}, bf16[96,768]{1,0:T(8,128)(2,1)S(1)}, u32[]{:S(2)}, u32[]{:S(2)}) collective-permute-start(bf16[96,768]{1,0:T(8,128)(2,1)S(1)} %get-tuple-element.187), channel_id=1, source_target_pairs={{0,4},{1,5},{2,6},{3,7},{4,0},{5,1},{6,2},{7,3},{8,12},{9,13},{10,... | collective-permute-start | bytes 442376 | tf_op jit(solution)/shard_map/ppermute | solution.py:799
  131.5 17.9 %collective-permute-start.37 = (bf16[96,768]{1,0:T(8,128)(2,1)S(1)}, bf16[96,768]{1,0:T(8,128)(2,1)S(1)}, u32[]{:S(2)}, u32[]{:S(2)}) collective-permute-start(bf16[96,768]{1,0:T(8,128)(2,1)S(1)} %get-tuple-element.188), channel_id=1, source_target_pairs={{0,6},{1,7},{2,4},{3,5},{4,2},{5,3},{6,0},{7,1},{8,14},{9,15},{10,... | collective-permute-start | bytes 442376 | tf_op jit(solution)/shard_map/ppermute | solution.py:799
  137.6 5.3 %collective-permute-start.38 = (bf16[32,768]{1,0:T(8,128)(2,1)S(1)}, bf16[32,768]{1,0:T(8,128)(2,1)S(1)}, u32[]{:S(2)}, u32[]{:S(2)}) collective-permute-start(bf16[32,768]{1,0:T(8,128)(2,1)S(1)} %get-tuple-element.194), channel_id=1, source_target_pairs={{0,8},{8,0},{16,24},{24,16},{1,9},{9,1},{17,25},{25,17},{2,10},{10... | collective-permute-start | bytes 147464 | tf_op jit(solution)/shard_map/ppermute | solution.py:807
  140.7 7.8 %collective-permute-start.39 = (bf16[32,768]{1,0:T(8,128)(2,1)S(1)}, bf16[32,768]{1,0:T(8,128)(2,1)S(1)}, u32[]{:S(2)}, u32[]{:S(2)}) collective-permute-start(bf16[32,768]{1,0:T(8,128)(2,1)S(1)} %get-tuple-element.195), channel_id=1, source_target_pairs={{0,16},{8,24},{16,0},{24,8},{1,17},{9,25},{17,1},{25,9},{2,18},{10... | collective-permute-start | bytes 147464 | tf_op jit(solution)/shard_map/ppermute | solution.py:807
  142.8 6.0 %collective-permute-start.40 = (bf16[32,768]{1,0:T(8,128)(2,1)S(1)}, bf16[32,768]{1,0:T(8,128)(2,1)S(1)}, u32[]{:S(2)}, u32[]{:S(2)}) collective-permute-start(bf16[32,768]{1,0:T(8,128)(2,1)S(1)} %get-tuple-element.196), channel_id=1, source_target_pairs={{0,24},{8,16},{16,8},{24,0},{1,25},{9,17},{17,9},{25,1},{2,26},{10... | collective-permute-start | bytes 147464 | tf_op jit(solution)/shard_map/ppermute | solution.py:807
  (20 other events, 93.3 us)

commit v3 on v2

--- a/solution.py
+++ b/solution.py
@@ -344,6 +344,7 @@
 wide = jnp.float32
 VMEM = pl.BlockSpec(memory_space=pltpu.VMEM)
 SMEM = pl.BlockSpec(memory_space=pltpu.SMEM)
+HBM = pl.BlockSpec(memory_space=pltpu.HBM)
 
 def padded_bytes(shape, dtype):
     shape = (1, 1) + tuple(shape)
@@ -354,20 +355,21 @@
     return rows * lanes * size
 
 
-def call(kernel, outs, ins, scratch=(), extra=8, small=0):
+def call(kernel, outs, ins, scratch=(), extra=6, small=0, far=(), work=0):
     shapes = [jax.ShapeDtypeStruct(s, d) for s, d in outs]
-    held = [(s, d) for s, d in outs] + [(x.shape, x.dtype) for x in ins[small:]]
-    held += [(s.shape, s.dtype) for s in scratch]
-    limit = sum(padded_bytes(s, d) for s, d in held) + extra * 1024 * 1024
+    held = [(s, d) for s, d in outs]
+    held += [(x.shape, x.dtype) for i, x in enumerate(ins) if i >= small and i not in far]
+    held += [(s.shape, s.dtype) for s in scratch if s.memory_space == pltpu.VMEM]
+    limit = sum(padded_bytes(s, d) for s, d in held) + extra * 2**20
     return pl.pallas_call(
         kernel,
         out_shape=shapes,
-        in_specs=[SMEM] * small + [VMEM] * (len(ins) - small),
+        in_specs=[SMEM if i < small else HBM if i in far else VMEM for i in range(len(ins))],
         out_specs=[VMEM] * len(outs),
         scratch_shapes=list(scratch),
-        compiler_params=pltpu.CompilerParams(vmem_limit_bytes=min(limit, 60 * 1024 * 1024)),
+        compiler_params=pltpu.CompilerParams(vmem_limit_bytes=min(limit, 60 * 2**20)),
         cost_estimate=pl.CostEstimate(
-            flops=1000,
+            flops=int(1000 + work * 1.1e9),
             bytes_accessed=1000,
             transcendentals=0,
         ),
@@ -426,15 +428,32 @@
     return jnp.where(first, one, two), jnp.where(first | second, place, -1)
 
 
-def entry_kernel(resid, gain, weight, qbias, vbias, s0, s1, s2, s3, hidden_out, root_out, buf):
+def entry_kernel(
+    resid_far, gain_far, weight_far, qbias_far, vbias_far, s0, s1, s2, s3, hidden_out, root_out,
+    buf, resid, gain, weight, qbias, vbias, sems,
+):
     me = here()[0]
+    copies = [
+        pltpu.make_async_copy(a, b, sems.at[i])
+        for i, (a, b) in enumerate(
+            [(resid_far, resid), (gain_far, gain), (qbias_far, qbias), (vbias_far, vbias)]
+            + [(weight_far.at[:, pl.ds(i * D, D)], weight.at[i]) for i in range(3)]
+        )
+    ]
+    for copy in copies:
+        copy.start()
+    copies[0].wait()
     full = full_of(resid[...].astype(wide))
     root = jnp.sqrt(jnp.mean(full * full, axis=1, keepdims=True) + epsilon)
     root_out[...] = root
+    copies[1].wait()
     hidden = (full / root * row(gain)).astype(low)
     hidden_out[...] = hidden
+    copies[2].wait()
+    copies[3].wait()
     for i in range(3):
-        p = jnp.dot(hidden, weight[:, i * D : (i + 1) * D], preferred_element_type=wide)
+        copies[4 + i].wait()
+        p = jnp.dot(hidden, weight[i], preferred_element_type=wide)
         if i == 0:
             p = (p + row(qbias)) * 0.125
         if i == 2:
@@ -507,7 +526,8 @@
 
 def middle_kernel(
     spans, offsets, lengths, p0, p1, p2, p3, out_weight, out_bias, resid, root_in, cot, gain, up_weight, up_bias, push,
-    d0, d1, d2, d3, a0, a1, a2, a3, n0, n1, n2, n3, branch_own, middle, middle_grad, vector, dbuf, abuf, nbuf,
+    d0, d1, d2, d3, act_keep, act_send, n0, n1, n2, n3, branch_own, middle, middle_grad, vector,
+    dbuf, abuf, nbuf,
 ):
     me, bucket, core = here()
     branch = row(out_bias)
@@ -551,7 +571,7 @@
         dbuf[j ^ me] = packed(back[:, j * SPLIT : (j + 1) * SPLIT])
     for r in range(4):
         (d0, d1, d2, d3)[r][...] = dbuf[r]
-        (a0, a1, a2, a3)[r][...] = abuf[r]
+        (act_keep, act_send)[r % 2][r // 2 * 160 : r // 2 * 160 + 160, :] = abuf[r]
         (n0, n1, n2, n3)[r][...] = nbuf[r]
     ends = [limits(spans, offsets, lengths, bucket, me, core, half)[1] for half in range(2)]
     valid = jnp.where(jnp.concatenate(ends, axis=0) >= 0, 1.0, 0.0)
@@ -565,12 +585,13 @@
     vector[...] = jnp.concatenate(sums, axis=0)
 
 
-def closing_kernel(a0, a1, a2, a3, weight, middle, bias, out):
+def closing_kernel(act_keep, act_send, weight, middle, bias, out):
     bucket = here()[1]
     acc = middle[...] + row(bias)
-    for d, a in enumerate((a0, a1, a2, a3)):
+    for d in range(4):
         w = weight[pl.ds(pl.multiple_of((bucket ^ d) * D, D), D), :]
-        acc = acc + jnp.dot(a[...], w, preferred_element_type=wide)
+        a = (act_keep, act_send)[d % 2][d // 2 * 160 : d // 2 * 160 + 160, :]
+        acc = acc + jnp.dot(a, w, preferred_element_type=wide)
     out[...] = acc.astype(low)
 
 
@@ -610,8 +631,8 @@
 
 
 def late_kernel(
-    query_grad, both_grad, arrive_one, arrive_two, i0, i1, i2, i3, a0, a1, a2, a3, c0, c1, c2, c3, p0, p1, p2, p3, branch_own, columns, gain, vector,
-    h0, h1, h2, h3, keep_x, keep_z, send, left, right, heads, xbuf, zbuf, obuf,
+    query_grad, both_grad, arrive_one, arrive_two, i0, i1, i2, i3, act_keep, act_came, c0, c1, p0, p1, p2, p3, branch_own, columns, gain, vector,
+    h0, h1, h2, h3, keep_x, keep_z, send, left, right, heads, xbuf, zbuf,
 ):
     me, bucket, core = here()
     arrived = jnp.concatenate([arrive_one[...].astype(wide), arrive_two[...].astype(wide)], axis=0)
@@ -644,53 +665,69 @@
             for part in thirds:
                 starts = [b * 192 + j * 48 + c * 24 for j in range(4)]
                 block.append(jnp.concatenate([part[s : s + 24] for s in starts], axis=1))
-            block.append(jnp.zeros((8, D), wide))
-            zbuf[c ^ core, b ^ bucket] = jnp.concatenate(block, axis=0).astype(low)
-    for d in range(4):
-        cot = (c0, c1, c2, c3)[d][...].astype(wide)
-        right[d * 160 : (d + 1) * 160, :] = jnp.concatenate([cot, jnp.zeros((160, 1), wide)], axis=1).astype(low)
-        left[d * 160 : (d + 1) * 160, :] = (a0, a1, a2, a3)[d][...]
-    down = tn(left[...], right[...])
-    for j in range(4):
-        for c in range(2):
-            s = j * 192 + c * 96
-            xbuf[c ^ core, j ^ me, 0:96, :] = down[s : s + 96].astype(low)
+            zbuf[c ^ core, b ^ bucket, 0:72, :] = jnp.concatenate(block, axis=0)
     for r, p in enumerate((p0, p1, p2, p3)):
         out = tn(unpacked(p[...]).astype(low), branch_own[...])
         for j in range(4):
             for c in range(2):
                 s = j * 48 + c * 24
-                obuf[c ^ core, j ^ me, me ^ r ^ bucket] = out[s : s + 24]
-    for c in range(2):
-        for r in range(4):
-            xbuf[c, r, 96:192, :] = jnp.concatenate([obuf[c, r, d] for d in range(4)], axis=0).astype(low)
+                zbuf[c ^ core, me ^ r ^ bucket, 72 + j * 24 : 96 + j * 24, :] = out[s : s + 24]
+    for d, c in enumerate((c0, c1)):
+        cot = c[...].astype(wide)
+        right[d * 160 : (d + 1) * 160, :] = jnp.concatenate([cot, jnp.zeros((160, 1), wide)], axis=1).astype(low)
+    for half in range(2):
+        left[0:160, :] = act_keep[half * 160 : half * 160 + 160, :]
+        left[160:320, :] = act_came[half * 160 : half * 160 + 160, :]
+        down = tn(left[0:320, :], right[0:320, :])
+        for j in range(4):
+            for c in range(2):
+                s = j * 192 + c * 96
+                xbuf[c ^ core, j ^ me, half * 96 : half * 96 + 96, :] = down[s : s + 96].astype(low)
     keep_x[...] = xbuf[0]
-    keep_z[...] = zbuf[0]
     for r in range(4):
+        keep_z[r] = zbuf[0, r]
         send[r * 192 : (r + 1) * 192, :] = xbuf[1, r]
-        send[768 + r * 80 : 848 + r * 80, :] = zbuf[1, r]
+        block = jnp.concatenate([zbuf[1, r], jnp.zeros((8, D), wide)], axis=0)
+        send[768 + r * 176 : 944 + r * 176, :] = block.astype(low)
     hi, lo = split_pair(total)
-    send[1088:1104, :] = hi
-    send[1104:1120, :] = lo
-
-
-def late_sum_kernel(keep_x, keep_z, send, arrived, h0, h1, h2, h3, x0, x1, x2, x3, z0, z1, z2, z3):
-    own = send[1088:1104, :].astype(wide) + send[1104:1120, :].astype(wide)
-    hi, lo = split_pair(own + (arrived[1088:1104, :].astype(wide) + arrived[1104:1120, :].astype(wide)))
+    send[1472:1488, :] = hi
+    send[1488:1504, :] = lo
+
+
+def late_sum_kernel(keep_x, keep_z, send, arrived, h0, h1, h2, h3, x0, x1, x2, x3, z_keep, z_send):
+    own = send[1472:1488, :].astype(wide) + send[1488:1504, :].astype(wide)
+    hi, lo = split_pair(own + (arrived[1472:1488, :].astype(wide) + arrived[1488:1504, :].astype(wide)))
+    blocks = []
     for r in range(4):
-        x, z, h = (x0, x1, x2, x3)[r], (z0, z1, z2, z3)[r], (h0, h1, h2, h3)[r]
+        x, h = (x0, x1, x2, x3)[r], (h0, h1, h2, h3)[r]
         x[0:192, :] = (keep_x[r].astype(wide) + arrived[r * 192 : (r + 1) * 192, :].astype(wide)).astype(low)
         x[192:272, 0:384] = h[0:80, :]
         x[192:272, 384:768] = h[80:160, :]
         x[272:352, 0:384] = h[160:240, :]
         x[272:352, 384:768] = jnp.zeros((80, 384), low)
-        came = arrived[768 + r * 80 : 848 + r * 80, :].astype(wide)
-        z[0:80, :] = (keep_z[r].astype(wide) + came).astype(low)
-        z[80:96, :] = hi
-        z[96:112, :] = lo
-
-
-def up_grad_kernel(n0, n1, n2, n3, keep, send, left, right, buf):
+        came = arrived[768 + r * 176 : 944 + r * 176, :].astype(wide)
+        blocks.append(keep_z[r] + came[0:168])
+    z_keep[0:168, :] = blocks[0]
+    z_keep[168:336, :] = blocks[2]
+    sums = [hi.astype(wide)[0:12], lo.astype(wide)[0:12], jnp.zeros((8, D), wide)]
+    z_send[...] = jnp.concatenate([blocks[1], blocks[3]] + sums, axis=0).astype(low)
+
+
+def pair_sum(own, came, start):
+    a = own[start : start + 12] + own[start + 12 : start + 24]
+    b = came[start : start + 12] + came[start + 12 : start + 24]
+    return a + b
+
+
+def late_mid_kernel(z_keep, z_send, came, z_own, z_next):
+    came = came[...].astype(wide)
+    hi, lo = split_pair(pair_sum(z_send[...].astype(wide), came, 336))
+    z_own[...] = z_keep[0:168, :] + came[0:168]
+    block = [z_keep[168:336, :] + came[168:336], hi.astype(wide), lo.astype(wide)]
+    z_next[...] = jnp.concatenate(block, axis=0).astype(low)
+
+
+def up_grad_kernel(n0, n1, n2, n3, keep, send_one, send_two, send_three, left, right, buf):
     me, bucket, core = here()
     for r in range(4):
         rows = slice(r * 160, (r + 1) * 160)
@@ -704,44 +741,57 @@
             block = jnp.concatenate([up[s : s + 24] for s in starts], axis=0)
             buf[c ^ core, b ^ bucket] = block.astype(low)
     keep[...] = buf[0]
-    send[...] = buf[1]
-
-
-def up_sum_kernel(keep, arrived, z0, z1, z2, z3):
-    for d, z in enumerate((z0, z1, z2, z3)):
-        z[...] = (keep[d].astype(wide) + arrived[d].astype(wide)).astype(low)
-
-
-def final_send_kernel(z0, z1, z2, z3, w0, w1, w2, w3, f0, f1, f2, f3, buf, vec):
-    me, bucket, core = here()
-    zs = (z0, z1, z2, z3)
-    ins = sum(z[0:72, :].astype(wide) for z in zs)
-    ups = sum(w[...].astype(wide) for w in (w0, w1, w2, w3))
-    for d, z in enumerate(zs):
-        vec[bucket ^ d] = z[80:96, :].astype(wide) + z[96:112, :].astype(wide)
-    hi, lo = split_pair(vec[0] + vec[1] + vec[2] + vec[3])
-    pad = jnp.zeros((8, D), wide)
+    send_one[0:96, :] = buf[1, 0]
+    send_one[96:128, :] = buf[1, 1, 0:32, :]
+    send_two[0:64, :] = buf[1, 1, 32:96, :]
+    send_two[64:128, :] = buf[1, 2, 0:64, :]
+    send_three[0:32, :] = buf[1, 2, 64:96, :]
+    send_three[32:128, :] = buf[1, 3]
+
+
+def up_sum_kernel(keep, arrive_one, arrive_two, arrive_three, w_keep, w_send):
+    parts = [a[...].astype(wide) for a in (arrive_one, arrive_two, arrive_three)]
+    arrived = jnp.concatenate(parts, axis=0)
+    for d in range(4):
+        total = keep[d].astype(wide) + arrived[d * 96 : (d + 1) * 96]
+        if d % 2 == 0:
+            w_keep[d // 2] = total
+        else:
+            w_send[d // 2] = total.astype(low)
+
+
+def up_mid_kernel(w_keep, came, w_own, w_next):
+    w_own[...] = w_keep[0] + came[0].astype(wide)
+    w_next[...] = (w_keep[1] + came[1].astype(wide)).astype(low)
+
+
+def final_send_kernel(z_own, z_next, z_came, w_own, w_came, f0, f1, f2, f3, buf):
+    me = here()[0]
+    came = z_came[...].astype(wide)
+    ins = z_own[...] + came[0:168]
+    ups = w_own[...] + w_came[...].astype(wide)
+    hi, lo = split_pair(pair_sum(z_next[...].astype(wide), came, 168))
+    sums = [hi.astype(wide), lo.astype(wide)]
     rest = jnp.zeros((24, SPLIT), wide)
     for j in range(4):
         lanes = slice(j * SPLIT, (j + 1) * SPLIT)
         wide_rows = [ins[i * 24 : (i + 1) * 24, lanes] for i in range(3)] + [rest]
-        block = [ups[j * 24 : (j + 1) * 24], pad, jnp.concatenate(wide_rows, axis=1), pad]
+        block = [ups[j * 24 : (j + 1) * 24], jnp.concatenate(wide_rows, axis=1)]
+        block += [ins[72 + j * 24 : 96 + j * 24]] + sums
         buf[j ^ me] = jnp.concatenate(block, axis=0).astype(low)
     for r, f in enumerate((f0, f1, f2, f3)):
-        f[0:16, :] = hi
-        f[16:32, :] = lo
-        f[32:96, :] = buf[r]
+        f[...] = buf[r]
 
 
 def final_kernel(
-    lengths, f0, f1, f2, f3, in_total, up_total, first, query, value, output, second, up_bias, down, stats, buf
+    lengths, f0, f1, f2, f3, in_total, up_total, out_total, first, query, value, output, second, up_bias, down, stats, buf
 ):
     me = here()[0]
     for r, f in enumerate((f0, f1, f2, f3)):
         buf[r ^ me] = f[...].astype(wide)
-    total = buf[0, 0:16] + buf[0, 16:32]
+    total = buf[0, 72:84] + buf[0, 84:96]
     for j in (1, 2, 3):
-        total = total + (buf[j, 0:16] + buf[j, 16:32])
+        total = total + (buf[j, 72:84] + buf[j, 84:96])
     first[...] = total[0]
     query[...] = total[1]
     value[...] = total[2]
@@ -754,10 +804,11 @@
     for b in (1, 2, 3):
         count = count + lengths[b, 0] + lengths[b, 1]
     stats[...] = total[10, :2] / count.astype(wide)
+    out_total[...] = (buf[0, 48:72] + buf[1, 48:72] + buf[2, 48:72] + buf[3, 48:72])[:, :DC]
     for j in range(4):
-        up_total[:, j * D : (j + 1) * D] = buf[j, 32:56, :]
+        up_total[:, j * D : (j + 1) * D] = buf[j, 0:24, :]
     for i in range(3):
-        piece = jnp.concatenate([buf[j, 64:88, i * SPLIT : (i + 1) * SPLIT] for j in range(4)], axis=1)
+        piece = jnp.concatenate([buf[j, 24:48, i * SPLIT : (i + 1) * SPLIT] for j in range(4)], axis=1)
         in_total[:, i * D : (i + 1) * D] = piece
 
 
@@ -781,19 +832,16 @@
     out[...] = (middle_grad[...] + f - last)[:, :DC].astype(low)
 
 
-def down_sum_kernel(x0, x1, x2, x3, down_total, o0, o1, o2, o3):
+def down_sum_kernel(x0, x1, x2, x3, own, other):
     total = x0[0:192, :].astype(wide)
     for x in (x1, x2, x3):
         total = total + x[0:192, :].astype(wide)
-    down_total[...] = total[0:96, :DC]
-    for d, o in enumerate((o0, o1, o2, o3)):
-        block = [total[96 + d * 24 : 120 + d * 24], jnp.zeros((8, D), wide)]
-        o[...] = jnp.concatenate(block, axis=0).astype(low)
-
-
-def out_sum_kernel(o0, o1, o2, o3, out_total):
-    total = o0[...].astype(wide) + o1[...].astype(wide) + o2[...].astype(wide) + o3[...].astype(wide)
-    out_total[...] = total[0:24, :DC]
+    own[...] = total[0:96]
+    other[...] = total[96:192].astype(low)
+
+
+def down_final_kernel(own, came, down_total):
+    down_total[...] = (own[...] + came[...].astype(wide))[:, :DC]
 
 def swap_chip(block, step):
     return lax.ppermute(block, "blk", [(k, k ^ (2 * step)) for k in range(8)])
@@ -809,11 +857,6 @@
 
 def exchange(blocks):
     got = {r: swap_chip(blocks[r], r) for r in (3, 1, 2)}
-    return [blocks[0], got[1], got[2], got[3]]
-
-
-def over_buckets(blocks):
-    got = {d: shift_bucket(blocks[d], d) for d in (2, 1, 3)}
     return [blocks[0], got[1], got[2], got[3]]
 
 
@@ -842,17 +885,26 @@
     where = [span_order, offsets, lengths]
     packed_block = ((240, 2 * SPLIT), low)
     token = ((160, D), low)
-    cots = over_buckets([out_cotangent] * 4)
     s0, s1, s2, s3, hidden, root_one = call(
         entry_kernel,
         [packed_block] * 4 + [token, ((160, 1), wide)],
         [residual_in, first_gain, input_weight, query_bias, value_bias],
-        [pltpu.VMEM((4, 240, 2 * SPLIT), low)],
+        [
+            pltpu.VMEM((4, 240, 2 * SPLIT), low),
+            pltpu.VMEM((160, DC), low),
+            pltpu.VMEM((D,), wide),
+            pltpu.VMEM((3, D, D), low),
+            pltpu.VMEM((D,), wide),
+            pltpu.VMEM((D,), wide),
+            pltpu.SemaphoreType.DMA((7,)),
+        ],
+        extra=60,
+        far=range(5),
     )
     got = exchange([s0, s1, s2, s3])
     (push,) = call(push_kernel, [((160, FF), wide)], [out_cotangent, down_weight])
     hiddens = exchange([hidden] * 4)
-    got = list(after(got, push, cots[1], cots[3]))
+    got = list(after(got, push))
     query, own_both = call(assemble_kernel, [((640, SPLIT), low), ((640, 2 * SPLIT), low)], got)
     sib_both = swap_core(own_both)
     backed = ((80, 2 * SPLIT), low)
@@ -862,15 +914,17 @@
         where + [query, own_both, sib_both],
         [pltpu.VMEM((1280, SPLIT), low), pltpu.VMEM((3, 1280, SPLIT), low), pltpu.VMEM((640, 1280), wide)],
         small=3,
+        work=7,
     )
     back = exchange([b0, b1, b2, b3])
-    back = list(after(back, cots[2], *hiddens[1:]))
+    (cot,) = after([out_cotangent], b0)
+    cots = [out_cotangent, shift_bucket(cot, 1)]
+    back = list(after(back, *hiddens[1:]))
     (columns,) = call(columns_kernel, [((D, 3 * SPLIT), low)], after([input_weight], b0))
     outs = call(
         middle_kernel,
         [backed] * 4
-        + [token] * 4
-        + [((320, D), low)] * 4
+        + [((320, D), low)] * 6
         + [token, ((160, DC), wide), ((160, D), wide), ((16, D), wide)],
         where
         + back
@@ -879,16 +933,18 @@
         [pltpu.VMEM((4, 80, 2 * SPLIT), low), pltpu.VMEM((4, 160, D), low), pltpu.VMEM((4, 320, D), low)],
         small=3,
     )
-    actives, lates = list(outs[4:8]), list(outs[8:12])
-    branch_own, middle, middle_grad, vector = outs[12:]
+    act_keep, act_send = outs[4:6]
+    lates = list(outs[6:10])
+    branch_own, middle, middle_grad, vector = outs[10:]
     grads = exchange(outs[:4])
+    grads = list(after(grads, cots[1]))
     (residual_out,) = call(
         closing_kernel,
         [((160, DC), low)],
-        actives + [down_weight, middle, down_bias],
-    )
-    actives = over_buckets(actives)
-    lates = exchange(after(lates, grads[1]))
+        [act_keep, act_send, down_weight, middle, down_bias],
+    )
+    act_came = shift_bucket(act_send, 1)
+    lates = exchange(after(lates, *grads[1:]))
     query_grad, both_grad, *away = call(
         backward_kernel,
         [((640, SPLIT), low), ((640, 2 * SPLIT), wide)] + [((320, 2 * SPLIT), low)] * 2,
@@ -900,58 +956,71 @@
             pltpu.VMEM((640, 1280), low),
         ],
     )
-    arrived = [swap_core(x) for x in after(away, *actives[1:])]
+    arrived = [swap_core(x) for x in after(away, act_came)]
     arrived = list(after(arrived, lates[1], lates[2]))
     outs = call(
         late_kernel,
-        [packed_block] * 4 + [((4, 192, D), low), ((4, 80, D), low), ((1120, D), low)],
-        [query_grad, both_grad] + arrived + hiddens + actives + cots + back + [branch_own, columns, first_gain, vector],
+        [packed_block] * 4 + [((4, 192, D), low), ((4, 168, D), wide), ((1504, D), low)],
+        [query_grad, both_grad] + arrived + hiddens + [act_keep, act_came] + cots + back + [branch_own, columns, first_gain, vector],
         [
             pltpu.VMEM((640, D), low),
             pltpu.VMEM((640, D), low),
             pltpu.VMEM((640, 3 * SPLIT), low),
             pltpu.VMEM((2, 4, 192, D), low),
-            pltpu.VMEM((2, 4, 80, D), low),
-            pltpu.VMEM((2, 4, 4, 24, D), wide),
+            pltpu.VMEM((2, 4, 168, D), wide),
         ],
     )
     homes = list(outs[:4])
     keep_x, keep_z, send = outs[4:]
     outs = call(
         late_sum_kernel,
-        [((352, D), low)] * 4 + [((112, D), low)] * 4,
+        [((352, D), low)] * 4 + [((336, D), wide), ((368, D), low)],
         [keep_x, keep_z, send, swap_core(send)] + homes,
     )
-    in_z = over_buckets(outs[4:])
     home = exchange(outs[:4])
-    keep, send = call(
+    z_keep, z_send = outs[4:]
+    z_own, z_next = call(
+        late_mid_kernel,
+        [((168, D), wide), ((192, D), low)],
+        [z_keep, z_send, shift_bucket(z_send, 1)],
+    )
+    z_came = shift_bucket(z_next, 2)
+    keep, *send = call(
         up_grad_kernel,
-        [((4, 96, D), low)] * 2,
-        list(after(lates, *in_z[1:])),
-        [
-            pltpu.VMEM((640, D), low),
-            pltpu.VMEM((640, D), low),
-            pltpu.VMEM((2, 4, 96, D), low),
-        ],
-    )
-    up_z = over_buckets(call(up_sum_kernel, [((96, D), low)] * 4, [keep, swap_core(send)]))
-    down_total, *pieces = call(down_sum_kernel, [((96, DC), wide)] + [((32, D), low)] * 4, home)
-    (out_total,) = call(out_sum_kernel, [((24, DC), wide)], over_buckets(pieces))
+        [((4, 96, D), low)] + [((128, D), low)] * 3,
+        lates,
+        [pltpu.VMEM((640, D), low), pltpu.VMEM((640, D), low), pltpu.VMEM((2, 4, 96, D), low)],
+    )
+    w_keep, w_send = call(
+        up_sum_kernel,
+        [((2, 96, D), wide), ((2, 96, D), low)],
+        [keep] + [swap_core(x) for x in send],
+    )
+    w_own, w_next = call(
+        up_mid_kernel,
+        [((96, D), wide), ((96, D), low)],
+        [w_keep, shift_bucket(w_send, 1)],
+    )
+    w_came = shift_bucket(w_next, 2)
+    finals = call(
+        final_send_kernel,
+        [((96, D), low)] * 4,
+        [z_own, z_next, z_came, w_own, w_came],
+        [pltpu.VMEM((4, 96, D), low)],
+    )
+    down_own, down_other = call(down_sum_kernel, [((96, D), wide), ((96, D), low)], home)
+    (down_total,) = call(
+        down_final_kernel, [((96, DC), wide)], [down_own, shift_bucket(down_other, 2)]
+    )
     (residual_grad,) = call(
         home_kernel,
         [((160, DC), low)],
         home + [input_weight, residual_in, first_gain, middle_grad],
         [pltpu.VMEM((4, 240, 2 * SPLIT), low)],
     )
-    finals = call(
-        final_send_kernel,
-        [((96, D), low)] * 4,
-        in_z + up_z,
-        [pltpu.VMEM((4, 64, D), low), pltpu.VMEM((4, 16, D), wide)],
-    )
-    in_total, up_total, first, query_sum, value_sum, output, second, up_sum_bias, down, stats = call(
+    in_total, up_total, out_total, first, query_sum, value_sum, output, second, up_sum_bias, down, stats = call(
         final_kernel,
-        [((24, 3 * D), wide), ((24, FF), wide)]
+        [((24, 3 * D), wide), ((24, FF), wide), ((24, DC), wide)]
         + [((D,), wide)] * 3
         + [((DC,), wide), ((D,), wide), ((FF,), wide), ((DC,), wide), ((2,), wide)],
         [lengths] + exchange(finals),

time: 152 us -> 127 us (0.84)
  starting transfers between devices: 52.8 us -> 37 us
  local copies, waits for them, and re-layouts: 12.2 us -> 2.52 us
  Pallas kernels: 38.8 us -> 41 us
  waiting for transfers between devices: 46.3 us -> 44.6 us
    ppermute x15 -> x7, starting transfers between devices: 27.2 us -> 9.63 us  [shift_bucket(): return lax.ppermute(block, 'bucket', [(b, b ^ step) for b in range(4)])]
    ppermute x15 -> x7, waiting for transfers between devices: 28.4 us -> 11.6 us  [shift_bucket(): return lax.ppermute(block, 'bucket', [(b, b ^ step) for b in range(4)])]
    ppermute x21, waiting for transfers between devices: 15 us -> 29 us  [swap_chip(): return lax.ppermute(block, 'blk', [(k, k ^ 2 * step) for k in range(8)])]
    unnamed x55 -> x39, local copies, waits for them, and re-layouts: 12.2 us -> 2.52 us
    pallas_call x17 -> x19, Pallas kernels: 38.8 us -> 41 us  [call(): pl.pallas_call(kernel, out_shape=shapes, in_specs=[SMEM if i < small else...]
    ppermute x5 -> x7, waiting for transfers between devices: 2.88 us -> 4.04 us  [swap_core(): return lax.ppermute(block, 'blk', [(k, k ^ 1) for k in range(8)])]
  transfers between devices with their start and end apart: 41 -> 35, of which waited for: 16 -> 14; matrix products, arithmetic and copies ran while one was open for 1% -> 0% of each run, Pallas kernels for 17% -> 24%
where the time goes in v3:
time: 127 us; the launch traced here: 126 us
  waiting for transfers between devices  44.6 us (35%)
  Pallas kernels  41 us (32%)
  starting transfers between devices  37 us (29%)
  local copies, waits for them, and re-layouts  2.52 us (2%)
    pallas_call x19, Pallas kernels, call(): pl.pallas_call(kernel, out_shape=shapes, in_specs=[SMEM if i < small else...  41 us
    ppermute x21, waiting for transfers between devices, swap_chip(): return lax.ppermute(block, 'blk', [(k, k ^ 2 * step) for k in range(8)])  29 us
    ppermute x21, starting transfers between devices, swap_chip(): return lax.ppermute(block, 'blk', [(k, k ^ 2 * step) for k in range(8)])  25.9 us
    ppermute x7, waiting for transfers between devices, shift_bucket(): return lax.ppermute(block, 'bucket', [(b, b ^ step) for b in range(4)])  11.6 us
    ppermute x7, starting transfers between devices, shift_bucket(): return lax.ppermute(block, 'bucket', [(b, b ^ step) for b in range(4)])  9.63 us
    ppermute x7, waiting for transfers between devices, swap_core(): return lax.ppermute(block, 'blk', [(k, k ^ 1) for k in range(8)])  4.04 us
  transfers between devices with their start and end apart: 35, of which 14 were waited for; matrix products, arithmetic and copies ran while one was open for 0% of the time, Pallas kernels for 24%

profile of v3, /device:TPU:0, one launch (start us, length us, event | category | flops | bytes accessed | tf_op | source)
XLA Modules:
  0.0 126.4 jit_solution(3389429471311813453)
XLA Ops:
  0.7 4.0 %shard_map.263 = (bf16[240,384]{1,0:T(8,128)(2,1)}, bf16[240,384]{1,0:T(8,128)(2,1)}, bf16[240,384]{1,0:T(8,128)(2,1)}, bf16[240,384]{1,0:T(8,128)(2,1)}, bf16[160,768]{1,0:T(8,128)(2,1)}, /*index=5*/f32[160,1]{1,0:T(8,128)}) custom-call(bf16[160,767]{1,0:T(8,128)(2,1)} %resid.3, f32[768]{0:T(1024)} %gain.5, bf16[768,2304]{1,0:T(8,128)(2,1)} %weight.6, ...), custom_call_target="tpu_custom_call" | custom-call | flops 1000 | bytes 1000 | tf_op jit(solution)/shard_map/pallas_call | solution.py:364
  4.6 3.0 %collective-permute-start = (bf16[240,384]{1,0:T(8,128)(2,1)}, bf16[240,384]{1,0:T(8,128)(2,1)S(1)}, u32[]{:S(2)}, u32[]{:S(2)}) collective-permute-start(bf16[240,384]{1,0:T(8,128)(2,1)} %get-tuple-element.109), channel_id=1, source_target_pairs={{0,2},{1,3},{2,0},{3,1},{4,6},{5,7},{6,4},{7,5},{8,10},{9,11},{10,... | collective-permute-start | bytes 552968 | tf_op jit(solution)/shard_map/ppermute | solution.py:847
  7.6 1.5 %collective-permute-start.1 = (bf16[240,384]{1,0:T(8,128)(2,1)}, bf16[240,384]{1,0:T(8,128)(2,1)S(1)}, u32[]{:S(2)}, u32[]{:S(2)}) collective-permute-start(bf16[240,384]{1,0:T(8,128)(2,1)} %get-tuple-element.110), channel_id=1, source_target_pairs={{0,4},{1,5},{2,6},{3,7},{4,0},{5,1},{6,2},{7,3},{8,12},{9,13},{10,... | collective-permute-start | bytes 552968 | tf_op jit(solution)/shard_map/ppermute | solution.py:847
  9.2 2.3 %copy-done.1 = bf16[3072,767]{1,0:T(8,128)(2,1)S(1)} copy-done((bf16[3072,767]{1,0:T(8,128)(2,1)S(1)}, bf16[3072,767]{1,0:T(8,128)(2,1)}, u32[]{:S(2)}) %copy-start.1) | copy-done | bytes 4712472
  11.5 1.7 %shard_map.264.push = f32[160,3072]{1,0:T(8,128)S(1)} custom-call(bf16[160,767]{1,0:T(8,128)(2,1)S(1)} %copy-done.3, bf16[3072,767]{1,0:T(8,128)(2,1)S(1)} %copy-done.1), custom_call_target="tpu_custom_call" | custom-call | flops 1000 | bytes 1000 | tf_op jit(solution)/shard_map/pallas_call | solution.py:364
  13.3 4.6 %collective-permute-done.1.p2 = bf16[240,384]{1,0:T(8,128)(2,1)S(1)} collective-permute-done((bf16[240,384]{1,0:T(8,128)(2,1)}, bf16[240,384]{1,0:T(8,128)(2,1)S(1)}, u32[]{:S(2)}, u32[]{:S(2)}) %collective-permute-start.1) | collective-permute-done | bytes 184352 | tf_op jit(solution)/shard_map/ppermute | solution.py:847
  18.4 1.3 %collective-permute-start.7 = (bf16[160,768]{1,0:T(8,128)(2,1)}, bf16[160,768]{1,0:T(8,128)(2,1)}, u32[]{:S(2)}, u32[]{:S(2)}) collective-permute-start(bf16[160,768]{1,0:T(8,128)(2,1)} %get-tuple-element.122.i0), channel_id=1, source_target_pairs={{0,2},{1,3},{2,0},{3,1},{4,6},{5,7},{6,4},{7,5},{8,10},{9,11},{10,... | collective-permute-start | bytes 737288 | tf_op jit(solution)/shard_map/ppermute | solution.py:847
  19.7 0.8 collective-permute-start.8
  20.5 1.4 %collective-permute-start.9 = (bf16[160,768]{1,0:T(8,128)(2,1)}, bf16[160,768]{1,0:T(8,128)(2,1)}, u32[]{:S(2)}, u32[]{:S(2)}) collective-permute-start(bf16[160,768]{1,0:T(8,128)(2,1)} %get-tuple-element.122.i0), channel_id=1, source_target_pairs={{0,6},{1,7},{2,4},{3,5},{4,2},{5,3},{6,0},{7,1},{8,14},{9,15},{10,... | collective-permute-start | bytes 737288 | tf_op jit(solution)/shard_map/ppermute | solution.py:847
  22.2 7.0 %shard_map.266 = (bf16[3,640,1280]{2,1,0:T(8,128)(2,1)S(1)}, f32[640,192]{1,0:T(8,128)S(1)}, bf16[80,384]{1,0:T(8,128)(2,1)S(1)}, bf16[80,384]{1,0:T(8,128)(2,1)...) custom-call(s32[16]{0:T(128)S(1)} %copy-done.12, s32[1,2]{1,0:T(1,128)S(1)} %copy-done.13, ...), custom_call_target="tpu_custom_call" | custom-call | flops 7700000768 | bytes 1000 | tf_op jit(solution)/shard_map/pallas_call | solution.py:364
  29.2 1.3 %collective-permute-start.4 = (bf16[80,384]{1,0:T(8,128)(2,1)S(1)}, bf16[80,384]{1,0:T(8,128)(2,1)S(1)}, u32[]{:S(2)}, u32[]{:S(2)}) collective-permute-start(bf16[80,384]{1,0:T(8,128)(2,1)S(1)} %get-tuple-element.119), channel_id=1, source_target_pairs={{0,2},{1,3},{2,0},{3,1},{4,6},{5,7},{6,4},{7,5},{8,10},{9,11},{10,... | collective-permute-start | bytes 184328 | tf_op jit(solution)/shard_map/ppermute | solution.py:847
  30.5 0.8 collective-permute-start.5
  31.3 1.4 %collective-permute-start.6 = (bf16[80,384]{1,0:T(8,128)(2,1)S(1)}, bf16[80,384]{1,0:T(8,128)(2,1)S(1)}, u32[]{:S(2)}, u32[]{:S(2)}) collective-permute-start(bf16[80,384]{1,0:T(8,128)(2,1)S(1)} %get-tuple-element.121), channel_id=1, source_target_pairs={{0,6},{1,7},{2,4},{3,5},{4,2},{5,3},{6,0},{7,1},{8,14},{9,15},{10,... | collective-permute-start | bytes 184328 | tf_op jit(solution)/shard_map/ppermute | solution.py:847
  32.7 1.6 %collective-permute-start.13 = (bf16[160,767]{1,0:T(8,128)(2,1)S(1)}, bf16[160,767]{1,0:T(8,128)(2,1)S(1)}, u32[]{:S(2)}, u32[]{:S(2)}) collective-permute-start(bf16[160,767]{1,0:T(8,128)(2,1)S(1)} %copy-done.3), channel_id=1, source_target_pairs={{0,8},{8,0},{16,24},{24,16},{1,9},{9,1},{17,25},{25,17},{2,10},{10... | collective-permute-start | bytes 736328 | tf_op jit(solution)/shard_map/ppermute | solution.py:855
  34.3 1.0 collective-permute-done.5.p2
  35.3 1.1 collective-permute-done.6.p3
  36.5 6.1 %shard_map.267 = (bf16[80,384]{1,0:T(8,128)(2,1)S(1)}, bf16[80,384]{1,0:T(8,128)(2,1)S(1)}, bf16[80,384]{1,0:T(8,128)(2,1)S(1)}, bf16[80,384]{1,0:T(8,128)(2,1)S...) custom-call(s32[16]{0:T(128)S(1)} %copy-done.12, ...), custom_call_target="tpu_custom_call" | custom-call | flops 1000 | bytes 1000 | tf_op jit(solution)/shard_map/pallas_call | solution.py:364
  42.6 1.6 %collective-permute-start.14 = (bf16[320,768]{1,0:T(8,128)(2,1)S(1)}, bf16[320,768]{1,0:T(8,128)(2,1)S(1)}, u32[]{:S(2)}, u32[]{:S(2)}) collective-permute-start(bf16[320,768]{1,0:T(8,128)(2,1)S(1)} %get-tuple-element.129.act_send), channel_id=1, source_target_pairs={{0,8},{8,0},{16,24},{24,16},{1,9},{9,1},{17,25},{25,17},{2,10},{10... | collective-permute-start | bytes 1474568 | tf_op jit(solution)/shard_map/ppermute | solution.py:855
  44.2 1.5 %collective-permute-start.10 = (bf16[80,384]{1,0:T(8,128)(2,1)S(1)}, bf16[80,384]{1,0:T(8,128)(2,1)S(1)}, u32[]{:S(2)}, u32[]{:S(2)}) collective-permute-start(bf16[80,384]{1,0:T(8,128)(2,1)S(1)} %get-tuple-element.132), channel_id=1, source_target_pairs={{0,2},{1,3},{2,0},{3,1},{4,6},{5,7},{6,4},{7,5},{8,10},{9,11},{10,... | collective-permute-start | bytes 184328 | tf_op jit(solution)/shard_map/ppermute | solution.py:847
  46.2 1.5 %collective-permute-start.12 = (bf16[80,384]{1,0:T(8,128)(2,1)S(1)}, bf16[80,384]{1,0:T(8,128)(2,1)S(1)}, u32[]{:S(2)}, u32[]{:S(2)}) collective-permute-start(bf16[80,384]{1,0:T(8,128)(2,1)S(1)} %get-tuple-element.134), channel_id=1, source_target_pairs={{0,6},{1,7},{2,4},{3,5},{4,2},{5,3},{6,0},{7,1},{8,14},{9,15},{10,... | collective-permute-start | bytes 184328 | tf_op jit(solution)/shard_map/ppermute | solution.py:847
  47.7 0.7 collective-permute-done.10.d1
  48.4 1.5 %collective-permute-done.11.d2 = bf16[80,384]{1,0:T(8,128)(2,1)S(1)} collective-permute-done((bf16[80,384]{1,0:T(8,128)(2,1)S(1)}, bf16[80,384]{1,0:T(8,128)(2,1)S(1)}, u32[]{:S(2)}, u32[]{:S(2)}) %collective-permute-start.11) | collective-permute-done | bytes 61472 | tf_op jit(solution)/shard_map/ppermute | solution.py:847
  49.9 1.8 %collective-permute-done.12.d3 = bf16[80,384]{1,0:T(8,128)(2,1)S(1)} collective-permute-done((bf16[80,384]{1,0:T(8,128)(2,1)S(1)}, bf16[80,384]{1,0:T(8,128)(2,1)S(1)}, u32[]{:S(2)}, u32[]{:S(2)}) %collective-permute-start.12) | collective-permute-done | bytes 61472 | tf_op jit(solution)/shard_map/ppermute | solution.py:847
  51.7 1.4 %collective-permute-start.17 = (bf16[320,768]{1,0:T(8,128)(2,1)S(1)}, bf16[320,768]{1,0:T(8,128)(2,1)S(1)}, u32[]{:S(2)}, u32[]{:S(2)}) collective-permute-start(bf16[320,768]{1,0:T(8,128)(2,1)S(1)} %get-tuple-element.152), channel_id=1, source_target_pairs={{0,2},{1,3},{2,0},{3,1},{4,6},{5,7},{6,4},{7,5},{8,10},{9,11},{10,... | collective-permute-start | bytes 1474568 | tf_op jit(solution)/shard_map/ppermute | solution.py:847
  53.1 0.9 collective-permute-start.18
  54.0 8.2 %shard_map.269 = (bf16[640,192]{1,0:T(8,128)(2,1)S(1)}, f32[640,384]{1,0:T(8,128)S(1)}, bf16[320,384]{1,0:T(8,128)(2,1)S(1)}, bf16[320,384]{1,0:T(8,128)(2,1)S(1)}) custom-call(bf16[80,384]{1,0:T(8,128)(2,1)S(1)} %get-tuple-element.136.d0, bf16[80,384]{1,0:T(8,128)(2,1)S(1)} %collective-permute-done.10.d1, bf16[80,384]{1,0:T(8,128)(2,1)S(1)} %collective-permute-done.11.d2, ...), custom_call_target="tpu_custom_call" | custom-call | flops 1000 | bytes 1000 | tf_op jit(solution)/shard_map/pallas_call | solution.py:364
  63.2 0.6 collective-permute-done.15.arrive_one
  64.2 4.7 %shard_map.271 = (bf16[240,384]{1,0:T(8,128)(2,1)S(1)}, bf16[240,384]{1,0:T(8,128)(2,1)S(1)}, bf16[240,384]{1,0:T(8,128)(2,1)S(1)}, bf16[240,384]{1,0:T(8,128)(2...) custom-call(bf16[640,192]{1,0:T(8,128)(2,1)S(1)} %get-tuple-element.142.query_g, ...), custom_call_target="tpu_custom_call" | custom-call | flops 1000 | bytes 1000 | tf_op jit(solution)/shard_map/pallas_call | solution.py:364
  69.1 1.2 collective-permute-start.25
  70.3 3.1 %collective-permute-done.19.arrived = bf16[1504,768]{1,0:T(8,128)(2,1)S(1)} collective-permute-done((bf16[1504,768]{1,0:T(8,128)(2,1)S(1)}, bf16[1504,768]{1,0:T(8,128)(2,1)S(1)}, u32[]{:S(2)}, u32[]{:S(2)}) %collective-permute-start.19) | collective-permute-done | bytes 2310176 | tf_op jit(solution)/shard_map/ppermute | solution.py:851
  73.4 0.6 shard_map.272
  74.5 8.9 %collective-permute-done.25.n3 = bf16[320,768]{1,0:T(8,128)(2,1)S(1)} collective-permute-done((bf16[320,768]{1,0:T(8,128)(2,1)S(1)}, bf16[320,768]{1,0:T(8,128)(2,1)S(1)}, u32[]{:S(2)}, u32[]{:S(2)}) %collective-permute-start.25) | collective-permute-done | bytes 491552 | tf_op jit(solution)/shard_map/ppermute | solution.py:847
  83.4 1.2 shard_map.275
  85.3 1.4 %collective-permute-start.20 = (bf16[352,768]{1,0:T(8,128)(2,1)S(1)}, bf16[352,768]{1,0:T(8,128)(2,1)S(1)}, u32[]{:S(2)}, u32[]{:S(2)}) collective-permute-start(bf16[352,768]{1,0:T(8,128)(2,1)S(1)} %get-tuple-element.167), channel_id=1, source_target_pairs={{0,2},{1,3},{2,0},{3,1},{4,6},{5,7},{6,4},{7,5},{8,10},{9,11},{10,... | collective-permute-start | bytes 1622024 | tf_op jit(solution)/shard_map/ppermute | solution.py:847
  86.7 0.5 collective-permute-start.21
  87.2 1.8 %collective-permute-start.22 = (bf16[352,768]{1,0:T(8,128)(2,1)S(1)}, bf16[352,768]{1,0:T(8,128)(2,1)S(1)}, u32[]{:S(2)}, u32[]{:S(2)}) collective-permute-start(bf16[352,768]{1,0:T(8,128)(2,1)S(1)} %get-tuple-element.169), channel_id=1, source_target_pairs={{0,6},{1,7},{2,4},{3,5},{4,2},{5,3},{6,0},{7,1},{8,14},{9,15},{10,... | collective-permute-start | bytes 1622024 | tf_op jit(solution)/shard_map/ppermute | solution.py:847
  89.8 2.7 %collective-permute-start.24 = (bf16[192,768]{1,0:T(8,128)(2,1)S(1)}, bf16[192,768]{1,0:T(8,128)(2,1)S(1)}, u32[]{:S(2)}, u32[]{:S(2)}) collective-permute-start(bf16[192,768]{1,0:T(8,128)(2,1)S(1)} %get-tuple-element.174.z_next), channel_id=1, source_target_pairs={{0,16},{8,24},{16,0},{24,8},{1,17},{9,25},{17,1},{25,9},{2,18},{10... | collective-permute-start | bytes 884744 | tf_op jit(solution)/shard_map/ppermute | solution.py:855
  92.5 11.6 %collective-permute-done.29.came = bf16[2,96,768]{2,1,0:T(8,128)(2,1)S(1)} collective-permute-done((bf16[2,96,768]{2,1,0:T(8,128)(2,1)S(1)}, bf16[2,96,768]{2,1,0:T(8,128)(2,1)S(1)}, u32[]{:S(2)}, u32[]{:S(2)}) %collective-permute-start.29) | collective-permute-done | bytes 294944 | tf_op jit(solution)/shard_map/ppermute | solution.py:855
  104.2 8.5 %collective-permute-done.21.x2 = bf16[352,768]{1,0:T(8,128)(2,1)S(1)} collective-permute-done((bf16[352,768]{1,0:T(8,128)(2,1)S(1)}, bf16[352,768]{1,0:T(8,128)(2,1)S(1)}, u32[]{:S(2)}, u32[]{:S(2)}) %collective-permute-start.21) | collective-permute-done | bytes 540704 | tf_op jit(solution)/shard_map/ppermute | solution.py:847
  112.8 2.7 %collective-permute-start.34 = (bf16[96,768]{1,0:T(8,128)(2,1)S(1)}, bf16[96,768]{1,0:T(8,128)(2,1)S(1)}, u32[]{:S(2)}, u32[]{:S(2)}) collective-permute-start(bf16[96,768]{1,0:T(8,128)(2,1)S(1)} %get-tuple-element.199), channel_id=1, source_target_pairs={{0,16},{8,24},{16,0},{24,8},{1,17},{9,25},{17,1},{25,9},{2,18},{10... | collective-permute-start | bytes 442376 | tf_op jit(solution)/shard_map/ppermute | solution.py:855
  115.7 0.9 collective-permute-start.31
  116.5 0.9 collective-permute-start.32
  117.5 1.8 %collective-permute-start.33 = (bf16[96,768]{1,0:T(8,128)(2,1)S(1)}, bf16[96,768]{1,0:T(8,128)(2,1)S(1)}, u32[]{:S(2)}, u32[]{:S(2)}) collective-permute-start(bf16[96,768]{1,0:T(8,128)(2,1)S(1)} %get-tuple-element.188), channel_id=1, source_target_pairs={{0,6},{1,7},{2,4},{3,5},{4,2},{5,3},{6,0},{7,1},{8,14},{9,15},{10,... | collective-permute-start | bytes 442376 | tf_op jit(solution)/shard_map/ppermute | solution.py:847
  119.2 1.7 %shard_map.268 = bf16[160,767]{1,0:T(8,128)(2,1)} custom-call(bf16[320,768]{1,0:T(8,128)(2,1)S(1)} %get-tuple-element.128.act_keep, bf16[320,768]{1,0:T(8,128)(2,1)S(1)} %get-tuple-element.129.act_send, bf16[3072,767]{1,0:T(8,128)(2,1)S(1)} %bitcast.1, f32[160,767]{1,0:T(8,128)S(1)} %get-tuple-element.130.middle, f32[767]{0:T(1024)S(1)} %copy-done.11), custom_call_target="tpu_custom_call" | custom-call | flops 1000 | bytes 1000 | tf_op jit(solution)/shard_map/pallas_call | solution.py:364
  120.9 2.3 %shard_map.273 = bf16[160,767]{1,0:T(8,128)(2,1)} custom-call(bf16[352,768]{1,0:T(8,128)(2,1)S(1)} %get-tuple-element.166.x0, bf16[352,768]{1,0:T(8,128)(2,1)S(1)} %collective-permute-done.20.x1, bf16[352,768]{1,0:T(8,128)(2,1)S(1)} %collective-permute-done.21.x2, bf16[352,768]{1,0:T(8,128)(2,1)S(1)} %collective-permute-done.22.x3, ...), custom_call_target="tpu_custom_call" | custom-call | flops 1000 | bytes 1000 | tf_op jit(solution)/shard_map/pallas_call | solution.py:364
  123.2 0.7 shard_map.281
  123.9 0.7 collective-permute-done.32.f2
  124.6 1.5 %shard_map.279 = (f32[24,2304]{1,0:T(8,128)}, f32[24,3072]{1,0:T(8,128)}, f32[24,767]{1,0:T(8,128)}, f32[768]{0:T(1024)}, f32[768]{0:T(1024)}, /*index=5*/f32[76...) custom-call(s32[4,2]{1,0:T(4,128)S(1)} %copy.31.lengths, ...), custom_call_target="tpu_custom_call" | custom-call | flops 1000 | bytes 1000 | tf_op jit(solution)/shard_map/pallas_call | solution.py:364
  (82 shorter events, 5.3 us)
Async XLA Ops:
  4.6 8.7 %collective-permute-start = (bf16[240,384]{1,0:T(8,128)(2,1)}, bf16[240,384]{1,0:T(8,128)(2,1)S(1)}, u32[]{:S(2)}, u32[]{:S(2)}) collective-permute-start(bf16[240,384]{1,0:T(8,128)(2,1)} %get-tuple-element.109), channel_id=1, source_target_pairs={{0,2},{1,3},{2,0},{3,1},{4,6},{5,7},{6,4},{7,5},{8,10},{9,11},{10,... | collective-permute-start | bytes 552968 | tf_op jit(solution)/shard_map/ppermute | solution.py:847
  7.6 10.3 %collective-permute-start.1 = (bf16[240,384]{1,0:T(8,128)(2,1)}, bf16[240,384]{1,0:T(8,128)(2,1)S(1)}, u32[]{:S(2)}, u32[]{:S(2)}) collective-permute-start(bf16[240,384]{1,0:T(8,128)(2,1)} %get-tuple-element.110), channel_id=1, source_target_pairs={{0,4},{1,5},{2,6},{3,7},{4,0},{5,1},{6,2},{7,3},{8,12},{9,13},{10,... | collective-permute-start | bytes 552968 | tf_op jit(solution)/shard_map/ppermute | solution.py:847
  9.1 8.7 %collective-permute-start.2 = (bf16[240,384]{1,0:T(8,128)(2,1)}, bf16[240,384]{1,0:T(8,128)(2,1)S(1)}, u32[]{:S(2)}, u32[]{:S(2)}) collective-permute-start(bf16[240,384]{1,0:T(8,128)(2,1)} %get-tuple-element.111), channel_id=1, source_target_pairs={{0,6},{1,7},{2,4},{3,5},{4,2},{5,3},{6,0},{7,1},{8,14},{9,15},{10,... | collective-permute-start | bytes 552968 | tf_op jit(solution)/shard_map/ppermute | solution.py:847
  11.5 10.6 %copy-start.12 = (s32[16]{0:T(128)S(1)}, s32[16]{0:T(128)}, u32[]{:S(2)}) copy-start(s32[16]{0:T(128)} %spans.3) | copy-start | bytes 196
  11.5 10.6 %copy-start.13 = (s32[1,2]{1,0:T(1,128)S(1)}, s32[1,2]{1,0:T(1,128)}, u32[]{:S(2)}) copy-start(s32[1,2]{1,0:T(1,128)} %offsets.3) | copy-start | bytes 28
  18.3 3.7 %collective-permute-start.3 = (bf16[640,384]{1,0:T(8,128)(2,1)S(1)}, bf16[640,384]{1,0:T(8,128)(2,1)S(1)}, u32[]{:S(2)}, u32[]{:S(2)}) collective-permute-start(bf16[640,384]{1,0:T(8,128)(2,1)S(1)} %get-tuple-element.117.own), channel_id=1, source_target_pairs={{0,1},{1,0},{2,3},{3,2},{4,5},{5,4},{6,7},{7,6},{8,9},{9,8},{10,11... | collective-permute-start | bytes 1474568 | tf_op jit(solution)/shard_map/ppermute | solution.py:851
  18.4 12.9 %collective-permute-start.7 = (bf16[160,768]{1,0:T(8,128)(2,1)}, bf16[160,768]{1,0:T(8,128)(2,1)}, u32[]{:S(2)}, u32[]{:S(2)}) collective-permute-start(bf16[160,768]{1,0:T(8,128)(2,1)} %get-tuple-element.122.i0), channel_id=1, source_target_pairs={{0,2},{1,3},{2,0},{3,1},{4,6},{5,7},{6,4},{7,5},{8,10},{9,11},{10,... | collective-permute-start | bytes 737288 | tf_op jit(solution)/shard_map/ppermute | solution.py:847
  19.7 13.0 %collective-permute-start.8 = (bf16[160,768]{1,0:T(8,128)(2,1)}, bf16[160,768]{1,0:T(8,128)(2,1)}, u32[]{:S(2)}, u32[]{:S(2)}) collective-permute-start(bf16[160,768]{1,0:T(8,128)(2,1)} %get-tuple-element.122.i0), channel_id=1, source_target_pairs={{0,4},{1,5},{2,6},{3,7},{4,0},{5,1},{6,2},{7,3},{8,12},{9,13},{10,... | collective-permute-start | bytes 737288 | tf_op jit(solution)/shard_map/ppermute | solution.py:847
  20.5 13.8 %collective-permute-start.9 = (bf16[160,768]{1,0:T(8,128)(2,1)}, bf16[160,768]{1,0:T(8,128)(2,1)}, u32[]{:S(2)}, u32[]{:S(2)}) collective-permute-start(bf16[160,768]{1,0:T(8,128)(2,1)} %get-tuple-element.122.i0), channel_id=1, source_target_pairs={{0,6},{1,7},{2,4},{3,5},{4,2},{5,3},{6,0},{7,1},{8,14},{9,15},{10,... | collective-permute-start | bytes 737288 | tf_op jit(solution)/shard_map/ppermute | solution.py:847
  22.1 14.3 %slice-start.2 = ((s8[4718592]{0:T(1024)(128)(4,1)}), s8[4194304]{0:T(1024)(128)(4,1)S(1)}, s32[]{:S(2)}) async-start(s8[4718592]{0:T(1024)(128)(4,1)} %bitcast.2), calls=%async_computation.2 | async-start | bytes 8388608
  22.1 14.3 %slice-start.3 = ((s8[4718592]{0:T(1024)(128)(4,1)}), s8[524288]{0:T(1024)(128)(4,1)S(1)}, s32[]{:S(2)}) async-start(s8[4718592]{0:T(1024)(128)(4,1)} %bitcast.2), calls=%async_computation.3 | async-start | bytes 1048576
  22.1 14.3 %copy-start.2 = (bf16[160,767]{1,0:T(8,128)(2,1)S(1)}, bf16[160,767]{1,0:T(8,128)(2,1)}, u32[]{:S(2)}) copy-start(bf16[160,767]{1,0:T(8,128)(2,1)} %resid.3) | copy-start | bytes 736324
  22.1 14.3 %copy-start.4 = (bf16[768,767]{1,0:T(8,128)(2,1)S(1)}, bf16[768,767]{1,0:T(8,128)(2,1)}, u32[]{:S(2)}) copy-start(bf16[768,767]{1,0:T(8,128)(2,1)} %out_weight.1) | copy-start | bytes 3534340
  22.1 14.3 %copy-start.6 = (f32[160,1]{1,0:T(8,128)S(1)}, f32[160,1]{1,0:T(8,128)}, u32[]{:S(2)}) copy-start(f32[160,1]{1,0:T(8,128)} %get-tuple-element.127.root_in) | copy-start | bytes 1924
  22.1 14.3 %copy-start.8 = (f32[3072]{0:T(1024)S(1)}, f32[3072]{0:T(1024)}, u32[]{:S(2)}) copy-start(f32[3072]{0:T(1024)} %up_bias.1) | copy-start | bytes 36868
  22.1 14.3 %copy-start.9 = (f32[767]{0:T(1024)S(1)}, f32[767]{0:T(1024)}, u32[]{:S(2)}) copy-start(f32[767]{0:T(1024)} %out_bias.1) | copy-start | bytes 9208
  22.2 14.3 %copy-start.10 = (f32[768]{0:T(1024)S(1)}, f32[768]{0:T(1024)}, u32[]{:S(2)}) copy-start(f32[768]{0:T(1024)} %gain.3) | copy-start | bytes 9220
  29.2 5.1 %collective-permute-start.4 = (bf16[80,384]{1,0:T(8,128)(2,1)S(1)}, bf16[80,384]{1,0:T(8,128)(2,1)S(1)}, u32[]{:S(2)}, u32[]{:S(2)}) collective-permute-start(bf16[80,384]{1,0:T(8,128)(2,1)S(1)} %get-tuple-element.119), channel_id=1, source_target_pairs={{0,2},{1,3},{2,0},{3,1},{4,6},{5,7},{6,4},{7,5},{8,10},{9,11},{10,... | collective-permute-start | bytes 184328 | tf_op jit(solution)/shard_map/ppermute | solution.py:847
  30.5 4.8 %collective-permute-start.5 = (bf16[80,384]{1,0:T(8,128)(2,1)S(1)}, bf16[80,384]{1,0:T(8,128)(2,1)S(1)}, u32[]{:S(2)}, u32[]{:S(2)}) collective-permute-start(bf16[80,384]{1,0:T(8,128)(2,1)S(1)} %get-tuple-element.120), channel_id=1, source_target_pairs={{0,4},{1,5},{2,6},{3,7},{4,0},{5,1},{6,2},{7,3},{8,12},{9,13},{10,... | collective-permute-start | bytes 184328 | tf_op jit(solution)/shard_map/ppermute | solution.py:847
  31.3 5.1 %collective-permute-start.6 = (bf16[80,384]{1,0:T(8,128)(2,1)S(1)}, bf16[80,384]{1,0:T(8,128)(2,1)S(1)}, u32[]{:S(2)}, u32[]{:S(2)}) collective-permute-start(bf16[80,384]{1,0:T(8,128)(2,1)S(1)} %get-tuple-element.121), channel_id=1, source_target_pairs={{0,6},{1,7},{2,4},{3,5},{4,2},{5,3},{6,0},{7,1},{8,14},{9,15},{10,... | collective-permute-start | bytes 184328 | tf_op jit(solution)/shard_map/ppermute | solution.py:847
  32.7 19.0 %collective-permute-start.13 = (bf16[160,767]{1,0:T(8,128)(2,1)S(1)}, bf16[160,767]{1,0:T(8,128)(2,1)S(1)}, u32[]{:S(2)}, u32[]{:S(2)}) collective-permute-start(bf16[160,767]{1,0:T(8,128)(2,1)S(1)} %copy-done.3), channel_id=1, source_target_pairs={{0,8},{8,0},{16,24},{24,16},{1,9},{9,1},{17,25},{25,17},{2,10},{10... | collective-permute-start | bytes 736328 | tf_op jit(solution)/shard_map/ppermute | solution.py:855
  42.6 19.7 %collective-permute-start.14 = (bf16[320,768]{1,0:T(8,128)(2,1)S(1)}, bf16[320,768]{1,0:T(8,128)(2,1)S(1)}, u32[]{:S(2)}, u32[]{:S(2)}) collective-permute-start(bf16[320,768]{1,0:T(8,128)(2,1)S(1)} %get-tuple-element.129.act_send), channel_id=1, source_target_pairs={{0,8},{8,0},{16,24},{24,16},{1,9},{9,1},{17,25},{25,17},{2,10},{10... | collective-permute-start | bytes 1474568 | tf_op jit(solution)/shard_map/ppermute | solution.py:855
  44.2 4.2 %collective-permute-start.10 = (bf16[80,384]{1,0:T(8,128)(2,1)S(1)}, bf16[80,384]{1,0:T(8,128)(2,1)S(1)}, u32[]{:S(2)}, u32[]{:S(2)}) collective-permute-start(bf16[80,384]{1,0:T(8,128)(2,1)S(1)} %get-tuple-element.132), channel_id=1, source_target_pairs={{0,2},{1,3},{2,0},{3,1},{4,6},{5,7},{6,4},{7,5},{8,10},{9,11},{10,... | collective-permute-start | bytes 184328 | tf_op jit(solution)/shard_map/ppermute | solution.py:847
  45.7 4.2 %collective-permute-start.11 = (bf16[80,384]{1,0:T(8,128)(2,1)S(1)}, bf16[80,384]{1,0:T(8,128)(2,1)S(1)}, u32[]{:S(2)}, u32[]{:S(2)}) collective-permute-start(bf16[80,384]{1,0:T(8,128)(2,1)S(1)} %get-tuple-element.133), channel_id=1, source_target_pairs={{0,4},{1,5},{2,6},{3,7},{4,0},{5,1},{6,2},{7,3},{8,12},{9,13},{10,... | collective-permute-start | bytes 184328 | tf_op jit(solution)/shard_map/ppermute | solution.py:847
  46.2 5.5 %collective-permute-start.12 = (bf16[80,384]{1,0:T(8,128)(2,1)S(1)}, bf16[80,384]{1,0:T(8,128)(2,1)S(1)}, u32[]{:S(2)}, u32[]{:S(2)}) collective-permute-start(bf16[80,384]{1,0:T(8,128)(2,1)S(1)} %get-tuple-element.134), channel_id=1, source_target_pairs={{0,6},{1,7},{2,4},{3,5},{4,2},{5,3},{6,0},{7,1},{8,14},{9,15},{10,... | collective-permute-start | bytes 184328 | tf_op jit(solution)/shard_map/ppermute | solution.py:847
  51.7 11.5 %collective-permute-start.17 = (bf16[320,768]{1,0:T(8,128)(2,1)S(1)}, bf16[320,768]{1,0:T(8,128)(2,1)S(1)}, u32[]{:S(2)}, u32[]{:S(2)}) collective-permute-start(bf16[320,768]{1,0:T(8,128)(2,1)S(1)} %get-tuple-element.152), channel_id=1, source_target_pairs={{0,2},{1,3},{2,0},{3,1},{4,6},{5,7},{6,4},{7,5},{8,10},{9,11},{10,... | collective-permute-start | bytes 1474568 | tf_op jit(solution)/shard_map/ppermute | solution.py:847
  53.1 10.1 %collective-permute-start.18 = (bf16[320,768]{1,0:T(8,128)(2,1)S(1)}, bf16[320,768]{1,0:T(8,128)(2,1)S(1)}, u32[]{:S(2)}, u32[]{:S(2)}) collective-permute-start(bf16[320,768]{1,0:T(8,128)(2,1)S(1)} %get-tuple-element.153), channel_id=1, source_target_pairs={{0,4},{1,5},{2,6},{3,7},{4,0},{5,1},{6,2},{7,3},{8,12},{9,13},{10,... | collective-permute-start | bytes 1474568 | tf_op jit(solution)/shard_map/ppermute | solution.py:847
  62.2 1.6 %collective-permute-start.15 = (bf16[320,384]{1,0:T(8,128)(2,1)S(1)}, bf16[320,384]{1,0:T(8,128)(2,1)S(1)}, u32[]{:S(2)}, u32[]{:S(2)}) collective-permute-start(bf16[320,384]{1,0:T(8,128)(2,1)S(1)} %get-tuple-element.146), channel_id=1, source_target_pairs={{0,1},{1,0},{2,3},{3,2},{4,5},{5,4},{6,7},{7,6},{8,9},{9,8},{10,11... | collective-permute-start | bytes 737288 | tf_op jit(solution)/shard_map/ppermute | solution.py:851
  62.3 1.9 %collective-permute-start.16 = (bf16[320,384]{1,0:T(8,128)(2,1)S(1)}, bf16[320,384]{1,0:T(8,128)(2,1)S(1)}, u32[]{:S(2)}, u32[]{:S(2)}) collective-permute-start(bf16[320,384]{1,0:T(8,128)(2,1)S(1)} %get-tuple-element.147), channel_id=1, source_target_pairs={{0,1},{1,0},{2,3},{3,2},{4,5},{5,4},{6,7},{7,6},{8,9},{9,8},{10,11... | collective-permute-start | bytes 737288 | tf_op jit(solution)/shard_map/ppermute | solution.py:851
  68.8 4.5 %collective-permute-start.19 = (bf16[1504,768]{1,0:T(8,128)(2,1)S(1)}, bf16[1504,768]{1,0:T(8,128)(2,1)S(1)}, u32[]{:S(2)}, u32[]{:S(2)}) collective-permute-start(bf16[1504,768]{1,0:T(8,128)(2,1)S(1)} %get-tuple-element.161.send), channel_id=1, source_target_pairs={{0,1},{1,0},{2,3},{3,2},{4,5},{5,4},{6,7},{7,6},{8,9},{9,8},{10,11... | collective-permute-start | bytes 6930440 | tf_op jit(solution)/shard_map/ppermute | solution.py:851
  69.1 14.4 %collective-permute-start.25 = (bf16[320,768]{1,0:T(8,128)(2,1)S(1)}, bf16[320,768]{1,0:T(8,128)(2,1)S(1)}, u32[]{:S(2)}, u32[]{:S(2)}) collective-permute-start(bf16[320,768]{1,0:T(8,128)(2,1)S(1)} %get-tuple-element.176), channel_id=1, source_target_pairs={{0,6},{1,7},{2,4},{3,5},{4,2},{5,3},{6,0},{7,1},{8,14},{9,15},{10,... | collective-permute-start | bytes 1474568 | tf_op jit(solution)/shard_map/ppermute | solution.py:847
  73.4 45.8 %slice-start = ((s8[4718592]{0:T(1024)(128)(4,1)}), s8[524288]{0:T(1024)(128)(4,1)S(1)}, s32[]{:S(2)}) async-start(s8[4718592]{0:T(1024)(128)(4,1)} %bitcast), calls=%async_computation | async-start | bytes 1048576
  74.0 45.2 %slice-start.1 = ((s8[4718592]{0:T(1024)(128)(4,1)}), s8[4194304]{0:T(1024)(128)(4,1)S(1)}, s32[]{:S(2)}) async-start(s8[4718592]{0:T(1024)(128)(4,1)} %bitcast), calls=%async_computation.1 | async-start | bytes 8388608
  74.0 15.7 %collective-permute-start.23 = (bf16[368,768]{1,0:T(8,128)(2,1)S(1)}, bf16[368,768]{1,0:T(8,128)(2,1)S(1)}, u32[]{:S(2)}, u32[]{:S(2)}) collective-permute-start(bf16[368,768]{1,0:T(8,128)(2,1)S(1)} %get-tuple-element.172.z_send), channel_id=1, source_target_pairs={{0,8},{8,0},{16,24},{24,16},{1,9},{9,1},{17,25},{25,17},{2,10},{10... | collective-permute-start | bytes 1695752 | tf_op jit(solution)/shard_map/ppermute | solution.py:855
  84.6 2.1 %collective-permute-start.26 = (bf16[128,768]{1,0:T(8,128)(2,1)S(1)}, bf16[128,768]{1,0:T(8,128)(2,1)S(1)}, u32[]{:S(2)}, u32[]{:S(2)}) collective-permute-start(bf16[128,768]{1,0:T(8,128)(2,1)S(1)} %get-tuple-element.178), channel_id=1, source_target_pairs={{0,1},{1,0},{2,3},{3,2},{4,5},{5,4},{6,7},{7,6},{8,9},{9,8},{10,11... | collective-permute-start | bytes 589832 | tf_op jit(solution)/shard_map/ppermute | solution.py:851
  84.7 2.5 %collective-permute-start.27 = (bf16[128,768]{1,0:T(8,128)(2,1)S(1)}, bf16[128,768]{1,0:T(8,128)(2,1)S(1)}, u32[]{:S(2)}, u32[]{:S(2)}) collective-permute-start(bf16[128,768]{1,0:T(8,128)(2,1)S(1)} %get-tuple-element.179), channel_id=1, source_target_pairs={{0,1},{1,0},{2,3},{3,2},{4,5},{5,4},{6,7},{7,6},{8,9},{9,8},{10,11... | collective-permute-start | bytes 589832 | tf_op jit(solution)/shard_map/ppermute | solution.py:851
  85.2 3.8 %collective-permute-start.28 = (bf16[128,768]{1,0:T(8,128)(2,1)S(1)}, bf16[128,768]{1,0:T(8,128)(2,1)S(1)}, u32[]{:S(2)}, u32[]{:S(2)}) collective-permute-start(bf16[128,768]{1,0:T(8,128)(2,1)S(1)} %get-tuple-element.180), channel_id=1, source_target_pairs={{0,1},{1,0},{2,3},{3,2},{4,5},{5,4},{6,7},{7,6},{8,9},{9,8},{10,11... | collective-permute-start | bytes 589832 | tf_op jit(solution)/shard_map/ppermute | solution.py:851
  85.3 18.9 %collective-permute-start.20 = (bf16[352,768]{1,0:T(8,128)(2,1)S(1)}, bf16[352,768]{1,0:T(8,128)(2,1)S(1)}, u32[]{:S(2)}, u32[]{:S(2)}) collective-permute-start(bf16[352,768]{1,0:T(8,128)(2,1)S(1)} %get-tuple-element.167), channel_id=1, source_target_pairs={{0,2},{1,3},{2,0},{3,1},{4,6},{5,7},{6,4},{7,5},{8,10},{9,11},{10,... | collective-permute-start | bytes 1622024 | tf_op jit(solution)/shard_map/ppermute | solution.py:847
  86.7 25.9 %collective-permute-start.21 = (bf16[352,768]{1,0:T(8,128)(2,1)S(1)}, bf16[352,768]{1,0:T(8,128)(2,1)S(1)}, u32[]{:S(2)}, u32[]{:S(2)}) collective-permute-start(bf16[352,768]{1,0:T(8,128)(2,1)S(1)} %get-tuple-element.168), channel_id=1, source_target_pairs={{0,4},{1,5},{2,6},{3,7},{4,0},{5,1},{6,2},{7,3},{8,12},{9,13},{10,... | collective-permute-start | bytes 1622024 | tf_op jit(solution)/shard_map/ppermute | solution.py:847
  87.2 25.4 %collective-permute-start.22 = (bf16[352,768]{1,0:T(8,128)(2,1)S(1)}, bf16[352,768]{1,0:T(8,128)(2,1)S(1)}, u32[]{:S(2)}, u32[]{:S(2)}) collective-permute-start(bf16[352,768]{1,0:T(8,128)(2,1)S(1)} %get-tuple-element.169), channel_id=1, source_target_pairs={{0,6},{1,7},{2,4},{3,5},{4,2},{5,3},{6,0},{7,1},{8,14},{9,15},{10,... | collective-permute-start | bytes 1622024 | tf_op jit(solution)/shard_map/ppermute | solution.py:847
  89.2 14.9 %collective-permute-start.29 = (bf16[2,96,768]{2,1,0:T(8,128)(2,1)S(1)}, bf16[2,96,768]{2,1,0:T(8,128)(2,1)S(1)}, u32[]{:S(2)}, u32[]{:S(2)}) collective-permute-start(bf16[2,96,768]{2,1,0:T(8,128)(2,1)S(1)} %get-tuple-element.182), channel_id=1, source_target_pairs={{0,8},{8,0},{16,24},{24,16},{1,9},{9,1},{17,25},{25,17},{2,10},{10... | collective-permute-start | bytes 884744 | tf_op jit(solution)/shard_map/ppermute | solution.py:855
  89.8 29.4 %copy-start.11 = (f32[767]{0:T(1024)S(1)}, f32[767]{0:T(1024)}, u32[]{:S(2)}) copy-start(f32[767]{0:T(1024)} %bias.1) | copy-start | bytes 9208
  89.8 25.7 %collective-permute-start.24 = (bf16[192,768]{1,0:T(8,128)(2,1)S(1)}, bf16[192,768]{1,0:T(8,128)(2,1)S(1)}, u32[]{:S(2)}, u32[]{:S(2)}) collective-permute-start(bf16[192,768]{1,0:T(8,128)(2,1)S(1)} %get-tuple-element.174.z_next), channel_id=1, source_target_pairs={{0,16},{8,24},{16,0},{24,8},{1,17},{9,25},{17,1},{25,9},{2,18},{10... | collective-permute-start | bytes 884744 | tf_op jit(solution)/shard_map/ppermute | solution.py:855
  104.1 11.4 %collective-permute-start.30 = (bf16[96,768]{1,0:T(8,128)(2,1)S(1)}, bf16[96,768]{1,0:T(8,128)(2,1)S(1)}, u32[]{:S(2)}, u32[]{:S(2)}) collective-permute-start(bf16[96,768]{1,0:T(8,128)(2,1)S(1)} %get-tuple-element.184), channel_id=1, source_target_pairs={{0,16},{8,24},{16,0},{24,8},{1,17},{9,25},{17,1},{25,9},{2,18},{10... | collective-permute-start | bytes 442376 | tf_op jit(solution)/shard_map/ppermute | solution.py:855
  112.8 10.4 %collective-permute-start.34 = (bf16[96,768]{1,0:T(8,128)(2,1)S(1)}, bf16[96,768]{1,0:T(8,128)(2,1)S(1)}, u32[]{:S(2)}, u32[]{:S(2)}) collective-permute-start(bf16[96,768]{1,0:T(8,128)(2,1)S(1)} %get-tuple-element.199), channel_id=1, source_target_pairs={{0,16},{8,24},{16,0},{24,8},{1,17},{9,25},{17,1},{25,9},{2,18},{10... | collective-permute-start | bytes 442376 | tf_op jit(solution)/shard_map/ppermute | solution.py:855
  115.7 8.3 %collective-permute-start.31 = (bf16[96,768]{1,0:T(8,128)(2,1)S(1)}, bf16[96,768]{1,0:T(8,128)(2,1)S(1)}, u32[]{:S(2)}, u32[]{:S(2)}) collective-permute-start(bf16[96,768]{1,0:T(8,128)(2,1)S(1)} %get-tuple-element.186), channel_id=1, source_target_pairs={{0,2},{1,3},{2,0},{3,1},{4,6},{5,7},{6,4},{7,5},{8,10},{9,11},{10,... | collective-permute-start | bytes 442376 | tf_op jit(solution)/shard_map/ppermute | solution.py:847
  116.5 8.1 %collective-permute-start.32 = (bf16[96,768]{1,0:T(8,128)(2,1)S(1)}, bf16[96,768]{1,0:T(8,128)(2,1)S(1)}, u32[]{:S(2)}, u32[]{:S(2)}) collective-permute-start(bf16[96,768]{1,0:T(8,128)(2,1)S(1)} %get-tuple-element.187), channel_id=1, source_target_pairs={{0,4},{1,5},{2,6},{3,7},{4,0},{5,1},{6,2},{7,3},{8,12},{9,13},{10,... | collective-permute-start | bytes 442376 | tf_op jit(solution)/shard_map/ppermute | solution.py:847
  117.5 7.2 %collective-permute-start.33 = (bf16[96,768]{1,0:T(8,128)(2,1)S(1)}, bf16[96,768]{1,0:T(8,128)(2,1)S(1)}, u32[]{:S(2)}, u32[]{:S(2)}) collective-permute-start(bf16[96,768]{1,0:T(8,128)(2,1)S(1)} %get-tuple-element.188), channel_id=1, source_target_pairs={{0,6},{1,7},{2,4},{3,5},{4,2},{5,3},{6,0},{7,1},{8,14},{9,15},{10,... | collective-permute-start | bytes 442376 | tf_op jit(solution)/shard_map/ppermute | solution.py:847
  (6 other events, 38.4 us)

commit v4 on v3

--- a/solution.py
+++ b/solution.py
@@ -489,7 +489,7 @@
 
 
 def forward_kernel(
-    spans, offsets, lengths, query, own, sib, chance, attended, b0, b1, b2, b3, keys, vals, scores
+    spans, offsets, lengths, query, own, sib, chance, attended, b0, b1, b2, b3, keys, vals, scores, lows, highs
 ):
     me, bucket, core = here()
     keys[:640, :] = own[:, :SPLIT]
@@ -503,12 +503,17 @@
         chip = ((blk % 8) // 2) ^ me
         span = spans[chip * 4 + (core ^ (blk // 8)) * 2 + blk % 2]
         place = jnp.where((lane >= blk * 80) & (lane < (blk + 1) * 80), lane + (span - blk) * 80, place)
+    for blk in range(8):
+        rows = slice(blk * 80, (blk + 1) * 80)
+        lo, hi = limits(spans, offsets, lengths, bucket, (blk // 2) ^ me, core, blk % 2)
+        lows[rows, :] = lo
+        highs[rows, :] = hi
     q = query[...].astype(wide)
     for h in range(3):
         scores[...] = nt(head_mask(q, h).astype(low), keys[...])
         for blk in range(8):
             rows = slice(blk * 80, (blk + 1) * 80)
-            lo, hi = limits(spans, offsets, lengths, bucket, (blk // 2) ^ me, core, blk % 2)
+            lo, hi = lows[rows, :], highs[rows, :]
             s = jnp.where((place >= lo) & (place <= hi), scores[rows, :], masked_value)
             peak = jnp.max(s, axis=1, keepdims=True)
             w = jnp.exp(s - peak)
@@ -596,7 +601,8 @@
 
 
 def backward_kernel(
-    d0, d1, d2, d3, query, own, sib, chance, attended, query_grad, both_grad, away_one, away_two, keys, vals, grads, slopes
+    d0, d1, d2, d3, query, own, sib, chance, attended, query_grad, both_grad, away_one, away_two,
+    keys, vals, grads, slopes, keys_turned, vals_turned, pushes,
 ):
     for r, d in enumerate((d0, d1, d2, d3)):
         grads[r * 160 : (r + 1) * 160, :] = unpacked(d[...]).astype(low)
@@ -605,23 +611,24 @@
         keys[h] = head_mask(k, h).astype(low)
     vals[:640, :] = own[:, SPLIT:].astype(wide).astype(low)
     vals[640:, :] = sib[:, SPLIT:].astype(wide).astype(low)
+    g = grads[...].astype(wide)
+    q_turned = jnp.transpose(query[...].astype(wide)).astype(low)
+    g_turned = jnp.transpose(g).astype(low)
     dq = jnp.zeros((640, SPLIT), wide)
-    dk = jnp.zeros((1280, SPLIT), wide)
-    dv = jnp.zeros((1280, SPLIT), wide)
-    g = grads[...].astype(wide)
-    q = query[...].astype(wide)
     for h in range(3):
         gh = head_mask(g, h)
-        gl = gh.astype(low)
         delta = jnp.sum(gh * attended[...], axis=1, keepdims=True)
-        for r in range(4):
-            rows = slice(r * 160, (r + 1) * 160)
-            push = nt(gl[rows, :], vals[...])
-            slopes[rows, :] = (chance[h, rows, :].astype(wide) * (push - delta[rows, :])).astype(low)
+        pushes[...] = nt(gh.astype(low), vals[...])
+        for r in range(8):
+            rows = slice(r * 80, (r + 1) * 80)
+            slopes[rows, :] = (chance[h, rows, :].astype(wide) * (pushes[rows, :] - delta[rows, :])).astype(low)
         dq = dq + jnp.dot(slopes[...], keys[h], preferred_element_type=wide)
-        dk = dk + tn(slopes[...], head_mask(q, h).astype(low))
-        dv = dv + tn(chance[h], gl)
+        rows = slice(h * 64, (h + 1) * 64)
+        keys_turned[rows, :] = jnp.dot(q_turned[rows], slopes[...], preferred_element_type=wide)
+        vals_turned[rows, :] = jnp.dot(g_turned[rows], chance[h], preferred_element_type=wide)
     query_grad[...] = (dq * 0.125).astype(low)
+    dk = jnp.transpose(keys_turned[...])
+    dv = jnp.transpose(vals_turned[...])
     both_grad[:, :SPLIT] = dk[:640]
     both_grad[:, SPLIT:] = dv[:640]
     away_one[:, :SPLIT] = dk[640:960].astype(low)
@@ -912,7 +919,8 @@
         forward_kernel,
         [((3, 640, 1280), low), ((640, SPLIT), wide)] + [backed] * 4,
         where + [query, own_both, sib_both],
-        [pltpu.VMEM((1280, SPLIT), low), pltpu.VMEM((3, 1280, SPLIT), low), pltpu.VMEM((640, 1280), wide)],
+        [pltpu.VMEM((1280, SPLIT), low), pltpu.VMEM((3, 1280, SPLIT), low), pltpu.VMEM((640, 1280), wide)]
+        + [pltpu.VMEM((640, 1), jnp.int32)] * 2,
         small=3,
         work=7,
     )
@@ -954,6 +962,9 @@
             pltpu.VMEM((1280, SPLIT), low),
             pltpu.VMEM((640, SPLIT), low),
             pltpu.VMEM((640, 1280), low),
+            pltpu.VMEM((SPLIT, 1280), wide),
+            pltpu.VMEM((SPLIT, 1280), wide),
+            pltpu.VMEM((640, 1280), wide),
         ],
     )
     arrived = [swap_core(x) for x in after(away, act_came)]

time: 127 us -> 124 us (0.976)
  Pallas kernels: 41 us -> 38.4 us
    pallas_call x19, Pallas kernels: 41 us -> 38.4 us  [call(): pl.pallas_call(kernel, out_shape=shapes, in_specs=[SMEM if i < small else...]
    ppermute x7, waiting for transfers between devices: 4.04 us -> 2.53 us  [swap_core(): return lax.ppermute(block, 'blk', [(k, k ^ 1) for k in range(8)])]
    ppermute x21, waiting for transfers between devices: 29 us -> 30.4 us  [swap_chip(): return lax.ppermute(block, 'blk', [(k, k ^ 2 * step) for k in range(8)])]
  transfers between devices with their start and end apart: 35 -> 35, of which waited for: 14 -> 15; matrix products, arithmetic and copies ran while one was open for 0% -> 0% of each run, Pallas kernels for 24% -> 22%
where the time goes in v4:
time: 124 us
  waiting for transfers between devices  44.5 us (36%)
  Pallas kernels  38.4 us (31%)
  starting transfers between devices  37.4 us (30%)
  local copies, waits for them, and re-layouts  2.52 us (2%)
    pallas_call x19, Pallas kernels, call(): pl.pallas_call(kernel, out_shape=shapes, in_specs=[SMEM if i < small else...  38.4 us
    ppermute x21, waiting for transfers between devices, swap_chip(): return lax.ppermute(block, 'blk', [(k, k ^ 2 * step) for k in range(8)])  30.4 us
    ppermute x21, starting transfers between devices, swap_chip(): return lax.ppermute(block, 'blk', [(k, k ^ 2 * step) for k in range(8)])  26.4 us
    ppermute x7, waiting for transfers between devices, shift_bucket(): return lax.ppermute(block, 'bucket', [(b, b ^ step) for b in range(4)])  11.6 us
    ppermute x7, starting transfers between devices, shift_bucket(): return lax.ppermute(block, 'bucket', [(b, b ^ step) for b in range(4)])  9.62 us
    ppermute x7, waiting for transfers between devices, swap_core(): return lax.ppermute(block, 'blk', [(k, k ^ 1) for k in range(8)])  2.53 us
    unnamed x39, local copies, waits for them, and re-layouts  2.52 us
  transfers between devices with their start and end apart: 35, of which 15 were waited for; matrix products, arithmetic and copies ran while one was open for 0% of the time, Pallas kernels for 22%

profile of v4, /device:TPU:0, one launch (start us, length us, event | category | flops | bytes accessed | tf_op | source)
XLA Modules:
  0.0 123.9 jit_solution(15103329224628487548)
XLA Ops:
  0.7 4.0 %shard_map.263 = (bf16[240,384]{1,0:T(8,128)(2,1)}, bf16[240,384]{1,0:T(8,128)(2,1)}, bf16[240,384]{1,0:T(8,128)(2,1)}, bf16[240,384]{1,0:T(8,128)(2,1)}, bf16[160,768]{1,0:T(8,128)(2,1)}, /*index=5*/f32[160,1]{1,0:T(8,128)}) custom-call(bf16[160,767]{1,0:T(8,128)(2,1)} %resid.3, f32[768]{0:T(1024)} %gain.5, bf16[768,2304]{1,0:T(8,128)(2,1)} %weight.6, ...), custom_call_target="tpu_custom_call" | custom-call | flops 1000 | bytes 1000 | tf_op jit(solution)/shard_map/pallas_call | solution.py:364
  4.6 3.0 %collective-permute-start = (bf16[240,384]{1,0:T(8,128)(2,1)}, bf16[240,384]{1,0:T(8,128)(2,1)S(1)}, u32[]{:S(2)}, u32[]{:S(2)}) collective-permute-start(bf16[240,384]{1,0:T(8,128)(2,1)} %get-tuple-element.109), channel_id=1, source_target_pairs={{0,2},{1,3},{2,0},{3,1},{4,6},{5,7},{6,4},{7,5},{8,10},{9,11},{10,... | collective-permute-start | bytes 552968 | tf_op jit(solution)/shard_map/ppermute | solution.py:854
  7.6 1.5 %collective-permute-start.1 = (bf16[240,384]{1,0:T(8,128)(2,1)}, bf16[240,384]{1,0:T(8,128)(2,1)S(1)}, u32[]{:S(2)}, u32[]{:S(2)}) collective-permute-start(bf16[240,384]{1,0:T(8,128)(2,1)} %get-tuple-element.110), channel_id=1, source_target_pairs={{0,4},{1,5},{2,6},{3,7},{4,0},{5,1},{6,2},{7,3},{8,12},{9,13},{10,... | collective-permute-start | bytes 552968 | tf_op jit(solution)/shard_map/ppermute | solution.py:854
  9.2 2.3 %copy-done.1 = bf16[3072,767]{1,0:T(8,128)(2,1)S(1)} copy-done((bf16[3072,767]{1,0:T(8,128)(2,1)S(1)}, bf16[3072,767]{1,0:T(8,128)(2,1)}, u32[]{:S(2)}) %copy-start.1) | copy-done | bytes 4712472
  11.5 1.7 %shard_map.264.push = f32[160,3072]{1,0:T(8,128)S(1)} custom-call(bf16[160,767]{1,0:T(8,128)(2,1)S(1)} %copy-done.3, bf16[3072,767]{1,0:T(8,128)(2,1)S(1)} %copy-done.1), custom_call_target="tpu_custom_call" | custom-call | flops 1000 | bytes 1000 | tf_op jit(solution)/shard_map/pallas_call | solution.py:364
  13.3 4.6 %collective-permute-done.1.p2 = bf16[240,384]{1,0:T(8,128)(2,1)S(1)} collective-permute-done((bf16[240,384]{1,0:T(8,128)(2,1)}, bf16[240,384]{1,0:T(8,128)(2,1)S(1)}, u32[]{:S(2)}, u32[]{:S(2)}) %collective-permute-start.1) | collective-permute-done | bytes 184352 | tf_op jit(solution)/shard_map/ppermute | solution.py:854
  18.4 1.3 %collective-permute-start.7 = (bf16[160,768]{1,0:T(8,128)(2,1)}, bf16[160,768]{1,0:T(8,128)(2,1)}, u32[]{:S(2)}, u32[]{:S(2)}) collective-permute-start(bf16[160,768]{1,0:T(8,128)(2,1)} %get-tuple-element.122.i0), channel_id=1, source_target_pairs={{0,2},{1,3},{2,0},{3,1},{4,6},{5,7},{6,4},{7,5},{8,10},{9,11},{10,... | collective-permute-start | bytes 737288 | tf_op jit(solution)/shard_map/ppermute | solution.py:854
  19.7 0.8 collective-permute-start.8
  20.5 1.4 %collective-permute-start.9 = (bf16[160,768]{1,0:T(8,128)(2,1)}, bf16[160,768]{1,0:T(8,128)(2,1)}, u32[]{:S(2)}, u32[]{:S(2)}) collective-permute-start(bf16[160,768]{1,0:T(8,128)(2,1)} %get-tuple-element.122.i0), channel_id=1, source_target_pairs={{0,6},{1,7},{2,4},{3,5},{4,2},{5,3},{6,0},{7,1},{8,14},{9,15},{10,... | collective-permute-start | bytes 737288 | tf_op jit(solution)/shard_map/ppermute | solution.py:854
  22.2 6.9 %shard_map.266 = (bf16[3,640,1280]{2,1,0:T(8,128)(2,1)S(1)}, f32[640,192]{1,0:T(8,128)S(1)}, bf16[80,384]{1,0:T(8,128)(2,1)S(1)}, bf16[80,384]{1,0:T(8,128)(2,1)...) custom-call(s32[16]{0:T(128)S(1)} %copy-done.12, s32[1,2]{1,0:T(1,128)S(1)} %copy-done.13, ...), custom_call_target="tpu_custom_call" | custom-call | flops 7700000768 | bytes 1000 | tf_op jit(solution)/shard_map/pallas_call | solution.py:364
  29.1 1.3 %collective-permute-start.4 = (bf16[80,384]{1,0:T(8,128)(2,1)S(1)}, bf16[80,384]{1,0:T(8,128)(2,1)S(1)}, u32[]{:S(2)}, u32[]{:S(2)}) collective-permute-start(bf16[80,384]{1,0:T(8,128)(2,1)S(1)} %get-tuple-element.119), channel_id=1, source_target_pairs={{0,2},{1,3},{2,0},{3,1},{4,6},{5,7},{6,4},{7,5},{8,10},{9,11},{10,... | collective-permute-start | bytes 184328 | tf_op jit(solution)/shard_map/ppermute | solution.py:854
  30.4 0.8 collective-permute-start.5
  31.2 1.4 %collective-permute-start.6 = (bf16[80,384]{1,0:T(8,128)(2,1)S(1)}, bf16[80,384]{1,0:T(8,128)(2,1)S(1)}, u32[]{:S(2)}, u32[]{:S(2)}) collective-permute-start(bf16[80,384]{1,0:T(8,128)(2,1)S(1)} %get-tuple-element.121), channel_id=1, source_target_pairs={{0,6},{1,7},{2,4},{3,5},{4,2},{5,3},{6,0},{7,1},{8,14},{9,15},{10,... | collective-permute-start | bytes 184328 | tf_op jit(solution)/shard_map/ppermute | solution.py:854
  32.6 1.6 %collective-permute-start.13 = (bf16[160,767]{1,0:T(8,128)(2,1)S(1)}, bf16[160,767]{1,0:T(8,128)(2,1)S(1)}, u32[]{:S(2)}, u32[]{:S(2)}) collective-permute-start(bf16[160,767]{1,0:T(8,128)(2,1)S(1)} %copy-done.3), channel_id=1, source_target_pairs={{0,8},{8,0},{16,24},{24,16},{1,9},{9,1},{17,25},{25,17},{2,10},{10... | collective-permute-start | bytes 736328 | tf_op jit(solution)/shard_map/ppermute | solution.py:862
  34.2 1.0 collective-permute-done.5.p2
  35.3 1.1 collective-permute-done.6.p3
  36.4 6.0 %shard_map.267 = (bf16[80,384]{1,0:T(8,128)(2,1)S(1)}, bf16[80,384]{1,0:T(8,128)(2,1)S(1)}, bf16[80,384]{1,0:T(8,128)(2,1)S(1)}, bf16[80,384]{1,0:T(8,128)(2,1)S...) custom-call(s32[16]{0:T(128)S(1)} %copy-done.12, ...), custom_call_target="tpu_custom_call" | custom-call | flops 1000 | bytes 1000 | tf_op jit(solution)/shard_map/pallas_call | solution.py:364
  42.4 1.6 %collective-permute-start.14 = (bf16[320,768]{1,0:T(8,128)(2,1)S(1)}, bf16[320,768]{1,0:T(8,128)(2,1)S(1)}, u32[]{:S(2)}, u32[]{:S(2)}) collective-permute-start(bf16[320,768]{1,0:T(8,128)(2,1)S(1)} %get-tuple-element.129.act_send), channel_id=1, source_target_pairs={{0,8},{8,0},{16,24},{24,16},{1,9},{9,1},{17,25},{25,17},{2,10},{10... | collective-permute-start | bytes 1474568 | tf_op jit(solution)/shard_map/ppermute | solution.py:862
  44.1 1.5 %collective-permute-start.10 = (bf16[80,384]{1,0:T(8,128)(2,1)S(1)}, bf16[80,384]{1,0:T(8,128)(2,1)S(1)}, u32[]{:S(2)}, u32[]{:S(2)}) collective-permute-start(bf16[80,384]{1,0:T(8,128)(2,1)S(1)} %get-tuple-element.132), channel_id=1, source_target_pairs={{0,2},{1,3},{2,0},{3,1},{4,6},{5,7},{6,4},{7,5},{8,10},{9,11},{10,... | collective-permute-start | bytes 184328 | tf_op jit(solution)/shard_map/ppermute | solution.py:854
  46.1 1.5 %collective-permute-start.12 = (bf16[80,384]{1,0:T(8,128)(2,1)S(1)}, bf16[80,384]{1,0:T(8,128)(2,1)S(1)}, u32[]{:S(2)}, u32[]{:S(2)}) collective-permute-start(bf16[80,384]{1,0:T(8,128)(2,1)S(1)} %get-tuple-element.134), channel_id=1, source_target_pairs={{0,6},{1,7},{2,4},{3,5},{4,2},{5,3},{6,0},{7,1},{8,14},{9,15},{10,... | collective-permute-start | bytes 184328 | tf_op jit(solution)/shard_map/ppermute | solution.py:854
  47.6 0.7 collective-permute-done.10.d1
  48.3 1.5 %collective-permute-done.11.d2 = bf16[80,384]{1,0:T(8,128)(2,1)S(1)} collective-permute-done((bf16[80,384]{1,0:T(8,128)(2,1)S(1)}, bf16[80,384]{1,0:T(8,128)(2,1)S(1)}, u32[]{:S(2)}, u32[]{:S(2)}) %collective-permute-start.11) | collective-permute-done | bytes 61472 | tf_op jit(solution)/shard_map/ppermute | solution.py:854
  49.8 1.9 %collective-permute-done.12.d3 = bf16[80,384]{1,0:T(8,128)(2,1)S(1)} collective-permute-done((bf16[80,384]{1,0:T(8,128)(2,1)S(1)}, bf16[80,384]{1,0:T(8,128)(2,1)S(1)}, u32[]{:S(2)}, u32[]{:S(2)}) %collective-permute-start.12) | collective-permute-done | bytes 61472 | tf_op jit(solution)/shard_map/ppermute | solution.py:854
  51.6 1.2 collective-permute-start.17
  52.8 1.0 collective-permute-start.18
  53.9 5.6 %shard_map.269 = (bf16[640,192]{1,0:T(8,128)(2,1)S(1)}, f32[640,384]{1,0:T(8,128)S(1)}, bf16[320,384]{1,0:T(8,128)(2,1)S(1)}, bf16[320,384]{1,0:T(8,128)(2,1)S(1)}) custom-call(bf16[80,384]{1,0:T(8,128)(2,1)S(1)} %get-tuple-element.136.d0, bf16[80,384]{1,0:T(8,128)(2,1)S(1)} %collective-permute-done.10.d1, bf16[80,384]{1,0:T(8,128)(2,1)S(1)} %collective-permute-done.11.d2, ...), custom_call_target="tpu_custom_call" | custom-call | flops 1000 | bytes 1000 | tf_op jit(solution)/shard_map/pallas_call | solution.py:364
  60.5 1.0 collective-permute-done.17.n1
  61.8 4.7 %shard_map.271 = (bf16[240,384]{1,0:T(8,128)(2,1)S(1)}, bf16[240,384]{1,0:T(8,128)(2,1)S(1)}, bf16[240,384]{1,0:T(8,128)(2,1)S(1)}, bf16[240,384]{1,0:T(8,128)(2...) custom-call(bf16[640,192]{1,0:T(8,128)(2,1)S(1)} %get-tuple-element.142.query_g, ...), custom_call_target="tpu_custom_call" | custom-call | flops 1000 | bytes 1000 | tf_op jit(solution)/shard_map/pallas_call | solution.py:364
  66.6 1.9 %collective-permute-start.25 = (bf16[320,768]{1,0:T(8,128)(2,1)S(1)}, bf16[320,768]{1,0:T(8,128)(2,1)S(1)}, u32[]{:S(2)}, u32[]{:S(2)}) collective-permute-start(bf16[320,768]{1,0:T(8,128)(2,1)S(1)} %get-tuple-element.176), channel_id=1, source_target_pairs={{0,6},{1,7},{2,4},{3,5},{4,2},{5,3},{6,0},{7,1},{8,14},{9,15},{10,... | collective-permute-start | bytes 1474568 | tf_op jit(solution)/shard_map/ppermute | solution.py:854
  68.5 2.5 %collective-permute-done.19.arrived = bf16[1504,768]{1,0:T(8,128)(2,1)S(1)} collective-permute-done((bf16[1504,768]{1,0:T(8,128)(2,1)S(1)}, bf16[1504,768]{1,0:T(8,128)(2,1)S(1)}, u32[]{:S(2)}, u32[]{:S(2)}) %collective-permute-start.19) | collective-permute-done | bytes 2310176 | tf_op jit(solution)/shard_map/ppermute | solution.py:858
  72.2 8.9 %collective-permute-done.25.n3 = bf16[320,768]{1,0:T(8,128)(2,1)S(1)} collective-permute-done((bf16[320,768]{1,0:T(8,128)(2,1)S(1)}, bf16[320,768]{1,0:T(8,128)(2,1)S(1)}, u32[]{:S(2)}, u32[]{:S(2)}) %collective-permute-start.25) | collective-permute-done | bytes 491552 | tf_op jit(solution)/shard_map/ppermute | solution.py:854
  81.1 1.2 shard_map.275
  83.0 1.2 collective-permute-start.20
  84.2 1.2 collective-permute-start.21
  85.4 1.1 collective-permute-start.22
  87.3 2.7 %collective-permute-start.24 = (bf16[192,768]{1,0:T(8,128)(2,1)S(1)}, bf16[192,768]{1,0:T(8,128)(2,1)S(1)}, u32[]{:S(2)}, u32[]{:S(2)}) collective-permute-start(bf16[192,768]{1,0:T(8,128)(2,1)S(1)} %get-tuple-element.174.z_next), channel_id=1, source_target_pairs={{0,16},{8,24},{16,0},{24,8},{1,17},{9,25},{17,1},{25,9},{2,18},{10... | collective-permute-start | bytes 884744 | tf_op jit(solution)/shard_map/ppermute | solution.py:862
  89.9 11.6 %collective-permute-done.29.came = bf16[2,96,768]{2,1,0:T(8,128)(2,1)S(1)} collective-permute-done((bf16[2,96,768]{2,1,0:T(8,128)(2,1)S(1)}, bf16[2,96,768]{2,1,0:T(8,128)(2,1)S(1)}, u32[]{:S(2)}, u32[]{:S(2)}) %collective-permute-start.29) | collective-permute-done | bytes 294944 | tf_op jit(solution)/shard_map/ppermute | solution.py:862
  101.7 7.2 %collective-permute-done.21.x2 = bf16[352,768]{1,0:T(8,128)(2,1)S(1)} collective-permute-done((bf16[352,768]{1,0:T(8,128)(2,1)S(1)}, bf16[352,768]{1,0:T(8,128)(2,1)S(1)}, u32[]{:S(2)}, u32[]{:S(2)}) %collective-permute-start.21) | collective-permute-done | bytes 540704 | tf_op jit(solution)/shard_map/ppermute | solution.py:854
  108.9 1.3 %collective-permute-done.22.x3 = bf16[352,768]{1,0:T(8,128)(2,1)S(1)} collective-permute-done((bf16[352,768]{1,0:T(8,128)(2,1)S(1)}, bf16[352,768]{1,0:T(8,128)(2,1)S(1)}, u32[]{:S(2)}, u32[]{:S(2)}) %collective-permute-start.22) | collective-permute-done | bytes 540704 | tf_op jit(solution)/shard_map/ppermute | solution.py:854
  110.3 2.7 %collective-permute-start.34 = (bf16[96,768]{1,0:T(8,128)(2,1)S(1)}, bf16[96,768]{1,0:T(8,128)(2,1)S(1)}, u32[]{:S(2)}, u32[]{:S(2)}) collective-permute-start(bf16[96,768]{1,0:T(8,128)(2,1)S(1)} %get-tuple-element.199), channel_id=1, source_target_pairs={{0,16},{8,24},{16,0},{24,8},{1,17},{9,25},{17,1},{25,9},{2,18},{10... | collective-permute-start | bytes 442376 | tf_op jit(solution)/shard_map/ppermute | solution.py:862
  113.2 0.9 collective-permute-start.31
  114.1 1.4 %collective-permute-start.32 = (bf16[96,768]{1,0:T(8,128)(2,1)S(1)}, bf16[96,768]{1,0:T(8,128)(2,1)S(1)}, u32[]{:S(2)}, u32[]{:S(2)}) collective-permute-start(bf16[96,768]{1,0:T(8,128)(2,1)S(1)} %get-tuple-element.187), channel_id=1, source_target_pairs={{0,4},{1,5},{2,6},{3,7},{4,0},{5,1},{6,2},{7,3},{8,12},{9,13},{10,... | collective-permute-start | bytes 442376 | tf_op jit(solution)/shard_map/ppermute | solution.py:854
  115.6 1.2 collective-permute-start.33
  116.8 1.7 %shard_map.268 = bf16[160,767]{1,0:T(8,128)(2,1)} custom-call(bf16[320,768]{1,0:T(8,128)(2,1)S(1)} %get-tuple-element.128.act_keep, bf16[320,768]{1,0:T(8,128)(2,1)S(1)} %get-tuple-element.129.act_send, bf16[3072,767]{1,0:T(8,128)(2,1)S(1)} %bitcast.1, f32[160,767]{1,0:T(8,128)S(1)} %get-tuple-element.130.middle, f32[767]{0:T(1024)S(1)} %copy-done.11), custom_call_target="tpu_custom_call" | custom-call | flops 1000 | bytes 1000 | tf_op jit(solution)/shard_map/pallas_call | solution.py:364
  118.4 2.3 %shard_map.273 = bf16[160,767]{1,0:T(8,128)(2,1)} custom-call(bf16[352,768]{1,0:T(8,128)(2,1)S(1)} %get-tuple-element.166.x0, bf16[352,768]{1,0:T(8,128)(2,1)S(1)} %collective-permute-done.20.x1, bf16[352,768]{1,0:T(8,128)(2,1)S(1)} %collective-permute-done.21.x2, bf16[352,768]{1,0:T(8,128)(2,1)S(1)} %collective-permute-done.22.x3, ...), custom_call_target="tpu_custom_call" | custom-call | flops 1000 | bytes 1000 | tf_op jit(solution)/shard_map/pallas_call | solution.py:364
  120.7 0.7 shard_map.281
  121.4 0.7 collective-permute-done.32.f2
  122.2 1.5 %shard_map.279 = (f32[24,2304]{1,0:T(8,128)}, f32[24,3072]{1,0:T(8,128)}, f32[24,767]{1,0:T(8,128)}, f32[768]{0:T(1024)}, f32[768]{0:T(1024)}, /*index=5*/f32[76...) custom-call(s32[4,2]{1,0:T(4,128)S(1)} %copy.31.lengths, ...), custom_call_target="tpu_custom_call" | custom-call | flops 1000 | bytes 1000 | tf_op jit(solution)/shard_map/pallas_call | solution.py:364
  (82 shorter events, 5.7 us)
Async XLA Ops:
  4.6 8.7 %collective-permute-start = (bf16[240,384]{1,0:T(8,128)(2,1)}, bf16[240,384]{1,0:T(8,128)(2,1)S(1)}, u32[]{:S(2)}, u32[]{:S(2)}) collective-permute-start(bf16[240,384]{1,0:T(8,128)(2,1)} %get-tuple-element.109), channel_id=1, source_target_pairs={{0,2},{1,3},{2,0},{3,1},{4,6},{5,7},{6,4},{7,5},{8,10},{9,11},{10,... | collective-permute-start | bytes 552968 | tf_op jit(solution)/shard_map/ppermute | solution.py:854
  7.6 10.3 %collective-permute-start.1 = (bf16[240,384]{1,0:T(8,128)(2,1)}, bf16[240,384]{1,0:T(8,128)(2,1)S(1)}, u32[]{:S(2)}, u32[]{:S(2)}) collective-permute-start(bf16[240,384]{1,0:T(8,128)(2,1)} %get-tuple-element.110), channel_id=1, source_target_pairs={{0,4},{1,5},{2,6},{3,7},{4,0},{5,1},{6,2},{7,3},{8,12},{9,13},{10,... | collective-permute-start | bytes 552968 | tf_op jit(solution)/shard_map/ppermute | solution.py:854
  9.1 8.7 %collective-permute-start.2 = (bf16[240,384]{1,0:T(8,128)(2,1)}, bf16[240,384]{1,0:T(8,128)(2,1)S(1)}, u32[]{:S(2)}, u32[]{:S(2)}) collective-permute-start(bf16[240,384]{1,0:T(8,128)(2,1)} %get-tuple-element.111), channel_id=1, source_target_pairs={{0,6},{1,7},{2,4},{3,5},{4,2},{5,3},{6,0},{7,1},{8,14},{9,15},{10,... | collective-permute-start | bytes 552968 | tf_op jit(solution)/shard_map/ppermute | solution.py:854
  11.5 10.6 %copy-start.12 = (s32[16]{0:T(128)S(1)}, s32[16]{0:T(128)}, u32[]{:S(2)}) copy-start(s32[16]{0:T(128)} %spans.3) | copy-start | bytes 196
  11.5 10.6 %copy-start.13 = (s32[1,2]{1,0:T(1,128)S(1)}, s32[1,2]{1,0:T(1,128)}, u32[]{:S(2)}) copy-start(s32[1,2]{1,0:T(1,128)} %offsets.3) | copy-start | bytes 28
  18.3 3.7 %collective-permute-start.3 = (bf16[640,384]{1,0:T(8,128)(2,1)S(1)}, bf16[640,384]{1,0:T(8,128)(2,1)S(1)}, u32[]{:S(2)}, u32[]{:S(2)}) collective-permute-start(bf16[640,384]{1,0:T(8,128)(2,1)S(1)} %get-tuple-element.117.own), channel_id=1, source_target_pairs={{0,1},{1,0},{2,3},{3,2},{4,5},{5,4},{6,7},{7,6},{8,9},{9,8},{10,11... | collective-permute-start | bytes 1474568 | tf_op jit(solution)/shard_map/ppermute | solution.py:858
  18.4 12.8 %collective-permute-start.7 = (bf16[160,768]{1,0:T(8,128)(2,1)}, bf16[160,768]{1,0:T(8,128)(2,1)}, u32[]{:S(2)}, u32[]{:S(2)}) collective-permute-start(bf16[160,768]{1,0:T(8,128)(2,1)} %get-tuple-element.122.i0), channel_id=1, source_target_pairs={{0,2},{1,3},{2,0},{3,1},{4,6},{5,7},{6,4},{7,5},{8,10},{9,11},{10,... | collective-permute-start | bytes 737288 | tf_op jit(solution)/shard_map/ppermute | solution.py:854
  19.7 12.9 %collective-permute-start.8 = (bf16[160,768]{1,0:T(8,128)(2,1)}, bf16[160,768]{1,0:T(8,128)(2,1)}, u32[]{:S(2)}, u32[]{:S(2)}) collective-permute-start(bf16[160,768]{1,0:T(8,128)(2,1)} %get-tuple-element.122.i0), channel_id=1, source_target_pairs={{0,4},{1,5},{2,6},{3,7},{4,0},{5,1},{6,2},{7,3},{8,12},{9,13},{10,... | collective-permute-start | bytes 737288 | tf_op jit(solution)/shard_map/ppermute | solution.py:854
  20.5 13.7 %collective-permute-start.9 = (bf16[160,768]{1,0:T(8,128)(2,1)}, bf16[160,768]{1,0:T(8,128)(2,1)}, u32[]{:S(2)}, u32[]{:S(2)}) collective-permute-start(bf16[160,768]{1,0:T(8,128)(2,1)} %get-tuple-element.122.i0), channel_id=1, source_target_pairs={{0,6},{1,7},{2,4},{3,5},{4,2},{5,3},{6,0},{7,1},{8,14},{9,15},{10,... | collective-permute-start | bytes 737288 | tf_op jit(solution)/shard_map/ppermute | solution.py:854
  22.1 14.3 %slice-start.2 = ((s8[4718592]{0:T(1024)(128)(4,1)}), s8[4194304]{0:T(1024)(128)(4,1)S(1)}, s32[]{:S(2)}) async-start(s8[4718592]{0:T(1024)(128)(4,1)} %bitcast.2), calls=%async_computation.2 | async-start | bytes 8388608
  22.1 14.3 %slice-start.3 = ((s8[4718592]{0:T(1024)(128)(4,1)}), s8[524288]{0:T(1024)(128)(4,1)S(1)}, s32[]{:S(2)}) async-start(s8[4718592]{0:T(1024)(128)(4,1)} %bitcast.2), calls=%async_computation.3 | async-start | bytes 1048576
  22.1 14.2 %copy-start.2 = (bf16[160,767]{1,0:T(8,128)(2,1)S(1)}, bf16[160,767]{1,0:T(8,128)(2,1)}, u32[]{:S(2)}) copy-start(bf16[160,767]{1,0:T(8,128)(2,1)} %resid.3) | copy-start | bytes 736324
  22.1 14.2 %copy-start.4 = (bf16[768,767]{1,0:T(8,128)(2,1)S(1)}, bf16[768,767]{1,0:T(8,128)(2,1)}, u32[]{:S(2)}) copy-start(bf16[768,767]{1,0:T(8,128)(2,1)} %out_weight.1) | copy-start | bytes 3534340
  22.1 14.2 %copy-start.6 = (f32[160,1]{1,0:T(8,128)S(1)}, f32[160,1]{1,0:T(8,128)}, u32[]{:S(2)}) copy-start(f32[160,1]{1,0:T(8,128)} %get-tuple-element.127.root_in) | copy-start | bytes 1924
  22.1 14.2 %copy-start.8 = (f32[3072]{0:T(1024)S(1)}, f32[3072]{0:T(1024)}, u32[]{:S(2)}) copy-start(f32[3072]{0:T(1024)} %up_bias.1) | copy-start | bytes 36868
  22.1 14.2 %copy-start.9 = (f32[767]{0:T(1024)S(1)}, f32[767]{0:T(1024)}, u32[]{:S(2)}) copy-start(f32[767]{0:T(1024)} %out_bias.1) | copy-start | bytes 9208
  22.2 14.2 %copy-start.10 = (f32[768]{0:T(1024)S(1)}, f32[768]{0:T(1024)}, u32[]{:S(2)}) copy-start(f32[768]{0:T(1024)} %gain.3) | copy-start | bytes 9220
  29.1 5.1 %collective-permute-start.4 = (bf16[80,384]{1,0:T(8,128)(2,1)S(1)}, bf16[80,384]{1,0:T(8,128)(2,1)S(1)}, u32[]{:S(2)}, u32[]{:S(2)}) collective-permute-start(bf16[80,384]{1,0:T(8,128)(2,1)S(1)} %get-tuple-element.119), channel_id=1, source_target_pairs={{0,2},{1,3},{2,0},{3,1},{4,6},{5,7},{6,4},{7,5},{8,10},{9,11},{10,... | collective-permute-start | bytes 184328 | tf_op jit(solution)/shard_map/ppermute | solution.py:854
  30.4 4.9 %collective-permute-start.5 = (bf16[80,384]{1,0:T(8,128)(2,1)S(1)}, bf16[80,384]{1,0:T(8,128)(2,1)S(1)}, u32[]{:S(2)}, u32[]{:S(2)}) collective-permute-start(bf16[80,384]{1,0:T(8,128)(2,1)S(1)} %get-tuple-element.120), channel_id=1, source_target_pairs={{0,4},{1,5},{2,6},{3,7},{4,0},{5,1},{6,2},{7,3},{8,12},{9,13},{10,... | collective-permute-start | bytes 184328 | tf_op jit(solution)/shard_map/ppermute | solution.py:854
  31.2 5.1 %collective-permute-start.6 = (bf16[80,384]{1,0:T(8,128)(2,1)S(1)}, bf16[80,384]{1,0:T(8,128)(2,1)S(1)}, u32[]{:S(2)}, u32[]{:S(2)}) collective-permute-start(bf16[80,384]{1,0:T(8,128)(2,1)S(1)} %get-tuple-element.121), channel_id=1, source_target_pairs={{0,6},{1,7},{2,4},{3,5},{4,2},{5,3},{6,0},{7,1},{8,14},{9,15},{10,... | collective-permute-start | bytes 184328 | tf_op jit(solution)/shard_map/ppermute | solution.py:854
  32.6 19.0 %collective-permute-start.13 = (bf16[160,767]{1,0:T(8,128)(2,1)S(1)}, bf16[160,767]{1,0:T(8,128)(2,1)S(1)}, u32[]{:S(2)}, u32[]{:S(2)}) collective-permute-start(bf16[160,767]{1,0:T(8,128)(2,1)S(1)} %copy-done.3), channel_id=1, source_target_pairs={{0,8},{8,0},{16,24},{24,16},{1,9},{9,1},{17,25},{25,17},{2,10},{10... | collective-permute-start | bytes 736328 | tf_op jit(solution)/shard_map/ppermute | solution.py:862
  42.4 17.1 %collective-permute-start.14 = (bf16[320,768]{1,0:T(8,128)(2,1)S(1)}, bf16[320,768]{1,0:T(8,128)(2,1)S(1)}, u32[]{:S(2)}, u32[]{:S(2)}) collective-permute-start(bf16[320,768]{1,0:T(8,128)(2,1)S(1)} %get-tuple-element.129.act_send), channel_id=1, source_target_pairs={{0,8},{8,0},{16,24},{24,16},{1,9},{9,1},{17,25},{25,17},{2,10},{10... | collective-permute-start | bytes 1474568 | tf_op jit(solution)/shard_map/ppermute | solution.py:862
  44.1 4.2 %collective-permute-start.10 = (bf16[80,384]{1,0:T(8,128)(2,1)S(1)}, bf16[80,384]{1,0:T(8,128)(2,1)S(1)}, u32[]{:S(2)}, u32[]{:S(2)}) collective-permute-start(bf16[80,384]{1,0:T(8,128)(2,1)S(1)} %get-tuple-element.132), channel_id=1, source_target_pairs={{0,2},{1,3},{2,0},{3,1},{4,6},{5,7},{6,4},{7,5},{8,10},{9,11},{10,... | collective-permute-start | bytes 184328 | tf_op jit(solution)/shard_map/ppermute | solution.py:854
  45.6 4.2 %collective-permute-start.11 = (bf16[80,384]{1,0:T(8,128)(2,1)S(1)}, bf16[80,384]{1,0:T(8,128)(2,1)S(1)}, u32[]{:S(2)}, u32[]{:S(2)}) collective-permute-start(bf16[80,384]{1,0:T(8,128)(2,1)S(1)} %get-tuple-element.133), channel_id=1, source_target_pairs={{0,4},{1,5},{2,6},{3,7},{4,0},{5,1},{6,2},{7,3},{8,12},{9,13},{10,... | collective-permute-start | bytes 184328 | tf_op jit(solution)/shard_map/ppermute | solution.py:854
  46.1 5.6 %collective-permute-start.12 = (bf16[80,384]{1,0:T(8,128)(2,1)S(1)}, bf16[80,384]{1,0:T(8,128)(2,1)S(1)}, u32[]{:S(2)}, u32[]{:S(2)}) collective-permute-start(bf16[80,384]{1,0:T(8,128)(2,1)S(1)} %get-tuple-element.134), channel_id=1, source_target_pairs={{0,6},{1,7},{2,4},{3,5},{4,2},{5,3},{6,0},{7,1},{8,14},{9,15},{10,... | collective-permute-start | bytes 184328 | tf_op jit(solution)/shard_map/ppermute | solution.py:854
  51.6 9.8 %collective-permute-start.17 = (bf16[320,768]{1,0:T(8,128)(2,1)S(1)}, bf16[320,768]{1,0:T(8,128)(2,1)S(1)}, u32[]{:S(2)}, u32[]{:S(2)}) collective-permute-start(bf16[320,768]{1,0:T(8,128)(2,1)S(1)} %get-tuple-element.152), channel_id=1, source_target_pairs={{0,2},{1,3},{2,0},{3,1},{4,6},{5,7},{6,4},{7,5},{8,10},{9,11},{10,... | collective-permute-start | bytes 1474568 | tf_op jit(solution)/shard_map/ppermute | solution.py:854
  52.8 8.9 %collective-permute-start.18 = (bf16[320,768]{1,0:T(8,128)(2,1)S(1)}, bf16[320,768]{1,0:T(8,128)(2,1)S(1)}, u32[]{:S(2)}, u32[]{:S(2)}) collective-permute-start(bf16[320,768]{1,0:T(8,128)(2,1)S(1)} %get-tuple-element.153), channel_id=1, source_target_pairs={{0,4},{1,5},{2,6},{3,7},{4,0},{5,1},{6,2},{7,3},{8,12},{9,13},{10,... | collective-permute-start | bytes 1474568 | tf_op jit(solution)/shard_map/ppermute | solution.py:854
  59.5 2.3 %collective-permute-start.15 = (bf16[320,384]{1,0:T(8,128)(2,1)S(1)}, bf16[320,384]{1,0:T(8,128)(2,1)S(1)}, u32[]{:S(2)}, u32[]{:S(2)}) collective-permute-start(bf16[320,384]{1,0:T(8,128)(2,1)S(1)} %get-tuple-element.146), channel_id=1, source_target_pairs={{0,1},{1,0},{2,3},{3,2},{4,5},{5,4},{6,7},{7,6},{8,9},{9,8},{10,11... | collective-permute-start | bytes 737288 | tf_op jit(solution)/shard_map/ppermute | solution.py:858
  59.6 2.2 %collective-permute-start.16 = (bf16[320,384]{1,0:T(8,128)(2,1)S(1)}, bf16[320,384]{1,0:T(8,128)(2,1)S(1)}, u32[]{:S(2)}, u32[]{:S(2)}) collective-permute-start(bf16[320,384]{1,0:T(8,128)(2,1)S(1)} %get-tuple-element.147), channel_id=1, source_target_pairs={{0,1},{1,0},{2,3},{3,2},{4,5},{5,4},{6,7},{7,6},{8,9},{9,8},{10,11... | collective-permute-start | bytes 737288 | tf_op jit(solution)/shard_map/ppermute | solution.py:858
  66.5 4.5 %collective-permute-start.19 = (bf16[1504,768]{1,0:T(8,128)(2,1)S(1)}, bf16[1504,768]{1,0:T(8,128)(2,1)S(1)}, u32[]{:S(2)}, u32[]{:S(2)}) collective-permute-start(bf16[1504,768]{1,0:T(8,128)(2,1)S(1)} %get-tuple-element.161.send), channel_id=1, source_target_pairs={{0,1},{1,0},{2,3},{3,2},{4,5},{5,4},{6,7},{7,6},{8,9},{9,8},{10,11... | collective-permute-start | bytes 6930440 | tf_op jit(solution)/shard_map/ppermute | solution.py:858
  66.6 14.5 %collective-permute-start.25 = (bf16[320,768]{1,0:T(8,128)(2,1)S(1)}, bf16[320,768]{1,0:T(8,128)(2,1)S(1)}, u32[]{:S(2)}, u32[]{:S(2)}) collective-permute-start(bf16[320,768]{1,0:T(8,128)(2,1)S(1)} %get-tuple-element.176), channel_id=1, source_target_pairs={{0,6},{1,7},{2,4},{3,5},{4,2},{5,3},{6,0},{7,1},{8,14},{9,15},{10,... | collective-permute-start | bytes 1474568 | tf_op jit(solution)/shard_map/ppermute | solution.py:854
  71.0 45.7 %slice-start = ((s8[4718592]{0:T(1024)(128)(4,1)}), s8[524288]{0:T(1024)(128)(4,1)S(1)}, s32[]{:S(2)}) async-start(s8[4718592]{0:T(1024)(128)(4,1)} %bitcast), calls=%async_computation | async-start | bytes 1048576
  71.6 45.1 %slice-start.1 = ((s8[4718592]{0:T(1024)(128)(4,1)}), s8[4194304]{0:T(1024)(128)(4,1)S(1)}, s32[]{:S(2)}) async-start(s8[4718592]{0:T(1024)(128)(4,1)} %bitcast), calls=%async_computation.1 | async-start | bytes 8388608
  71.6 15.5 %collective-permute-start.23 = (bf16[368,768]{1,0:T(8,128)(2,1)S(1)}, bf16[368,768]{1,0:T(8,128)(2,1)S(1)}, u32[]{:S(2)}, u32[]{:S(2)}) collective-permute-start(bf16[368,768]{1,0:T(8,128)(2,1)S(1)} %get-tuple-element.172.z_send), channel_id=1, source_target_pairs={{0,8},{8,0},{16,24},{24,16},{1,9},{9,1},{17,25},{25,17},{2,10},{10... | collective-permute-start | bytes 1695752 | tf_op jit(solution)/shard_map/ppermute | solution.py:862
  82.3 1.9 %collective-permute-start.26 = (bf16[128,768]{1,0:T(8,128)(2,1)S(1)}, bf16[128,768]{1,0:T(8,128)(2,1)S(1)}, u32[]{:S(2)}, u32[]{:S(2)}) collective-permute-start(bf16[128,768]{1,0:T(8,128)(2,1)S(1)} %get-tuple-element.178), channel_id=1, source_target_pairs={{0,1},{1,0},{2,3},{3,2},{4,5},{5,4},{6,7},{7,6},{8,9},{9,8},{10,11... | collective-permute-start | bytes 589832 | tf_op jit(solution)/shard_map/ppermute | solution.py:858
  82.4 3.0 %collective-permute-start.27 = (bf16[128,768]{1,0:T(8,128)(2,1)S(1)}, bf16[128,768]{1,0:T(8,128)(2,1)S(1)}, u32[]{:S(2)}, u32[]{:S(2)}) collective-permute-start(bf16[128,768]{1,0:T(8,128)(2,1)S(1)} %get-tuple-element.179), channel_id=1, source_target_pairs={{0,1},{1,0},{2,3},{3,2},{4,5},{5,4},{6,7},{7,6},{8,9},{9,8},{10,11... | collective-permute-start | bytes 589832 | tf_op jit(solution)/shard_map/ppermute | solution.py:858
  82.9 3.6 %collective-permute-start.28 = (bf16[128,768]{1,0:T(8,128)(2,1)S(1)}, bf16[128,768]{1,0:T(8,128)(2,1)S(1)}, u32[]{:S(2)}, u32[]{:S(2)}) collective-permute-start(bf16[128,768]{1,0:T(8,128)(2,1)S(1)} %get-tuple-element.180), channel_id=1, source_target_pairs={{0,1},{1,0},{2,3},{3,2},{4,5},{5,4},{6,7},{7,6},{8,9},{9,8},{10,11... | collective-permute-start | bytes 589832 | tf_op jit(solution)/shard_map/ppermute | solution.py:858
  83.0 18.7 %collective-permute-start.20 = (bf16[352,768]{1,0:T(8,128)(2,1)S(1)}, bf16[352,768]{1,0:T(8,128)(2,1)S(1)}, u32[]{:S(2)}, u32[]{:S(2)}) collective-permute-start(bf16[352,768]{1,0:T(8,128)(2,1)S(1)} %get-tuple-element.167), channel_id=1, source_target_pairs={{0,2},{1,3},{2,0},{3,1},{4,6},{5,7},{6,4},{7,5},{8,10},{9,11},{10,... | collective-permute-start | bytes 1622024 | tf_op jit(solution)/shard_map/ppermute | solution.py:854
  84.2 24.7 %collective-permute-start.21 = (bf16[352,768]{1,0:T(8,128)(2,1)S(1)}, bf16[352,768]{1,0:T(8,128)(2,1)S(1)}, u32[]{:S(2)}, u32[]{:S(2)}) collective-permute-start(bf16[352,768]{1,0:T(8,128)(2,1)S(1)} %get-tuple-element.168), channel_id=1, source_target_pairs={{0,4},{1,5},{2,6},{3,7},{4,0},{5,1},{6,2},{7,3},{8,12},{9,13},{10,... | collective-permute-start | bytes 1622024 | tf_op jit(solution)/shard_map/ppermute | solution.py:854
  85.4 24.8 %collective-permute-start.22 = (bf16[352,768]{1,0:T(8,128)(2,1)S(1)}, bf16[352,768]{1,0:T(8,128)(2,1)S(1)}, u32[]{:S(2)}, u32[]{:S(2)}) collective-permute-start(bf16[352,768]{1,0:T(8,128)(2,1)S(1)} %get-tuple-element.169), channel_id=1, source_target_pairs={{0,6},{1,7},{2,4},{3,5},{4,2},{5,3},{6,0},{7,1},{8,14},{9,15},{10,... | collective-permute-start | bytes 1622024 | tf_op jit(solution)/shard_map/ppermute | solution.py:854
  86.6 14.9 %collective-permute-start.29 = (bf16[2,96,768]{2,1,0:T(8,128)(2,1)S(1)}, bf16[2,96,768]{2,1,0:T(8,128)(2,1)S(1)}, u32[]{:S(2)}, u32[]{:S(2)}) collective-permute-start(bf16[2,96,768]{2,1,0:T(8,128)(2,1)S(1)} %get-tuple-element.182), channel_id=1, source_target_pairs={{0,8},{8,0},{16,24},{24,16},{1,9},{9,1},{17,25},{25,17},{2,10},{10... | collective-permute-start | bytes 884744 | tf_op jit(solution)/shard_map/ppermute | solution.py:862
  87.3 29.5 %copy-start.11 = (f32[767]{0:T(1024)S(1)}, f32[767]{0:T(1024)}, u32[]{:S(2)}) copy-start(f32[767]{0:T(1024)} %bias.1) | copy-start | bytes 9208
  87.3 25.7 %collective-permute-start.24 = (bf16[192,768]{1,0:T(8,128)(2,1)S(1)}, bf16[192,768]{1,0:T(8,128)(2,1)S(1)}, u32[]{:S(2)}, u32[]{:S(2)}) collective-permute-start(bf16[192,768]{1,0:T(8,128)(2,1)S(1)} %get-tuple-element.174.z_next), channel_id=1, source_target_pairs={{0,16},{8,24},{16,0},{24,8},{1,17},{9,25},{17,1},{25,9},{2,18},{10... | collective-permute-start | bytes 884744 | tf_op jit(solution)/shard_map/ppermute | solution.py:862
  101.6 11.4 %collective-permute-start.30 = (bf16[96,768]{1,0:T(8,128)(2,1)S(1)}, bf16[96,768]{1,0:T(8,128)(2,1)S(1)}, u32[]{:S(2)}, u32[]{:S(2)}) collective-permute-start(bf16[96,768]{1,0:T(8,128)(2,1)S(1)} %get-tuple-element.184), channel_id=1, source_target_pairs={{0,16},{8,24},{16,0},{24,8},{1,17},{9,25},{17,1},{25,9},{2,18},{10... | collective-permute-start | bytes 442376 | tf_op jit(solution)/shard_map/ppermute | solution.py:862
  110.3 10.4 %collective-permute-start.34 = (bf16[96,768]{1,0:T(8,128)(2,1)S(1)}, bf16[96,768]{1,0:T(8,128)(2,1)S(1)}, u32[]{:S(2)}, u32[]{:S(2)}) collective-permute-start(bf16[96,768]{1,0:T(8,128)(2,1)S(1)} %get-tuple-element.199), channel_id=1, source_target_pairs={{0,16},{8,24},{16,0},{24,8},{1,17},{9,25},{17,1},{25,9},{2,18},{10... | collective-permute-start | bytes 442376 | tf_op jit(solution)/shard_map/ppermute | solution.py:862
  113.2 8.3 %collective-permute-start.31 = (bf16[96,768]{1,0:T(8,128)(2,1)S(1)}, bf16[96,768]{1,0:T(8,128)(2,1)S(1)}, u32[]{:S(2)}, u32[]{:S(2)}) collective-permute-start(bf16[96,768]{1,0:T(8,128)(2,1)S(1)} %get-tuple-element.186), channel_id=1, source_target_pairs={{0,2},{1,3},{2,0},{3,1},{4,6},{5,7},{6,4},{7,5},{8,10},{9,11},{10,... | collective-permute-start | bytes 442376 | tf_op jit(solution)/shard_map/ppermute | solution.py:854
  114.1 8.0 %collective-permute-start.32 = (bf16[96,768]{1,0:T(8,128)(2,1)S(1)}, bf16[96,768]{1,0:T(8,128)(2,1)S(1)}, u32[]{:S(2)}, u32[]{:S(2)}) collective-permute-start(bf16[96,768]{1,0:T(8,128)(2,1)S(1)} %get-tuple-element.187), channel_id=1, source_target_pairs={{0,4},{1,5},{2,6},{3,7},{4,0},{5,1},{6,2},{7,3},{8,12},{9,13},{10,... | collective-permute-start | bytes 442376 | tf_op jit(solution)/shard_map/ppermute | solution.py:854
  115.6 6.6 %collective-permute-start.33 = (bf16[96,768]{1,0:T(8,128)(2,1)S(1)}, bf16[96,768]{1,0:T(8,128)(2,1)S(1)}, u32[]{:S(2)}, u32[]{:S(2)}) collective-permute-start(bf16[96,768]{1,0:T(8,128)(2,1)S(1)} %get-tuple-element.188), channel_id=1, source_target_pairs={{0,6},{1,7},{2,4},{3,5},{4,2},{5,3},{6,0},{7,1},{8,14},{9,15},{10,... | collective-permute-start | bytes 442376 | tf_op jit(solution)/shard_map/ppermute | solution.py:854
  (6 other events, 36.2 us)

commit v5 on v4

--- a/solution.py
+++ b/solution.py
@@ -464,9 +464,21 @@
         s[...] = buf[r]
 
 
-def push_kernel(cot, weight, out):
+def push_kernel(spans, offsets, lengths, cot, weight, out, bounds, places):
+    me, bucket, core = here()
     for i in range(4):
         out[:, i * D : (i + 1) * D] = nt(cot[...], weight[i * D : (i + 1) * D, :])
+    lane = lax.broadcasted_iota(jnp.int32, (1, 1280), 1)
+    place = lane
+    for blk in range(16):
+        chip = ((blk % 8) // 2) ^ me
+        span = spans[chip * 4 + (core ^ (blk // 8)) * 2 + blk % 2]
+        place = jnp.where((lane >= blk * 80) & (lane < (blk + 1) * 80), lane + (span - blk) * 80, place)
+    places[...] = place
+    for blk in range(8):
+        lo, hi = limits(spans, offsets, lengths, bucket, (blk // 2) ^ me, core, blk % 2)
+        bounds[blk * 80 : (blk + 1) * 80, 0:1] = lo
+        bounds[blk * 80 : (blk + 1) * 80, 1:2] = hi
 
 
 def columns_kernel(weight, out):
@@ -489,31 +501,20 @@
 
 
 def forward_kernel(
-    spans, offsets, lengths, query, own, sib, chance, attended, b0, b1, b2, b3, keys, vals, scores, lows, highs
+    bounds, places, query, own, sib, chance, attended, b0, b1, b2, b3, keys, vals, scores
 ):
-    me, bucket, core = here()
     keys[:640, :] = own[:, :SPLIT]
     keys[640:, :] = sib[:, :SPLIT]
     v = jnp.concatenate([own[:, SPLIT:].astype(wide), sib[:, SPLIT:].astype(wide)], axis=0)
     for h in range(3):
         vals[h] = head_mask(v, h).astype(low)
-    lane = lax.broadcasted_iota(jnp.int32, (1, 1280), 1)
-    place = lane
-    for blk in range(16):
-        chip = ((blk % 8) // 2) ^ me
-        span = spans[chip * 4 + (core ^ (blk // 8)) * 2 + blk % 2]
-        place = jnp.where((lane >= blk * 80) & (lane < (blk + 1) * 80), lane + (span - blk) * 80, place)
-    for blk in range(8):
-        rows = slice(blk * 80, (blk + 1) * 80)
-        lo, hi = limits(spans, offsets, lengths, bucket, (blk // 2) ^ me, core, blk % 2)
-        lows[rows, :] = lo
-        highs[rows, :] = hi
+    place = places[...]
     q = query[...].astype(wide)
     for h in range(3):
         scores[...] = nt(head_mask(q, h).astype(low), keys[...])
         for blk in range(8):
             rows = slice(blk * 80, (blk + 1) * 80)
-            lo, hi = lows[rows, :], highs[rows, :]
+            lo, hi = bounds[rows, 0:1], bounds[rows, 1:2]
             s = jnp.where((place >= lo) & (place <= hi), scores[rows, :], masked_value)
             peak = jnp.max(s, axis=1, keepdims=True)
             w = jnp.exp(s - peak)
@@ -530,7 +531,7 @@
 
 
 def middle_kernel(
-    spans, offsets, lengths, p0, p1, p2, p3, out_weight, out_bias, resid, root_in, cot, gain, up_weight, up_bias, push,
+    bounds, p0, p1, p2, p3, out_weight, out_bias, resid, root_in, cot, gain, up_weight, up_bias, push,
     d0, d1, d2, d3, act_keep, act_send, n0, n1, n2, n3, branch_own, middle, middle_grad, vector,
     dbuf, abuf, nbuf,
 ):
@@ -553,9 +554,12 @@
     for blk in range(4):
         cols = slice(blk * D, (blk + 1) * D)
         u = jnp.dot(hidden, up_weight[:, cols], preferred_element_type=wide) + up_bias[cols].reshape(1, D)
-        t = jnp.tanh(c * (u + 0.044715 * u * u * u))
-        abuf[blk ^ bucket] = (0.5 * u * (1.0 + t)).astype(low)
-        slope = 0.5 * (1.0 + t) + 0.5 * u * (1.0 - t * t) * (c * (1.0 + 3 * 0.044715 * u * u))
+        square = u * u
+        t = jnp.tanh(u * (c + (c * 0.044715) * square))
+        gate = 0.5 + 0.5 * t
+        act = u * gate
+        abuf[blk ^ bucket] = act.astype(low)
+        slope = gate + act * (1.0 - t) * (c + (3 * c * 0.044715) * square)
         g = (push[:, cols] * slope).astype(low)
         nbuf[blk ^ me, 160:320, :] = g
         up_sums.append(jnp.sum(g.astype(wide), axis=0, keepdims=True))
@@ -578,8 +582,7 @@
         (d0, d1, d2, d3)[r][...] = dbuf[r]
         (act_keep, act_send)[r % 2][r // 2 * 160 : r // 2 * 160 + 160, :] = abuf[r]
         (n0, n1, n2, n3)[r][...] = nbuf[r]
-    ends = [limits(spans, offsets, lengths, bucket, me, core, half)[1] for half in range(2)]
-    valid = jnp.where(jnp.concatenate(ends, axis=0) >= 0, 1.0, 0.0)
+    valid = jnp.where(bounds[0:160, 1:2] >= 0, 1.0, 0.0)
     one = jnp.sum(valid * root_in[...], axis=0, keepdims=True)
     two = jnp.sum(valid * root, axis=0, keepdims=True)
     at = lax.broadcasted_iota(jnp.int32, (1, D), 1)
@@ -909,7 +912,12 @@
         far=range(5),
     )
     got = exchange([s0, s1, s2, s3])
-    (push,) = call(push_kernel, [((160, FF), wide)], [out_cotangent, down_weight])
+    push, bounds, places = call(
+        push_kernel,
+        [((160, FF), wide), ((640, 2), jnp.int32), ((1, 1280), jnp.int32)],
+        where + [out_cotangent, down_weight],
+        small=3,
+    )
     hiddens = exchange([hidden] * 4)
     got = list(after(got, push))
     query, own_both = call(assemble_kernel, [((640, SPLIT), low), ((640, 2 * SPLIT), low)], got)
@@ -918,10 +926,8 @@
     chance, attended, b0, b1, b2, b3 = call(
         forward_kernel,
         [((3, 640, 1280), low), ((640, SPLIT), wide)] + [backed] * 4,
-        where + [query, own_both, sib_both],
-        [pltpu.VMEM((1280, SPLIT), low), pltpu.VMEM((3, 1280, SPLIT), low), pltpu.VMEM((640, 1280), wide)]
-        + [pltpu.VMEM((640, 1), jnp.int32)] * 2,
-        small=3,
+        [bounds, places, query, own_both, sib_both],
+        [pltpu.VMEM((1280, SPLIT), low), pltpu.VMEM((3, 1280, SPLIT), low), pltpu.VMEM((640, 1280), wide)],
         work=7,
     )
     back = exchange([b0, b1, b2, b3])
@@ -934,12 +940,11 @@
         [backed] * 4
         + [((320, D), low)] * 6
         + [token, ((160, DC), wide), ((160, D), wide), ((16, D), wide)],
-        where
+        [bounds]
         + back
         + [output_weight, output_bias, residual_in, root_one, out_cotangent, second_gain]
         + [up_weight, up_bias, push],
         [pltpu.VMEM((4, 80, 2 * SPLIT), low), pltpu.VMEM((4, 160, D), low), pltpu.VMEM((4, 320, D), low)],
-        small=3,
     )
     act_keep, act_send = outs[4:6]
     lates = list(outs[6:10])

time: 124 us -> 122 us (0.984)
  Pallas kernels: 38.4 us -> 36.5 us
    pallas_call x19, Pallas kernels: 38.4 us -> 36.5 us  [call(): pl.pallas_call(kernel, out_shape=shapes, in_specs=[SMEM if i < small else...]
    unnamed x39 -> x41, local copies, waits for them, and re-layouts: 2.52 us -> 2.52 us
  transfers between devices with their start and end apart: 35 -> 35, of which waited for: 15 -> 13; matrix products, arithmetic and copies ran while one was open for 0% -> 0% of each run, Pallas kernels for 22% -> 22%
where the time goes in v5:
time: 122 us
  waiting for transfers between devices  44.2 us (36%)
  starting transfers between devices  37.1 us (30%)
  Pallas kernels  36.5 us (30%)
  local copies, waits for them, and re-layouts  2.52 us (2%)
    pallas_call x19, Pallas kernels, call(): pl.pallas_call(kernel, out_shape=shapes, in_specs=[SMEM if i < small else...  36.5 us
    ppermute x21, waiting for transfers between devices, swap_chip(): return lax.ppermute(block, 'blk', [(k, k ^ 2 * step) for k in range(8)])  29.7 us
    ppermute x21, starting transfers between devices, swap_chip(): return lax.ppermute(block, 'blk', [(k, k ^ 2 * step) for k in range(8)])  26.1 us
    ppermute x7, waiting for transfers between devices, shift_bucket(): return lax.ppermute(block, 'bucket', [(b, b ^ step) for b in range(4)])  11.6 us
    ppermute x7, starting transfers between devices, shift_bucket(): return lax.ppermute(block, 'bucket', [(b, b ^ step) for b in range(4)])  9.65 us
    ppermute x7, waiting for transfers between devices, swap_core(): return lax.ppermute(block, 'blk', [(k, k ^ 1) for k in range(8)])  2.86 us
    unnamed x41, local copies, waits for them, and re-layouts  2.52 us
  transfers between devices with their start and end apart: 35, of which 13 were waited for; matrix products, arithmetic and copies ran while one was open for 0% of the time, Pallas kernels for 22%

profile of v5, /device:TPU:0, one launch (start us, length us, event | category | flops | bytes accessed | tf_op | source)
XLA Modules:
  0.0 121.5 jit_solution(16210937071366149333)
XLA Ops:
  0.7 4.0 %shard_map.264 = (bf16[240,384]{1,0:T(8,128)(2,1)}, bf16[240,384]{1,0:T(8,128)(2,1)}, bf16[240,384]{1,0:T(8,128)(2,1)}, bf16[240,384]{1,0:T(8,128)(2,1)}, bf16[160,768]{1,0:T(8,128)(2,1)}, /*index=5*/f32[160,1]{1,0:T(8,128)}) custom-call(bf16[160,767]{1,0:T(8,128)(2,1)} %resid.3, f32[768]{0:T(1024)} %gain.5, bf16[768,2304]{1,0:T(8,128)(2,1)} %weight.6, ...), custom_call_target="tpu_custom_call" | custom-call | flops 1000 | bytes 1000 | tf_op jit(solution)/shard_map/pallas_call | solution.py:364
  4.7 3.0 %collective-permute-start = (bf16[240,384]{1,0:T(8,128)(2,1)}, bf16[240,384]{1,0:T(8,128)(2,1)S(1)}, u32[]{:S(2)}, u32[]{:S(2)}) collective-permute-start(bf16[240,384]{1,0:T(8,128)(2,1)} %get-tuple-element.114), channel_id=1, source_target_pairs={{0,2},{1,3},{2,0},{3,1},{4,6},{5,7},{6,4},{7,5},{8,10},{9,11},{10,... | collective-permute-start | bytes 552968 | tf_op jit(solution)/shard_map/ppermute | solution.py:857
  7.7 1.5 %collective-permute-start.1 = (bf16[240,384]{1,0:T(8,128)(2,1)}, bf16[240,384]{1,0:T(8,128)(2,1)S(1)}, u32[]{:S(2)}, u32[]{:S(2)}) collective-permute-start(bf16[240,384]{1,0:T(8,128)(2,1)} %get-tuple-element.115), channel_id=1, source_target_pairs={{0,4},{1,5},{2,6},{3,7},{4,0},{5,1},{6,2},{7,3},{8,12},{9,13},{10,... | collective-permute-start | bytes 552968 | tf_op jit(solution)/shard_map/ppermute | solution.py:857
  9.3 2.3 %copy-done.1 = bf16[3072,767]{1,0:T(8,128)(2,1)S(1)} copy-done((bf16[3072,767]{1,0:T(8,128)(2,1)S(1)}, bf16[3072,767]{1,0:T(8,128)(2,1)}, u32[]{:S(2)}) %copy-start.1) | copy-done | bytes 4712472
  11.7 2.4 %shard_map.263 = (f32[160,3072]{1,0:T(8,128)S(1)}, s32[640,2]{1,0:T(8,128)S(1)}, s32[1,1280]{1,0:T(1,128)S(1)}) custom-call(s32[16]{0:T(128)S(1)} %copy-done.13, s32[1,2]{1,0:T(1,128)S(1)} %copy-done.14, s32[4,2]{1,0:T(4,128)S(1)} %copy.30.lengths, bf16[160,767]{1,0:T(8,128)(2,1)S(1)} %copy-done.2, bf16[3072,767]{1,0:T(8,128)(2,1)S(1)} %copy-done.1), custom_call_target="tpu_custom_call" | custom-call | flops 1000 | bytes 1000 | tf_op jit(solution)/shard_map/pallas_call | solution.py:364
  14.1 3.9 %collective-permute-done.1.p2 = bf16[240,384]{1,0:T(8,128)(2,1)S(1)} collective-permute-done((bf16[240,384]{1,0:T(8,128)(2,1)}, bf16[240,384]{1,0:T(8,128)(2,1)S(1)}, u32[]{:S(2)}, u32[]{:S(2)}) %collective-permute-start.1) | collective-permute-done | bytes 184352 | tf_op jit(solution)/shard_map/ppermute | solution.py:857
  18.5 1.3 %collective-permute-start.7 = (bf16[160,768]{1,0:T(8,128)(2,1)S(1)}, bf16[160,768]{1,0:T(8,128)(2,1)S(1)}, u32[]{:S(2)}, u32[]{:S(2)}) collective-permute-start(bf16[160,768]{1,0:T(8,128)(2,1)S(1)} %copy-done.5), channel_id=1, source_target_pairs={{0,2},{1,3},{2,0},{3,1},{4,6},{5,7},{6,4},{7,5},{8,10},{9,11},{10,... | collective-permute-start | bytes 737288 | tf_op jit(solution)/shard_map/ppermute | solution.py:857
  19.8 0.8 collective-permute-start.8
  20.6 1.4 %collective-permute-start.9 = (bf16[160,768]{1,0:T(8,128)(2,1)S(1)}, bf16[160,768]{1,0:T(8,128)(2,1)S(1)}, u32[]{:S(2)}, u32[]{:S(2)}) collective-permute-start(bf16[160,768]{1,0:T(8,128)(2,1)S(1)} %copy-done.5), channel_id=1, source_target_pairs={{0,6},{1,7},{2,4},{3,5},{4,2},{5,3},{6,0},{7,1},{8,14},{9,15},{10,... | collective-permute-start | bytes 737288 | tf_op jit(solution)/shard_map/ppermute | solution.py:857
  22.1 6.6 %shard_map.266 = (bf16[3,640,1280]{2,1,0:T(8,128)(2,1)S(1)}, f32[640,192]{1,0:T(8,128)S(1)}, bf16[80,384]{1,0:T(8,128)(2,1)S(1)}, bf16[80,384]{1,0:T(8,128)(2,1)...) custom-call(s32[640,2]{1,0:T(8,128)S(1)} %get-tuple-element.111.bounds, ...), custom_call_target="tpu_custom_call" | custom-call | flops 7700000768 | bytes 1000 | tf_op jit(solution)/shard_map/pallas_call | solution.py:364
  28.7 1.3 %collective-permute-start.4 = (bf16[80,384]{1,0:T(8,128)(2,1)S(1)}, bf16[80,384]{1,0:T(8,128)(2,1)S(1)}, u32[]{:S(2)}, u32[]{:S(2)}) collective-permute-start(bf16[80,384]{1,0:T(8,128)(2,1)S(1)} %get-tuple-element.125), channel_id=1, source_target_pairs={{0,2},{1,3},{2,0},{3,1},{4,6},{5,7},{6,4},{7,5},{8,10},{9,11},{10,... | collective-permute-start | bytes 184328 | tf_op jit(solution)/shard_map/ppermute | solution.py:857
  30.0 0.8 collective-permute-start.5
  30.9 1.4 %collective-permute-start.6 = (bf16[80,384]{1,0:T(8,128)(2,1)S(1)}, bf16[80,384]{1,0:T(8,128)(2,1)S(1)}, u32[]{:S(2)}, u32[]{:S(2)}) collective-permute-start(bf16[80,384]{1,0:T(8,128)(2,1)S(1)} %get-tuple-element.127), channel_id=1, source_target_pairs={{0,6},{1,7},{2,4},{3,5},{4,2},{5,3},{6,0},{7,1},{8,14},{9,15},{10,... | collective-permute-start | bytes 184328 | tf_op jit(solution)/shard_map/ppermute | solution.py:857
  32.3 1.6 %collective-permute-start.13 = (bf16[160,767]{1,0:T(8,128)(2,1)S(1)}, bf16[160,767]{1,0:T(8,128)(2,1)S(1)}, u32[]{:S(2)}, u32[]{:S(2)}) collective-permute-start(bf16[160,767]{1,0:T(8,128)(2,1)S(1)} %copy-done.2), channel_id=1, source_target_pairs={{0,8},{8,0},{16,24},{24,16},{1,9},{9,1},{17,25},{25,17},{2,10},{10... | collective-permute-start | bytes 736328 | tf_op jit(solution)/shard_map/ppermute | solution.py:865
  33.9 1.0 collective-permute-done.5.p2
  34.8 1.1 collective-permute-done.6.p3
  36.1 5.1 %shard_map.267 = (bf16[80,384]{1,0:T(8,128)(2,1)S(1)}, bf16[80,384]{1,0:T(8,128)(2,1)S(1)}, bf16[80,384]{1,0:T(8,128)(2,1)S(1)}, bf16[80,384]{1,0:T(8,128)(2,1)S...) custom-call(s32[640,2]{1,0:T(8,128)S(1)} %get-tuple-element.111.boun, ...), custom_call_target="tpu_custom_call" | custom-call | flops 1000 | bytes 1000 | tf_op jit(solution)/shard_map/pallas_call | solution.py:364
  41.1 1.6 %collective-permute-start.14 = (bf16[320,768]{1,0:T(8,128)(2,1)S(1)}, bf16[320,768]{1,0:T(8,128)(2,1)S(1)}, u32[]{:S(2)}, u32[]{:S(2)}) collective-permute-start(bf16[320,768]{1,0:T(8,128)(2,1)S(1)} %get-tuple-element.135.act_send), channel_id=1, source_target_pairs={{0,8},{8,0},{16,24},{24,16},{1,9},{9,1},{17,25},{25,17},{2,10},{10... | collective-permute-start | bytes 1474568 | tf_op jit(solution)/shard_map/ppermute | solution.py:865
  42.8 1.5 %collective-permute-start.10 = (bf16[80,384]{1,0:T(8,128)(2,1)S(1)}, bf16[80,384]{1,0:T(8,128)(2,1)S(1)}, u32[]{:S(2)}, u32[]{:S(2)}) collective-permute-start(bf16[80,384]{1,0:T(8,128)(2,1)S(1)} %get-tuple-element.138), channel_id=1, source_target_pairs={{0,2},{1,3},{2,0},{3,1},{4,6},{5,7},{6,4},{7,5},{8,10},{9,11},{10,... | collective-permute-start | bytes 184328 | tf_op jit(solution)/shard_map/ppermute | solution.py:857
  44.8 1.5 %collective-permute-start.12 = (bf16[80,384]{1,0:T(8,128)(2,1)S(1)}, bf16[80,384]{1,0:T(8,128)(2,1)S(1)}, u32[]{:S(2)}, u32[]{:S(2)}) collective-permute-start(bf16[80,384]{1,0:T(8,128)(2,1)S(1)} %get-tuple-element.140), channel_id=1, source_target_pairs={{0,6},{1,7},{2,4},{3,5},{4,2},{5,3},{6,0},{7,1},{8,14},{9,15},{10,... | collective-permute-start | bytes 184328 | tf_op jit(solution)/shard_map/ppermute | solution.py:857
  46.3 0.7 collective-permute-done.10.d1
  47.0 1.5 %collective-permute-done.11.d2 = bf16[80,384]{1,0:T(8,128)(2,1)S(1)} collective-permute-done((bf16[80,384]{1,0:T(8,128)(2,1)S(1)}, bf16[80,384]{1,0:T(8,128)(2,1)S(1)}, u32[]{:S(2)}, u32[]{:S(2)}) %collective-permute-start.11) | collective-permute-done | bytes 61472 | tf_op jit(solution)/shard_map/ppermute | solution.py:857
  48.5 1.8 %collective-permute-done.12.d3 = bf16[80,384]{1,0:T(8,128)(2,1)S(1)} collective-permute-done((bf16[80,384]{1,0:T(8,128)(2,1)S(1)}, bf16[80,384]{1,0:T(8,128)(2,1)S(1)}, u32[]{:S(2)}, u32[]{:S(2)}) %collective-permute-start.12) | collective-permute-done | bytes 61472 | tf_op jit(solution)/shard_map/ppermute | solution.py:857
  50.3 1.2 collective-permute-start.17
  51.5 0.9 collective-permute-start.18
  52.4 5.6 %shard_map.269 = (bf16[640,192]{1,0:T(8,128)(2,1)S(1)}, f32[640,384]{1,0:T(8,128)S(1)}, bf16[320,384]{1,0:T(8,128)(2,1)S(1)}, bf16[320,384]{1,0:T(8,128)(2,1)S(1)}) custom-call(bf16[80,384]{1,0:T(8,128)(2,1)S(1)} %get-tuple-element.142.d0, bf16[80,384]{1,0:T(8,128)(2,1)S(1)} %collective-permute-done.10.d1, bf16[80,384]{1,0:T(8,128)(2,1)S(1)} %collective-permute-done.11.d2, ...), custom_call_target="tpu_custom_call" | custom-call | flops 1000 | bytes 1000 | tf_op jit(solution)/shard_map/pallas_call | solution.py:364
  59.0 1.5 %collective-permute-done.17.n1 = bf16[320,768]{1,0:T(8,128)(2,1)S(1)} collective-permute-done((bf16[320,768]{1,0:T(8,128)(2,1)S(1)}, bf16[320,768]{1,0:T(8,128)(2,1)S(1)}, u32[]{:S(2)}, u32[]{:S(2)}) %collective-permute-start.17) | collective-permute-done | bytes 491552 | tf_op jit(solution)/shard_map/ppermute | solution.py:857
  60.6 3.3 %shard_map.271 = (bf16[240,384]{1,0:T(8,128)(2,1)S(1)}, bf16[240,384]{1,0:T(8,128)(2,1)S(1)}, bf16[240,384]{1,0:T(8,128)(2,1)S(1)}, bf16[240,384]{1,0:T(8,128)(2...) custom-call(bf16[640,192]{1,0:T(8,128)(2,1)S(1)} %get-tuple-element.148.query_g, ...), custom_call_target="tpu_custom_call" | custom-call | flops 1000 | bytes 1000 | tf_op jit(solution)/shard_map/pallas_call | solution.py:364
  64.0 1.6 %collective-permute-start.25 = (bf16[320,768]{1,0:T(8,128)(2,1)S(1)}, bf16[320,768]{1,0:T(8,128)(2,1)S(1)}, u32[]{:S(2)}, u32[]{:S(2)}) collective-permute-start(bf16[320,768]{1,0:T(8,128)(2,1)S(1)} %get-tuple-element.182), channel_id=1, source_target_pairs={{0,6},{1,7},{2,4},{3,5},{4,2},{5,3},{6,0},{7,1},{8,14},{9,15},{10,... | collective-permute-start | bytes 1474568 | tf_op jit(solution)/shard_map/ppermute | solution.py:857
  65.6 2.8 %collective-permute-done.19.arrived = bf16[1504,768]{1,0:T(8,128)(2,1)S(1)} collective-permute-done((bf16[1504,768]{1,0:T(8,128)(2,1)S(1)}, bf16[1504,768]{1,0:T(8,128)(2,1)S(1)}, u32[]{:S(2)}, u32[]{:S(2)}) %collective-permute-start.19) | collective-permute-done | bytes 2310176 | tf_op jit(solution)/shard_map/ppermute | solution.py:861
  68.5 0.6 shard_map.272
  69.6 8.9 %collective-permute-done.25.n3 = bf16[320,768]{1,0:T(8,128)(2,1)S(1)} collective-permute-done((bf16[320,768]{1,0:T(8,128)(2,1)S(1)}, bf16[320,768]{1,0:T(8,128)(2,1)S(1)}, u32[]{:S(2)}, u32[]{:S(2)}) %collective-permute-start.25) | collective-permute-done | bytes 491552 | tf_op jit(solution)/shard_map/ppermute | solution.py:857
  78.5 1.2 shard_map.275
  80.4 1.4 %collective-permute-start.20 = (bf16[352,768]{1,0:T(8,128)(2,1)S(1)}, bf16[352,768]{1,0:T(8,128)(2,1)S(1)}, u32[]{:S(2)}, u32[]{:S(2)}) collective-permute-start(bf16[352,768]{1,0:T(8,128)(2,1)S(1)} %get-tuple-element.173), channel_id=1, source_target_pairs={{0,2},{1,3},{2,0},{3,1},{4,6},{5,7},{6,4},{7,5},{8,10},{9,11},{10,... | collective-permute-start | bytes 1622024 | tf_op jit(solution)/shard_map/ppermute | solution.py:857
  81.8 0.9 collective-permute-start.21
  82.7 1.4 %collective-permute-start.22 = (bf16[352,768]{1,0:T(8,128)(2,1)S(1)}, bf16[352,768]{1,0:T(8,128)(2,1)S(1)}, u32[]{:S(2)}, u32[]{:S(2)}) collective-permute-start(bf16[352,768]{1,0:T(8,128)(2,1)S(1)} %get-tuple-element.175), channel_id=1, source_target_pairs={{0,6},{1,7},{2,4},{3,5},{4,2},{5,3},{6,0},{7,1},{8,14},{9,15},{10,... | collective-permute-start | bytes 1622024 | tf_op jit(solution)/shard_map/ppermute | solution.py:857
  84.9 2.6 %collective-permute-start.24 = (bf16[192,768]{1,0:T(8,128)(2,1)S(1)}, bf16[192,768]{1,0:T(8,128)(2,1)S(1)}, u32[]{:S(2)}, u32[]{:S(2)}) collective-permute-start(bf16[192,768]{1,0:T(8,128)(2,1)S(1)} %get-tuple-element.180.z_next), channel_id=1, source_target_pairs={{0,16},{8,24},{16,0},{24,8},{1,17},{9,25},{17,1},{25,9},{2,18},{10... | collective-permute-start | bytes 884744 | tf_op jit(solution)/shard_map/ppermute | solution.py:865
  87.6 11.6 %collective-permute-done.29.came = bf16[2,96,768]{2,1,0:T(8,128)(2,1)S(1)} collective-permute-done((bf16[2,96,768]{2,1,0:T(8,128)(2,1)S(1)}, bf16[2,96,768]{2,1,0:T(8,128)(2,1)S(1)}, u32[]{:S(2)}, u32[]{:S(2)}) %collective-permute-start.29) | collective-permute-done | bytes 294944 | tf_op jit(solution)/shard_map/ppermute | solution.py:865
  99.3 8.5 %collective-permute-done.21.x2 = bf16[352,768]{1,0:T(8,128)(2,1)S(1)} collective-permute-done((bf16[352,768]{1,0:T(8,128)(2,1)S(1)}, bf16[352,768]{1,0:T(8,128)(2,1)S(1)}, u32[]{:S(2)}, u32[]{:S(2)}) %collective-permute-start.21) | collective-permute-done | bytes 540704 | tf_op jit(solution)/shard_map/ppermute | solution.py:857
  107.9 2.7 %collective-permute-start.34 = (bf16[96,768]{1,0:T(8,128)(2,1)S(1)}, bf16[96,768]{1,0:T(8,128)(2,1)S(1)}, u32[]{:S(2)}, u32[]{:S(2)}) collective-permute-start(bf16[96,768]{1,0:T(8,128)(2,1)S(1)} %get-tuple-element.205), channel_id=1, source_target_pairs={{0,16},{8,24},{16,0},{24,8},{1,17},{9,25},{17,1},{25,9},{2,18},{10... | collective-permute-start | bytes 442376 | tf_op jit(solution)/shard_map/ppermute | solution.py:865
  110.8 0.9 collective-permute-start.31
  111.6 1.2 %collective-permute-start.32 = (bf16[96,768]{1,0:T(8,128)(2,1)S(1)}, bf16[96,768]{1,0:T(8,128)(2,1)S(1)}, u32[]{:S(2)}, u32[]{:S(2)}) collective-permute-start(bf16[96,768]{1,0:T(8,128)(2,1)S(1)} %get-tuple-element.193), channel_id=1, source_target_pairs={{0,4},{1,5},{2,6},{3,7},{4,0},{5,1},{6,2},{7,3},{8,12},{9,13},{10,... | collective-permute-start | bytes 442376 | tf_op jit(solution)/shard_map/ppermute | solution.py:857
  112.9 1.4 %collective-permute-start.33 = (bf16[96,768]{1,0:T(8,128)(2,1)S(1)}, bf16[96,768]{1,0:T(8,128)(2,1)S(1)}, u32[]{:S(2)}, u32[]{:S(2)}) collective-permute-start(bf16[96,768]{1,0:T(8,128)(2,1)S(1)} %get-tuple-element.194), channel_id=1, source_target_pairs={{0,6},{1,7},{2,4},{3,5},{4,2},{5,3},{6,0},{7,1},{8,14},{9,15},{10,... | collective-permute-start | bytes 442376 | tf_op jit(solution)/shard_map/ppermute | solution.py:857
  114.3 1.7 %shard_map.268 = bf16[160,767]{1,0:T(8,128)(2,1)} custom-call(bf16[320,768]{1,0:T(8,128)(2,1)S(1)} %get-tuple-element.134.act_keep, bf16[320,768]{1,0:T(8,128)(2,1)S(1)} %get-tuple-element.135.act_send, bf16[3072,767]{1,0:T(8,128)(2,1)S(1)} %bitcast.1, f32[160,767]{1,0:T(8,128)S(1)} %get-tuple-element.136.middle, f32[767]{0:T(1024)S(1)} %copy-done.12), custom_call_target="tpu_custom_call" | custom-call | flops 1000 | bytes 1000 | tf_op jit(solution)/shard_map/pallas_call | solution.py:364
  116.0 2.3 %shard_map.273 = bf16[160,767]{1,0:T(8,128)(2,1)} custom-call(bf16[352,768]{1,0:T(8,128)(2,1)S(1)} %get-tuple-element.172.x0, bf16[352,768]{1,0:T(8,128)(2,1)S(1)} %collective-permute-done.20.x1, bf16[352,768]{1,0:T(8,128)(2,1)S(1)} %collective-permute-done.21.x2, bf16[352,768]{1,0:T(8,128)(2,1)S(1)} %collective-permute-done.22.x3, ...), custom_call_target="tpu_custom_call" | custom-call | flops 1000 | bytes 1000 | tf_op jit(solution)/shard_map/pallas_call | solution.py:364
  118.3 0.7 shard_map.281
  119.0 0.8 collective-permute-done.32.f2
  119.8 1.5 %shard_map.279 = (f32[24,2304]{1,0:T(8,128)}, f32[24,3072]{1,0:T(8,128)}, f32[24,767]{1,0:T(8,128)}, f32[768]{0:T(1024)}, f32[768]{0:T(1024)}, /*index=5*/f32[76...) custom-call(s32[4,2]{1,0:T(4,128)S(1)} %copy.30.lengths, ...), custom_call_target="tpu_custom_call" | custom-call | flops 1000 | bytes 1000 | tf_op jit(solution)/shard_map/pallas_call | solution.py:364
  (84 shorter events, 4.8 us)
Async XLA Ops:
  0.7 8.7 %copy-start.13 = (s32[16]{0:T(128)S(1)}, s32[16]{0:T(128)}, u32[]{:S(2)}) copy-start(s32[16]{0:T(128)} %spans.1) | copy-start | bytes 196
  0.7 8.6 %copy-start.14 = (s32[1,2]{1,0:T(1,128)S(1)}, s32[1,2]{1,0:T(1,128)}, u32[]{:S(2)}) copy-start(s32[1,2]{1,0:T(1,128)} %offsets.1) | copy-start | bytes 28
  4.7 9.4 %collective-permute-start = (bf16[240,384]{1,0:T(8,128)(2,1)}, bf16[240,384]{1,0:T(8,128)(2,1)S(1)}, u32[]{:S(2)}, u32[]{:S(2)}) collective-permute-start(bf16[240,384]{1,0:T(8,128)(2,1)} %get-tuple-element.114), channel_id=1, source_target_pairs={{0,2},{1,3},{2,0},{3,1},{4,6},{5,7},{6,4},{7,5},{8,10},{9,11},{10,... | collective-permute-start | bytes 552968 | tf_op jit(solution)/shard_map/ppermute | solution.py:857
  7.7 10.3 %collective-permute-start.1 = (bf16[240,384]{1,0:T(8,128)(2,1)}, bf16[240,384]{1,0:T(8,128)(2,1)S(1)}, u32[]{:S(2)}, u32[]{:S(2)}) collective-permute-start(bf16[240,384]{1,0:T(8,128)(2,1)} %get-tuple-element.115), channel_id=1, source_target_pairs={{0,4},{1,5},{2,6},{3,7},{4,0},{5,1},{6,2},{7,3},{8,12},{9,13},{10,... | collective-permute-start | bytes 552968 | tf_op jit(solution)/shard_map/ppermute | solution.py:857
  9.2 8.7 %collective-permute-start.2 = (bf16[240,384]{1,0:T(8,128)(2,1)}, bf16[240,384]{1,0:T(8,128)(2,1)S(1)}, u32[]{:S(2)}, u32[]{:S(2)}) collective-permute-start(bf16[240,384]{1,0:T(8,128)(2,1)} %get-tuple-element.116), channel_id=1, source_target_pairs={{0,6},{1,7},{2,4},{3,5},{4,2},{5,3},{6,0},{7,1},{8,14},{9,15},{10,... | collective-permute-start | bytes 552968 | tf_op jit(solution)/shard_map/ppermute | solution.py:857
  18.4 3.6 %collective-permute-start.3 = (bf16[640,384]{1,0:T(8,128)(2,1)S(1)}, bf16[640,384]{1,0:T(8,128)(2,1)S(1)}, u32[]{:S(2)}, u32[]{:S(2)}) collective-permute-start(bf16[640,384]{1,0:T(8,128)(2,1)S(1)} %get-tuple-element.123.own), channel_id=1, source_target_pairs={{0,1},{1,0},{2,3},{3,2},{4,5},{5,4},{6,7},{7,6},{8,9},{9,8},{10,11... | collective-permute-start | bytes 1474568 | tf_op jit(solution)/shard_map/ppermute | solution.py:861
  18.5 12.4 %collective-permute-start.7 = (bf16[160,768]{1,0:T(8,128)(2,1)S(1)}, bf16[160,768]{1,0:T(8,128)(2,1)S(1)}, u32[]{:S(2)}, u32[]{:S(2)}) collective-permute-start(bf16[160,768]{1,0:T(8,128)(2,1)S(1)} %copy-done.5), channel_id=1, source_target_pairs={{0,2},{1,3},{2,0},{3,1},{4,6},{5,7},{6,4},{7,5},{8,10},{9,11},{10,... | collective-permute-start | bytes 737288 | tf_op jit(solution)/shard_map/ppermute | solution.py:857
  19.8 12.5 %collective-permute-start.8 = (bf16[160,768]{1,0:T(8,128)(2,1)S(1)}, bf16[160,768]{1,0:T(8,128)(2,1)S(1)}, u32[]{:S(2)}, u32[]{:S(2)}) collective-permute-start(bf16[160,768]{1,0:T(8,128)(2,1)S(1)} %copy-done.5), channel_id=1, source_target_pairs={{0,4},{1,5},{2,6},{3,7},{4,0},{5,1},{6,2},{7,3},{8,12},{9,13},{10,... | collective-permute-start | bytes 737288 | tf_op jit(solution)/shard_map/ppermute | solution.py:857
  20.6 13.3 %collective-permute-start.9 = (bf16[160,768]{1,0:T(8,128)(2,1)S(1)}, bf16[160,768]{1,0:T(8,128)(2,1)S(1)}, u32[]{:S(2)}, u32[]{:S(2)}) collective-permute-start(bf16[160,768]{1,0:T(8,128)(2,1)S(1)} %copy-done.5), channel_id=1, source_target_pairs={{0,6},{1,7},{2,4},{3,5},{4,2},{5,3},{6,0},{7,1},{8,14},{9,15},{10,... | collective-permute-start | bytes 737288 | tf_op jit(solution)/shard_map/ppermute | solution.py:857
  22.0 13.9 %slice-start.2 = ((s8[4718592]{0:T(1024)(128)(4,1)}), s8[4194304]{0:T(1024)(128)(4,1)S(1)}, s32[]{:S(2)}) async-start(s8[4718592]{0:T(1024)(128)(4,1)} %bitcast.2), calls=%async_computation.2 | async-start | bytes 8388608
  22.0 13.9 %slice-start.3 = ((s8[4718592]{0:T(1024)(128)(4,1)}), s8[524288]{0:T(1024)(128)(4,1)S(1)}, s32[]{:S(2)}) async-start(s8[4718592]{0:T(1024)(128)(4,1)} %bitcast.2), calls=%async_computation.3 | async-start | bytes 1048576
  22.0 13.9 %copy-start.3 = (bf16[160,767]{1,0:T(8,128)(2,1)S(1)}, bf16[160,767]{1,0:T(8,128)(2,1)}, u32[]{:S(2)}) copy-start(bf16[160,767]{1,0:T(8,128)(2,1)} %resid.3) | copy-start | bytes 736324
  22.0 13.9 %copy-start.4 = (bf16[768,767]{1,0:T(8,128)(2,1)S(1)}, bf16[768,767]{1,0:T(8,128)(2,1)}, u32[]{:S(2)}) copy-start(bf16[768,767]{1,0:T(8,128)(2,1)} %out_weight.1) | copy-start | bytes 3534340
  22.1 13.9 %copy-start.7 = (f32[160,1]{1,0:T(8,128)S(1)}, f32[160,1]{1,0:T(8,128)}, u32[]{:S(2)}) copy-start(f32[160,1]{1,0:T(8,128)} %get-tuple-element.133.root_in) | copy-start | bytes 1924
  22.1 13.9 %copy-start.9 = (f32[3072]{0:T(1024)S(1)}, f32[3072]{0:T(1024)}, u32[]{:S(2)}) copy-start(f32[3072]{0:T(1024)} %up_bias.1) | copy-start | bytes 36868
  22.1 13.9 %copy-start.10 = (f32[767]{0:T(1024)S(1)}, f32[767]{0:T(1024)}, u32[]{:S(2)}) copy-start(f32[767]{0:T(1024)} %out_bias.1) | copy-start | bytes 9208
  22.1 13.9 %copy-start.11 = (f32[768]{0:T(1024)S(1)}, f32[768]{0:T(1024)}, u32[]{:S(2)}) copy-start(f32[768]{0:T(1024)} %gain.3) | copy-start | bytes 9220
  28.7 5.1 %collective-permute-start.4 = (bf16[80,384]{1,0:T(8,128)(2,1)S(1)}, bf16[80,384]{1,0:T(8,128)(2,1)S(1)}, u32[]{:S(2)}, u32[]{:S(2)}) collective-permute-start(bf16[80,384]{1,0:T(8,128)(2,1)S(1)} %get-tuple-element.125), channel_id=1, source_target_pairs={{0,2},{1,3},{2,0},{3,1},{4,6},{5,7},{6,4},{7,5},{8,10},{9,11},{10,... | collective-permute-start | bytes 184328 | tf_op jit(solution)/shard_map/ppermute | solution.py:857
  30.0 4.8 %collective-permute-start.5 = (bf16[80,384]{1,0:T(8,128)(2,1)S(1)}, bf16[80,384]{1,0:T(8,128)(2,1)S(1)}, u32[]{:S(2)}, u32[]{:S(2)}) collective-permute-start(bf16[80,384]{1,0:T(8,128)(2,1)S(1)} %get-tuple-element.126), channel_id=1, source_target_pairs={{0,4},{1,5},{2,6},{3,7},{4,0},{5,1},{6,2},{7,3},{8,12},{9,13},{10,... | collective-permute-start | bytes 184328 | tf_op jit(solution)/shard_map/ppermute | solution.py:857
  30.9 5.1 %collective-permute-start.6 = (bf16[80,384]{1,0:T(8,128)(2,1)S(1)}, bf16[80,384]{1,0:T(8,128)(2,1)S(1)}, u32[]{:S(2)}, u32[]{:S(2)}) collective-permute-start(bf16[80,384]{1,0:T(8,128)(2,1)S(1)} %get-tuple-element.127), channel_id=1, source_target_pairs={{0,6},{1,7},{2,4},{3,5},{4,2},{5,3},{6,0},{7,1},{8,14},{9,15},{10,... | collective-permute-start | bytes 184328 | tf_op jit(solution)/shard_map/ppermute | solution.py:857
  32.3 18.0 %collective-permute-start.13 = (bf16[160,767]{1,0:T(8,128)(2,1)S(1)}, bf16[160,767]{1,0:T(8,128)(2,1)S(1)}, u32[]{:S(2)}, u32[]{:S(2)}) collective-permute-start(bf16[160,767]{1,0:T(8,128)(2,1)S(1)} %copy-done.2), channel_id=1, source_target_pairs={{0,8},{8,0},{16,24},{24,16},{1,9},{9,1},{17,25},{25,17},{2,10},{10... | collective-permute-start | bytes 736328 | tf_op jit(solution)/shard_map/ppermute | solution.py:865
  41.1 16.9 %collective-permute-start.14 = (bf16[320,768]{1,0:T(8,128)(2,1)S(1)}, bf16[320,768]{1,0:T(8,128)(2,1)S(1)}, u32[]{:S(2)}, u32[]{:S(2)}) collective-permute-start(bf16[320,768]{1,0:T(8,128)(2,1)S(1)} %get-tuple-element.135.act_send), channel_id=1, source_target_pairs={{0,8},{8,0},{16,24},{24,16},{1,9},{9,1},{17,25},{25,17},{2,10},{10... | collective-permute-start | bytes 1474568 | tf_op jit(solution)/shard_map/ppermute | solution.py:865
  42.8 4.2 %collective-permute-start.10 = (bf16[80,384]{1,0:T(8,128)(2,1)S(1)}, bf16[80,384]{1,0:T(8,128)(2,1)S(1)}, u32[]{:S(2)}, u32[]{:S(2)}) collective-permute-start(bf16[80,384]{1,0:T(8,128)(2,1)S(1)} %get-tuple-element.138), channel_id=1, source_target_pairs={{0,2},{1,3},{2,0},{3,1},{4,6},{5,7},{6,4},{7,5},{8,10},{9,11},{10,... | collective-permute-start | bytes 184328 | tf_op jit(solution)/shard_map/ppermute | solution.py:857
  44.3 4.2 %collective-permute-start.11 = (bf16[80,384]{1,0:T(8,128)(2,1)S(1)}, bf16[80,384]{1,0:T(8,128)(2,1)S(1)}, u32[]{:S(2)}, u32[]{:S(2)}) collective-permute-start(bf16[80,384]{1,0:T(8,128)(2,1)S(1)} %get-tuple-element.139), channel_id=1, source_target_pairs={{0,4},{1,5},{2,6},{3,7},{4,0},{5,1},{6,2},{7,3},{8,12},{9,13},{10,... | collective-permute-start | bytes 184328 | tf_op jit(solution)/shard_map/ppermute | solution.py:857
  44.8 5.5 %collective-permute-start.12 = (bf16[80,384]{1,0:T(8,128)(2,1)S(1)}, bf16[80,384]{1,0:T(8,128)(2,1)S(1)}, u32[]{:S(2)}, u32[]{:S(2)}) collective-permute-start(bf16[80,384]{1,0:T(8,128)(2,1)S(1)} %get-tuple-element.140), channel_id=1, source_target_pairs={{0,6},{1,7},{2,4},{3,5},{4,2},{5,3},{6,0},{7,1},{8,14},{9,15},{10,... | collective-permute-start | bytes 184328 | tf_op jit(solution)/shard_map/ppermute | solution.py:857
  50.3 10.2 %collective-permute-start.17 = (bf16[320,768]{1,0:T(8,128)(2,1)S(1)}, bf16[320,768]{1,0:T(8,128)(2,1)S(1)}, u32[]{:S(2)}, u32[]{:S(2)}) collective-permute-start(bf16[320,768]{1,0:T(8,128)(2,1)S(1)} %get-tuple-element.158), channel_id=1, source_target_pairs={{0,2},{1,3},{2,0},{3,1},{4,6},{5,7},{6,4},{7,5},{8,10},{9,11},{10,... | collective-permute-start | bytes 1474568 | tf_op jit(solution)/shard_map/ppermute | solution.py:857
  51.5 9.1 %collective-permute-start.18 = (bf16[320,768]{1,0:T(8,128)(2,1)S(1)}, bf16[320,768]{1,0:T(8,128)(2,1)S(1)}, u32[]{:S(2)}, u32[]{:S(2)}) collective-permute-start(bf16[320,768]{1,0:T(8,128)(2,1)S(1)} %get-tuple-element.159), channel_id=1, source_target_pairs={{0,4},{1,5},{2,6},{3,7},{4,0},{5,1},{6,2},{7,3},{8,12},{9,13},{10,... | collective-permute-start | bytes 1474568 | tf_op jit(solution)/shard_map/ppermute | solution.py:857
  58.0 2.5 %collective-permute-start.15 = (bf16[320,384]{1,0:T(8,128)(2,1)S(1)}, bf16[320,384]{1,0:T(8,128)(2,1)S(1)}, u32[]{:S(2)}, u32[]{:S(2)}) collective-permute-start(bf16[320,384]{1,0:T(8,128)(2,1)S(1)} %get-tuple-element.152), channel_id=1, source_target_pairs={{0,1},{1,0},{2,3},{3,2},{4,5},{5,4},{6,7},{7,6},{8,9},{9,8},{10,11... | collective-permute-start | bytes 737288 | tf_op jit(solution)/shard_map/ppermute | solution.py:861
  58.1 2.5 %collective-permute-start.16 = (bf16[320,384]{1,0:T(8,128)(2,1)S(1)}, bf16[320,384]{1,0:T(8,128)(2,1)S(1)}, u32[]{:S(2)}, u32[]{:S(2)}) collective-permute-start(bf16[320,384]{1,0:T(8,128)(2,1)S(1)} %get-tuple-element.153), channel_id=1, source_target_pairs={{0,1},{1,0},{2,3},{3,2},{4,5},{5,4},{6,7},{7,6},{8,9},{9,8},{10,11... | collective-permute-start | bytes 737288 | tf_op jit(solution)/shard_map/ppermute | solution.py:861
  63.9 4.5 %collective-permute-start.19 = (bf16[1504,768]{1,0:T(8,128)(2,1)S(1)}, bf16[1504,768]{1,0:T(8,128)(2,1)S(1)}, u32[]{:S(2)}, u32[]{:S(2)}) collective-permute-start(bf16[1504,768]{1,0:T(8,128)(2,1)S(1)} %get-tuple-element.167.send), channel_id=1, source_target_pairs={{0,1},{1,0},{2,3},{3,2},{4,5},{5,4},{6,7},{7,6},{8,9},{9,8},{10,11... | collective-permute-start | bytes 6930440 | tf_op jit(solution)/shard_map/ppermute | solution.py:861
  64.0 14.5 %collective-permute-start.25 = (bf16[320,768]{1,0:T(8,128)(2,1)S(1)}, bf16[320,768]{1,0:T(8,128)(2,1)S(1)}, u32[]{:S(2)}, u32[]{:S(2)}) collective-permute-start(bf16[320,768]{1,0:T(8,128)(2,1)S(1)} %get-tuple-element.182), channel_id=1, source_target_pairs={{0,6},{1,7},{2,4},{3,5},{4,2},{5,3},{6,0},{7,1},{8,14},{9,15},{10,... | collective-permute-start | bytes 1474568 | tf_op jit(solution)/shard_map/ppermute | solution.py:857
  68.5 45.9 %slice-start = ((s8[4718592]{0:T(1024)(128)(4,1)}), s8[524288]{0:T(1024)(128)(4,1)S(1)}, s32[]{:S(2)}) async-start(s8[4718592]{0:T(1024)(128)(4,1)} %bitcast), calls=%async_computation | async-start | bytes 1048576
  69.1 45.2 %slice-start.1 = ((s8[4718592]{0:T(1024)(128)(4,1)}), s8[4194304]{0:T(1024)(128)(4,1)S(1)}, s32[]{:S(2)}) async-start(s8[4718592]{0:T(1024)(128)(4,1)} %bitcast), calls=%async_computation.1 | async-start | bytes 8388608
  69.1 15.7 %collective-permute-start.23 = (bf16[368,768]{1,0:T(8,128)(2,1)S(1)}, bf16[368,768]{1,0:T(8,128)(2,1)S(1)}, u32[]{:S(2)}, u32[]{:S(2)}) collective-permute-start(bf16[368,768]{1,0:T(8,128)(2,1)S(1)} %get-tuple-element.178.z_send), channel_id=1, source_target_pairs={{0,8},{8,0},{16,24},{24,16},{1,9},{9,1},{17,25},{25,17},{2,10},{10... | collective-permute-start | bytes 1695752 | tf_op jit(solution)/shard_map/ppermute | solution.py:865
  79.8 2.1 %collective-permute-start.26 = (bf16[128,768]{1,0:T(8,128)(2,1)S(1)}, bf16[128,768]{1,0:T(8,128)(2,1)S(1)}, u32[]{:S(2)}, u32[]{:S(2)}) collective-permute-start(bf16[128,768]{1,0:T(8,128)(2,1)S(1)} %get-tuple-element.184), channel_id=1, source_target_pairs={{0,1},{1,0},{2,3},{3,2},{4,5},{5,4},{6,7},{7,6},{8,9},{9,8},{10,11... | collective-permute-start | bytes 589832 | tf_op jit(solution)/shard_map/ppermute | solution.py:861
  79.8 2.8 %collective-permute-start.27 = (bf16[128,768]{1,0:T(8,128)(2,1)S(1)}, bf16[128,768]{1,0:T(8,128)(2,1)S(1)}, u32[]{:S(2)}, u32[]{:S(2)}) collective-permute-start(bf16[128,768]{1,0:T(8,128)(2,1)S(1)} %get-tuple-element.185), channel_id=1, source_target_pairs={{0,1},{1,0},{2,3},{3,2},{4,5},{5,4},{6,7},{7,6},{8,9},{9,8},{10,11... | collective-permute-start | bytes 589832 | tf_op jit(solution)/shard_map/ppermute | solution.py:861
  80.3 3.8 %collective-permute-start.28 = (bf16[128,768]{1,0:T(8,128)(2,1)S(1)}, bf16[128,768]{1,0:T(8,128)(2,1)S(1)}, u32[]{:S(2)}, u32[]{:S(2)}) collective-permute-start(bf16[128,768]{1,0:T(8,128)(2,1)S(1)} %get-tuple-element.186), channel_id=1, source_target_pairs={{0,1},{1,0},{2,3},{3,2},{4,5},{5,4},{6,7},{7,6},{8,9},{9,8},{10,11... | collective-permute-start | bytes 589832 | tf_op jit(solution)/shard_map/ppermute | solution.py:861
  80.4 18.9 %collective-permute-start.20 = (bf16[352,768]{1,0:T(8,128)(2,1)S(1)}, bf16[352,768]{1,0:T(8,128)(2,1)S(1)}, u32[]{:S(2)}, u32[]{:S(2)}) collective-permute-start(bf16[352,768]{1,0:T(8,128)(2,1)S(1)} %get-tuple-element.173), channel_id=1, source_target_pairs={{0,2},{1,3},{2,0},{3,1},{4,6},{5,7},{6,4},{7,5},{8,10},{9,11},{10,... | collective-permute-start | bytes 1622024 | tf_op jit(solution)/shard_map/ppermute | solution.py:857
  81.8 25.9 %collective-permute-start.21 = (bf16[352,768]{1,0:T(8,128)(2,1)S(1)}, bf16[352,768]{1,0:T(8,128)(2,1)S(1)}, u32[]{:S(2)}, u32[]{:S(2)}) collective-permute-start(bf16[352,768]{1,0:T(8,128)(2,1)S(1)} %get-tuple-element.174), channel_id=1, source_target_pairs={{0,4},{1,5},{2,6},{3,7},{4,0},{5,1},{6,2},{7,3},{8,12},{9,13},{10,... | collective-permute-start | bytes 1622024 | tf_op jit(solution)/shard_map/ppermute | solution.py:857
  82.7 25.1 %collective-permute-start.22 = (bf16[352,768]{1,0:T(8,128)(2,1)S(1)}, bf16[352,768]{1,0:T(8,128)(2,1)S(1)}, u32[]{:S(2)}, u32[]{:S(2)}) collective-permute-start(bf16[352,768]{1,0:T(8,128)(2,1)S(1)} %get-tuple-element.175), channel_id=1, source_target_pairs={{0,6},{1,7},{2,4},{3,5},{4,2},{5,3},{6,0},{7,1},{8,14},{9,15},{10,... | collective-permute-start | bytes 1622024 | tf_op jit(solution)/shard_map/ppermute | solution.py:857
  84.3 14.9 %collective-permute-start.29 = (bf16[2,96,768]{2,1,0:T(8,128)(2,1)S(1)}, bf16[2,96,768]{2,1,0:T(8,128)(2,1)S(1)}, u32[]{:S(2)}, u32[]{:S(2)}) collective-permute-start(bf16[2,96,768]{2,1,0:T(8,128)(2,1)S(1)} %get-tuple-element.188), channel_id=1, source_target_pairs={{0,8},{8,0},{16,24},{24,16},{1,9},{9,1},{17,25},{25,17},{2,10},{10... | collective-permute-start | bytes 884744 | tf_op jit(solution)/shard_map/ppermute | solution.py:865
  84.9 29.4 %copy-start.12 = (f32[767]{0:T(1024)S(1)}, f32[767]{0:T(1024)}, u32[]{:S(2)}) copy-start(f32[767]{0:T(1024)} %bias.1) | copy-start | bytes 9208
  84.9 25.6 %collective-permute-start.24 = (bf16[192,768]{1,0:T(8,128)(2,1)S(1)}, bf16[192,768]{1,0:T(8,128)(2,1)S(1)}, u32[]{:S(2)}, u32[]{:S(2)}) collective-permute-start(bf16[192,768]{1,0:T(8,128)(2,1)S(1)} %get-tuple-element.180.z_next), channel_id=1, source_target_pairs={{0,16},{8,24},{16,0},{24,8},{1,17},{9,25},{17,1},{25,9},{2,18},{10... | collective-permute-start | bytes 884744 | tf_op jit(solution)/shard_map/ppermute | solution.py:865
  99.2 11.4 %collective-permute-start.30 = (bf16[96,768]{1,0:T(8,128)(2,1)S(1)}, bf16[96,768]{1,0:T(8,128)(2,1)S(1)}, u32[]{:S(2)}, u32[]{:S(2)}) collective-permute-start(bf16[96,768]{1,0:T(8,128)(2,1)S(1)} %get-tuple-element.190), channel_id=1, source_target_pairs={{0,16},{8,24},{16,0},{24,8},{1,17},{9,25},{17,1},{25,9},{2,18},{10... | collective-permute-start | bytes 442376 | tf_op jit(solution)/shard_map/ppermute | solution.py:865
  107.9 10.4 %collective-permute-start.34 = (bf16[96,768]{1,0:T(8,128)(2,1)S(1)}, bf16[96,768]{1,0:T(8,128)(2,1)S(1)}, u32[]{:S(2)}, u32[]{:S(2)}) collective-permute-start(bf16[96,768]{1,0:T(8,128)(2,1)S(1)} %get-tuple-element.205), channel_id=1, source_target_pairs={{0,16},{8,24},{16,0},{24,8},{1,17},{9,25},{17,1},{25,9},{2,18},{10... | collective-permute-start | bytes 442376 | tf_op jit(solution)/shard_map/ppermute | solution.py:865
  110.8 8.3 %collective-permute-start.31 = (bf16[96,768]{1,0:T(8,128)(2,1)S(1)}, bf16[96,768]{1,0:T(8,128)(2,1)S(1)}, u32[]{:S(2)}, u32[]{:S(2)}) collective-permute-start(bf16[96,768]{1,0:T(8,128)(2,1)S(1)} %get-tuple-element.192), channel_id=1, source_target_pairs={{0,2},{1,3},{2,0},{3,1},{4,6},{5,7},{6,4},{7,5},{8,10},{9,11},{10,... | collective-permute-start | bytes 442376 | tf_op jit(solution)/shard_map/ppermute | solution.py:857
  111.6 8.2 %collective-permute-start.32 = (bf16[96,768]{1,0:T(8,128)(2,1)S(1)}, bf16[96,768]{1,0:T(8,128)(2,1)S(1)}, u32[]{:S(2)}, u32[]{:S(2)}) collective-permute-start(bf16[96,768]{1,0:T(8,128)(2,1)S(1)} %get-tuple-element.193), channel_id=1, source_target_pairs={{0,4},{1,5},{2,6},{3,7},{4,0},{5,1},{6,2},{7,3},{8,12},{9,13},{10,... | collective-permute-start | bytes 442376 | tf_op jit(solution)/shard_map/ppermute | solution.py:857
  112.9 6.9 %collective-permute-start.33 = (bf16[96,768]{1,0:T(8,128)(2,1)S(1)}, bf16[96,768]{1,0:T(8,128)(2,1)S(1)}, u32[]{:S(2)}, u32[]{:S(2)}) collective-permute-start(bf16[96,768]{1,0:T(8,128)(2,1)S(1)} %get-tuple-element.194), channel_id=1, source_target_pairs={{0,6},{1,7},{2,4},{3,5},{4,2},{5,3},{6,0},{7,1},{8,14},{9,15},{10,... | collective-permute-start | bytes 442376 | tf_op jit(solution)/shard_map/ppermute | solution.py:857
  (7 other events, 41.4 us)

commit v6 on v5

--- a/solution.py
+++ b/solution.py
@@ -713,8 +713,9 @@
         x[0:192, :] = (keep_x[r].astype(wide) + arrived[r * 192 : (r + 1) * 192, :].astype(wide)).astype(low)
         x[192:272, 0:384] = h[0:80, :]
         x[192:272, 384:768] = h[80:160, :]
-        x[272:352, 0:384] = h[160:240, :]
-        x[272:352, 384:768] = jnp.zeros((80, 384), low)
+        v = h[160:240, :].astype(wide)
+        v = jnp.concatenate([v[:40], v[40:]], axis=1)
+        x[272:320, :] = jnp.concatenate([v, jnp.zeros((8, D), wide)], axis=0).astype(low)
         came = arrived[768 + r * 176 : 944 + r * 176, :].astype(wide)
         blocks.append(keep_z[r] + came[0:168])
     z_keep[0:168, :] = blocks[0]
@@ -827,7 +828,8 @@
     for r, x in enumerate((x0, x1, x2, x3)):
         buf[r ^ me, 0:80, :] = x[192:272, 0:384]
         buf[r ^ me, 80:160, :] = x[192:272, 384:768]
-        buf[r ^ me, 160:240, :] = x[272:352, 0:384]
+        v = x[272:320, :].astype(wide)
+        buf[r ^ me, 160:240, :] = jnp.concatenate([v[:40, :384], v[:40, 384:]], axis=0).astype(low)
     e = jnp.zeros((160, D), wide)
     for i in range(3):
         g = jnp.concatenate([unpacked(buf[j, i * 80 : (i + 1) * 80, :]) for j in range(4)], axis=1)
@@ -990,7 +992,7 @@
     keep_x, keep_z, send = outs[4:]
     outs = call(
         late_sum_kernel,
-        [((352, D), low)] * 4 + [((336, D), wide), ((368, D), low)],
+        [((320, D), low)] * 4 + [((336, D), wide), ((368, D), low)],
         [keep_x, keep_z, send, swap_core(send)] + homes,
     )
     home = exchange(outs[:4])

time: 122 us -> 120 us (0.984)
  waiting for transfers between devices: 44.2 us -> 42.2 us
    ppermute x21, waiting for transfers between devices: 29.7 us -> 27.7 us  [swap_chip(): return lax.ppermute(block, 'blk', [(k, k ^ 2 * step) for k in range(8)])]
  transfers between devices with their start and end apart: 35 -> 35, of which waited for: 13 -> 13; matrix products, arithmetic and copies ran while one was open for 0% -> 0% of each run, Pallas kernels for 22% -> 23%
where the time goes in v6:
time: 120 us; the launch traced here: 119 us
  waiting for transfers between devices  42.2 us (35%)
  starting transfers between devices  37.1 us (31%)
  Pallas kernels  36.5 us (30%)
  local copies, waits for them, and re-layouts  2.52 us (2%)
    pallas_call x19, Pallas kernels, call(): pl.pallas_call(kernel, out_shape=shapes, in_specs=[SMEM if i < small else...  36.5 us
    ppermute x21, waiting for transfers between devices, swap_chip(): return lax.ppermute(block, 'blk', [(k, k ^ 2 * step) for k in range(8)])  27.7 us
    ppermute x21, starting transfers between devices, swap_chip(): return lax.ppermute(block, 'blk', [(k, k ^ 2 * step) for k in range(8)])  26 us
    ppermute x7, waiting for transfers between devices, shift_bucket(): return lax.ppermute(block, 'bucket', [(b, b ^ step) for b in range(4)])  11.6 us
    ppermute x7, starting transfers between devices, shift_bucket(): return lax.ppermute(block, 'bucket', [(b, b ^ step) for b in range(4)])  9.67 us
    ppermute x7, waiting for transfers between devices, swap_core(): return lax.ppermute(block, 'blk', [(k, k ^ 1) for k in range(8)])  2.89 us
    unnamed x41, local copies, waits for them, and re-layouts  2.52 us
  transfers between devices with their start and end apart: 35, of which 13 were waited for; matrix products, arithmetic and copies ran while one was open for 0% of the time, Pallas kernels for 23%

profile of v6, /device:TPU:0, one launch (start us, length us, event | category | flops | bytes accessed | tf_op | source)
XLA Modules:
  0.0 119.4 jit_solution(15718500735445608540)
XLA Ops:
  0.7 4.0 %shard_map.264 = (bf16[240,384]{1,0:T(8,128)(2,1)}, bf16[240,384]{1,0:T(8,128)(2,1)}, bf16[240,384]{1,0:T(8,128)(2,1)}, bf16[240,384]{1,0:T(8,128)(2,1)}, bf16[160,768]{1,0:T(8,128)(2,1)}, /*index=5*/f32[160,1]{1,0:T(8,128)}) custom-call(bf16[160,767]{1,0:T(8,128)(2,1)} %resid.3, f32[768]{0:T(1024)} %gain.5, bf16[768,2304]{1,0:T(8,128)(2,1)} %weight.6, ...), custom_call_target="tpu_custom_call" | custom-call | flops 1000 | bytes 1000 | tf_op jit(solution)/shard_map/pallas_call | solution.py:364
  4.7 3.0 %collective-permute-start = (bf16[240,384]{1,0:T(8,128)(2,1)}, bf16[240,384]{1,0:T(8,128)(2,1)S(1)}, u32[]{:S(2)}, u32[]{:S(2)}) collective-permute-start(bf16[240,384]{1,0:T(8,128)(2,1)} %get-tuple-element.114), channel_id=1, source_target_pairs={{0,2},{1,3},{2,0},{3,1},{4,6},{5,7},{6,4},{7,5},{8,10},{9,11},{10,... | collective-permute-start | bytes 552968 | tf_op jit(solution)/shard_map/ppermute | solution.py:859
  7.7 1.5 %collective-permute-start.1 = (bf16[240,384]{1,0:T(8,128)(2,1)}, bf16[240,384]{1,0:T(8,128)(2,1)S(1)}, u32[]{:S(2)}, u32[]{:S(2)}) collective-permute-start(bf16[240,384]{1,0:T(8,128)(2,1)} %get-tuple-element.115), channel_id=1, source_target_pairs={{0,4},{1,5},{2,6},{3,7},{4,0},{5,1},{6,2},{7,3},{8,12},{9,13},{10,... | collective-permute-start | bytes 552968 | tf_op jit(solution)/shard_map/ppermute | solution.py:859
  9.3 2.3 %copy-done.1 = bf16[3072,767]{1,0:T(8,128)(2,1)S(1)} copy-done((bf16[3072,767]{1,0:T(8,128)(2,1)S(1)}, bf16[3072,767]{1,0:T(8,128)(2,1)}, u32[]{:S(2)}) %copy-start.1) | copy-done | bytes 4712472
  11.7 2.4 %shard_map.263 = (f32[160,3072]{1,0:T(8,128)S(1)}, s32[640,2]{1,0:T(8,128)S(1)}, s32[1,1280]{1,0:T(1,128)S(1)}) custom-call(s32[16]{0:T(128)S(1)} %copy-done.13, s32[1,2]{1,0:T(1,128)S(1)} %copy-done.14, s32[4,2]{1,0:T(4,128)S(1)} %copy.30.lengths, bf16[160,767]{1,0:T(8,128)(2,1)S(1)} %copy-done.2, bf16[3072,767]{1,0:T(8,128)(2,1)S(1)} %copy-done.1), custom_call_target="tpu_custom_call" | custom-call | flops 1000 | bytes 1000 | tf_op jit(solution)/shard_map/pallas_call | solution.py:364
  14.1 3.9 %collective-permute-done.1.p2 = bf16[240,384]{1,0:T(8,128)(2,1)S(1)} collective-permute-done((bf16[240,384]{1,0:T(8,128)(2,1)}, bf16[240,384]{1,0:T(8,128)(2,1)S(1)}, u32[]{:S(2)}, u32[]{:S(2)}) %collective-permute-start.1) | collective-permute-done | bytes 184352 | tf_op jit(solution)/shard_map/ppermute | solution.py:859
  18.5 1.3 %collective-permute-start.7 = (bf16[160,768]{1,0:T(8,128)(2,1)S(1)}, bf16[160,768]{1,0:T(8,128)(2,1)S(1)}, u32[]{:S(2)}, u32[]{:S(2)}) collective-permute-start(bf16[160,768]{1,0:T(8,128)(2,1)S(1)} %copy-done.5), channel_id=1, source_target_pairs={{0,2},{1,3},{2,0},{3,1},{4,6},{5,7},{6,4},{7,5},{8,10},{9,11},{10,... | collective-permute-start | bytes 737288 | tf_op jit(solution)/shard_map/ppermute | solution.py:859
  19.8 0.8 collective-permute-start.8
  20.6 1.4 %collective-permute-start.9 = (bf16[160,768]{1,0:T(8,128)(2,1)S(1)}, bf16[160,768]{1,0:T(8,128)(2,1)S(1)}, u32[]{:S(2)}, u32[]{:S(2)}) collective-permute-start(bf16[160,768]{1,0:T(8,128)(2,1)S(1)} %copy-done.5), channel_id=1, source_target_pairs={{0,6},{1,7},{2,4},{3,5},{4,2},{5,3},{6,0},{7,1},{8,14},{9,15},{10,... | collective-permute-start | bytes 737288 | tf_op jit(solution)/shard_map/ppermute | solution.py:859
  22.1 6.6 %shard_map.266 = (bf16[3,640,1280]{2,1,0:T(8,128)(2,1)S(1)}, f32[640,192]{1,0:T(8,128)S(1)}, bf16[80,384]{1,0:T(8,128)(2,1)S(1)}, bf16[80,384]{1,0:T(8,128)(2,1)...) custom-call(s32[640,2]{1,0:T(8,128)S(1)} %get-tuple-element.111.bounds, ...), custom_call_target="tpu_custom_call" | custom-call | flops 7700000768 | bytes 1000 | tf_op jit(solution)/shard_map/pallas_call | solution.py:364
  28.7 1.3 %collective-permute-start.4 = (bf16[80,384]{1,0:T(8,128)(2,1)S(1)}, bf16[80,384]{1,0:T(8,128)(2,1)S(1)}, u32[]{:S(2)}, u32[]{:S(2)}) collective-permute-start(bf16[80,384]{1,0:T(8,128)(2,1)S(1)} %get-tuple-element.125), channel_id=1, source_target_pairs={{0,2},{1,3},{2,0},{3,1},{4,6},{5,7},{6,4},{7,5},{8,10},{9,11},{10,... | collective-permute-start | bytes 184328 | tf_op jit(solution)/shard_map/ppermute | solution.py:859
  30.0 0.8 collective-permute-start.5
  30.9 1.4 %collective-permute-start.6 = (bf16[80,384]{1,0:T(8,128)(2,1)S(1)}, bf16[80,384]{1,0:T(8,128)(2,1)S(1)}, u32[]{:S(2)}, u32[]{:S(2)}) collective-permute-start(bf16[80,384]{1,0:T(8,128)(2,1)S(1)} %get-tuple-element.127), channel_id=1, source_target_pairs={{0,6},{1,7},{2,4},{3,5},{4,2},{5,3},{6,0},{7,1},{8,14},{9,15},{10,... | collective-permute-start | bytes 184328 | tf_op jit(solution)/shard_map/ppermute | solution.py:859
  32.3 1.6 %collective-permute-start.13 = (bf16[160,767]{1,0:T(8,128)(2,1)S(1)}, bf16[160,767]{1,0:T(8,128)(2,1)S(1)}, u32[]{:S(2)}, u32[]{:S(2)}) collective-permute-start(bf16[160,767]{1,0:T(8,128)(2,1)S(1)} %copy-done.2), channel_id=1, source_target_pairs={{0,8},{8,0},{16,24},{24,16},{1,9},{9,1},{17,25},{25,17},{2,10},{10... | collective-permute-start | bytes 736328 | tf_op jit(solution)/shard_map/ppermute | solution.py:867
  33.9 1.0 collective-permute-done.5.p2
  34.8 1.1 collective-permute-done.6.p3
  36.0 5.1 %shard_map.267 = (bf16[80,384]{1,0:T(8,128)(2,1)S(1)}, bf16[80,384]{1,0:T(8,128)(2,1)S(1)}, bf16[80,384]{1,0:T(8,128)(2,1)S(1)}, bf16[80,384]{1,0:T(8,128)(2,1)S...) custom-call(s32[640,2]{1,0:T(8,128)S(1)} %get-tuple-element.111.boun, ...), custom_call_target="tpu_custom_call" | custom-call | flops 1000 | bytes 1000 | tf_op jit(solution)/shard_map/pallas_call | solution.py:364
  41.1 1.6 %collective-permute-start.14 = (bf16[320,768]{1,0:T(8,128)(2,1)S(1)}, bf16[320,768]{1,0:T(8,128)(2,1)S(1)}, u32[]{:S(2)}, u32[]{:S(2)}) collective-permute-start(bf16[320,768]{1,0:T(8,128)(2,1)S(1)} %get-tuple-element.135.act_send), channel_id=1, source_target_pairs={{0,8},{8,0},{16,24},{24,16},{1,9},{9,1},{17,25},{25,17},{2,10},{10... | collective-permute-start | bytes 1474568 | tf_op jit(solution)/shard_map/ppermute | solution.py:867
  42.8 1.5 %collective-permute-start.10 = (bf16[80,384]{1,0:T(8,128)(2,1)S(1)}, bf16[80,384]{1,0:T(8,128)(2,1)S(1)}, u32[]{:S(2)}, u32[]{:S(2)}) collective-permute-start(bf16[80,384]{1,0:T(8,128)(2,1)S(1)} %get-tuple-element.138), channel_id=1, source_target_pairs={{0,2},{1,3},{2,0},{3,1},{4,6},{5,7},{6,4},{7,5},{8,10},{9,11},{10,... | collective-permute-start | bytes 184328 | tf_op jit(solution)/shard_map/ppermute | solution.py:859
  44.8 1.5 %collective-permute-start.12 = (bf16[80,384]{1,0:T(8,128)(2,1)S(1)}, bf16[80,384]{1,0:T(8,128)(2,1)S(1)}, u32[]{:S(2)}, u32[]{:S(2)}) collective-permute-start(bf16[80,384]{1,0:T(8,128)(2,1)S(1)} %get-tuple-element.140), channel_id=1, source_target_pairs={{0,6},{1,7},{2,4},{3,5},{4,2},{5,3},{6,0},{7,1},{8,14},{9,15},{10,... | collective-permute-start | bytes 184328 | tf_op jit(solution)/shard_map/ppermute | solution.py:859
  46.2 0.7 collective-permute-done.10.d1
  47.0 1.5 %collective-permute-done.11.d2 = bf16[80,384]{1,0:T(8,128)(2,1)S(1)} collective-permute-done((bf16[80,384]{1,0:T(8,128)(2,1)S(1)}, bf16[80,384]{1,0:T(8,128)(2,1)S(1)}, u32[]{:S(2)}, u32[]{:S(2)}) %collective-permute-start.11) | collective-permute-done | bytes 61472 | tf_op jit(solution)/shard_map/ppermute | solution.py:859
  48.5 1.8 %collective-permute-done.12.d3 = bf16[80,384]{1,0:T(8,128)(2,1)S(1)} collective-permute-done((bf16[80,384]{1,0:T(8,128)(2,1)S(1)}, bf16[80,384]{1,0:T(8,128)(2,1)S(1)}, u32[]{:S(2)}, u32[]{:S(2)}) %collective-permute-start.12) | collective-permute-done | bytes 61472 | tf_op jit(solution)/shard_map/ppermute | solution.py:859
  50.3 1.2 collective-permute-start.17
  51.5 0.9 collective-permute-start.18
  52.3 5.6 %shard_map.269 = (bf16[640,192]{1,0:T(8,128)(2,1)S(1)}, f32[640,384]{1,0:T(8,128)S(1)}, bf16[320,384]{1,0:T(8,128)(2,1)S(1)}, bf16[320,384]{1,0:T(8,128)(2,1)S(1)}) custom-call(bf16[80,384]{1,0:T(8,128)(2,1)S(1)} %get-tuple-element.142.d0, bf16[80,384]{1,0:T(8,128)(2,1)S(1)} %collective-permute-done.10.d1, bf16[80,384]{1,0:T(8,128)(2,1)S(1)} %collective-permute-done.11.d2, ...), custom_call_target="tpu_custom_call" | custom-call | flops 1000 | bytes 1000 | tf_op jit(solution)/shard_map/pallas_call | solution.py:364
  59.0 1.5 %collective-permute-done.17.n1 = bf16[320,768]{1,0:T(8,128)(2,1)S(1)} collective-permute-done((bf16[320,768]{1,0:T(8,128)(2,1)S(1)}, bf16[320,768]{1,0:T(8,128)(2,1)S(1)}, u32[]{:S(2)}, u32[]{:S(2)}) %collective-permute-start.17) | collective-permute-done | bytes 491552 | tf_op jit(solution)/shard_map/ppermute | solution.py:859
  60.6 3.3 %shard_map.271 = (bf16[240,384]{1,0:T(8,128)(2,1)S(1)}, bf16[240,384]{1,0:T(8,128)(2,1)S(1)}, bf16[240,384]{1,0:T(8,128)(2,1)S(1)}, bf16[240,384]{1,0:T(8,128)(2...) custom-call(bf16[640,192]{1,0:T(8,128)(2,1)S(1)} %get-tuple-element.148.query_g, ...), custom_call_target="tpu_custom_call" | custom-call | flops 1000 | bytes 1000 | tf_op jit(solution)/shard_map/pallas_call | solution.py:364
  64.0 1.6 %collective-permute-start.25 = (bf16[320,768]{1,0:T(8,128)(2,1)S(1)}, bf16[320,768]{1,0:T(8,128)(2,1)S(1)}, u32[]{:S(2)}, u32[]{:S(2)}) collective-permute-start(bf16[320,768]{1,0:T(8,128)(2,1)S(1)} %get-tuple-element.182), channel_id=1, source_target_pairs={{0,6},{1,7},{2,4},{3,5},{4,2},{5,3},{6,0},{7,1},{8,14},{9,15},{10,... | collective-permute-start | bytes 1474568 | tf_op jit(solution)/shard_map/ppermute | solution.py:859
  65.6 2.9 %collective-permute-done.19.arrived = bf16[1504,768]{1,0:T(8,128)(2,1)S(1)} collective-permute-done((bf16[1504,768]{1,0:T(8,128)(2,1)S(1)}, bf16[1504,768]{1,0:T(8,128)(2,1)S(1)}, u32[]{:S(2)}, u32[]{:S(2)}) %collective-permute-start.19) | collective-permute-done | bytes 2310176 | tf_op jit(solution)/shard_map/ppermute | solution.py:863
  68.5 0.6 shard_map.272
  69.6 9.0 %collective-permute-done.25.n3 = bf16[320,768]{1,0:T(8,128)(2,1)S(1)} collective-permute-done((bf16[320,768]{1,0:T(8,128)(2,1)S(1)}, bf16[320,768]{1,0:T(8,128)(2,1)S(1)}, u32[]{:S(2)}, u32[]{:S(2)}) %collective-permute-start.25) | collective-permute-done | bytes 491552 | tf_op jit(solution)/shard_map/ppermute | solution.py:859
  78.5 1.2 %shard_map.275 = (bf16[4,96,768]{2,1,0:T(8,128)(2,1)S(1)}, bf16[128,768]{1,0:T(8,128)(2,1)S(1)}, bf16[128,768]{1,0:T(8,128)(2,1)S(1)}, bf16[128,768]{1,0:T(8,128)(2,1)S(1)}) custom-call(bf16[320,768]{1,0:T(8,128)(2,1)S(1)} %get-tuple-element.181.n0, bf16[320,768]{1,0:T(8,128)(2,1)S(1)} %collective-permute-done.17.n1, ...), custom_call_target="tpu_custom_call" | custom-call | flops 1000 | bytes 1000 | tf_op jit(solution)/shard_map/pallas_call | solution.py:364
  80.4 1.4 %collective-permute-start.20 = (bf16[320,768]{1,0:T(8,128)(2,1)S(1)}, bf16[320,768]{1,0:T(8,128)(2,1)S(1)}, u32[]{:S(2)}, u32[]{:S(2)}) collective-permute-start(bf16[320,768]{1,0:T(8,128)(2,1)S(1)} %get-tuple-element.173), channel_id=1, source_target_pairs={{0,2},{1,3},{2,0},{3,1},{4,6},{5,7},{6,4},{7,5},{8,10},{9,11},{10,... | collective-permute-start | bytes 1474568 | tf_op jit(solution)/shard_map/ppermute | solution.py:859
  81.8 0.9 collective-permute-start.21
  82.7 1.4 %collective-permute-start.22 = (bf16[320,768]{1,0:T(8,128)(2,1)S(1)}, bf16[320,768]{1,0:T(8,128)(2,1)S(1)}, u32[]{:S(2)}, u32[]{:S(2)}) collective-permute-start(bf16[320,768]{1,0:T(8,128)(2,1)S(1)} %get-tuple-element.175), channel_id=1, source_target_pairs={{0,6},{1,7},{2,4},{3,5},{4,2},{5,3},{6,0},{7,1},{8,14},{9,15},{10,... | collective-permute-start | bytes 1474568 | tf_op jit(solution)/shard_map/ppermute | solution.py:859
  84.9 2.6 %collective-permute-start.24 = (bf16[192,768]{1,0:T(8,128)(2,1)S(1)}, bf16[192,768]{1,0:T(8,128)(2,1)S(1)}, u32[]{:S(2)}, u32[]{:S(2)}) collective-permute-start(bf16[192,768]{1,0:T(8,128)(2,1)S(1)} %get-tuple-element.180.z_next), channel_id=1, source_target_pairs={{0,16},{8,24},{16,0},{24,8},{1,17},{9,25},{17,1},{25,9},{2,18},{10... | collective-permute-start | bytes 884744 | tf_op jit(solution)/shard_map/ppermute | solution.py:867
  87.6 11.6 %collective-permute-done.29.came = bf16[2,96,768]{2,1,0:T(8,128)(2,1)S(1)} collective-permute-done((bf16[2,96,768]{2,1,0:T(8,128)(2,1)S(1)}, bf16[2,96,768]{2,1,0:T(8,128)(2,1)S(1)}, u32[]{:S(2)}, u32[]{:S(2)}) %collective-permute-start.29) | collective-permute-done | bytes 294944 | tf_op jit(solution)/shard_map/ppermute | solution.py:867
  99.3 6.4 %collective-permute-done.21.x2 = bf16[320,768]{1,0:T(8,128)(2,1)S(1)} collective-permute-done((bf16[320,768]{1,0:T(8,128)(2,1)S(1)}, bf16[320,768]{1,0:T(8,128)(2,1)S(1)}, u32[]{:S(2)}, u32[]{:S(2)}) %collective-permute-start.21) | collective-permute-done | bytes 491552 | tf_op jit(solution)/shard_map/ppermute | solution.py:859
  105.8 2.7 %collective-permute-start.34 = (bf16[96,768]{1,0:T(8,128)(2,1)S(1)}, bf16[96,768]{1,0:T(8,128)(2,1)S(1)}, u32[]{:S(2)}, u32[]{:S(2)}) collective-permute-start(bf16[96,768]{1,0:T(8,128)(2,1)S(1)} %get-tuple-element.205), channel_id=1, source_target_pairs={{0,16},{8,24},{16,0},{24,8},{1,17},{9,25},{17,1},{25,9},{2,18},{10... | collective-permute-start | bytes 442376 | tf_op jit(solution)/shard_map/ppermute | solution.py:867
  108.7 0.9 collective-permute-start.31
  109.6 1.2 collective-permute-start.32
  110.7 1.5 %collective-permute-start.33 = (bf16[96,768]{1,0:T(8,128)(2,1)S(1)}, bf16[96,768]{1,0:T(8,128)(2,1)S(1)}, u32[]{:S(2)}, u32[]{:S(2)}) collective-permute-start(bf16[96,768]{1,0:T(8,128)(2,1)S(1)} %get-tuple-element.194), channel_id=1, source_target_pairs={{0,6},{1,7},{2,4},{3,5},{4,2},{5,3},{6,0},{7,1},{8,14},{9,15},{10,... | collective-permute-start | bytes 442376 | tf_op jit(solution)/shard_map/ppermute | solution.py:859
  112.2 1.7 %shard_map.268 = bf16[160,767]{1,0:T(8,128)(2,1)} custom-call(bf16[320,768]{1,0:T(8,128)(2,1)S(1)} %get-tuple-element.134.act_keep, bf16[320,768]{1,0:T(8,128)(2,1)S(1)} %get-tuple-element.135.act_send, bf16[3072,767]{1,0:T(8,128)(2,1)S(1)} %bitcast.1, f32[160,767]{1,0:T(8,128)S(1)} %get-tuple-element.136.middle, f32[767]{0:T(1024)S(1)} %copy-done.12), custom_call_target="tpu_custom_call" | custom-call | flops 1000 | bytes 1000 | tf_op jit(solution)/shard_map/pallas_call | solution.py:364
  113.9 2.3 %shard_map.273 = bf16[160,767]{1,0:T(8,128)(2,1)} custom-call(bf16[320,768]{1,0:T(8,128)(2,1)S(1)} %get-tuple-element.172.x0, bf16[320,768]{1,0:T(8,128)(2,1)S(1)} %collective-permute-done.20.x1, bf16[320,768]{1,0:T(8,128)(2,1)S(1)} %collective-permute-done.21.x2, bf16[320,768]{1,0:T(8,128)(2,1)S(1)} %collective-permute-done.22.x3, ...), custom_call_target="tpu_custom_call" | custom-call | flops 1000 | bytes 1000 | tf_op jit(solution)/shard_map/pallas_call | solution.py:364
  116.2 0.7 shard_map.281
  116.9 0.8 collective-permute-done.32.f2
  117.7 1.5 %shard_map.279 = (f32[24,2304]{1,0:T(8,128)}, f32[24,3072]{1,0:T(8,128)}, f32[24,767]{1,0:T(8,128)}, f32[768]{0:T(1024)}, f32[768]{0:T(1024)}, /*index=5*/f32[76...) custom-call(s32[4,2]{1,0:T(4,128)S(1)} %copy.30.lengths, ...), custom_call_target="tpu_custom_call" | custom-call | flops 1000 | bytes 1000 | tf_op jit(solution)/shard_map/pallas_call | solution.py:364
  (84 shorter events, 4.9 us)
Async XLA Ops:
  0.7 8.7 %copy-start.13 = (s32[16]{0:T(128)S(1)}, s32[16]{0:T(128)}, u32[]{:S(2)}) copy-start(s32[16]{0:T(128)} %spans.1) | copy-start | bytes 196
  0.7 8.6 %copy-start.14 = (s32[1,2]{1,0:T(1,128)S(1)}, s32[1,2]{1,0:T(1,128)}, u32[]{:S(2)}) copy-start(s32[1,2]{1,0:T(1,128)} %offsets.1) | copy-start | bytes 28
  4.7 9.4 %collective-permute-start = (bf16[240,384]{1,0:T(8,128)(2,1)}, bf16[240,384]{1,0:T(8,128)(2,1)S(1)}, u32[]{:S(2)}, u32[]{:S(2)}) collective-permute-start(bf16[240,384]{1,0:T(8,128)(2,1)} %get-tuple-element.114), channel_id=1, source_target_pairs={{0,2},{1,3},{2,0},{3,1},{4,6},{5,7},{6,4},{7,5},{8,10},{9,11},{10,... | collective-permute-start | bytes 552968 | tf_op jit(solution)/shard_map/ppermute | solution.py:859
  7.7 10.3 %collective-permute-start.1 = (bf16[240,384]{1,0:T(8,128)(2,1)}, bf16[240,384]{1,0:T(8,128)(2,1)S(1)}, u32[]{:S(2)}, u32[]{:S(2)}) collective-permute-start(bf16[240,384]{1,0:T(8,128)(2,1)} %get-tuple-element.115), channel_id=1, source_target_pairs={{0,4},{1,5},{2,6},{3,7},{4,0},{5,1},{6,2},{7,3},{8,12},{9,13},{10,... | collective-permute-start | bytes 552968 | tf_op jit(solution)/shard_map/ppermute | solution.py:859
  9.2 8.7 %collective-permute-start.2 = (bf16[240,384]{1,0:T(8,128)(2,1)}, bf16[240,384]{1,0:T(8,128)(2,1)S(1)}, u32[]{:S(2)}, u32[]{:S(2)}) collective-permute-start(bf16[240,384]{1,0:T(8,128)(2,1)} %get-tuple-element.116), channel_id=1, source_target_pairs={{0,6},{1,7},{2,4},{3,5},{4,2},{5,3},{6,0},{7,1},{8,14},{9,15},{10,... | collective-permute-start | bytes 552968 | tf_op jit(solution)/shard_map/ppermute | solution.py:859
  18.4 3.6 %collective-permute-start.3 = (bf16[640,384]{1,0:T(8,128)(2,1)S(1)}, bf16[640,384]{1,0:T(8,128)(2,1)S(1)}, u32[]{:S(2)}, u32[]{:S(2)}) collective-permute-start(bf16[640,384]{1,0:T(8,128)(2,1)S(1)} %get-tuple-element.123.own), channel_id=1, source_target_pairs={{0,1},{1,0},{2,3},{3,2},{4,5},{5,4},{6,7},{7,6},{8,9},{9,8},{10,11... | collective-permute-start | bytes 1474568 | tf_op jit(solution)/shard_map/ppermute | solution.py:863
  18.5 12.4 %collective-permute-start.7 = (bf16[160,768]{1,0:T(8,128)(2,1)S(1)}, bf16[160,768]{1,0:T(8,128)(2,1)S(1)}, u32[]{:S(2)}, u32[]{:S(2)}) collective-permute-start(bf16[160,768]{1,0:T(8,128)(2,1)S(1)} %copy-done.5), channel_id=1, source_target_pairs={{0,2},{1,3},{2,0},{3,1},{4,6},{5,7},{6,4},{7,5},{8,10},{9,11},{10,... | collective-permute-start | bytes 737288 | tf_op jit(solution)/shard_map/ppermute | solution.py:859
  19.8 12.5 %collective-permute-start.8 = (bf16[160,768]{1,0:T(8,128)(2,1)S(1)}, bf16[160,768]{1,0:T(8,128)(2,1)S(1)}, u32[]{:S(2)}, u32[]{:S(2)}) collective-permute-start(bf16[160,768]{1,0:T(8,128)(2,1)S(1)} %copy-done.5), channel_id=1, source_target_pairs={{0,4},{1,5},{2,6},{3,7},{4,0},{5,1},{6,2},{7,3},{8,12},{9,13},{10,... | collective-permute-start | bytes 737288 | tf_op jit(solution)/shard_map/ppermute | solution.py:859
  20.6 13.3 %collective-permute-start.9 = (bf16[160,768]{1,0:T(8,128)(2,1)S(1)}, bf16[160,768]{1,0:T(8,128)(2,1)S(1)}, u32[]{:S(2)}, u32[]{:S(2)}) collective-permute-start(bf16[160,768]{1,0:T(8,128)(2,1)S(1)} %copy-done.5), channel_id=1, source_target_pairs={{0,6},{1,7},{2,4},{3,5},{4,2},{5,3},{6,0},{7,1},{8,14},{9,15},{10,... | collective-permute-start | bytes 737288 | tf_op jit(solution)/shard_map/ppermute | solution.py:859
  22.0 13.9 %slice-start.2 = ((s8[4718592]{0:T(1024)(128)(4,1)}), s8[4194304]{0:T(1024)(128)(4,1)S(1)}, s32[]{:S(2)}) async-start(s8[4718592]{0:T(1024)(128)(4,1)} %bitcast.2), calls=%async_computation.2 | async-start | bytes 8388608
  22.0 13.9 %slice-start.3 = ((s8[4718592]{0:T(1024)(128)(4,1)}), s8[524288]{0:T(1024)(128)(4,1)S(1)}, s32[]{:S(2)}) async-start(s8[4718592]{0:T(1024)(128)(4,1)} %bitcast.2), calls=%async_computation.3 | async-start | bytes 1048576
  22.0 13.9 %copy-start.3 = (bf16[160,767]{1,0:T(8,128)(2,1)S(1)}, bf16[160,767]{1,0:T(8,128)(2,1)}, u32[]{:S(2)}) copy-start(bf16[160,767]{1,0:T(8,128)(2,1)} %resid.3) | copy-start | bytes 736324
  22.0 13.9 %copy-start.4 = (bf16[768,767]{1,0:T(8,128)(2,1)S(1)}, bf16[768,767]{1,0:T(8,128)(2,1)}, u32[]{:S(2)}) copy-start(bf16[768,767]{1,0:T(8,128)(2,1)} %out_weight.1) | copy-start | bytes 3534340
  22.1 13.9 %copy-start.7 = (f32[160,1]{1,0:T(8,128)S(1)}, f32[160,1]{1,0:T(8,128)}, u32[]{:S(2)}) copy-start(f32[160,1]{1,0:T(8,128)} %get-tuple-element.133.root_in) | copy-start | bytes 1924
  22.1 13.9 %copy-start.9 = (f32[3072]{0:T(1024)S(1)}, f32[3072]{0:T(1024)}, u32[]{:S(2)}) copy-start(f32[3072]{0:T(1024)} %up_bias.1) | copy-start | bytes 36868
  22.1 13.9 %copy-start.10 = (f32[767]{0:T(1024)S(1)}, f32[767]{0:T(1024)}, u32[]{:S(2)}) copy-start(f32[767]{0:T(1024)} %out_bias.1) | copy-start | bytes 9208
  22.1 13.9 %copy-start.11 = (f32[768]{0:T(1024)S(1)}, f32[768]{0:T(1024)}, u32[]{:S(2)}) copy-start(f32[768]{0:T(1024)} %gain.3) | copy-start | bytes 9220
  28.7 5.1 %collective-permute-start.4 = (bf16[80,384]{1,0:T(8,128)(2,1)S(1)}, bf16[80,384]{1,0:T(8,128)(2,1)S(1)}, u32[]{:S(2)}, u32[]{:S(2)}) collective-permute-start(bf16[80,384]{1,0:T(8,128)(2,1)S(1)} %get-tuple-element.125), channel_id=1, source_target_pairs={{0,2},{1,3},{2,0},{3,1},{4,6},{5,7},{6,4},{7,5},{8,10},{9,11},{10,... | collective-permute-start | bytes 184328 | tf_op jit(solution)/shard_map/ppermute | solution.py:859
  30.0 4.8 %collective-permute-start.5 = (bf16[80,384]{1,0:T(8,128)(2,1)S(1)}, bf16[80,384]{1,0:T(8,128)(2,1)S(1)}, u32[]{:S(2)}, u32[]{:S(2)}) collective-permute-start(bf16[80,384]{1,0:T(8,128)(2,1)S(1)} %get-tuple-element.126), channel_id=1, source_target_pairs={{0,4},{1,5},{2,6},{3,7},{4,0},{5,1},{6,2},{7,3},{8,12},{9,13},{10,... | collective-permute-start | bytes 184328 | tf_op jit(solution)/shard_map/ppermute | solution.py:859
  30.9 5.1 %collective-permute-start.6 = (bf16[80,384]{1,0:T(8,128)(2,1)S(1)}, bf16[80,384]{1,0:T(8,128)(2,1)S(1)}, u32[]{:S(2)}, u32[]{:S(2)}) collective-permute-start(bf16[80,384]{1,0:T(8,128)(2,1)S(1)} %get-tuple-element.127), channel_id=1, source_target_pairs={{0,6},{1,7},{2,4},{3,5},{4,2},{5,3},{6,0},{7,1},{8,14},{9,15},{10,... | collective-permute-start | bytes 184328 | tf_op jit(solution)/shard_map/ppermute | solution.py:859
  32.3 18.0 %collective-permute-start.13 = (bf16[160,767]{1,0:T(8,128)(2,1)S(1)}, bf16[160,767]{1,0:T(8,128)(2,1)S(1)}, u32[]{:S(2)}, u32[]{:S(2)}) collective-permute-start(bf16[160,767]{1,0:T(8,128)(2,1)S(1)} %copy-done.2), channel_id=1, source_target_pairs={{0,8},{8,0},{16,24},{24,16},{1,9},{9,1},{17,25},{25,17},{2,10},{10... | collective-permute-start | bytes 736328 | tf_op jit(solution)/shard_map/ppermute | solution.py:867
  41.1 16.9 %collective-permute-start.14 = (bf16[320,768]{1,0:T(8,128)(2,1)S(1)}, bf16[320,768]{1,0:T(8,128)(2,1)S(1)}, u32[]{:S(2)}, u32[]{:S(2)}) collective-permute-start(bf16[320,768]{1,0:T(8,128)(2,1)S(1)} %get-tuple-element.135.act_send), channel_id=1, source_target_pairs={{0,8},{8,0},{16,24},{24,16},{1,9},{9,1},{17,25},{25,17},{2,10},{10... | collective-permute-start | bytes 1474568 | tf_op jit(solution)/shard_map/ppermute | solution.py:867
  42.8 4.2 %collective-permute-start.10 = (bf16[80,384]{1,0:T(8,128)(2,1)S(1)}, bf16[80,384]{1,0:T(8,128)(2,1)S(1)}, u32[]{:S(2)}, u32[]{:S(2)}) collective-permute-start(bf16[80,384]{1,0:T(8,128)(2,1)S(1)} %get-tuple-element.138), channel_id=1, source_target_pairs={{0,2},{1,3},{2,0},{3,1},{4,6},{5,7},{6,4},{7,5},{8,10},{9,11},{10,... | collective-permute-start | bytes 184328 | tf_op jit(solution)/shard_map/ppermute | solution.py:859
  44.2 4.2 %collective-permute-start.11 = (bf16[80,384]{1,0:T(8,128)(2,1)S(1)}, bf16[80,384]{1,0:T(8,128)(2,1)S(1)}, u32[]{:S(2)}, u32[]{:S(2)}) collective-permute-start(bf16[80,384]{1,0:T(8,128)(2,1)S(1)} %get-tuple-element.139), channel_id=1, source_target_pairs={{0,4},{1,5},{2,6},{3,7},{4,0},{5,1},{6,2},{7,3},{8,12},{9,13},{10,... | collective-permute-start | bytes 184328 | tf_op jit(solution)/shard_map/ppermute | solution.py:859
  44.8 5.5 %collective-permute-start.12 = (bf16[80,384]{1,0:T(8,128)(2,1)S(1)}, bf16[80,384]{1,0:T(8,128)(2,1)S(1)}, u32[]{:S(2)}, u32[]{:S(2)}) collective-permute-start(bf16[80,384]{1,0:T(8,128)(2,1)S(1)} %get-tuple-element.140), channel_id=1, source_target_pairs={{0,6},{1,7},{2,4},{3,5},{4,2},{5,3},{6,0},{7,1},{8,14},{9,15},{10,... | collective-permute-start | bytes 184328 | tf_op jit(solution)/shard_map/ppermute | solution.py:859
  50.3 10.2 %collective-permute-start.17 = (bf16[320,768]{1,0:T(8,128)(2,1)S(1)}, bf16[320,768]{1,0:T(8,128)(2,1)S(1)}, u32[]{:S(2)}, u32[]{:S(2)}) collective-permute-start(bf16[320,768]{1,0:T(8,128)(2,1)S(1)} %get-tuple-element.158), channel_id=1, source_target_pairs={{0,2},{1,3},{2,0},{3,1},{4,6},{5,7},{6,4},{7,5},{8,10},{9,11},{10,... | collective-permute-start | bytes 1474568 | tf_op jit(solution)/shard_map/ppermute | solution.py:859
  51.5 9.1 %collective-permute-start.18 = (bf16[320,768]{1,0:T(8,128)(2,1)S(1)}, bf16[320,768]{1,0:T(8,128)(2,1)S(1)}, u32[]{:S(2)}, u32[]{:S(2)}) collective-permute-start(bf16[320,768]{1,0:T(8,128)(2,1)S(1)} %get-tuple-element.159), channel_id=1, source_target_pairs={{0,4},{1,5},{2,6},{3,7},{4,0},{5,1},{6,2},{7,3},{8,12},{9,13},{10,... | collective-permute-start | bytes 1474568 | tf_op jit(solution)/shard_map/ppermute | solution.py:859
  58.0 2.6 %collective-permute-start.15 = (bf16[320,384]{1,0:T(8,128)(2,1)S(1)}, bf16[320,384]{1,0:T(8,128)(2,1)S(1)}, u32[]{:S(2)}, u32[]{:S(2)}) collective-permute-start(bf16[320,384]{1,0:T(8,128)(2,1)S(1)} %get-tuple-element.152), channel_id=1, source_target_pairs={{0,1},{1,0},{2,3},{3,2},{4,5},{5,4},{6,7},{7,6},{8,9},{9,8},{10,11... | collective-permute-start | bytes 737288 | tf_op jit(solution)/shard_map/ppermute | solution.py:863
  58.1 2.5 %collective-permute-start.16 = (bf16[320,384]{1,0:T(8,128)(2,1)S(1)}, bf16[320,384]{1,0:T(8,128)(2,1)S(1)}, u32[]{:S(2)}, u32[]{:S(2)}) collective-permute-start(bf16[320,384]{1,0:T(8,128)(2,1)S(1)} %get-tuple-element.153), channel_id=1, source_target_pairs={{0,1},{1,0},{2,3},{3,2},{4,5},{5,4},{6,7},{7,6},{8,9},{9,8},{10,11... | collective-permute-start | bytes 737288 | tf_op jit(solution)/shard_map/ppermute | solution.py:863
  63.9 4.5 %collective-permute-start.19 = (bf16[1504,768]{1,0:T(8,128)(2,1)S(1)}, bf16[1504,768]{1,0:T(8,128)(2,1)S(1)}, u32[]{:S(2)}, u32[]{:S(2)}) collective-permute-start(bf16[1504,768]{1,0:T(8,128)(2,1)S(1)} %get-tuple-element.167.send), channel_id=1, source_target_pairs={{0,1},{1,0},{2,3},{3,2},{4,5},{5,4},{6,7},{7,6},{8,9},{9,8},{10,11... | collective-permute-start | bytes 6930440 | tf_op jit(solution)/shard_map/ppermute | solution.py:863
  64.0 14.5 %collective-permute-start.25 = (bf16[320,768]{1,0:T(8,128)(2,1)S(1)}, bf16[320,768]{1,0:T(8,128)(2,1)S(1)}, u32[]{:S(2)}, u32[]{:S(2)}) collective-permute-start(bf16[320,768]{1,0:T(8,128)(2,1)S(1)} %get-tuple-element.182), channel_id=1, source_target_pairs={{0,6},{1,7},{2,4},{3,5},{4,2},{5,3},{6,0},{7,1},{8,14},{9,15},{10,... | collective-permute-start | bytes 1474568 | tf_op jit(solution)/shard_map/ppermute | solution.py:859
  68.5 43.8 %slice-start = ((s8[4718592]{0:T(1024)(128)(4,1)}), s8[524288]{0:T(1024)(128)(4,1)S(1)}, s32[]{:S(2)}) async-start(s8[4718592]{0:T(1024)(128)(4,1)} %bitcast), calls=%async_computation | async-start | bytes 1048576
  69.0 43.2 %slice-start.1 = ((s8[4718592]{0:T(1024)(128)(4,1)}), s8[4194304]{0:T(1024)(128)(4,1)S(1)}, s32[]{:S(2)}) async-start(s8[4718592]{0:T(1024)(128)(4,1)} %bitcast), calls=%async_computation.1 | async-start | bytes 8388608
  69.0 15.8 %collective-permute-start.23 = (bf16[368,768]{1,0:T(8,128)(2,1)S(1)}, bf16[368,768]{1,0:T(8,128)(2,1)S(1)}, u32[]{:S(2)}, u32[]{:S(2)}) collective-permute-start(bf16[368,768]{1,0:T(8,128)(2,1)S(1)} %get-tuple-element.178.z_send), channel_id=1, source_target_pairs={{0,8},{8,0},{16,24},{24,16},{1,9},{9,1},{17,25},{25,17},{2,10},{10... | collective-permute-start | bytes 1695752 | tf_op jit(solution)/shard_map/ppermute | solution.py:867
  79.8 2.1 %collective-permute-start.26 = (bf16[128,768]{1,0:T(8,128)(2,1)S(1)}, bf16[128,768]{1,0:T(8,128)(2,1)S(1)}, u32[]{:S(2)}, u32[]{:S(2)}) collective-permute-start(bf16[128,768]{1,0:T(8,128)(2,1)S(1)} %get-tuple-element.184), channel_id=1, source_target_pairs={{0,1},{1,0},{2,3},{3,2},{4,5},{5,4},{6,7},{7,6},{8,9},{9,8},{10,11... | collective-permute-start | bytes 589832 | tf_op jit(solution)/shard_map/ppermute | solution.py:863
  79.8 2.9 %collective-permute-start.27 = (bf16[128,768]{1,0:T(8,128)(2,1)S(1)}, bf16[128,768]{1,0:T(8,128)(2,1)S(1)}, u32[]{:S(2)}, u32[]{:S(2)}) collective-permute-start(bf16[128,768]{1,0:T(8,128)(2,1)S(1)} %get-tuple-element.185), channel_id=1, source_target_pairs={{0,1},{1,0},{2,3},{3,2},{4,5},{5,4},{6,7},{7,6},{8,9},{9,8},{10,11... | collective-permute-start | bytes 589832 | tf_op jit(solution)/shard_map/ppermute | solution.py:863
  80.3 3.8 %collective-permute-start.28 = (bf16[128,768]{1,0:T(8,128)(2,1)S(1)}, bf16[128,768]{1,0:T(8,128)(2,1)S(1)}, u32[]{:S(2)}, u32[]{:S(2)}) collective-permute-start(bf16[128,768]{1,0:T(8,128)(2,1)S(1)} %get-tuple-element.186), channel_id=1, source_target_pairs={{0,1},{1,0},{2,3},{3,2},{4,5},{5,4},{6,7},{7,6},{8,9},{9,8},{10,11... | collective-permute-start | bytes 589832 | tf_op jit(solution)/shard_map/ppermute | solution.py:863
  80.4 18.9 %collective-permute-start.20 = (bf16[320,768]{1,0:T(8,128)(2,1)S(1)}, bf16[320,768]{1,0:T(8,128)(2,1)S(1)}, u32[]{:S(2)}, u32[]{:S(2)}) collective-permute-start(bf16[320,768]{1,0:T(8,128)(2,1)S(1)} %get-tuple-element.173), channel_id=1, source_target_pairs={{0,2},{1,3},{2,0},{3,1},{4,6},{5,7},{6,4},{7,5},{8,10},{9,11},{10,... | collective-permute-start | bytes 1474568 | tf_op jit(solution)/shard_map/ppermute | solution.py:859
  81.8 23.8 %collective-permute-start.21 = (bf16[320,768]{1,0:T(8,128)(2,1)S(1)}, bf16[320,768]{1,0:T(8,128)(2,1)S(1)}, u32[]{:S(2)}, u32[]{:S(2)}) collective-permute-start(bf16[320,768]{1,0:T(8,128)(2,1)S(1)} %get-tuple-element.174), channel_id=1, source_target_pairs={{0,4},{1,5},{2,6},{3,7},{4,0},{5,1},{6,2},{7,3},{8,12},{9,13},{10,... | collective-permute-start | bytes 1474568 | tf_op jit(solution)/shard_map/ppermute | solution.py:859
  82.7 22.9 %collective-permute-start.22 = (bf16[320,768]{1,0:T(8,128)(2,1)S(1)}, bf16[320,768]{1,0:T(8,128)(2,1)S(1)}, u32[]{:S(2)}, u32[]{:S(2)}) collective-permute-start(bf16[320,768]{1,0:T(8,128)(2,1)S(1)} %get-tuple-element.175), channel_id=1, source_target_pairs={{0,6},{1,7},{2,4},{3,5},{4,2},{5,3},{6,0},{7,1},{8,14},{9,15},{10,... | collective-permute-start | bytes 1474568 | tf_op jit(solution)/shard_map/ppermute | solution.py:859
  84.3 14.9 %collective-permute-start.29 = (bf16[2,96,768]{2,1,0:T(8,128)(2,1)S(1)}, bf16[2,96,768]{2,1,0:T(8,128)(2,1)S(1)}, u32[]{:S(2)}, u32[]{:S(2)}) collective-permute-start(bf16[2,96,768]{2,1,0:T(8,128)(2,1)S(1)} %get-tuple-element.188), channel_id=1, source_target_pairs={{0,8},{8,0},{16,24},{24,16},{1,9},{9,1},{17,25},{25,17},{2,10},{10... | collective-permute-start | bytes 884744 | tf_op jit(solution)/shard_map/ppermute | solution.py:867
  84.9 27.3 %copy-start.12 = (f32[767]{0:T(1024)S(1)}, f32[767]{0:T(1024)}, u32[]{:S(2)}) copy-start(f32[767]{0:T(1024)} %bias.1) | copy-start | bytes 9208
  84.9 23.5 %collective-permute-start.24 = (bf16[192,768]{1,0:T(8,128)(2,1)S(1)}, bf16[192,768]{1,0:T(8,128)(2,1)S(1)}, u32[]{:S(2)}, u32[]{:S(2)}) collective-permute-start(bf16[192,768]{1,0:T(8,128)(2,1)S(1)} %get-tuple-element.180.z_next), channel_id=1, source_target_pairs={{0,16},{8,24},{16,0},{24,8},{1,17},{9,25},{17,1},{25,9},{2,18},{10... | collective-permute-start | bytes 884744 | tf_op jit(solution)/shard_map/ppermute | solution.py:867
  99.2 9.3 %collective-permute-start.30 = (bf16[96,768]{1,0:T(8,128)(2,1)S(1)}, bf16[96,768]{1,0:T(8,128)(2,1)S(1)}, u32[]{:S(2)}, u32[]{:S(2)}) collective-permute-start(bf16[96,768]{1,0:T(8,128)(2,1)S(1)} %get-tuple-element.190), channel_id=1, source_target_pairs={{0,16},{8,24},{16,0},{24,8},{1,17},{9,25},{17,1},{25,9},{2,18},{10... | collective-permute-start | bytes 442376 | tf_op jit(solution)/shard_map/ppermute | solution.py:867
  105.8 10.4 %collective-permute-start.34 = (bf16[96,768]{1,0:T(8,128)(2,1)S(1)}, bf16[96,768]{1,0:T(8,128)(2,1)S(1)}, u32[]{:S(2)}, u32[]{:S(2)}) collective-permute-start(bf16[96,768]{1,0:T(8,128)(2,1)S(1)} %get-tuple-element.205), channel_id=1, source_target_pairs={{0,16},{8,24},{16,0},{24,8},{1,17},{9,25},{17,1},{25,9},{2,18},{10... | collective-permute-start | bytes 442376 | tf_op jit(solution)/shard_map/ppermute | solution.py:867
  108.7 8.3 %collective-permute-start.31 = (bf16[96,768]{1,0:T(8,128)(2,1)S(1)}, bf16[96,768]{1,0:T(8,128)(2,1)S(1)}, u32[]{:S(2)}, u32[]{:S(2)}) collective-permute-start(bf16[96,768]{1,0:T(8,128)(2,1)S(1)} %get-tuple-element.192), channel_id=1, source_target_pairs={{0,2},{1,3},{2,0},{3,1},{4,6},{5,7},{6,4},{7,5},{8,10},{9,11},{10,... | collective-permute-start | bytes 442376 | tf_op jit(solution)/shard_map/ppermute | solution.py:859
  109.6 8.2 %collective-permute-start.32 = (bf16[96,768]{1,0:T(8,128)(2,1)S(1)}, bf16[96,768]{1,0:T(8,128)(2,1)S(1)}, u32[]{:S(2)}, u32[]{:S(2)}) collective-permute-start(bf16[96,768]{1,0:T(8,128)(2,1)S(1)} %get-tuple-element.193), channel_id=1, source_target_pairs={{0,4},{1,5},{2,6},{3,7},{4,0},{5,1},{6,2},{7,3},{8,12},{9,13},{10,... | collective-permute-start | bytes 442376 | tf_op jit(solution)/shard_map/ppermute | solution.py:859
  110.7 7.0 %collective-permute-start.33 = (bf16[96,768]{1,0:T(8,128)(2,1)S(1)}, bf16[96,768]{1,0:T(8,128)(2,1)S(1)}, u32[]{:S(2)}, u32[]{:S(2)}) collective-permute-start(bf16[96,768]{1,0:T(8,128)(2,1)S(1)} %get-tuple-element.194), channel_id=1, source_target_pairs={{0,6},{1,7},{2,4},{3,5},{4,2},{5,3},{6,0},{7,1},{8,14},{9,15},{10,... | collective-permute-start | bytes 442376 | tf_op jit(solution)/shard_map/ppermute | solution.py:859
  (7 other events, 41.5 us)

commit v7 on v6

--- a/solution.py
+++ b/solution.py
@@ -720,7 +720,7 @@
         blocks.append(keep_z[r] + came[0:168])
     z_keep[0:168, :] = blocks[0]
     z_keep[168:336, :] = blocks[2]
-    sums = [hi.astype(wide)[0:12], lo.astype(wide)[0:12], jnp.zeros((8, D), wide)]
+    sums = [hi.astype(wide)[0:12], lo.astype(wide)[0:12]]
     z_send[...] = jnp.concatenate([blocks[1], blocks[3]] + sums, axis=0).astype(low)
 
 
@@ -738,7 +738,7 @@
     z_next[...] = jnp.concatenate(block, axis=0).astype(low)
 
 
-def up_grad_kernel(n0, n1, n2, n3, keep, send_one, send_two, send_three, left, right, buf):
+def up_grad_kernel(n0, n1, n2, n3, keep, send_one, send_two, left, right, buf):
     me, bucket, core = here()
     for r in range(4):
         rows = slice(r * 160, (r + 1) * 160)
@@ -752,19 +752,13 @@
             block = jnp.concatenate([up[s : s + 24] for s in starts], axis=0)
             buf[c ^ core, b ^ bucket] = block.astype(low)
     keep[...] = buf[0]
-    send_one[0:96, :] = buf[1, 0]
-    send_one[96:128, :] = buf[1, 1, 0:32, :]
-    send_two[0:64, :] = buf[1, 1, 32:96, :]
-    send_two[64:128, :] = buf[1, 2, 0:64, :]
-    send_three[0:32, :] = buf[1, 2, 64:96, :]
-    send_three[32:128, :] = buf[1, 3]
-
-
-def up_sum_kernel(keep, arrive_one, arrive_two, arrive_three, w_keep, w_send):
-    parts = [a[...].astype(wide) for a in (arrive_one, arrive_two, arrive_three)]
-    arrived = jnp.concatenate(parts, axis=0)
+    send_one[...] = buf[1, 0:2]
+    send_two[...] = buf[1, 2:4]
+
+
+def up_sum_kernel(keep, arrive_one, arrive_two, w_keep, w_send):
     for d in range(4):
-        total = keep[d].astype(wide) + arrived[d * 96 : (d + 1) * 96]
+        total = keep[d].astype(wide) + (arrive_one, arrive_two)[d // 2][d % 2].astype(wide)
         if d % 2 == 0:
             w_keep[d // 2] = total
         else:
@@ -992,7 +986,7 @@
     keep_x, keep_z, send = outs[4:]
     outs = call(
         late_sum_kernel,
-        [((320, D), low)] * 4 + [((336, D), wide), ((368, D), low)],
+        [((320, D), low)] * 4 + [((336, D), wide), ((360, D), low)],
         [keep_x, keep_z, send, swap_core(send)] + homes,
     )
     home = exchange(outs[:4])
@@ -1005,8 +999,8 @@
     z_came = shift_bucket(z_next, 2)
     keep, *send = call(
         up_grad_kernel,
-        [((4, 96, D), low)] + [((128, D), low)] * 3,
-        lates,
+        [((4, 96, D), low)] + [((2, 96, D), low)] * 2,
+        list(after(lates, z_send)),
         [pltpu.VMEM((640, D), low), pltpu.VMEM((640, D), low), pltpu.VMEM((2, 4, 96, D), low)],
     )
     w_keep, w_send = call(

time: 120 us -> 119 us (level)
    ppermute x7 -> x6, waiting for transfers between devices: 2.89 us -> 2.88 us  [swap_core(): return lax.ppermute(block, 'blk', [(k, k ^ 1) for k in range(8)])]
  transfers between devices with their start and end apart: 35 -> 34, of which waited for: 13 -> 13; matrix products, arithmetic and copies ran while one was open for 0% -> 0% of each run, Pallas kernels for 23% -> 23%
where the time goes in v7:
time: 119 us
  waiting for transfers between devices  41.9 us (35%)
  starting transfers between devices  36.8 us (31%)
  Pallas kernels  36.5 us (31%)
  local copies, waits for them, and re-layouts  2.52 us (2%)
  between operations  1.19 us (1%)
    pallas_call x19, Pallas kernels, call(): pl.pallas_call(kernel, out_shape=shapes, in_specs=[SMEM if i < small else...  36.5 us
    ppermute x21, waiting for transfers between devices, swap_chip(): return lax.ppermute(block, 'blk', [(k, k ^ 2 * step) for k in range(8)])  27.8 us
    ppermute x21, starting transfers between devices, swap_chip(): return lax.ppermute(block, 'blk', [(k, k ^ 2 * step) for k in range(8)])  25.8 us
    ppermute x7, waiting for transfers between devices, shift_bucket(): return lax.ppermute(block, 'bucket', [(b, b ^ step) for b in range(4)])  11.2 us
    ppermute x7, starting transfers between devices, shift_bucket(): return lax.ppermute(block, 'bucket', [(b, b ^ step) for b in range(4)])  9.67 us
    ppermute x6, waiting for transfers between devices, swap_core(): return lax.ppermute(block, 'blk', [(k, k ^ 1) for k in range(8)])  2.88 us
    unnamed x41, local copies, waits for them, and re-layouts  2.52 us
  transfers between devices with their start and end apart: 34, of which 13 were waited for; matrix products, arithmetic and copies ran while one was open for 0% of the time, Pallas kernels for 23%

profile of v7, /device:TPU:0, one launch (start us, length us, event | category | flops | bytes accessed | tf_op | source)
XLA Modules:
  0.0 118.9 jit_solution(2689403706409470061)
XLA Ops:
  0.7 4.0 %shard_map.264 = (bf16[240,384]{1,0:T(8,128)(2,1)}, bf16[240,384]{1,0:T(8,128)(2,1)}, bf16[240,384]{1,0:T(8,128)(2,1)}, bf16[240,384]{1,0:T(8,128)(2,1)}, bf16[160,768]{1,0:T(8,128)(2,1)}, /*index=5*/f32[160,1]{1,0:T(8,128)}) custom-call(bf16[160,767]{1,0:T(8,128)(2,1)} %resid.3, f32[768]{0:T(1024)} %gain.5, bf16[768,2304]{1,0:T(8,128)(2,1)} %weight.6, ...), custom_call_target="tpu_custom_call" | custom-call | flops 1000 | bytes 1000 | tf_op jit(solution)/shard_map/pallas_call | solution.py:364
  4.7 3.0 %collective-permute-start = (bf16[240,384]{1,0:T(8,128)(2,1)}, bf16[240,384]{1,0:T(8,128)(2,1)S(1)}, u32[]{:S(2)}, u32[]{:S(2)}) collective-permute-start(bf16[240,384]{1,0:T(8,128)(2,1)} %get-tuple-element.117), channel_id=1, source_target_pairs={{0,2},{1,3},{2,0},{3,1},{4,6},{5,7},{6,4},{7,5},{8,10},{9,11},{10,... | collective-permute-start | bytes 552968 | tf_op jit(solution)/shard_map/ppermute | solution.py:853
  7.7 1.5 %collective-permute-start.1 = (bf16[240,384]{1,0:T(8,128)(2,1)}, bf16[240,384]{1,0:T(8,128)(2,1)S(1)}, u32[]{:S(2)}, u32[]{:S(2)}) collective-permute-start(bf16[240,384]{1,0:T(8,128)(2,1)} %get-tuple-element.118), channel_id=1, source_target_pairs={{0,4},{1,5},{2,6},{3,7},{4,0},{5,1},{6,2},{7,3},{8,12},{9,13},{10,... | collective-permute-start | bytes 552968 | tf_op jit(solution)/shard_map/ppermute | solution.py:853
  9.3 2.3 %copy-done.1 = bf16[3072,767]{1,0:T(8,128)(2,1)S(1)} copy-done((bf16[3072,767]{1,0:T(8,128)(2,1)S(1)}, bf16[3072,767]{1,0:T(8,128)(2,1)}, u32[]{:S(2)}) %copy-start.1) | copy-done | bytes 4712472
  11.7 2.4 %shard_map.263 = (f32[160,3072]{1,0:T(8,128)S(1)}, s32[640,2]{1,0:T(8,128)S(1)}, s32[1,1280]{1,0:T(1,128)S(1)}) custom-call(s32[16]{0:T(128)S(1)} %copy-done.13, s32[1,2]{1,0:T(1,128)S(1)} %copy-done.14, s32[4,2]{1,0:T(4,128)S(1)} %copy.30.lengths, bf16[160,767]{1,0:T(8,128)(2,1)S(1)} %copy-done.2, bf16[3072,767]{1,0:T(8,128)(2,1)S(1)} %copy-done.1), custom_call_target="tpu_custom_call" | custom-call | flops 1000 | bytes 1000 | tf_op jit(solution)/shard_map/pallas_call | solution.py:364
  14.1 3.9 %collective-permute-done.1.p2 = bf16[240,384]{1,0:T(8,128)(2,1)S(1)} collective-permute-done((bf16[240,384]{1,0:T(8,128)(2,1)}, bf16[240,384]{1,0:T(8,128)(2,1)S(1)}, u32[]{:S(2)}, u32[]{:S(2)}) %collective-permute-start.1) | collective-permute-done | bytes 184352 | tf_op jit(solution)/shard_map/ppermute | solution.py:853
  18.5 1.3 %collective-permute-start.7 = (bf16[160,768]{1,0:T(8,128)(2,1)S(1)}, bf16[160,768]{1,0:T(8,128)(2,1)S(1)}, u32[]{:S(2)}, u32[]{:S(2)}) collective-permute-start(bf16[160,768]{1,0:T(8,128)(2,1)S(1)} %copy-done.5), channel_id=1, source_target_pairs={{0,2},{1,3},{2,0},{3,1},{4,6},{5,7},{6,4},{7,5},{8,10},{9,11},{10,... | collective-permute-start | bytes 737288 | tf_op jit(solution)/shard_map/ppermute | solution.py:853
  19.8 0.8 collective-permute-start.8
  20.6 1.4 %collective-permute-start.9 = (bf16[160,768]{1,0:T(8,128)(2,1)S(1)}, bf16[160,768]{1,0:T(8,128)(2,1)S(1)}, u32[]{:S(2)}, u32[]{:S(2)}) collective-permute-start(bf16[160,768]{1,0:T(8,128)(2,1)S(1)} %copy-done.5), channel_id=1, source_target_pairs={{0,6},{1,7},{2,4},{3,5},{4,2},{5,3},{6,0},{7,1},{8,14},{9,15},{10,... | collective-permute-start | bytes 737288 | tf_op jit(solution)/shard_map/ppermute | solution.py:853
  22.1 6.6 %shard_map.266 = (bf16[3,640,1280]{2,1,0:T(8,128)(2,1)S(1)}, f32[640,192]{1,0:T(8,128)S(1)}, bf16[80,384]{1,0:T(8,128)(2,1)S(1)}, bf16[80,384]{1,0:T(8,128)(2,1)...) custom-call(s32[640,2]{1,0:T(8,128)S(1)} %get-tuple-element.114.bounds, ...), custom_call_target="tpu_custom_call" | custom-call | flops 7700000768 | bytes 1000 | tf_op jit(solution)/shard_map/pallas_call | solution.py:364
  28.7 1.3 %collective-permute-start.4 = (bf16[80,384]{1,0:T(8,128)(2,1)S(1)}, bf16[80,384]{1,0:T(8,128)(2,1)S(1)}, u32[]{:S(2)}, u32[]{:S(2)}) collective-permute-start(bf16[80,384]{1,0:T(8,128)(2,1)S(1)} %get-tuple-element.128), channel_id=1, source_target_pairs={{0,2},{1,3},{2,0},{3,1},{4,6},{5,7},{6,4},{7,5},{8,10},{9,11},{10,... | collective-permute-start | bytes 184328 | tf_op jit(solution)/shard_map/ppermute | solution.py:853
  30.0 0.8 collective-permute-start.5
  30.9 1.4 %collective-permute-start.6 = (bf16[80,384]{1,0:T(8,128)(2,1)S(1)}, bf16[80,384]{1,0:T(8,128)(2,1)S(1)}, u32[]{:S(2)}, u32[]{:S(2)}) collective-permute-start(bf16[80,384]{1,0:T(8,128)(2,1)S(1)} %get-tuple-element.130), channel_id=1, source_target_pairs={{0,6},{1,7},{2,4},{3,5},{4,2},{5,3},{6,0},{7,1},{8,14},{9,15},{10,... | collective-permute-start | bytes 184328 | tf_op jit(solution)/shard_map/ppermute | solution.py:853
  32.3 1.6 %collective-permute-start.13 = (bf16[160,767]{1,0:T(8,128)(2,1)S(1)}, bf16[160,767]{1,0:T(8,128)(2,1)S(1)}, u32[]{:S(2)}, u32[]{:S(2)}) collective-permute-start(bf16[160,767]{1,0:T(8,128)(2,1)S(1)} %copy-done.2), channel_id=1, source_target_pairs={{0,8},{8,0},{16,24},{24,16},{1,9},{9,1},{17,25},{25,17},{2,10},{10... | collective-permute-start | bytes 736328 | tf_op jit(solution)/shard_map/ppermute | solution.py:861
  33.9 1.0 collective-permute-done.5.p2
  34.8 1.1 collective-permute-done.6.p3
  36.0 5.1 %shard_map.267 = (bf16[80,384]{1,0:T(8,128)(2,1)S(1)}, bf16[80,384]{1,0:T(8,128)(2,1)S(1)}, bf16[80,384]{1,0:T(8,128)(2,1)S(1)}, bf16[80,384]{1,0:T(8,128)(2,1)S...) custom-call(s32[640,2]{1,0:T(8,128)S(1)} %get-tuple-element.114.boun, ...), custom_call_target="tpu_custom_call" | custom-call | flops 1000 | bytes 1000 | tf_op jit(solution)/shard_map/pallas_call | solution.py:364
  41.1 1.6 %collective-permute-start.14 = (bf16[320,768]{1,0:T(8,128)(2,1)S(1)}, bf16[320,768]{1,0:T(8,128)(2,1)S(1)}, u32[]{:S(2)}, u32[]{:S(2)}) collective-permute-start(bf16[320,768]{1,0:T(8,128)(2,1)S(1)} %get-tuple-element.138.act_send), channel_id=1, source_target_pairs={{0,8},{8,0},{16,24},{24,16},{1,9},{9,1},{17,25},{25,17},{2,10},{10... | collective-permute-start | bytes 1474568 | tf_op jit(solution)/shard_map/ppermute | solution.py:861
  42.8 1.5 %collective-permute-start.10 = (bf16[80,384]{1,0:T(8,128)(2,1)S(1)}, bf16[80,384]{1,0:T(8,128)(2,1)S(1)}, u32[]{:S(2)}, u32[]{:S(2)}) collective-permute-start(bf16[80,384]{1,0:T(8,128)(2,1)S(1)} %get-tuple-element.141), channel_id=1, source_target_pairs={{0,2},{1,3},{2,0},{3,1},{4,6},{5,7},{6,4},{7,5},{8,10},{9,11},{10,... | collective-permute-start | bytes 184328 | tf_op jit(solution)/shard_map/ppermute | solution.py:853
  44.8 1.5 %collective-permute-start.12 = (bf16[80,384]{1,0:T(8,128)(2,1)S(1)}, bf16[80,384]{1,0:T(8,128)(2,1)S(1)}, u32[]{:S(2)}, u32[]{:S(2)}) collective-permute-start(bf16[80,384]{1,0:T(8,128)(2,1)S(1)} %get-tuple-element.143), channel_id=1, source_target_pairs={{0,6},{1,7},{2,4},{3,5},{4,2},{5,3},{6,0},{7,1},{8,14},{9,15},{10,... | collective-permute-start | bytes 184328 | tf_op jit(solution)/shard_map/ppermute | solution.py:853
  46.2 0.7 collective-permute-done.10.d1
  47.0 1.5 %collective-permute-done.11.d2 = bf16[80,384]{1,0:T(8,128)(2,1)S(1)} collective-permute-done((bf16[80,384]{1,0:T(8,128)(2,1)S(1)}, bf16[80,384]{1,0:T(8,128)(2,1)S(1)}, u32[]{:S(2)}, u32[]{:S(2)}) %collective-permute-start.11) | collective-permute-done | bytes 61472 | tf_op jit(solution)/shard_map/ppermute | solution.py:853
  48.5 1.8 %collective-permute-done.12.d3 = bf16[80,384]{1,0:T(8,128)(2,1)S(1)} collective-permute-done((bf16[80,384]{1,0:T(8,128)(2,1)S(1)}, bf16[80,384]{1,0:T(8,128)(2,1)S(1)}, u32[]{:S(2)}, u32[]{:S(2)}) %collective-permute-start.12) | collective-permute-done | bytes 61472 | tf_op jit(solution)/shard_map/ppermute | solution.py:853
  50.3 1.2 collective-permute-start.17
  51.5 0.9 collective-permute-start.18
  52.3 5.6 %shard_map.269 = (bf16[640,192]{1,0:T(8,128)(2,1)S(1)}, f32[640,384]{1,0:T(8,128)S(1)}, bf16[320,384]{1,0:T(8,128)(2,1)S(1)}, bf16[320,384]{1,0:T(8,128)(2,1)S(1)}) custom-call(bf16[80,384]{1,0:T(8,128)(2,1)S(1)} %get-tuple-element.145.d0, bf16[80,384]{1,0:T(8,128)(2,1)S(1)} %collective-permute-done.10.d1, bf16[80,384]{1,0:T(8,128)(2,1)S(1)} %collective-permute-done.11.d2, ...), custom_call_target="tpu_custom_call" | custom-call | flops 1000 | bytes 1000 | tf_op jit(solution)/shard_map/pallas_call | solution.py:364
  59.0 1.5 %collective-permute-done.17.n1 = bf16[320,768]{1,0:T(8,128)(2,1)S(1)} collective-permute-done((bf16[320,768]{1,0:T(8,128)(2,1)S(1)}, bf16[320,768]{1,0:T(8,128)(2,1)S(1)}, u32[]{:S(2)}, u32[]{:S(2)}) %collective-permute-start.17) | collective-permute-done | bytes 491552 | tf_op jit(solution)/shard_map/ppermute | solution.py:853
  60.6 3.3 %shard_map.271 = (bf16[240,384]{1,0:T(8,128)(2,1)S(1)}, bf16[240,384]{1,0:T(8,128)(2,1)S(1)}, bf16[240,384]{1,0:T(8,128)(2,1)S(1)}, bf16[240,384]{1,0:T(8,128)(2...) custom-call(bf16[640,192]{1,0:T(8,128)(2,1)S(1)} %get-tuple-element.151.query_g, ...), custom_call_target="tpu_custom_call" | custom-call | flops 1000 | bytes 1000 | tf_op jit(solution)/shard_map/pallas_call | solution.py:364
  64.0 1.6 %collective-permute-start.25 = (bf16[320,768]{1,0:T(8,128)(2,1)S(1)}, bf16[320,768]{1,0:T(8,128)(2,1)S(1)}, u32[]{:S(2)}, u32[]{:S(2)}) collective-permute-start(bf16[320,768]{1,0:T(8,128)(2,1)S(1)} %get-tuple-element.185), channel_id=1, source_target_pairs={{0,6},{1,7},{2,4},{3,5},{4,2},{5,3},{6,0},{7,1},{8,14},{9,15},{10,... | collective-permute-start | bytes 1474568 | tf_op jit(solution)/shard_map/ppermute | solution.py:853
  65.6 2.9 %collective-permute-done.19.arrived = bf16[1504,768]{1,0:T(8,128)(2,1)S(1)} collective-permute-done((bf16[1504,768]{1,0:T(8,128)(2,1)S(1)}, bf16[1504,768]{1,0:T(8,128)(2,1)S(1)}, u32[]{:S(2)}, u32[]{:S(2)}) %collective-permute-start.19) | collective-permute-done | bytes 2310176 | tf_op jit(solution)/shard_map/ppermute | solution.py:857
  68.5 0.6 shard_map.272
  69.6 9.0 %collective-permute-done.25.n3 = bf16[320,768]{1,0:T(8,128)(2,1)S(1)} collective-permute-done((bf16[320,768]{1,0:T(8,128)(2,1)S(1)}, bf16[320,768]{1,0:T(8,128)(2,1)S(1)}, u32[]{:S(2)}, u32[]{:S(2)}) %collective-permute-start.25) | collective-permute-done | bytes 491552 | tf_op jit(solution)/shard_map/ppermute | solution.py:853
  78.5 1.2 %shard_map.275 = (bf16[4,96,768]{2,1,0:T(8,128)(2,1)S(1)}, bf16[2,96,768]{2,1,0:T(8,128)(2,1)S(1)}, bf16[2,96,768]{2,1,0:T(8,128)(2,1)S(1)}) custom-call(bf16[320,768]{1,0:T(8,128)(2,1)S(1)} %get-tuple-element.186.n0, bf16[320,768]{1,0:T(8,128)(2,1)S(1)} %collective-permute-done.17.n1, bf16[320,768]{1,0:T(8,128)(2,1)S(1)} %collective-permute-done.18.n2, ...), custom_call_target="tpu_custom_call" | custom-call | flops 1000 | bytes 1000 | tf_op jit(solution)/shard_map/pallas_call | solution.py:364
  80.3 1.4 %collective-permute-start.20 = (bf16[320,768]{1,0:T(8,128)(2,1)S(1)}, bf16[320,768]{1,0:T(8,128)(2,1)S(1)}, u32[]{:S(2)}, u32[]{:S(2)}) collective-permute-start(bf16[320,768]{1,0:T(8,128)(2,1)S(1)} %get-tuple-element.176), channel_id=1, source_target_pairs={{0,2},{1,3},{2,0},{3,1},{4,6},{5,7},{6,4},{7,5},{8,10},{9,11},{10,... | collective-permute-start | bytes 1474568 | tf_op jit(solution)/shard_map/ppermute | solution.py:853
  81.7 0.7 collective-permute-start.21
  82.4 1.4 %collective-permute-start.22 = (bf16[320,768]{1,0:T(8,128)(2,1)S(1)}, bf16[320,768]{1,0:T(8,128)(2,1)S(1)}, u32[]{:S(2)}, u32[]{:S(2)}) collective-permute-start(bf16[320,768]{1,0:T(8,128)(2,1)S(1)} %get-tuple-element.178), channel_id=1, source_target_pairs={{0,6},{1,7},{2,4},{3,5},{4,2},{5,3},{6,0},{7,1},{8,14},{9,15},{10,... | collective-permute-start | bytes 1474568 | tf_op jit(solution)/shard_map/ppermute | solution.py:853
  84.7 2.6 %collective-permute-start.24 = (bf16[192,768]{1,0:T(8,128)(2,1)S(1)}, bf16[192,768]{1,0:T(8,128)(2,1)S(1)}, u32[]{:S(2)}, u32[]{:S(2)}) collective-permute-start(bf16[192,768]{1,0:T(8,128)(2,1)S(1)} %get-tuple-element.183.z_next), channel_id=1, source_target_pairs={{0,16},{8,24},{16,0},{24,8},{1,17},{9,25},{17,1},{25,9},{2,18},{10... | collective-permute-start | bytes 884744 | tf_op jit(solution)/shard_map/ppermute | solution.py:861
  87.3 11.2 %collective-permute-done.28.came = bf16[2,96,768]{2,1,0:T(8,128)(2,1)S(1)} collective-permute-done((bf16[2,96,768]{2,1,0:T(8,128)(2,1)S(1)}, bf16[2,96,768]{2,1,0:T(8,128)(2,1)S(1)}, u32[]{:S(2)}, u32[]{:S(2)}) %collective-permute-start.28) | collective-permute-done | bytes 294944 | tf_op jit(solution)/shard_map/ppermute | solution.py:861
  98.6 6.5 %collective-permute-done.21.x2 = bf16[320,768]{1,0:T(8,128)(2,1)S(1)} collective-permute-done((bf16[320,768]{1,0:T(8,128)(2,1)S(1)}, bf16[320,768]{1,0:T(8,128)(2,1)S(1)}, u32[]{:S(2)}, u32[]{:S(2)}) %collective-permute-start.21) | collective-permute-done | bytes 491552 | tf_op jit(solution)/shard_map/ppermute | solution.py:853
  105.3 2.7 %collective-permute-start.33 = (bf16[96,768]{1,0:T(8,128)(2,1)S(1)}, bf16[96,768]{1,0:T(8,128)(2,1)S(1)}, u32[]{:S(2)}, u32[]{:S(2)}) collective-permute-start(bf16[96,768]{1,0:T(8,128)(2,1)S(1)} %get-tuple-element.211), channel_id=1, source_target_pairs={{0,16},{8,24},{16,0},{24,8},{1,17},{9,25},{17,1},{25,9},{2,18},{10... | collective-permute-start | bytes 442376 | tf_op jit(solution)/shard_map/ppermute | solution.py:861
  108.2 0.7 collective-permute-start.30
  108.9 1.4 %collective-permute-start.31 = (bf16[96,768]{1,0:T(8,128)(2,1)S(1)}, bf16[96,768]{1,0:T(8,128)(2,1)S(1)}, u32[]{:S(2)}, u32[]{:S(2)}) collective-permute-start(bf16[96,768]{1,0:T(8,128)(2,1)S(1)} %get-tuple-element.199), channel_id=1, source_target_pairs={{0,4},{1,5},{2,6},{3,7},{4,0},{5,1},{6,2},{7,3},{8,12},{9,13},{10,... | collective-permute-start | bytes 442376 | tf_op jit(solution)/shard_map/ppermute | solution.py:853
  110.3 1.5 %collective-permute-start.32 = (bf16[96,768]{1,0:T(8,128)(2,1)S(1)}, bf16[96,768]{1,0:T(8,128)(2,1)S(1)}, u32[]{:S(2)}, u32[]{:S(2)}) collective-permute-start(bf16[96,768]{1,0:T(8,128)(2,1)S(1)} %get-tuple-element.200), channel_id=1, source_target_pairs={{0,6},{1,7},{2,4},{3,5},{4,2},{5,3},{6,0},{7,1},{8,14},{9,15},{10,... | collective-permute-start | bytes 442376 | tf_op jit(solution)/shard_map/ppermute | solution.py:853
  111.8 1.7 %shard_map.268 = bf16[160,767]{1,0:T(8,128)(2,1)} custom-call(bf16[320,768]{1,0:T(8,128)(2,1)S(1)} %get-tuple-element.137.act_keep, bf16[320,768]{1,0:T(8,128)(2,1)S(1)} %get-tuple-element.138.act_send, bf16[3072,767]{1,0:T(8,128)(2,1)S(1)} %bitcast.1, f32[160,767]{1,0:T(8,128)S(1)} %get-tuple-element.139.middle, f32[767]{0:T(1024)S(1)} %copy-done.12), custom_call_target="tpu_custom_call" | custom-call | flops 1000 | bytes 1000 | tf_op jit(solution)/shard_map/pallas_call | solution.py:364
  113.4 2.3 %shard_map.273 = bf16[160,767]{1,0:T(8,128)(2,1)} custom-call(bf16[320,768]{1,0:T(8,128)(2,1)S(1)} %get-tuple-element.175.x0, bf16[320,768]{1,0:T(8,128)(2,1)S(1)} %collective-permute-done.20.x1, bf16[320,768]{1,0:T(8,128)(2,1)S(1)} %collective-permute-done.21.x2, bf16[320,768]{1,0:T(8,128)(2,1)S(1)} %collective-permute-done.22.x3, ...), custom_call_target="tpu_custom_call" | custom-call | flops 1000 | bytes 1000 | tf_op jit(solution)/shard_map/pallas_call | solution.py:364
  115.7 0.7 shard_map.281
  116.5 0.7 collective-permute-done.31.f2
  117.2 1.5 %shard_map.279 = (f32[24,2304]{1,0:T(8,128)}, f32[24,3072]{1,0:T(8,128)}, f32[24,767]{1,0:T(8,128)}, f32[768]{0:T(1024)}, f32[768]{0:T(1024)}, /*index=5*/f32[76...) custom-call(s32[4,2]{1,0:T(4,128)S(1)} %copy.30.lengths, ...), custom_call_target="tpu_custom_call" | custom-call | flops 1000 | bytes 1000 | tf_op jit(solution)/shard_map/pallas_call | solution.py:364
  (82 shorter events, 4.8 us)
Async XLA Ops:
  0.7 8.7 %copy-start.13 = (s32[16]{0:T(128)S(1)}, s32[16]{0:T(128)}, u32[]{:S(2)}) copy-start(s32[16]{0:T(128)} %spans.1) | copy-start | bytes 196
  0.7 8.6 %copy-start.14 = (s32[1,2]{1,0:T(1,128)S(1)}, s32[1,2]{1,0:T(1,128)}, u32[]{:S(2)}) copy-start(s32[1,2]{1,0:T(1,128)} %offsets.1) | copy-start | bytes 28
  0.7 8.6 %copy-start.2 = (bf16[160,767]{1,0:T(8,128)(2,1)S(1)}, bf16[160,767]{1,0:T(8,128)(2,1)}, u32[]{:S(2)}) copy-start(bf16[160,767]{1,0:T(8,128)(2,1)} %c0.1) | copy-start | bytes 736324
  4.7 9.4 %collective-permute-start = (bf16[240,384]{1,0:T(8,128)(2,1)}, bf16[240,384]{1,0:T(8,128)(2,1)S(1)}, u32[]{:S(2)}, u32[]{:S(2)}) collective-permute-start(bf16[240,384]{1,0:T(8,128)(2,1)} %get-tuple-element.117), channel_id=1, source_target_pairs={{0,2},{1,3},{2,0},{3,1},{4,6},{5,7},{6,4},{7,5},{8,10},{9,11},{10,... | collective-permute-start | bytes 552968 | tf_op jit(solution)/shard_map/ppermute | solution.py:853
  7.7 10.3 %collective-permute-start.1 = (bf16[240,384]{1,0:T(8,128)(2,1)}, bf16[240,384]{1,0:T(8,128)(2,1)S(1)}, u32[]{:S(2)}, u32[]{:S(2)}) collective-permute-start(bf16[240,384]{1,0:T(8,128)(2,1)} %get-tuple-element.118), channel_id=1, source_target_pairs={{0,4},{1,5},{2,6},{3,7},{4,0},{5,1},{6,2},{7,3},{8,12},{9,13},{10,... | collective-permute-start | bytes 552968 | tf_op jit(solution)/shard_map/ppermute | solution.py:853
  9.2 8.7 %collective-permute-start.2 = (bf16[240,384]{1,0:T(8,128)(2,1)}, bf16[240,384]{1,0:T(8,128)(2,1)S(1)}, u32[]{:S(2)}, u32[]{:S(2)}) collective-permute-start(bf16[240,384]{1,0:T(8,128)(2,1)} %get-tuple-element.119), channel_id=1, source_target_pairs={{0,6},{1,7},{2,4},{3,5},{4,2},{5,3},{6,0},{7,1},{8,14},{9,15},{10,... | collective-permute-start | bytes 552968 | tf_op jit(solution)/shard_map/ppermute | solution.py:853
  18.4 3.6 %collective-permute-start.3 = (bf16[640,384]{1,0:T(8,128)(2,1)S(1)}, bf16[640,384]{1,0:T(8,128)(2,1)S(1)}, u32[]{:S(2)}, u32[]{:S(2)}) collective-permute-start(bf16[640,384]{1,0:T(8,128)(2,1)S(1)} %get-tuple-element.126.own), channel_id=1, source_target_pairs={{0,1},{1,0},{2,3},{3,2},{4,5},{5,4},{6,7},{7,6},{8,9},{9,8},{10,11... | collective-permute-start | bytes 1474568 | tf_op jit(solution)/shard_map/ppermute | solution.py:857
  18.5 12.4 %collective-permute-start.7 = (bf16[160,768]{1,0:T(8,128)(2,1)S(1)}, bf16[160,768]{1,0:T(8,128)(2,1)S(1)}, u32[]{:S(2)}, u32[]{:S(2)}) collective-permute-start(bf16[160,768]{1,0:T(8,128)(2,1)S(1)} %copy-done.5), channel_id=1, source_target_pairs={{0,2},{1,3},{2,0},{3,1},{4,6},{5,7},{6,4},{7,5},{8,10},{9,11},{10,... | collective-permute-start | bytes 737288 | tf_op jit(solution)/shard_map/ppermute | solution.py:853
  19.8 12.5 %collective-permute-start.8 = (bf16[160,768]{1,0:T(8,128)(2,1)S(1)}, bf16[160,768]{1,0:T(8,128)(2,1)S(1)}, u32[]{:S(2)}, u32[]{:S(2)}) collective-permute-start(bf16[160,768]{1,0:T(8,128)(2,1)S(1)} %copy-done.5), channel_id=1, source_target_pairs={{0,4},{1,5},{2,6},{3,7},{4,0},{5,1},{6,2},{7,3},{8,12},{9,13},{10,... | collective-permute-start | bytes 737288 | tf_op jit(solution)/shard_map/ppermute | solution.py:853
  20.6 13.3 %collective-permute-start.9 = (bf16[160,768]{1,0:T(8,128)(2,1)S(1)}, bf16[160,768]{1,0:T(8,128)(2,1)S(1)}, u32[]{:S(2)}, u32[]{:S(2)}) collective-permute-start(bf16[160,768]{1,0:T(8,128)(2,1)S(1)} %copy-done.5), channel_id=1, source_target_pairs={{0,6},{1,7},{2,4},{3,5},{4,2},{5,3},{6,0},{7,1},{8,14},{9,15},{10,... | collective-permute-start | bytes 737288 | tf_op jit(solution)/shard_map/ppermute | solution.py:853
  22.0 13.9 %slice-start.2 = ((s8[4718592]{0:T(1024)(128)(4,1)}), s8[4194304]{0:T(1024)(128)(4,1)S(1)}, s32[]{:S(2)}) async-start(s8[4718592]{0:T(1024)(128)(4,1)} %bitcast.2), calls=%async_computation.2 | async-start | bytes 8388608
  22.0 13.9 %slice-start.3 = ((s8[4718592]{0:T(1024)(128)(4,1)}), s8[524288]{0:T(1024)(128)(4,1)S(1)}, s32[]{:S(2)}) async-start(s8[4718592]{0:T(1024)(128)(4,1)} %bitcast.2), calls=%async_computation.3 | async-start | bytes 1048576
  22.0 13.9 %copy-start.3 = (bf16[160,767]{1,0:T(8,128)(2,1)S(1)}, bf16[160,767]{1,0:T(8,128)(2,1)}, u32[]{:S(2)}) copy-start(bf16[160,767]{1,0:T(8,128)(2,1)} %resid.3) | copy-start | bytes 736324
  22.0 13.9 %copy-start.4 = (bf16[768,767]{1,0:T(8,128)(2,1)S(1)}, bf16[768,767]{1,0:T(8,128)(2,1)}, u32[]{:S(2)}) copy-start(bf16[768,767]{1,0:T(8,128)(2,1)} %out_weight.1) | copy-start | bytes 3534340
  22.1 13.9 %copy-start.7 = (f32[160,1]{1,0:T(8,128)S(1)}, f32[160,1]{1,0:T(8,128)}, u32[]{:S(2)}) copy-start(f32[160,1]{1,0:T(8,128)} %get-tuple-element.136.root_in) | copy-start | bytes 1924
  22.1 13.9 %copy-start.9 = (f32[3072]{0:T(1024)S(1)}, f32[3072]{0:T(1024)}, u32[]{:S(2)}) copy-start(f32[3072]{0:T(1024)} %up_bias.1) | copy-start | bytes 36868
  22.1 13.9 %copy-start.10 = (f32[767]{0:T(1024)S(1)}, f32[767]{0:T(1024)}, u32[]{:S(2)}) copy-start(f32[767]{0:T(1024)} %out_bias.1) | copy-start | bytes 9208
  22.1 13.9 %copy-start.11 = (f32[768]{0:T(1024)S(1)}, f32[768]{0:T(1024)}, u32[]{:S(2)}) copy-start(f32[768]{0:T(1024)} %gain.3) | copy-start | bytes 9220
  28.7 5.1 %collective-permute-start.4 = (bf16[80,384]{1,0:T(8,128)(2,1)S(1)}, bf16[80,384]{1,0:T(8,128)(2,1)S(1)}, u32[]{:S(2)}, u32[]{:S(2)}) collective-permute-start(bf16[80,384]{1,0:T(8,128)(2,1)S(1)} %get-tuple-element.128), channel_id=1, source_target_pairs={{0,2},{1,3},{2,0},{3,1},{4,6},{5,7},{6,4},{7,5},{8,10},{9,11},{10,... | collective-permute-start | bytes 184328 | tf_op jit(solution)/shard_map/ppermute | solution.py:853
  30.0 4.8 %collective-permute-start.5 = (bf16[80,384]{1,0:T(8,128)(2,1)S(1)}, bf16[80,384]{1,0:T(8,128)(2,1)S(1)}, u32[]{:S(2)}, u32[]{:S(2)}) collective-permute-start(bf16[80,384]{1,0:T(8,128)(2,1)S(1)} %get-tuple-element.129), channel_id=1, source_target_pairs={{0,4},{1,5},{2,6},{3,7},{4,0},{5,1},{6,2},{7,3},{8,12},{9,13},{10,... | collective-permute-start | bytes 184328 | tf_op jit(solution)/shard_map/ppermute | solution.py:853
  30.9 5.1 %collective-permute-start.6 = (bf16[80,384]{1,0:T(8,128)(2,1)S(1)}, bf16[80,384]{1,0:T(8,128)(2,1)S(1)}, u32[]{:S(2)}, u32[]{:S(2)}) collective-permute-start(bf16[80,384]{1,0:T(8,128)(2,1)S(1)} %get-tuple-element.130), channel_id=1, source_target_pairs={{0,6},{1,7},{2,4},{3,5},{4,2},{5,3},{6,0},{7,1},{8,14},{9,15},{10,... | collective-permute-start | bytes 184328 | tf_op jit(solution)/shard_map/ppermute | solution.py:853
  32.3 18.0 %collective-permute-start.13 = (bf16[160,767]{1,0:T(8,128)(2,1)S(1)}, bf16[160,767]{1,0:T(8,128)(2,1)S(1)}, u32[]{:S(2)}, u32[]{:S(2)}) collective-permute-start(bf16[160,767]{1,0:T(8,128)(2,1)S(1)} %copy-done.2), channel_id=1, source_target_pairs={{0,8},{8,0},{16,24},{24,16},{1,9},{9,1},{17,25},{25,17},{2,10},{10... | collective-permute-start | bytes 736328 | tf_op jit(solution)/shard_map/ppermute | solution.py:861
  41.1 16.9 %collective-permute-start.14 = (bf16[320,768]{1,0:T(8,128)(2,1)S(1)}, bf16[320,768]{1,0:T(8,128)(2,1)S(1)}, u32[]{:S(2)}, u32[]{:S(2)}) collective-permute-start(bf16[320,768]{1,0:T(8,128)(2,1)S(1)} %get-tuple-element.138.act_send), channel_id=1, source_target_pairs={{0,8},{8,0},{16,24},{24,16},{1,9},{9,1},{17,25},{25,17},{2,10},{10... | collective-permute-start | bytes 1474568 | tf_op jit(solution)/shard_map/ppermute | solution.py:861
  42.8 4.2 %collective-permute-start.10 = (bf16[80,384]{1,0:T(8,128)(2,1)S(1)}, bf16[80,384]{1,0:T(8,128)(2,1)S(1)}, u32[]{:S(2)}, u32[]{:S(2)}) collective-permute-start(bf16[80,384]{1,0:T(8,128)(2,1)S(1)} %get-tuple-element.141), channel_id=1, source_target_pairs={{0,2},{1,3},{2,0},{3,1},{4,6},{5,7},{6,4},{7,5},{8,10},{9,11},{10,... | collective-permute-start | bytes 184328 | tf_op jit(solution)/shard_map/ppermute | solution.py:853
  44.2 4.2 %collective-permute-start.11 = (bf16[80,384]{1,0:T(8,128)(2,1)S(1)}, bf16[80,384]{1,0:T(8,128)(2,1)S(1)}, u32[]{:S(2)}, u32[]{:S(2)}) collective-permute-start(bf16[80,384]{1,0:T(8,128)(2,1)S(1)} %get-tuple-element.142), channel_id=1, source_target_pairs={{0,4},{1,5},{2,6},{3,7},{4,0},{5,1},{6,2},{7,3},{8,12},{9,13},{10,... | collective-permute-start | bytes 184328 | tf_op jit(solution)/shard_map/ppermute | solution.py:853
  44.8 5.5 %collective-permute-start.12 = (bf16[80,384]{1,0:T(8,128)(2,1)S(1)}, bf16[80,384]{1,0:T(8,128)(2,1)S(1)}, u32[]{:S(2)}, u32[]{:S(2)}) collective-permute-start(bf16[80,384]{1,0:T(8,128)(2,1)S(1)} %get-tuple-element.143), channel_id=1, source_target_pairs={{0,6},{1,7},{2,4},{3,5},{4,2},{5,3},{6,0},{7,1},{8,14},{9,15},{10,... | collective-permute-start | bytes 184328 | tf_op jit(solution)/shard_map/ppermute | solution.py:853
  50.3 10.2 %collective-permute-start.17 = (bf16[320,768]{1,0:T(8,128)(2,1)S(1)}, bf16[320,768]{1,0:T(8,128)(2,1)S(1)}, u32[]{:S(2)}, u32[]{:S(2)}) collective-permute-start(bf16[320,768]{1,0:T(8,128)(2,1)S(1)} %get-tuple-element.161), channel_id=1, source_target_pairs={{0,2},{1,3},{2,0},{3,1},{4,6},{5,7},{6,4},{7,5},{8,10},{9,11},{10,... | collective-permute-start | bytes 1474568 | tf_op jit(solution)/shard_map/ppermute | solution.py:853
  51.5 9.1 %collective-permute-start.18 = (bf16[320,768]{1,0:T(8,128)(2,1)S(1)}, bf16[320,768]{1,0:T(8,128)(2,1)S(1)}, u32[]{:S(2)}, u32[]{:S(2)}) collective-permute-start(bf16[320,768]{1,0:T(8,128)(2,1)S(1)} %get-tuple-element.162), channel_id=1, source_target_pairs={{0,4},{1,5},{2,6},{3,7},{4,0},{5,1},{6,2},{7,3},{8,12},{9,13},{10,... | collective-permute-start | bytes 1474568 | tf_op jit(solution)/shard_map/ppermute | solution.py:853
  58.0 2.6 %collective-permute-start.15 = (bf16[320,384]{1,0:T(8,128)(2,1)S(1)}, bf16[320,384]{1,0:T(8,128)(2,1)S(1)}, u32[]{:S(2)}, u32[]{:S(2)}) collective-permute-start(bf16[320,384]{1,0:T(8,128)(2,1)S(1)} %get-tuple-element.155), channel_id=1, source_target_pairs={{0,1},{1,0},{2,3},{3,2},{4,5},{5,4},{6,7},{7,6},{8,9},{9,8},{10,11... | collective-permute-start | bytes 737288 | tf_op jit(solution)/shard_map/ppermute | solution.py:857
  58.1 2.5 %collective-permute-start.16 = (bf16[320,384]{1,0:T(8,128)(2,1)S(1)}, bf16[320,384]{1,0:T(8,128)(2,1)S(1)}, u32[]{:S(2)}, u32[]{:S(2)}) collective-permute-start(bf16[320,384]{1,0:T(8,128)(2,1)S(1)} %get-tuple-element.156), channel_id=1, source_target_pairs={{0,1},{1,0},{2,3},{3,2},{4,5},{5,4},{6,7},{7,6},{8,9},{9,8},{10,11... | collective-permute-start | bytes 737288 | tf_op jit(solution)/shard_map/ppermute | solution.py:857
  63.9 4.5 %collective-permute-start.19 = (bf16[1504,768]{1,0:T(8,128)(2,1)S(1)}, bf16[1504,768]{1,0:T(8,128)(2,1)S(1)}, u32[]{:S(2)}, u32[]{:S(2)}) collective-permute-start(bf16[1504,768]{1,0:T(8,128)(2,1)S(1)} %get-tuple-element.170.send), channel_id=1, source_target_pairs={{0,1},{1,0},{2,3},{3,2},{4,5},{5,4},{6,7},{7,6},{8,9},{9,8},{10,11... | collective-permute-start | bytes 6930440 | tf_op jit(solution)/shard_map/ppermute | solution.py:857
  64.0 14.5 %collective-permute-start.25 = (bf16[320,768]{1,0:T(8,128)(2,1)S(1)}, bf16[320,768]{1,0:T(8,128)(2,1)S(1)}, u32[]{:S(2)}, u32[]{:S(2)}) collective-permute-start(bf16[320,768]{1,0:T(8,128)(2,1)S(1)} %get-tuple-element.185), channel_id=1, source_target_pairs={{0,6},{1,7},{2,4},{3,5},{4,2},{5,3},{6,0},{7,1},{8,14},{9,15},{10,... | collective-permute-start | bytes 1474568 | tf_op jit(solution)/shard_map/ppermute | solution.py:853
  68.5 43.3 %slice-start = ((s8[4718592]{0:T(1024)(128)(4,1)}), s8[524288]{0:T(1024)(128)(4,1)S(1)}, s32[]{:S(2)}) async-start(s8[4718592]{0:T(1024)(128)(4,1)} %bitcast), calls=%async_computation | async-start | bytes 1048576
  69.0 42.8 %slice-start.1 = ((s8[4718592]{0:T(1024)(128)(4,1)}), s8[4194304]{0:T(1024)(128)(4,1)S(1)}, s32[]{:S(2)}) async-start(s8[4718592]{0:T(1024)(128)(4,1)} %bitcast), calls=%async_computation.1 | async-start | bytes 8388608
  69.0 15.5 %collective-permute-start.23 = (bf16[360,768]{1,0:T(8,128)(2,1)S(1)}, bf16[360,768]{1,0:T(8,128)(2,1)S(1)}, u32[]{:S(2)}, u32[]{:S(2)}) collective-permute-start(bf16[360,768]{1,0:T(8,128)(2,1)S(1)} %get-tuple-element.181.z_send), channel_id=1, source_target_pairs={{0,8},{8,0},{16,24},{24,16},{1,9},{9,1},{17,25},{25,17},{2,10},{10... | collective-permute-start | bytes 1658888 | tf_op jit(solution)/shard_map/ppermute | solution.py:861
  79.8 2.7 %collective-permute-start.26 = (bf16[2,96,768]{2,1,0:T(8,128)(2,1)S(1)}, bf16[2,96,768]{2,1,0:T(8,128)(2,1)S(1)}, u32[]{:S(2)}, u32[]{:S(2)}) collective-permute-start(bf16[2,96,768]{2,1,0:T(8,128)(2,1)S(1)} %get-tuple-element.191), channel_id=1, source_target_pairs={{0,1},{1,0},{2,3},{3,2},{4,5},{5,4},{6,7},{7,6},{8,9},{9,8},{10,11... | collective-permute-start | bytes 884744 | tf_op jit(solution)/shard_map/ppermute | solution.py:857
  79.8 4.0 %collective-permute-start.27 = (bf16[2,96,768]{2,1,0:T(8,128)(2,1)S(1)}, bf16[2,96,768]{2,1,0:T(8,128)(2,1)S(1)}, u32[]{:S(2)}, u32[]{:S(2)}) collective-permute-start(bf16[2,96,768]{2,1,0:T(8,128)(2,1)S(1)} %get-tuple-element.192), channel_id=1, source_target_pairs={{0,1},{1,0},{2,3},{3,2},{4,5},{5,4},{6,7},{7,6},{8,9},{9,8},{10,11... | collective-permute-start | bytes 884744 | tf_op jit(solution)/shard_map/ppermute | solution.py:857
  80.3 18.3 %collective-permute-start.20 = (bf16[320,768]{1,0:T(8,128)(2,1)S(1)}, bf16[320,768]{1,0:T(8,128)(2,1)S(1)}, u32[]{:S(2)}, u32[]{:S(2)}) collective-permute-start(bf16[320,768]{1,0:T(8,128)(2,1)S(1)} %get-tuple-element.176), channel_id=1, source_target_pairs={{0,2},{1,3},{2,0},{3,1},{4,6},{5,7},{6,4},{7,5},{8,10},{9,11},{10,... | collective-permute-start | bytes 1474568 | tf_op jit(solution)/shard_map/ppermute | solution.py:853
  81.7 23.5 %collective-permute-start.21 = (bf16[320,768]{1,0:T(8,128)(2,1)S(1)}, bf16[320,768]{1,0:T(8,128)(2,1)S(1)}, u32[]{:S(2)}, u32[]{:S(2)}) collective-permute-start(bf16[320,768]{1,0:T(8,128)(2,1)S(1)} %get-tuple-element.177), channel_id=1, source_target_pairs={{0,4},{1,5},{2,6},{3,7},{4,0},{5,1},{6,2},{7,3},{8,12},{9,13},{10,... | collective-permute-start | bytes 1474568 | tf_op jit(solution)/shard_map/ppermute | solution.py:853
  82.4 22.8 %collective-permute-start.22 = (bf16[320,768]{1,0:T(8,128)(2,1)S(1)}, bf16[320,768]{1,0:T(8,128)(2,1)S(1)}, u32[]{:S(2)}, u32[]{:S(2)}) collective-permute-start(bf16[320,768]{1,0:T(8,128)(2,1)S(1)} %get-tuple-element.178), channel_id=1, source_target_pairs={{0,6},{1,7},{2,4},{3,5},{4,2},{5,3},{6,0},{7,1},{8,14},{9,15},{10,... | collective-permute-start | bytes 1474568 | tf_op jit(solution)/shard_map/ppermute | solution.py:853
  84.0 14.5 %collective-permute-start.28 = (bf16[2,96,768]{2,1,0:T(8,128)(2,1)S(1)}, bf16[2,96,768]{2,1,0:T(8,128)(2,1)S(1)}, u32[]{:S(2)}, u32[]{:S(2)}) collective-permute-start(bf16[2,96,768]{2,1,0:T(8,128)(2,1)S(1)} %get-tuple-element.194), channel_id=1, source_target_pairs={{0,8},{8,0},{16,24},{24,16},{1,9},{9,1},{17,25},{25,17},{2,10},{10... | collective-permute-start | bytes 884744 | tf_op jit(solution)/shard_map/ppermute | solution.py:861
  84.6 27.1 %copy-start.12 = (f32[767]{0:T(1024)S(1)}, f32[767]{0:T(1024)}, u32[]{:S(2)}) copy-start(f32[767]{0:T(1024)} %bias.1) | copy-start | bytes 9208
  84.7 23.4 %collective-permute-start.24 = (bf16[192,768]{1,0:T(8,128)(2,1)S(1)}, bf16[192,768]{1,0:T(8,128)(2,1)S(1)}, u32[]{:S(2)}, u32[]{:S(2)}) collective-permute-start(bf16[192,768]{1,0:T(8,128)(2,1)S(1)} %get-tuple-element.183.z_next), channel_id=1, source_target_pairs={{0,16},{8,24},{16,0},{24,8},{1,17},{9,25},{17,1},{25,9},{2,18},{10... | collective-permute-start | bytes 884744 | tf_op jit(solution)/shard_map/ppermute | solution.py:861
  98.6 9.5 %collective-permute-start.29 = (bf16[96,768]{1,0:T(8,128)(2,1)S(1)}, bf16[96,768]{1,0:T(8,128)(2,1)S(1)}, u32[]{:S(2)}, u32[]{:S(2)}) collective-permute-start(bf16[96,768]{1,0:T(8,128)(2,1)S(1)} %get-tuple-element.196), channel_id=1, source_target_pairs={{0,16},{8,24},{16,0},{24,8},{1,17},{9,25},{17,1},{25,9},{2,18},{10... | collective-permute-start | bytes 442376 | tf_op jit(solution)/shard_map/ppermute | solution.py:861
  105.3 10.4 %collective-permute-start.33 = (bf16[96,768]{1,0:T(8,128)(2,1)S(1)}, bf16[96,768]{1,0:T(8,128)(2,1)S(1)}, u32[]{:S(2)}, u32[]{:S(2)}) collective-permute-start(bf16[96,768]{1,0:T(8,128)(2,1)S(1)} %get-tuple-element.211), channel_id=1, source_target_pairs={{0,16},{8,24},{16,0},{24,8},{1,17},{9,25},{17,1},{25,9},{2,18},{10... | collective-permute-start | bytes 442376 | tf_op jit(solution)/shard_map/ppermute | solution.py:861
  108.2 8.3 %collective-permute-start.30 = (bf16[96,768]{1,0:T(8,128)(2,1)S(1)}, bf16[96,768]{1,0:T(8,128)(2,1)S(1)}, u32[]{:S(2)}, u32[]{:S(2)}) collective-permute-start(bf16[96,768]{1,0:T(8,128)(2,1)S(1)} %get-tuple-element.198), channel_id=1, source_target_pairs={{0,2},{1,3},{2,0},{3,1},{4,6},{5,7},{6,4},{7,5},{8,10},{9,11},{10,... | collective-permute-start | bytes 442376 | tf_op jit(solution)/shard_map/ppermute | solution.py:853
  108.9 8.3 %collective-permute-start.31 = (bf16[96,768]{1,0:T(8,128)(2,1)S(1)}, bf16[96,768]{1,0:T(8,128)(2,1)S(1)}, u32[]{:S(2)}, u32[]{:S(2)}) collective-permute-start(bf16[96,768]{1,0:T(8,128)(2,1)S(1)} %get-tuple-element.199), channel_id=1, source_target_pairs={{0,4},{1,5},{2,6},{3,7},{4,0},{5,1},{6,2},{7,3},{8,12},{9,13},{10,... | collective-permute-start | bytes 442376 | tf_op jit(solution)/shard_map/ppermute | solution.py:853
  110.3 6.9 %collective-permute-start.32 = (bf16[96,768]{1,0:T(8,128)(2,1)S(1)}, bf16[96,768]{1,0:T(8,128)(2,1)S(1)}, u32[]{:S(2)}, u32[]{:S(2)}) collective-permute-start(bf16[96,768]{1,0:T(8,128)(2,1)S(1)} %get-tuple-element.200), channel_id=1, source_target_pairs={{0,6},{1,7},{2,4},{3,5},{4,2},{5,3},{6,0},{7,1},{8,14},{9,15},{10,... | collective-permute-start | bytes 442376 | tf_op jit(solution)/shard_map/ppermute | solution.py:853
  (6 other events, 32.8 us)
